TPU v7x, 32 devices: a whole 2x2x4 slice. The times are simulated.
32 devices in a mesh: parts: 2 (over x), fsdp: 16 (over z, y, core).
Axes of the slice: x: 2, y: 2, z: 4, core: 2. Of those that a mesh axis runs over, the one named last changes fastest.
Arguments:
- inputs: bfloat16 [8192, 8192], P(('parts', 'fsdp')), parts along dimension 0, may hold values from -6 to 6
- cotangent: bfloat16 [8192, 1024], P(('parts', 'fsdp')), parts along dimension 0, may hold values from -1.5 to 1.5
- frozen_value_weight: bfloat16 [8192, 1024], P('fsdp'), may hold values from -0.0625 to 0.0625
- adapter_down_weights: bfloat16 [1024, 131072], P('parts', 'fsdp'), parts along dimension 0, may hold values from -0.0625 to 0.0625
- adapter_up_weights: bfloat16 [1024, 16384], P('parts', 'fsdp'), parts along dimension 0, may hold values from -0.1875 to 0.1875
- padded_block_adapter: int32 [64], P('parts'), parts along dimension 0, may hold values from 0 to 511
- block_live_rows: int32 [64], P('parts'), parts along dimension 0, may hold values from 1 to 128, 2560 in all
- adapter_storage_row: int32 [1024], P('parts'), parts along dimension 0, may hold values from 0 to 511, each once
Outputs:
- input_gradient: bfloat16 [8192, 8192], P(('parts', 'fsdp')), parts along dimension 0
- down_grad: float32 [1024, 131072], P('parts', 'fsdp'), parts along dimension 0
- up_grad: float32 [1024, 16384], P('parts', 'fsdp'), parts along dimension 0
There are 2 independent parts, one for each index of `parts`. A program takes and returns all parts, laid end to end along the dimension named above; an argument that names none is the same for every part. Nothing has to cross between parts.
Inputs may be any that keep to these rules, and one draw needn't show every extreme that they name: `padded_block_adapter`: adapter ids below 512. `adapter_storage_row`: a permutation of the storage rows.
All inputs are finite; a program needn't handle non-finite values.
Results may differ from a plain program's by a relative error of at most 0.0032.
Values may be sent and summed in bfloat16 or wider, within the bound.
No kernel may reach another device: no remote copies, remote signals or barrier semaphores. Data moves between devices by JAX's collectives and lax.ppermute only.
A program may use at most 128 MiB of HBM per device.

v0:
```python
import jax
import jax.numpy as jnp
from jax import lax
from jax.sharding import PartitionSpec as P

ADAPTER_RANK = 16
ADAPTER_GROUP = 512
BLOCK = 128


adapter_scale = 2.0


def slot_lookup(padded_block_adapter, adapter_storage_row):
    matches = padded_block_adapter[:, None] == jnp.arange(ADAPTER_GROUP, dtype=jnp.int32)[None, :]
    return jnp.sum(jnp.where(matches, adapter_storage_row[None, :], 0), axis=1)


def body(
    inputs,
    cotangent,
    frozen_value_weight,
    adapter_down_weights,
    adapter_up_weights,
    padded_block_adapter,
    block_live_rows,
    adapter_storage_row,
):
    hidden_width = inputs.shape[1]
    kv_width = cotangent.shape[1]
    token_rows = inputs.shape[0]
    block_count = token_rows // BLOCK
    first_block = lax.axis_index("fsdp") * block_count
    live_rows = lax.dynamic_slice_in_dim(block_live_rows, first_block, block_count)
    positions = jnp.arange(BLOCK, dtype=jnp.int32)
    live_mask = positions[None, :] < live_rows[:, None]
    blocked_cot = cotangent.reshape(block_count, BLOCK, kv_width)
    masked_blocks = jnp.where(live_mask[:, :, None], blocked_cot, jnp.zeros_like(blocked_cot))
    masked = masked_blocks.reshape(token_rows, kv_width)
    block_storage_row = slot_lookup(padded_block_adapter, adapter_storage_row)
    down_weight_rows = jnp.take(adapter_down_weights, block_storage_row, axis=0)
    up_weight_rows = jnp.take(adapter_up_weights, block_storage_row, axis=0)
    down_mine, up_mine = (
        lax.all_to_all(down_weight_rows, "fsdp", split_axis=0, concat_axis=1, tiled=True),
        lax.all_to_all(up_weight_rows, "fsdp", split_axis=0, concat_axis=1, tiled=True),
    )
    frozen_gradient = lax.dot_general(
        masked,
        lax.all_gather(frozen_value_weight, "fsdp", axis=0, tiled=True),
        (((1,), (1,)), ((), ())),
        preferred_element_type=jnp.float32,
    )
    down_weight_matrix = down_mine.reshape(block_count, hidden_width, ADAPTER_RANK)
    up_weight_matrix = up_mine.reshape(block_count, ADAPTER_RANK, kv_width)
    blocked_in = inputs.reshape(block_count, BLOCK, hidden_width)
    rank_projection = jnp.einsum(
        "kbd,kdr->kbr", blocked_in, down_weight_matrix, preferred_element_type=jnp.float32
    ).astype(jnp.bfloat16)
    rank_space_gradient = jnp.einsum(
        "kbv,krv->kbr", masked_blocks, up_weight_matrix, preferred_element_type=jnp.float32
    ).astype(jnp.bfloat16)
    adapter_gradient_term = adapter_scale * jnp.einsum(
        "kbr,kdr->kbd", rank_space_gradient, down_weight_matrix, preferred_element_type=jnp.float32
    )
    input_gradient = (
        frozen_gradient + adapter_gradient_term.reshape(token_rows, hidden_width)
    ).astype(jnp.bfloat16)
    partial_down_weight = adapter_scale * jnp.einsum(
        "kbd,kbr->kdr", blocked_in, rank_space_gradient, preferred_element_type=jnp.float32
    )
    partial_up_weight = adapter_scale * jnp.einsum(
        "kbr,kbv->krv", rank_projection, masked_blocks, preferred_element_type=jnp.float32
    )
    partial_down_weight = partial_down_weight.reshape(block_count, hidden_width * ADAPTER_RANK)
    partial_up_weight = partial_up_weight.reshape(block_count, ADAPTER_RANK * kv_width)
    recv_down, recv_up = (
        lax.all_to_all(partial_down_weight, "fsdp", split_axis=1, concat_axis=0, tiled=True),
        lax.all_to_all(partial_up_weight, "fsdp", split_axis=1, concat_axis=0, tiled=True),
    )
    onehot = (
        jnp.arange(ADAPTER_GROUP, dtype=jnp.int32)[:, None] == block_storage_row[None, :]
    ).astype(jnp.float32)
    highest_precision = lax.Precision.HIGHEST
    down_grad = jnp.dot(
        onehot, recv_down, precision=highest_precision, preferred_element_type=jnp.float32
    )
    up_grad = jnp.dot(
        onehot, recv_up, precision=highest_precision, preferred_element_type=jnp.float32
    )
    return (input_gradient, down_grad, up_grad)


def solution(mesh):
    in_specs = (
        P(("parts", "fsdp"), None),
        P(("parts", "fsdp"), None),
        P("fsdp", None),
        P("parts", "fsdp"),
        P("parts", "fsdp"),
        P("parts"),
        P("parts"),
        P("parts"),
    )
    out_specs = (P(("parts", "fsdp"), None), P("parts", "fsdp"), P("parts", "fsdp"))
    return jax.shard_map(body, mesh=mesh, in_specs=in_specs, out_specs=out_specs, check_vma=False)
```

profile of v0, /device:TPU:0, one launch (start us, length us, event | category | flops | bytes accessed | tf_op | source)
XLA Modules:
  0.0 192.8 jit_solution(1412775038539448002)
XLA Ops:
  7.2 0.0 copy-start
  7.2 0.0 all-gather.2.cloned.1.call-start
  7.2 0.7 all-gather.2.cloned.1.call-update
  7.9 0.9 select_reduce_fusion
  8.8 0.1 reduce_sum.14
  8.9 0.0 copy-done
  8.9 0.6 gather_fusion
  9.5 0.0 copy-start.3
  9.5 0.0 copy-start.2
  9.6 0.8 broadcast_select_fusion.4
  10.4 7.4 %all-to-all-start = ((bf16[16,2,1024]{2,1,0:T(2,128)(2,1)}), bf16[16,2,1024]{2,1,0:T(2,128)(2,1)S(1)}, u32[]{:S(2)}, u32[]{:S(2)}) async-start(bf16[16,2,1024]{2,1,0:T(2,128)(2,1)} %broadcast_select_fusion.4), calls=%async_computation | async-start | bytes 131072 | tf_op jit(solution)/shard_map/all_to_all | solution.py:45
  17.8 6.3 %gather_fusion.1 = bf16[32,8192]{1,0:T(8,128)(2,1)S(1)} fusion(bf16[512,8192]{1,0:T(8,128)(2,1)} %param.11, s32[1024]{0:T(1024)S(1)} %pad_clamp_fusion), kind=kCustom, calls=%fused_computation.1 | custom fusion | bytes 1048704 | tf_op jit(solution)/shard_map/jit(_take)/gather | solution.py:41
  24.1 0.3 gather.15
  24.4 1.3 broadcast_select_fusion
  25.8 0.0 all-to-all-done
  25.8 6.0 %all-to-all-start.1 = ((bf16[16,2,8192]{2,1,0:T(2,128)(2,1)}), bf16[16,2,8192]{2,1,0:T(2,128)(2,1)S(1)}, u32[]{:S(2)}, u32[]{:S(2)}) async-start(bf16[16,2,8192]{2,1,0:T(2,128)(2,1)} %broadcast_select_fusion), calls=%async_computation.1 | async-start | bytes 1048576 | tf_op jit(solution)/shard_map/all_to_all | solution.py:44
  31.8 0.0 copy-done.3
  31.8 0.1 dynamic_slice.3
  31.9 0.1 fusion.17
  31.9 0.0 copy-done.2
  31.9 0.3 convolution_convert_fusion.1
  32.3 22.6 %all-to-all-done.1 = bf16[16,2,8192]{2,1,0:T(2,128)(2,1)S(1)} async-done(((bf16[16,2,8192]{2,1,0:T(2,128)(2,1)}), bf16[16,2,8192]{2,1,0:T(2,128)(2,1)S(1)}, u32[]{:S(2)}, u32[]{:S(2)}) %all-to-all-start.1) | async-done | bytes 524320 | tf_op jit(solution)/shard_map/all_to_all | solution.py:44
  54.8 0.3 copy.28
  55.1 4.5 %reshape.96 = bf16[2,8192,16]{2,1,0:T(8,128)(2,1)} reshape(bf16[2,16,8192]{2,1,0:T(8,128)(2,1)S(1)} %copy.28) | data formatting | bytes 1048576 | tf_op jit(solution)/shard_map/reshape | solution.py:53
  59.6 5.3 %convolution_multiply_fusion.2 = f32[2,16,1024]{2,1,0:T(8,128)S(1)} fusion(bf16[2,8192,16]{2,1,0:T(8,128)(2,1)} %reshape.96, bf16[2,128,8192]{2,1,0:T(8,128)(2,1)} %bitcast.27, bf16[2,128,1024]{2,1,0:T(8,128)(2,1)S(1)} %bitcast.31, pred[2,128]{1,0:T(4,128)(4,1)S(1)} %get-tuple-element.4), kind=kOutput, calls=%fused_computation.7 | convolution fusion | flops 75796480 | bytes 5374208 | tf_op jit(solution)/shard_map/kbr,kbv->krv/dot_general | solution.py:71
  64.9 0.8 copy.33
  65.7 9.9 %all-to-all-start.3 = ((f32[2,16,1024]{2,0,1:T(2,128)}), f32[2,16,1024]{2,0,1:T(2,128)S(1)}, u32[]{:S(2)}, u32[]{:S(2)}) async-start(f32[2,16,1024]{2,0,1:T(2,128)} %copy.33), calls=%async_computation.3 | async-start | bytes 262144 | tf_op jit(solution)/shard_map/all_to_all | solution.py:78
  75.6 3.8 %fusion.1 = f32[2,8192,16]{1,2,0:T(8,128)S(1)} fusion(bf16[2,128,16]{1,2,0:T(8,128)(2,1)S(1)} %convolution_convert_fusion.1, bf16[2,128,8192]{2,1,0:T(8,128)(2,1)} %bitcast.28), kind=kOutput, calls=%fused_computation.6 | convolution fusion | flops 67371008 | bytes 5251072 | tf_op jit(solution)/shard_map/kbd,kbr->kdr/dot_general | solution.py:68
  79.3 4.6 %copy.30 = f32[2,8192,16]{2,1,0:T(8,128)} copy(f32[2,8192,16]{1,2,0:T(8,128)S(1)} %fusion.1) | data formatting | bytes 2097152 | tf_op jit(solution)/shard_map/mul | solution.py:68
  83.9 7.9 %all_to_all.50 = f32[2,16,8192]{2,1,0:T(8,128)S(1)} reshape(f32[2,8192,16]{2,1,0:T(8,128)} %copy.30) | data formatting | bytes 2097152 | tf_op jit(solution)/shard_map/all_to_all | solution.py:77
  91.9 1.8 copy.31
  93.6 0.0 all-to-all-done.3
  93.6 6.0 %all-to-all-start.2 = ((f32[2,16,8192]{2,0,1:T(2,128)}), f32[2,16,8192]{2,0,1:T(2,128)S(1)}, u32[]{:S(2)}, u32[]{:S(2)}) async-start(f32[2,16,8192]{2,0,1:T(2,128)} %copy.31), calls=%async_computation.2 | async-start | bytes 2097152 | tf_op jit(solution)/shard_map/all_to_all | solution.py:77
  99.6 6.7 %convolution_multiply_fusion = f32[2,128,8192]{2,1,0:T(8,128)} fusion(bf16[2,128,16]{1,2,0:T(8,128)(2,1)S(1)} %convolution_convert_fusion.1, bf16[2,8192,16]{2,1,0:T(8,128)(2,1)} %reshape.96), kind=kOutput, calls=%fused_computation.2 | convolution fusion | flops 69206016 | bytes 8921088 | tf_op jit(solution)/shard_map/kbr,kdr->kbd/dot_general | solution.py:62
  106.3 0.1 all_to_all.56
  106.4 2.3 %fusion.4 = f32[512,1024]{1,0:T(8,128)} fusion(f32[32,1024]{1,0:T(8,128)S(1)} %all_to_all.56, s32[32]{0:T(128)S(1)} %select_reduce_fusion), kind=kOutput, calls=%fused_computation.15 | convolution fusion | flops 201342976 | bytes 2228352 | tf_op jit(solution)/shard_map/dot_general | solution.py:87
  108.7 30.8 %all-to-all-done.2 = f32[2,16,8192]{2,0,1:T(2,128)S(1)} async-done(((f32[2,16,8192]{2,0,1:T(2,128)}), f32[2,16,8192]{2,0,1:T(2,128)S(1)}, u32[]{:S(2)}, u32[]{:S(2)}) %all-to-all-start.2) | async-done | bytes 1048608 | tf_op jit(solution)/shard_map/all_to_all | solution.py:77
  139.5 0.7 all_to_all.53
  140.2 10.3 %fusion.5 = f32[512,8192]{1,0:T(8,128)} fusion(f32[32,8192]{1,0:T(8,128)S(1)} %all_to_all.53, s32[32]{0:T(128)S(1)} %select_reduce_fusion), kind=kOutput, calls=%fused_computation.16 | convolution fusion | flops 1610629120 | bytes 17825920 | tf_op jit(solution)/shard_map/dot_general | solution.py:84
  150.5 23.0 %all-gather.2.cloned.1.call-done = bf16[8192,1024]{1,0:T(8,128)(2,1)} async-done(((bf16[512,1024]{1,0:T(8,128)(2,1)}), bf16[8192,1024]{1,0:T(8,128)(2,1)}) %all-gather.2.cloned.1.call-update) | async-done | bytes 16777232 | tf_op jit(solution)/shard_map/all_gather | solution.py:49
  173.5 0.0 copy-start.1
  173.5 12.4 %fusion = bf16[256,8192]{1,0:T(8,128)(2,1)} fusion(f32[256,8192]{1,0:T(8,128)} %bitcast.26, bf16[8192,1024]{1,0:T(8,128)(2,1)} %all-gather.2.cloned.1.call-done, bf16[256,1024]{1,0:T(8,128)(2,1)S(1)} %copy-done.2, pred[256]{0:T(512)(128)(4,1)S(1)} %get-tuple-element.3), kind=kOutput, calls=%fused_computation.4 | convolution fusion | flops 4299423744 | bytes 29884672 | tf_op jit(solution)/shard_map/dot_general | solution.py:47
  185.9 0.0 copy-done.1
  (4 shorter events, 0.1 us)
Async XLA Ops:
  7.2 1.7 copy-start
  7.2 166.3 %all-gather.2.cloned.1.call-start = ((), (), s32[]{:S(2)}) async-start(), calls=%async_computation.4 | async-start | bytes 17825792 | tf_op jit(solution)/shard_map/all_gather | solution.py:49
  9.5 22.2 %copy-start.3 = (s32[32]{0:T(128)S(1)}, s32[32]{0:T(128)}, u32[]{:S(2)}) copy-start(s32[32]{0:T(128)} %param.14) | copy-start | bytes 388
  9.5 22.4 %copy-start.2 = (bf16[256,1024]{1,0:T(8,128)(2,1)S(1)}, bf16[256,1024]{1,0:T(8,128)(2,1)}, u32[]{:S(2)}) copy-start(bf16[256,1024]{1,0:T(8,128)(2,1)} %param.9) | copy-start | bytes 1572868
  10.4 15.4 %all-to-all-start = ((bf16[16,2,1024]{2,1,0:T(2,128)(2,1)}), bf16[16,2,1024]{2,1,0:T(2,128)(2,1)S(1)}, u32[]{:S(2)}, u32[]{:S(2)}) async-start(bf16[16,2,1024]{2,1,0:T(2,128)(2,1)} %broadcast_select_fusion.4), calls=%async_computation | async-start | bytes 131072 | tf_op jit(solution)/shard_map/all_to_all | solution.py:45
  25.8 29.1 %all-to-all-start.1 = ((bf16[16,2,8192]{2,1,0:T(2,128)(2,1)}), bf16[16,2,8192]{2,1,0:T(2,128)(2,1)S(1)}, u32[]{:S(2)}, u32[]{:S(2)}) async-start(bf16[16,2,8192]{2,1,0:T(2,128)(2,1)} %broadcast_select_fusion), calls=%async_computation.1 | async-start | bytes 1048576 | tf_op jit(solution)/shard_map/all_to_all | solution.py:44
  65.7 28.0 %all-to-all-start.3 = ((f32[2,16,1024]{2,0,1:T(2,128)}), f32[2,16,1024]{2,0,1:T(2,128)S(1)}, u32[]{:S(2)}, u32[]{:S(2)}) async-start(f32[2,16,1024]{2,0,1:T(2,128)} %copy.33), calls=%async_computation.3 | async-start | bytes 262144 | tf_op jit(solution)/shard_map/all_to_all | solution.py:78
  93.6 45.9 %all-to-all-start.2 = ((f32[2,16,8192]{2,0,1:T(2,128)}), f32[2,16,8192]{2,0,1:T(2,128)S(1)}, u32[]{:S(2)}, u32[]{:S(2)}) async-start(f32[2,16,8192]{2,0,1:T(2,128)} %copy.31), calls=%async_computation.2 | async-start | bytes 2097152 | tf_op jit(solution)/shard_map/all_to_all | solution.py:77
  173.5 12.4 %copy-start.1 = (bf16[512,1024]{1,0:T(8,128)(2,1)S(1)}, bf16[512,1024]{1,0:T(8,128)(2,1)}, u32[]{:S(2)}) copy-start(bf16[512,1024]{1,0:T(8,128)(2,1)} %param.12) | copy-start | bytes 3145732
Sparse Core Ops, SparseCore 0:
  10.2 163.3 all-gather.1
where the time goes:
time: 193 us
  waiting for transfers between devices  77.1 us (40%)
  matrix products  41.1 us (21%)
  starting transfers between devices  29.3 us (15%)
  local copies, waits for them, and re-layouts  28.1 us (15%)
  between operations  14.2 us (7%)
  other arithmetic  3.05 us (2%)
    all_to_all x1, waiting for transfers between devices, body(): lax.all_to_all(partial_down_weight, 'fsdp', split_axis=1, concat_axis=0,...  30.8 us
    all_gather x1, waiting for transfers between devices, body(): lax.all_gather(frozen_value_weight, 'fsdp', axis=0, tiled=True)  23 us
    all_to_all x1, waiting for transfers between devices, body(): lax.all_to_all(down_weight_rows, 'fsdp', split_axis=0, concat_axis=1, til...  22.6 us
    dot_general x1, matrix products, body(): lax.dot_general(masked, lax.all_gather(frozen_value_weight, 'fsdp', axis=...  12.4 us
    all_to_all x3, local copies, waits for them, and re-layouts, body(): lax.all_to_all(partial_down_weight, 'fsdp', split_axis=1, concat_axis=0,...  10.4 us
    dot_general x1, matrix products, body(): jnp.dot(onehot, recv_down, precision=highest_precision, preferred_element...  10.3 us
    all_to_all x1, starting transfers between devices, body(): lax.all_to_all(partial_up_weight, 'fsdp', split_axis=1, concat_axis=0, ti...  9.87 us
    all_to_all x1, starting transfers between devices, body(): lax.all_to_all(up_weight_rows, 'fsdp', split_axis=0, concat_axis=1, tiled...  7.39 us
  transfers between devices with their start and end apart: 5, of which 3 were waited for; matrix products, arithmetic and copies ran while one was open for 27% of the time, Pallas kernels for 0%

commit v1 on v0

--- a/solution.py
+++ b/solution.py
@@ -1,12 +1,17 @@
+import functools
+
 import jax
 import jax.numpy as jnp
 from jax import lax
+from jax.experimental import pallas as pl
+from jax.experimental.pallas import tpu as pltpu
 from jax.sharding import PartitionSpec as P
 
 ADAPTER_RANK = 16
 ADAPTER_GROUP = 512
 BLOCK = 128
-
+LANES = 128
+VMEM_LIMIT = 48 * 1024 * 1024
 
 adapter_scale = 2.0
 
@@ -16,7 +21,351 @@
     return jnp.sum(jnp.where(matches, adapter_storage_row[None, :], 0), axis=1)
 
 
-def body(
+def iota(shape, axis):
+    return lax.broadcasted_iota(jnp.int32, shape, axis)
+
+
+def dot_t(a, b):
+    return lax.dot_general(a, b, (((1,), (1,)), ((), ())), preferred_element_type=jnp.float32)
+
+
+def dot_n(a, b, precision=None):
+    return lax.dot_general(
+        a, b, (((1,), (0,)), ((), ())), precision=precision, preferred_element_type=jnp.float32
+    )
+
+
+def dot_0(a, b):
+    return lax.dot_general(a, b, (((0,), (0,)), ((), ())), preferred_element_type=jnp.float32)
+
+
+def spread_rows(flat, count):
+    rows = count * 8
+    repeat = (iota((rows, count), 0) // 8 == iota((rows, count), 1)).astype(jnp.bfloat16)
+    wide = dot_n(repeat, flat)
+    mine = iota((rows, LANES), 1) // 16 == iota((rows, LANES), 0) % 8
+    return jnp.where(mine, wide, 0.0).astype(jnp.bfloat16)
+
+
+def tiles_kernel(own_cot, far_cot, left, right, own_out, far_out):
+    step = pl.program_id(0)
+    half = pl.num_programs(0) // 2
+
+    def part(weight):
+        own_out[...] = dot_t(own_cot[...], weight[...])
+        far_out[...] = dot_t(far_cot[...], weight[...]).astype(far_out.dtype)
+
+    pl.when(step < half)(lambda: part(left))
+    pl.when(step >= half)(lambda: part(right))
+
+
+def product_tiles(own_cot, far_cot, left, right):
+    rows, depth = own_cot.shape
+    width = left.shape[0]
+    tile = 256
+    per = width // tile
+    whole = pl.BlockSpec((rows, depth), lambda i: (0, 0))
+    return pl.pallas_call(
+        tiles_kernel,
+        grid=(2 * per,),
+        in_specs=[
+            whole,
+            whole,
+            pl.BlockSpec((tile, depth), lambda i: (jnp.minimum(i, per - 1), 0)),
+            pl.BlockSpec((tile, depth), lambda i: (jnp.maximum(i - per, 0), 0)),
+        ],
+        out_specs=[
+            pl.BlockSpec((rows, tile), lambda i: (0, i)),
+            pl.BlockSpec((rows, tile), lambda i: (0, i)),
+        ],
+        out_shape=[
+            jax.ShapeDtypeStruct((rows, 2 * width), jnp.float32),
+            jax.ShapeDtypeStruct((rows, 2 * width), jnp.bfloat16),
+        ],
+        compiler_params=pltpu.CompilerParams(vmem_limit_bytes=VMEM_LIMIT),
+        cost_estimate=pl.CostEstimate(
+            flops=8 * rows * depth * width, bytes_accessed=6 * 1024 * 1024, transcendentals=0
+        ),
+        name="product_tiles",
+    )(own_cot, far_cot, left, right)
+
+
+def low_rank_columns(g8, a_rows, chunk):
+    parts = []
+    for k in range(a_rows.shape[0]):
+        spread = spread_rows(a_rows[k], chunk)
+        parts.append(dot_t(g8[k * BLOCK : (k + 1) * BLOCK, :], spread))
+    return adapter_scale * jnp.concatenate(parts, axis=0)
+
+
+def finish_kernel(meta, own, far, g8, a_rows, _, out):
+    half = own.shape[1]
+    lr = low_rank_columns(g8[...], a_rows[...], a_rows.shape[1])
+    mine, other = own[...], far[...].astype(jnp.float32)
+    first = meta[0] == 0
+    out[:, :half] = (jnp.where(first, mine, other) + lr[:, :half]).astype(out.dtype)
+    out[:, half:] = (jnp.where(first, other, mine) + lr[:, half:]).astype(out.dtype)
+
+
+def finish_columns(meta, own, far, g8, a_flat, out):
+    rows, both = own.shape
+    half = both // 2
+    chunk = 2 * half * ADAPTER_RANK // LANES
+    blocks = a_flat.shape[0]
+    return pl.pallas_call(
+        finish_kernel,
+        grid_spec=pltpu.PrefetchScalarGridSpec(
+            num_scalar_prefetch=1,
+            grid=(2,),
+            in_specs=[
+                pl.BlockSpec((rows, half), lambda j, m: (0, j)),
+                pl.BlockSpec((rows, half), lambda j, m: (0, j)),
+                pl.BlockSpec((rows, LANES), lambda j, m: (0, 0)),
+                pl.BlockSpec((blocks, chunk, LANES), lambda j, m: (0, m[1 + j], 0)),
+                pl.BlockSpec(memory_space=pl.ANY),
+            ],
+            out_specs=pl.BlockSpec((rows, 2 * half), lambda j, m: (0, m[1 + j])),
+        ),
+        out_shape=jax.ShapeDtypeStruct(out.shape, out.dtype),
+        input_output_aliases={5: 0},
+        compiler_params=pltpu.CompilerParams(vmem_limit_bytes=VMEM_LIMIT),
+        cost_estimate=pl.CostEstimate(
+            flops=8 * rows * LANES * half, bytes_accessed=3 * 1024 * 1024, transcendentals=0
+        ),
+        name="finish_columns",
+    )(meta, own, far, g8, a_flat, out)
+
+
+def own_kernel(meta, cot, first, second, g8, a_rows, out):
+    half = first.shape[0]
+    lr = low_rank_columns(g8[...], a_rows[...], a_rows.shape[1])
+    out[:, :half] = (dot_t(cot[...], first[...]) + lr[:, :half]).astype(out.dtype)
+    out[:, half:] = (dot_t(cot[...], second[...]) + lr[:, half:]).astype(out.dtype)
+
+
+def own_columns(meta, cot, first, second, g8, a_flat, width):
+    rows, depth = cot.shape
+    half = first.shape[0]
+    chunk = 2 * half * ADAPTER_RANK // LANES
+    blocks = a_flat.shape[0]
+    return pl.pallas_call(
+        own_kernel,
+        grid_spec=pltpu.PrefetchScalarGridSpec(
+            num_scalar_prefetch=1,
+            grid=(1,),
+            in_specs=[
+                pl.BlockSpec((rows, depth), lambda j, m: (0, 0)),
+                pl.BlockSpec((half, depth), lambda j, m: (0, 0)),
+                pl.BlockSpec((half, depth), lambda j, m: (0, 0)),
+                pl.BlockSpec((rows, LANES), lambda j, m: (0, 0)),
+                pl.BlockSpec((blocks, chunk, LANES), lambda j, m: (0, m[0], 0)),
+            ],
+            out_specs=pl.BlockSpec((rows, 2 * half), lambda j, m: (0, m[0])),
+        ),
+        out_shape=jax.ShapeDtypeStruct((rows, width), jnp.bfloat16),
+        compiler_params=pltpu.CompilerParams(vmem_limit_bytes=VMEM_LIMIT),
+        cost_estimate=pl.CostEstimate(
+            flops=4 * rows * depth * half, bytes_accessed=4 * 1024 * 1024, transcendentals=0
+        ),
+        name="own_columns",
+    )(meta, cot, first, second, g8, a_flat)
+
+
+def adapter_kernel(x, cot, recv, sent, g8_out):
+    devices = recv.shape[0]
+    rows = x.shape[0]
+    blocks = rows // BLOCK
+    width = x.shape[1]
+    chunk = width * ADAPTER_RANK // LANES // devices
+    up_chunk = cot.shape[1] * ADAPTER_RANK // LANES // devices
+    columns = width // devices
+    tiles = cot.shape[1] // LANES
+    lane = iota((BLOCK, LANES), 1)
+    square_from, square_to = iota((LANES, LANES), 0), iota((LANES, LANES), 1)
+    gather_rank = (square_from // 8 == square_to % 16).astype(jnp.float32)
+    gather_low = (square_from % 16 == square_to // 8).astype(jnp.float32)
+    fold = (iota((chunk, columns), 0) == iota((chunk, columns), 1) // 8).astype(jnp.bfloat16)
+    own_lanes = iota((columns, LANES), 1) // 16 == iota((columns, LANES), 0) % 8
+    down_rows = blocks * chunk
+    b_all = recv[:, down_rows : down_rows + blocks * up_chunk, :].astype(jnp.float32)
+    ups = []
+    for k in range(blocks):
+        m = cot[k * BLOCK : (k + 1) * BLOCK, :]
+        b_flat = b_all[:, k * up_chunk : (k + 1) * up_chunk, :].reshape(devices * up_chunk, LANES)
+        b_flat = b_flat.astype(jnp.bfloat16)
+        total = jnp.zeros((BLOCK, LANES), jnp.float32)
+        for t in range(tiles):
+            part = dot_t(m[:, t * LANES : (t + 1) * LANES], b_flat)
+            total = total + jnp.where(lane % tiles == t, part, 0.0)
+        g8 = dot_n(total, gather_rank, lax.Precision.HIGHEST).astype(jnp.bfloat16)
+        g8_out[k * BLOCK : (k + 1) * BLOCK, :] = g8
+        low = jnp.zeros((BLOCK, LANES), jnp.float32)
+        for j in range(devices):
+            x_part = x[k * BLOCK : (k + 1) * BLOCK, j * columns : (j + 1) * columns]
+            spread = spread_rows(recv[j, k * chunk : (k + 1) * chunk, :], chunk)
+            low = low + dot_n(x_part, spread)
+            wide = jnp.where(own_lanes, dot_0(x_part, g8), 0.0).astype(jnp.bfloat16)
+            folded = adapter_scale * dot_n(fold, wide)
+            sent[j, k * chunk : (k + 1) * chunk, :] = folded.astype(sent.dtype)
+        low8 = dot_n(low, gather_low, lax.Precision.HIGHEST).astype(jnp.bfloat16)
+        up = dot_0(low8, m)
+        flat = jnp.zeros((LANES, LANES), jnp.float32)
+        row = iota((LANES, LANES), 0)
+        for t in range(tiles):
+            flat = flat + jnp.where(row % tiles == t, up[:, t * LANES : (t + 1) * LANES], 0.0)
+        ups.append((adapter_scale * flat).reshape(devices, up_chunk, LANES))
+    sent[:, down_rows : down_rows + blocks * up_chunk, :] = jnp.concatenate(ups, axis=1).astype(
+        sent.dtype
+    )
+
+
+def adapter_terms(x, cot, recv):
+    rows = x.shape[0]
+    return pl.pallas_call(
+        adapter_kernel,
+        out_shape=[
+            jax.ShapeDtypeStruct(recv.shape, jnp.bfloat16),
+            jax.ShapeDtypeStruct((rows, LANES), jnp.bfloat16),
+        ],
+        compiler_params=pltpu.CompilerParams(vmem_limit_bytes=VMEM_LIMIT),
+        cost_estimate=pl.CostEstimate(
+            flops=8 * rows * x.shape[1] * LANES, bytes_accessed=8 * 1024 * 1024, transcendentals=0
+        ),
+        name="adapter_terms",
+    )(x, cot, recv)
+
+
+def ring_body(
+    inputs,
+    cotangent,
+    frozen_value_weight,
+    adapter_down_weights,
+    adapter_up_weights,
+    padded_block_adapter,
+    block_live_rows,
+    adapter_storage_row,
+    *,
+    devices,
+):
+    chips = devices // 2
+    token_rows, hidden_width = inputs.shape
+    block_count = token_rows // BLOCK
+    all_blocks = padded_block_adapter.shape[0]
+    shard = frozen_value_weight.shape[0]
+    index = lax.axis_index("fsdp")
+    core, chip = index % 2, index // 2
+    part = lax.axis_index("parts")
+    order = list(range(0, chips, 2)) + list(range(chips - 1, 0, -2))
+    place = {c: i for i, c in enumerate(order)}
+    order_array = jnp.array(order, jnp.int32)
+    my_place = jnp.array([place[c] for c in range(chips)], jnp.int32)[chip]
+    ring = []
+    for c in range(chips):
+        ring.append((2 * c, 2 * order[(place[c] + 1) % chips]))
+        ring.append((2 * c + 1, 2 * order[(place[c] - 1) % chips] + 1))
+    cores = [(i, i ^ 1) for i in range(devices)]
+    across = [(0, 1), (1, 0)]
+
+    live_rows = lax.dynamic_slice_in_dim(block_live_rows, index * block_count, block_count)
+    positions = jnp.arange(BLOCK, dtype=jnp.int32)
+    live_mask = positions[None, :] < live_rows[:, None]
+    blocked_cot = cotangent.reshape(block_count, BLOCK, -1)
+    masked = jnp.where(live_mask[:, :, None], blocked_cot, jnp.zeros_like(blocked_cot)).reshape(
+        cotangent.shape
+    )
+    far_masked = lax.ppermute(masked, "parts", across)
+    other_shard = lax.ppermute(frozen_value_weight, "fsdp", cores)
+    first_shard = jnp.where(core == 0, frozen_value_weight, other_shard)
+    second_shard = jnp.where(core == 0, other_shard, frozen_value_weight)
+    travelling = jnp.where(part == 0, first_shard, second_shard)
+
+    slots = slot_lookup(padded_block_adapter, adapter_storage_row)
+    per_down = adapter_down_weights.shape[1] // LANES
+    per_up = adapter_up_weights.shape[1] // LANES
+    down_rows = jnp.take(adapter_down_weights, slots, axis=0).reshape(devices, -1, LANES)
+    up_rows = jnp.take(adapter_up_weights, slots, axis=0).reshape(devices, -1, LANES)
+    payload = jnp.concatenate([down_rows, up_rows], axis=1)
+    recv = lax.all_to_all(payload, "fsdp", split_axis=0, concat_axis=0, tiled=True)
+    sent, g8 = adapter_terms(inputs, masked, recv)
+    a_flat = (
+        recv[:, : block_count * per_down, :]
+        .reshape(devices, block_count, per_down, LANES)
+        .transpose(1, 0, 2, 3)
+        .reshape(block_count, devices * per_down, LANES)
+    )
+    grads = lax.all_to_all(sent, "fsdp", split_axis=0, concat_axis=0, tiled=True)
+
+    held = []
+    for step in range(chips // 2 - 1):
+        travelling = lax.ppermute(travelling, "fsdp", ring)
+        forwarded = lax.ppermute(travelling, "fsdp", cores)
+        own, far = product_tiles(masked, far_masked, travelling, forwarded)
+        far = lax.ppermute(far, "parts", across)
+        direction = jnp.where(core == 0, -1, 1)
+        near_chip = order_array[(my_place + direction * (step + 1)) % chips]
+        far_chip = order_array[(my_place - direction * (step + 1)) % chips]
+        held.append((jnp.stack([part, near_chip, far_chip]).astype(jnp.int32), own, far))
+    piece = lax.dynamic_slice_in_dim(travelling, core * (shard // 2), shard // 2)
+    piece = lax.ppermute(piece, "fsdp", ring)
+    other_piece = lax.ppermute(piece, "fsdp", cores)
+    last = jnp.concatenate(
+        [
+            jnp.where(core == 0, piece, other_piece),
+            jnp.where(core == 0, other_piece, piece),
+        ],
+        axis=0,
+    )
+    own_last = dot_t(masked, last)
+    far_last = lax.ppermute(dot_t(far_masked, last).astype(jnp.bfloat16), "parts", across)
+
+    out = own_columns(
+        chip[None].astype(jnp.int32), masked, first_shard, second_shard, g8, a_flat, hidden_width
+    )
+    for meta, own, far in held:
+        out = finish_columns(meta, own, far, g8, a_flat, out)
+    opposite = order_array[(my_place + chips // 2) % chips]
+    meta = jnp.stack([part, opposite]).astype(jnp.int32)
+    out = finish_last(meta, own_last, far_last, g8, a_flat, out)
+
+    onehot = (
+        jnp.arange(ADAPTER_GROUP, dtype=jnp.int32)[:, None] == slots[None, :]
+    ).astype(jnp.bfloat16)
+    down = grads[:, : block_count * per_down, :].reshape(all_blocks, per_down * LANES)
+    up = grads[:, block_count * per_down :, :].reshape(all_blocks, per_up * LANES)
+    down_grad = jnp.dot(onehot, down, preferred_element_type=jnp.float32)
+    up_grad = jnp.dot(onehot, up, preferred_element_type=jnp.float32)
+    return (out, down_grad, up_grad)
+
+
+def finish_last(meta, own, far, g8, a_flat, out):
+    rows, half = own.shape
+    chunk = 2 * half * ADAPTER_RANK // LANES
+    blocks = a_flat.shape[0]
+    return pl.pallas_call(
+        finish_kernel,
+        grid_spec=pltpu.PrefetchScalarGridSpec(
+            num_scalar_prefetch=1,
+            grid=(1,),
+            in_specs=[
+                pl.BlockSpec((rows, half), lambda j, m: (0, 0)),
+                pl.BlockSpec((rows, half), lambda j, m: (0, 0)),
+                pl.BlockSpec((rows, LANES), lambda j, m: (0, 0)),
+                pl.BlockSpec((blocks, chunk, LANES), lambda j, m: (0, m[1], 0)),
+                pl.BlockSpec(memory_space=pl.ANY),
+            ],
+            out_specs=pl.BlockSpec((rows, 2 * half), lambda j, m: (0, m[1])),
+        ),
+        out_shape=jax.ShapeDtypeStruct(out.shape, out.dtype),
+        input_output_aliases={5: 0},
+        compiler_params=pltpu.CompilerParams(vmem_limit_bytes=VMEM_LIMIT),
+        cost_estimate=pl.CostEstimate(
+            flops=4 * rows * LANES * half, bytes_accessed=2 * 1024 * 1024, transcendentals=0
+        ),
+        name="finish_last",
+    )(meta, own, far, g8, a_flat, out)
+
+
+def gather_body(
     inputs,
     cotangent,
     frozen_value_weight,
@@ -91,6 +440,7 @@
 
 
 def solution(mesh):
+    devices = mesh.shape["fsdp"]
     in_specs = (
         P(("parts", "fsdp"), None),
         P(("parts", "fsdp"), None),
@@ -102,4 +452,15 @@
         P("parts"),
     )
     out_specs = (P(("parts", "fsdp"), None), P("parts", "fsdp"), P("parts", "fsdp"))
-    return jax.shard_map(body, mesh=mesh, in_specs=in_specs, out_specs=out_specs, check_vma=False)
+
+    def program(*arrays):
+        shard = arrays[2].shape[0] // devices
+        if mesh.shape["parts"] == 2 and devices % 4 == 0 and shard % 256 == 0:
+            body = functools.partial(ring_body, devices=devices)
+        else:
+            body = gather_body
+        return jax.shard_map(
+            body, mesh=mesh, in_specs=in_specs, out_specs=out_specs, check_vma=False
+        )(*arrays)
+
+    return program

time: 193 us -> 154 us (0.80)
  Pallas kernels: 0 us -> 40 us
  waiting for transfers between devices: 77.1 us -> 40.1 us
  matrix products: 41.1 us -> 12.2 us
  local copies, waits for them, and re-layouts: 28.1 us -> 17.9 us
  between operations: 14.2 us -> 5.55 us
  other arithmetic: 3.05 us -> 11.2 us
  starting transfers between devices: 29.3 us -> 25.3 us
    all_to_all x4 -> x2, waiting for transfers between devices: 53.4 us -> 12.1 us  [the longest x1 12.1 us: ring_body(): lax.all_to_all(payload, 'fsdp', split_axis=0, concat_axis=0, tiled=True)]
    pallas_call x0 -> x9, Pallas kernels: none -> 40 us  [the longest x3 13.8 us: product_tiles(): pl.pallas_call(tiles_kernel, grid=(2 * per,), in_specs=[whole, whole, pl....]
    dot_general x7 -> x4, matrix products: 41.1 us -> 12.2 us  [the longest x1 8.47 us: ring_body(): down_grad = jnp.dot(onehot, down, preferred_element_type=jnp.float32)]
    ppermute x0 -> x14, waiting for transfers between devices: none -> 28 us  [the longest x3 12.6 us: ring_body(): far = lax.ppermute(far, 'parts', across)]
    all_gather x1 -> x0, waiting for transfers between devices: 23 us -> none  [body(): lax.all_gather(frozen_value_weight, 'fsdp', axis=0, tiled=True)]
    all_to_all x4 -> x2, starting transfers between devices: 29.2 us -> 9.41 us  [the longest x1 4.93 us: ring_body(): lax.all_to_all(payload, 'fsdp', split_axis=0, concat_axis=0, tiled=True)]
    ppermute x0 -> x14, starting transfers between devices: none -> 15.9 us  [the longest x3 7.1 us: ring_body(): travelling = lax.ppermute(travelling, 'fsdp', ring)]
    all_to_all x5 -> x0, local copies, waits for them, and re-layouts: 10.8 us -> none  [the longest x3 10.4 us: body(): lax.all_to_all(partial_down_weight, 'fsdp', split_axis=1, concat_axis=0,...]
  transfers between devices with their start and end apart: 5 -> 16, of which waited for: 3 -> 7; matrix products, arithmetic and copies ran while one was open for 27% -> 22% of each run, Pallas kernels for 0% -> 25%
where the time goes in v1:
time: 154 us; the launch traced here: 152 us
  waiting for transfers between devices  40.1 us (26%)
  Pallas kernels  40 us (26%)
  starting transfers between devices  25.3 us (16%)
  local copies, waits for them, and re-layouts  17.9 us (12%)
  matrix products  12.2 us (8%)
  other arithmetic  11.2 us (7%)
  between operations  5.55 us (4%)
    pallas_call x3, Pallas kernels, product_tiles(): pl.pallas_call(tiles_kernel, grid=(2 * per,), in_specs=[whole, whole, pl....  13.8 us
    ppermute x3, waiting for transfers between devices, ring_body(): far = lax.ppermute(far, 'parts', across)  12.6 us
    pallas_call x1, Pallas kernels, adapter_terms(): pl.pallas_call(adapter_kernel, out_shape=[jax.ShapeDtypeStruct(recv.shape...  12.5 us
    ppermute x3, waiting for transfers between devices, ring_body(): travelling = lax.ppermute(travelling, 'fsdp', ring)  12.3 us
    all_to_all x1, waiting for transfers between devices, ring_body(): lax.all_to_all(payload, 'fsdp', split_axis=0, concat_axis=0, tiled=True)  12.1 us
    pallas_call x3, Pallas kernels, finish_columns(): pl.pallas_call(finish_kernel, grid_spec=pltpu.PrefetchScalarGridSpec(num_...  8.82 us
    dot_general x1, matrix products, ring_body(): down_grad = jnp.dot(onehot, down, preferred_element_type=jnp.float32)  8.47 us
    ppermute x3, starting transfers between devices, ring_body(): travelling = lax.ppermute(travelling, 'fsdp', ring)  7.1 us
  transfers between devices with their start and end apart: 16, of which 7 were waited for; matrix products, arithmetic and copies ran while one was open for 22% of the time, Pallas kernels for 25%

profile of v1, /device:TPU:0, one launch (start us, length us, event | category | flops | bytes accessed | tf_op | source)
XLA Modules:
  0.0 152.4 jit_solution(16357333263145284345)
XLA Ops:
  0.6 0.5 collective-permute-start
  1.2 2.5 %collective-permute-done = bf16[512,1024]{1,0:T(8,128)(2,1)S(1)} collective-permute-done((bf16[512,1024]{1,0:T(8,128)(2,1)}, bf16[512,1024]{1,0:T(8,128)(2,1)S(1)}, u32[]{:S(2)}, u32[]{:S(2)}) %collective-permute-start) | collective-permute-done | bytes 1048608 | tf_op jit(solution)/shard_map/ppermute | solution.py:277
  3.7 2.7 %broadcast_select_fusion.2 = (bf16[512,1024]{1,0:T(8,128)(2,1)}, bf16[512,1024]{1,0:T(8,128)(2,1)S(1)}, bf16[512,1024]{1,0:T(8,128)(2,1)}) fusion(pred[]{:T(512)S(6)} %eq.48, bf16[512,1024]{1,0:T(8,128)(2,1)S(1)} %collective-permute-done, bf16[512,1024]{1,0:T(8,128)(2,1)} %param.12, pred[]{:T(512)S(6)} %eq.47), kind=kLoop, calls=%fused_computation.6 | loop fusion | flops 1572864 | bytes 5242882 | tf_op jit(solution)/shard_map/jit(_where)/select_n | solution.py:280
  6.4 2.9 %collective-permute-start.1 = (bf16[512,1024]{1,0:T(8,128)(2,1)}, bf16[512,1024]{1,0:T(8,128)(2,1)}, u32[]{:S(2)}, u32[]{:S(2)}) collective-permute-start(bf16[512,1024]{1,0:T(8,128)(2,1)} %get-tuple-element.19), channel_id=1, source_target_pairs={{0,4},{1,3},{2,0},{3,7},{4,8},{5,1},{6,2},{7,11},{8,12},{9,5},{10,... | collective-permute-start | bytes 3145736 | tf_op jit(solution)/shard_map/ppermute | solution.py:300
  9.4 0.2 select_reduce_fusion
  9.5 0.1 reduce_sum.14
  9.7 0.6 gather_fusion.1
  10.3 0.1 copy.21
  10.5 0.1 copy.22
  10.5 11.8 %collective-permute-done.1.left = bf16[512,1024]{1,0:T(8,128)(2,1)} collective-permute-done((bf16[512,1024]{1,0:T(8,128)(2,1)}, bf16[512,1024]{1,0:T(8,128)(2,1)}, u32[]{:S(2)}, u32[]{:S(2)}) %collective-permute-start.1) | collective-permute-done | bytes 1048608 | tf_op jit(solution)/shard_map/ppermute | solution.py:300
  22.4 2.1 %collective-permute-start.2 = (bf16[512,1024]{1,0:T(8,128)(2,1)}, bf16[512,1024]{1,0:T(8,128)(2,1)}, u32[]{:S(2)}, u32[]{:S(2)}) collective-permute-start(bf16[512,1024]{1,0:T(8,128)(2,1)} %collective-permute-done.1.left), channel_id=1, source_target_pairs={{0,4},{1,3},{2,0},{3,7},{4,8},{5,1},{6,2},{7,11},{8,12},{9,5},{10,... | collective-permute-start | bytes 3145736 | tf_op jit(solution)/shard_map/ppermute | solution.py:300
  24.5 0.1 broadcast_select_fusion.7
  24.6 5.8 %gather_fusion = bf16[32,8192]{1,0:T(8,128)(2,1)S(1)} fusion(bf16[512,8192]{1,0:T(8,128)(2,1)} %param.13, s32[1024]{0:T(1024)S(1)} %pad_clamp_fusion), kind=kCustom, calls=%fused_computation | custom fusion | bytes 1048704 | tf_op jit(solution)/shard_map/jit(_take)/gather | solution.py:285
  30.4 0.2 gather.13
  30.7 0.1 broadcast_in_dim.66
  30.7 0.1 broadcast_in_dim.67
  30.8 0.3 broadcast_select_fusion.4
  31.2 0.9 pad_maximum_fusion.3
  32.0 4.9 %all-to-all-start = ((bf16[16,144,128]{2,1,0:T(8,128)(2,1)}), bf16[16,144,128]{2,1,0:T(8,128)(2,1)S(1)}, u32[]{:S(2)}, u32[]{:S(2)}) async-start(bf16[16,144,128]{2,1,0:T(8,128)(2,1)} %pad_maximum_fusion.3), calls=%async_computation | async-start | bytes 1179648 | tf_op jit(solution)/shard_map/all_to_all | solution.py:288
  37.0 0.1 dynamic_slice.32
  37.1 0.4 collective-permute-done.2.left
  37.5 2.1 %collective-permute-start.3 = (bf16[512,1024]{1,0:T(8,128)(2,1)}, bf16[512,1024]{1,0:T(8,128)(2,1)}, u32[]{:S(2)}, u32[]{:S(2)}) collective-permute-start(bf16[512,1024]{1,0:T(8,128)(2,1)} %collective-permute-done.2.left), channel_id=1, source_target_pairs={{0,4},{1,3},{2,0},{3,7},{4,8},{5,1},{6,2},{7,11},{8,12},{9,5},{10,... | collective-permute-start | bytes 3145736 | tf_op jit(solution)/shard_map/ppermute | solution.py:300
  39.7 0.9 broadcast_select_fusion.3.cot.own_cot
  40.6 12.1 %all-to-all-done.recv = bf16[16,144,128]{2,1,0:T(8,128)(2,1)S(1)} async-done(((bf16[16,144,128]{2,1,0:T(8,128)(2,1)}), bf16[16,144,128]{2,1,0:T(8,128)(2,1)S(1)}, u32[]{:S(2)}, u32[]{:S(2)}) %all-to-all-start) | async-done | bytes 589856 | tf_op jit(solution)/shard_map/all_to_all | solution.py:288
  52.7 2.2 %copy-done.4 = bf16[256,8192]{1,0:T(8,128)(2,1)S(1)} copy-done((bf16[256,8192]{1,0:T(8,128)(2,1)S(1)}, bf16[256,8192]{1,0:T(8,128)(2,1)}, u32[]{:S(2)}) %copy-start.4) | copy-done | bytes 4194328
  54.9 12.5 %adapter_terms.1 = (bf16[16,144,128]{2,1,0:T(8,128)(2,1)}, bf16[256,128]{1,0:T(8,128)(2,1)S(1)}) custom-call(bf16[256,8192]{1,0:T(8,128)(2,1)S(1)} %copy-done.4, bf16[256,1024]{1,0:T(8,128)(2,1)} %broadcast_select_fusion.3.cot.own_cot, bf16[16,144,128]{2,1,0:T(8,128)(2,1)S(1)} %all-to-all-done.recv), custom_call_target="tpu_custom_call" | custom-call | flops 2147483648 | bytes 8388608 | tf_op jit(solution)/shard_map/adapter_terms/pallas_call | solution.py:224
  67.4 4.5 %all-to-all-start.1 = ((bf16[16,144,128]{2,1,0:T(8,128)(2,1)}), bf16[16,144,128]{2,1,0:T(8,128)(2,1)}, u32[]{:S(2)}, u32[]{:S(2)}) async-start(bf16[16,144,128]{2,1,0:T(8,128)(2,1)} %get-tuple-element.18), calls=%async_computation.1 | async-start | bytes 1179648 | tf_op jit(solution)/shard_map/all_to_all | solution.py:296
  71.9 0.4 collective-permute-start.12
  72.2 0.2 collective-permute-start.10
  72.4 1.5 collective-permute-start.6
  73.9 0.6 dynamic_slice.30
  79.2 0.7 fusion.8
  79.9 0.7 pad_add_fusion.meta
  80.6 1.9 %constant_dynamic-slice_fusion = bf16[256,1024]{1,0:T(8,128)(2,1)} fusion(bf16[512,1024]{1,0:T(8,128)(2,1)} %collective-permute-done.3.left, s32[]{:T(128)S(6)} %select_n.156), kind=kLoop, calls=%fused_computation.32 | loop fusion | bytes 1048580 | tf_op jit(solution)/shard_map/dynamic_slice | solution.py:308
  82.5 1.8 %collective-permute-start.4 = (bf16[256,1024]{1,0:T(8,128)(2,1)}, bf16[256,1024]{1,0:T(8,128)(2,1)}, u32[]{:S(2)}, u32[]{:S(2)}) collective-permute-start(bf16[256,1024]{1,0:T(8,128)(2,1)} %constant_dynamic-slice_fusion), channel_id=1, source_target_pairs={{0,4},{1,3},{2,0},{3,7},{4,8},{5,1},{6,2},{7,11},{8,12},{9,5},{10,... | collective-permute-start | bytes 1572872 | tf_op jit(solution)/shard_map/ppermute | solution.py:309
  84.3 1.4 pad_add_fusion.3.meta
  85.7 1.3 pad_add_fusion.2.meta
  87.0 1.3 pad_add_fusion.1.meta
  88.4 1.2 copy-done.1
  89.6 3.0 %own_columns.1._ = bf16[256,8192]{1,0:T(8,128)(2,1)} custom-call(s32[1]{0:T(128)} %bitcast.10.meta, bf16[256,1024]{1,0:T(8,128)(2,1)} %broadcast_select_fusion.3.cot.own_cot, bf16[512,1024]{1,0:T(8,128)(2,1)S(1)} %copy-done.1, bf16[512,1024]{1,0:T(8,128)(2,1)S(1)} %get-tuple-element.20.second, bf16[256,128]{1,0:T(8,128)(2,1)S(1)} %get-tuple-element.11.g8, ...), custom_call_target="tpu_custom_call" | custom-call | flops 536870912 | bytes 4194304 | tf_op jit(solution)/shard_map/own_columns/pallas_call | solution.py:151
  92.6 1.1 slice.17
  93.7 1.0 reshape.73
  94.7 5.0 %product_tiles.5 = (f32[256,1024]{1,0:T(8,128)S(1)}, bf16[256,1024]{1,0:T(8,128)(2,1)}) custom-call(bf16[256,1024]{1,0:T(8,128)(2,1)} %broadcast_select_fusion.3.cot.own_cot, bf16[256,1024]{1,0:T(8,128)(2,1)S(1)} %collective-permute-done.6.far_cot, bf16[512,1024]{1,0:T(8,128)(2,1)} %collective-permute-done.1.left, ...), custom_call_target="tpu_custom_call" | custom-call | flops 1073741824 | bytes 6291456 | tf_op jit(solution)/shard_map/product_tiles/pallas_call | solution.py:68
  99.8 0.5 collective-permute-start.13
  100.3 1.0 copy-done.6
  101.3 4.7 %product_tiles.4 = (f32[256,1024]{1,0:T(8,128)S(1)}, bf16[256,1024]{1,0:T(8,128)(2,1)}) custom-call(bf16[256,1024]{1,0:T(8,128)(2,1)} %broadcast_select_fusion.3.cot.own_cot, bf16[256,1024]{1,0:T(8,128)(2,1)S(1)} %copy-done.6, bf16[512,1024]{1,0:T(8,128)(2,1)} %collective-permute-done.2.left, bf16[512,1024]{1,0:T(8,128)(2,1)} %collective-permute-done.10.right), custom_call_target="tpu_custom_call" | custom-call | flops 1073741824 | bytes 6291456 | tf_op jit(solution)/shard_map/product_tiles/pallas_call | solution.py:68
  106.1 1.5 collective-permute-start.11
  107.6 0.2 collective-permute-start.5
  107.8 8.5 %fusion.2 = f32[512,8192]{1,0:T(8,128)} fusion(bf16[32,8192]{1,0:T(8,128)(2,1)S(1)} %copy-done.8, s32[32]{0:T(128)S(1)} %select_reduce_fusion), kind=kOutput, calls=%fused_computation.15 | convolution fusion | flops 268451840 | bytes 17301632 | tf_op jit(solution)/shard_map/dot_general | solution.py:335
  116.3 0.8 slice.18
  117.1 1.7 %fusion.1 = f32[512,1024]{1,0:T(8,128)} fusion(bf16[32,1024]{1,0:T(8,128)(2,1)S(1)} %reshape.74, s32[32]{0:T(128)S(1)} %select_reduce_fusion), kind=kOutput, calls=%fused_computation.14 | convolution fusion | flops 33570816 | bytes 2162816 | tf_op jit(solution)/shard_map/dot_general | solution.py:336
  118.9 2.7 %finish_columns.3._ = bf16[256,8192]{1,0:T(8,128)(2,1)} custom-call(s32[3]{0:T(128)S(1)} %pad_add_fusion.3.meta, f32[256,1024]{1,0:T(8,128)S(1)} %get-tuple-element.16.own, bf16[256,1024]{1,0:T(8,128)(2,1)S(1)} %collective-permute-done.13.far, bf16[256,128]{1,0:T(8,128)(2,1)S(1)} %get-tuple-element.11.g8, ...), custom_call_target="tpu_custom_call", output_to_operand_aliasing={{}: (5, {})} | custom-call | flops 134217728 | bytes 3145728 | tf_op jit(solution)/shard_map/finish_columns/pallas_call | solution.py:115
  121.5 3.2 %collective-permute-done.11.far = bf16[256,1024]{1,0:T(8,128)(2,1)} collective-permute-done((bf16[256,1024]{1,0:T(8,128)(2,1)}, bf16[256,1024]{1,0:T(8,128)(2,1)}, u32[]{:S(2)}, u32[]{:S(2)}) %collective-permute-start.11) | collective-permute-done | bytes 524320 | tf_op jit(solution)/shard_map/ppermute | solution.py:303
  124.7 3.5 %finish_columns.4._ = bf16[256,8192]{1,0:T(8,128)(2,1)} custom-call(s32[3]{0:T(128)S(1)} %pad_add_fusion.2.meta, f32[256,1024]{1,0:T(8,128)S(1)} %copy-done.3, bf16[256,1024]{1,0:T(8,128)(2,1)} %collective-permute-done.11.far, bf16[256,128]{1,0:T(8,128)(2,1)S(1)} %get-tuple-element.11.g8, ...), custom_call_target="tpu_custom_call", output_to_operand_aliasing={{}: (5, {})} | custom-call | flops 134217728 | bytes 3145728 | tf_op jit(solution)/shard_map/finish_columns/pallas_call | solution.py:115
  128.2 4.0 %product_tiles.3 = (f32[256,1024]{1,0:T(8,128)S(1)}, bf16[256,1024]{1,0:T(8,128)(2,1)S(1)}) custom-call(bf16[256,1024]{1,0:T(8,128)(2,1)} %broadcast_select_fusion.3.cot.own_cot, bf16[256,1024]{1,0:T(8,128)(2,1)S(1)} %copy-done.7, bf16[512,1024]{1,0:T(8,128)(2,1)} %collective-permute-done.3.left, bf16[512,1024]{1,0:T(8,128)(2,1)} %collective-permute-done.8.right), custom_call_target="tpu_custom_call" | custom-call | flops 1073741824 | bytes 6291456 | tf_op jit(solution)/shard_map/product_tiles/pallas_call | solution.py:68
  132.3 0.6 collective-permute-start.9
  132.9 1.3 broadcast_select_fusion.6
  134.1 0.5 convolution_convert_fusion
  134.6 1.6 %collective-permute-start.7 = (bf16[256,512]{1,0:T(8,128)(2,1)S(1)}, bf16[256,512]{1,0:T(8,128)(2,1)S(1)}, u32[]{:S(2)}, u32[]{:S(2)}) collective-permute-start(bf16[256,512]{1,0:T(8,128)(2,1)S(1)} %convolution_convert_fusion), channel_id=1, source_target_pairs={{0,16},{16,0},{1,17},{17,1},{2,18},{18,2},{3,19},{19,3},{4,20},{20... | collective-permute-start | bytes 786440 | tf_op jit(solution)/shard_map/ppermute | solution.py:319
  136.2 1.5 fusion.own
  137.7 9.5 %collective-permute-done.9.far = bf16[256,1024]{1,0:T(8,128)(2,1)S(1)} collective-permute-done((bf16[256,1024]{1,0:T(8,128)(2,1)S(1)}, bf16[256,1024]{1,0:T(8,128)(2,1)S(1)}, u32[]{:S(2)}, u32[]{:S(2)}) %collective-permute-start.9) | collective-permute-done | bytes 524320 | tf_op jit(solution)/shard_map/ppermute | solution.py:303
  147.2 2.7 %finish_columns.5._ = bf16[256,8192]{1,0:T(8,128)(2,1)} custom-call(s32[3]{0:T(128)S(1)} %pad_add_fusion.1.meta, f32[256,1024]{1,0:T(8,128)S(1)} %get-tuple-element.12.own, bf16[256,1024]{1,0:T(8,128)(2,1)S(1)} %collective-permute-done.9.far, bf16[256,128]{1,0:T(8,128)(2,1)S(1)} %get-tuple-element.11.g8, ...), custom_call_target="tpu_custom_call", output_to_operand_aliasing={{}: (5, {})} | custom-call | flops 134217728 | bytes 3145728 | tf_op jit(solution)/shard_map/finish_columns/pallas_call | solution.py:115
  149.9 0.6 collective-permute-done.7.far
  150.4 1.9 %finish_last.1 = bf16[256,8192]{1,0:T(8,128)(2,1)} custom-call(s32[2]{0:T(128)S(1)} %pad_add_fusion.meta, f32[256,512]{1,0:T(8,128)S(1)} %fusion.own, bf16[256,512]{1,0:T(8,128)(2,1)S(1)} %collective-permute-done.7.far, bf16[256,128]{1,0:T(8,128)(2,1)S(1)} %get-tuple-element.11.g8, ...), custom_call_target="tpu_custom_call", output_to_operand_aliasing={{}: (5, {})} | custom-call | flops 67108864 | bytes 2097152 | tf_op jit(solution)/shard_map/finish_last/pallas_call | solution.py:344
  (46 shorter events, 0.3 us)
Async XLA Ops:
  0.6 9.0 %copy-start = (bf16[512,1024]{1,0:T(8,128)(2,1)S(1)}, bf16[512,1024]{1,0:T(8,128)(2,1)}, u32[]{:S(2)}) copy-start(bf16[512,1024]{1,0:T(8,128)(2,1)} %param.14) | copy-start | bytes 3145732
  0.6 3.0 %collective-permute-start = (bf16[512,1024]{1,0:T(8,128)(2,1)}, bf16[512,1024]{1,0:T(8,128)(2,1)S(1)}, u32[]{:S(2)}, u32[]{:S(2)}) collective-permute-start(bf16[512,1024]{1,0:T(8,128)(2,1)} %param.12), channel_id=1, source_target_pairs={{0,1},{1,0},{2,3},{3,2},{4,5},{5,4},{6,7},{7,6},{8,9},{9,8},{10,11... | collective-permute-start | bytes 3145736 | tf_op jit(solution)/shard_map/ppermute | solution.py:277
  1.2 8.2 %copy-start.11 = (s32[512]{0:T(512)S(1)}, s32[512]{0:T(512)}, u32[]{:S(2)}) copy-start(s32[512]{0:T(512)} %param.17) | copy-start | bytes 6148
  1.2 8.2 %copy-start.12 = (s32[32]{0:T(128)S(1)}, s32[32]{0:T(128)}, u32[]{:S(2)}) copy-start(s32[32]{0:T(128)} %param.15) | copy-start | bytes 388
  6.4 16.0 %collective-permute-start.1 = (bf16[512,1024]{1,0:T(8,128)(2,1)}, bf16[512,1024]{1,0:T(8,128)(2,1)}, u32[]{:S(2)}, u32[]{:S(2)}) collective-permute-start(bf16[512,1024]{1,0:T(8,128)(2,1)} %get-tuple-element.19), channel_id=1, source_target_pairs={{0,4},{1,3},{2,0},{3,7},{4,8},{5,1},{6,2},{7,11},{8,12},{9,5},{10,... | collective-permute-start | bytes 3145736 | tf_op jit(solution)/shard_map/ppermute | solution.py:300
  22.4 15.1 %collective-permute-start.2 = (bf16[512,1024]{1,0:T(8,128)(2,1)}, bf16[512,1024]{1,0:T(8,128)(2,1)}, u32[]{:S(2)}, u32[]{:S(2)}) collective-permute-start(bf16[512,1024]{1,0:T(8,128)(2,1)} %collective-permute-done.1.left), channel_id=1, source_target_pairs={{0,4},{1,3},{2,0},{3,7},{4,8},{5,1},{6,2},{7,11},{8,12},{9,5},{10,... | collective-permute-start | bytes 3145736 | tf_op jit(solution)/shard_map/ppermute | solution.py:300
  30.4 6.6 %copy-start.13 = (s32[32]{0:T(128)S(1)}, s32[32]{0:T(128)}, u32[]{:S(2)}) copy-start(s32[32]{0:T(128)} %param.16) | copy-start | bytes 388
  31.2 8.5 %copy-start.9 = (bf16[256,1024]{1,0:T(8,128)(2,1)S(1)}, bf16[256,1024]{1,0:T(8,128)(2,1)}, u32[]{:S(2)}) copy-start(bf16[256,1024]{1,0:T(8,128)(2,1)} %param.11) | copy-start | bytes 1572868
  32.0 20.6 %all-to-all-start = ((bf16[16,144,128]{2,1,0:T(8,128)(2,1)}), bf16[16,144,128]{2,1,0:T(8,128)(2,1)S(1)}, u32[]{:S(2)}, u32[]{:S(2)}) async-start(bf16[16,144,128]{2,1,0:T(8,128)(2,1)} %pad_maximum_fusion.3), calls=%async_computation | async-start | bytes 1179648 | tf_op jit(solution)/shard_map/all_to_all | solution.py:288
  37.5 43.1 %collective-permute-start.3 = (bf16[512,1024]{1,0:T(8,128)(2,1)}, bf16[512,1024]{1,0:T(8,128)(2,1)}, u32[]{:S(2)}, u32[]{:S(2)}) collective-permute-start(bf16[512,1024]{1,0:T(8,128)(2,1)} %collective-permute-done.2.left), channel_id=1, source_target_pairs={{0,4},{1,3},{2,0},{3,7},{4,8},{5,1},{6,2},{7,11},{8,12},{9,5},{10,... | collective-permute-start | bytes 3145736 | tf_op jit(solution)/shard_map/ppermute | solution.py:300
  52.7 2.2 %copy-start.4 = (bf16[256,8192]{1,0:T(8,128)(2,1)S(1)}, bf16[256,8192]{1,0:T(8,128)(2,1)}, u32[]{:S(2)}) copy-start(bf16[256,8192]{1,0:T(8,128)(2,1)} %x.1) | copy-start | bytes 12582916
  54.9 19.1 %copy-start.14 = (s32[8]{0:T(128)S(1)}, s32[8]{0:T(128)}, u32[]{:S(2)}) copy-start(s32[8]{0:T(128)} %constant.113.clone) | copy-start | bytes 100
  54.9 24.3 %copy-start.10 = (s32[8]{0:T(128)S(1)}, s32[8]{0:T(128)}, u32[]{:S(2)}) copy-start(s32[8]{0:T(128)} %constant.112.clone) | copy-start | bytes 100
  67.4 25.2 %all-to-all-start.1 = ((bf16[16,144,128]{2,1,0:T(8,128)(2,1)}), bf16[16,144,128]{2,1,0:T(8,128)(2,1)}, u32[]{:S(2)}, u32[]{:S(2)}) async-start(bf16[16,144,128]{2,1,0:T(8,128)(2,1)} %get-tuple-element.18), calls=%async_computation.1 | async-start | bytes 1179648 | tf_op jit(solution)/shard_map/all_to_all | solution.py:296
  71.9 22.8 %collective-permute-start.12 = (bf16[512,1024]{1,0:T(8,128)(2,1)}, bf16[512,1024]{1,0:T(8,128)(2,1)}, u32[]{:S(2)}, u32[]{:S(2)}) collective-permute-start(bf16[512,1024]{1,0:T(8,128)(2,1)} %collective-permute-done.1.left), channel_id=1, source_target_pairs={{0,1},{1,0},{2,3},{3,2},{4,5},{5,4},{6,7},{7,6},{8,9},{9,8},{10,11... | collective-permute-start | bytes 3145736 | tf_op jit(solution)/shard_map/ppermute | solution.py:301
  72.2 28.0 %collective-permute-start.10 = (bf16[512,1024]{1,0:T(8,128)(2,1)}, bf16[512,1024]{1,0:T(8,128)(2,1)}, u32[]{:S(2)}, u32[]{:S(2)}) collective-permute-start(bf16[512,1024]{1,0:T(8,128)(2,1)} %collective-permute-done.2.left), channel_id=1, source_target_pairs={{0,1},{1,0},{2,3},{3,2},{4,5},{5,4},{6,7},{7,6},{8,9},{9,8},{10,11... | collective-permute-start | bytes 3145736 | tf_op jit(solution)/shard_map/ppermute | solution.py:301
  72.4 22.3 %collective-permute-start.6 = (bf16[256,1024]{1,0:T(8,128)(2,1)}, bf16[256,1024]{1,0:T(8,128)(2,1)S(1)}, u32[]{:S(2)}, u32[]{:S(2)}) collective-permute-start(bf16[256,1024]{1,0:T(8,128)(2,1)} %broadcast_select_fusion.3.cot.own_cot), channel_id=1, source_target_pairs={{0,16},{16,0},{1,17},{17,1},{2,18},{18,2},{3,19},{19,3},{4,20},{20... | collective-permute-start | bytes 1572872 | tf_op jit(solution)/shard_map/ppermute | solution.py:276
  82.5 25.1 %collective-permute-start.4 = (bf16[256,1024]{1,0:T(8,128)(2,1)}, bf16[256,1024]{1,0:T(8,128)(2,1)}, u32[]{:S(2)}, u32[]{:S(2)}) collective-permute-start(bf16[256,1024]{1,0:T(8,128)(2,1)} %constant_dynamic-slice_fusion), channel_id=1, source_target_pairs={{0,4},{1,3},{2,0},{3,7},{4,8},{5,1},{6,2},{7,11},{8,12},{9,5},{10,... | collective-permute-start | bytes 1572872 | tf_op jit(solution)/shard_map/ppermute | solution.py:309
  88.4 1.2 copy-start.1
  94.7 5.0 %copy-start.5 = (bf16[256,1024]{1,0:T(8,128)(2,1)}, bf16[256,1024]{1,0:T(8,128)(2,1)S(1)}, u32[]{:S(2)}) copy-start(bf16[256,1024]{1,0:T(8,128)(2,1)S(1)} %collective-permute-done.6.far_cot) | copy-start | bytes 1572868
  94.7 13.1 %copy-start.8 = (bf16[32,8192]{1,0:T(8,128)(2,1)S(1)}, bf16[32,8192]{1,0:T(8,128)(2,1)}, u32[]{:S(2)}) copy-start(bf16[32,8192]{1,0:T(8,128)(2,1)} %reshape.73) | copy-start | bytes 1572868
  99.8 19.1 %collective-permute-start.13 = (bf16[256,1024]{1,0:T(8,128)(2,1)}, bf16[256,1024]{1,0:T(8,128)(2,1)S(1)}, u32[]{:S(2)}, u32[]{:S(2)}) collective-permute-start(bf16[256,1024]{1,0:T(8,128)(2,1)} %get-tuple-element.17), channel_id=1, source_target_pairs={{0,16},{16,0},{1,17},{17,1},{2,18},{18,2},{3,19},{19,3},{4,20},{20... | collective-permute-start | bytes 1572872 | tf_op jit(solution)/shard_map/ppermute | solution.py:303
  100.3 28.0 %collective-permute-start.8 = (bf16[512,1024]{1,0:T(8,128)(2,1)}, bf16[512,1024]{1,0:T(8,128)(2,1)}, u32[]{:S(2)}, u32[]{:S(2)}) collective-permute-start(bf16[512,1024]{1,0:T(8,128)(2,1)} %collective-permute-done.3.left), channel_id=1, source_target_pairs={{0,1},{1,0},{2,3},{3,2},{4,5},{5,4},{6,7},{7,6},{8,9},{9,8},{10,11... | collective-permute-start | bytes 3145736 | tf_op jit(solution)/shard_map/ppermute | solution.py:301
  100.3 1.0 copy-start.6
  106.1 10.2 %copy-start.2 = (f32[256,1024]{1,0:T(8,128)}, f32[256,1024]{1,0:T(8,128)S(1)}, u32[]{:S(2)}) copy-start(f32[256,1024]{1,0:T(8,128)S(1)} %get-tuple-element.14.own) | copy-start | bytes 3145732
  106.1 18.7 %collective-permute-start.11 = (bf16[256,1024]{1,0:T(8,128)(2,1)}, bf16[256,1024]{1,0:T(8,128)(2,1)}, u32[]{:S(2)}, u32[]{:S(2)}) collective-permute-start(bf16[256,1024]{1,0:T(8,128)(2,1)} %get-tuple-element.15), channel_id=1, source_target_pairs={{0,16},{16,0},{1,17},{17,1},{2,18},{18,2},{3,19},{19,3},{4,20},{20... | collective-permute-start | bytes 1572872 | tf_op jit(solution)/shard_map/ppermute | solution.py:303
  107.6 25.3 %collective-permute-start.5 = (bf16[256,1024]{1,0:T(8,128)(2,1)}, bf16[256,1024]{1,0:T(8,128)(2,1)}, u32[]{:S(2)}, u32[]{:S(2)}) collective-permute-start(bf16[256,1024]{1,0:T(8,128)(2,1)} %collective-permute-done.4), channel_id=1, source_target_pairs={{0,1},{1,0},{2,3},{3,2},{4,5},{5,4},{6,7},{7,6},{8,9},{9,8},{10,11... | collective-permute-start | bytes 1572872 | tf_op jit(solution)/shard_map/ppermute | solution.py:310
  118.9 5.8 %copy-start.3 = (f32[256,1024]{1,0:T(8,128)S(1)}, f32[256,1024]{1,0:T(8,128)}, u32[]{:S(2)}) copy-start(f32[256,1024]{1,0:T(8,128)} %copy-done.2) | copy-start | bytes 3145732
  124.7 3.5 %copy-start.7 = (bf16[256,1024]{1,0:T(8,128)(2,1)S(1)}, bf16[256,1024]{1,0:T(8,128)(2,1)}, u32[]{:S(2)}) copy-start(bf16[256,1024]{1,0:T(8,128)(2,1)} %copy-done.5) | copy-start | bytes 1572868
  132.3 14.9 %collective-permute-start.9 = (bf16[256,1024]{1,0:T(8,128)(2,1)S(1)}, bf16[256,1024]{1,0:T(8,128)(2,1)S(1)}, u32[]{:S(2)}, u32[]{:S(2)}) collective-permute-start(bf16[256,1024]{1,0:T(8,128)(2,1)S(1)} %get-tuple-element.13), channel_id=1, source_target_pairs={{0,16},{16,0},{1,17},{17,1},{2,18},{18,2},{3,19},{19,3},{4,20},{20... | collective-permute-start | bytes 1572872 | tf_op jit(solution)/shard_map/ppermute | solution.py:303
  134.6 15.8 %collective-permute-start.7 = (bf16[256,512]{1,0:T(8,128)(2,1)S(1)}, bf16[256,512]{1,0:T(8,128)(2,1)S(1)}, u32[]{:S(2)}, u32[]{:S(2)}) collective-permute-start(bf16[256,512]{1,0:T(8,128)(2,1)S(1)} %convolution_convert_fusion), channel_id=1, source_target_pairs={{0,16},{16,0},{1,17},{17,1},{2,18},{18,2},{3,19},{19,3},{4,20},{20... | collective-permute-start | bytes 786440 | tf_op jit(solution)/shard_map/ppermute | solution.py:319

commit v2 on v0

--- a/solution.py
+++ b/solution.py
@@ -1,12 +1,19 @@
+import functools
+
 import jax
 import jax.numpy as jnp
+import numpy as np
 from jax import lax
+from jax.experimental import pallas as pl
+from jax.experimental.pallas import tpu as pltpu
 from jax.sharding import PartitionSpec as P
 
 ADAPTER_RANK = 16
 ADAPTER_GROUP = 512
 BLOCK = 128
-
+LANES = 128
+PARAMS = pltpu.CompilerParams(vmem_limit_bytes=48 * 1024 * 1024)
+SMALL = pl.CostEstimate(flops=1, bytes_accessed=1, transcendentals=0)
 
 adapter_scale = 2.0
 
@@ -16,7 +23,593 @@
     return jnp.sum(jnp.where(matches, adapter_storage_row[None, :], 0), axis=1)
 
 
-def body(
+def iota(shape, axis):
+    return lax.broadcasted_iota(jnp.int32, shape, axis)
+
+
+def dot_t(a, b):
+    return lax.dot_general(a, b, (((1,), (1,)), ((), ())), preferred_element_type=jnp.float32)
+
+
+def dot_n(a, b, precision=None):
+    return lax.dot_general(
+        a, b, (((1,), (0,)), ((), ())), precision=precision, preferred_element_type=jnp.float32
+    )
+
+
+def dot_0(a, b):
+    return lax.dot_general(a, b, (((0,), (0,)), ((), ())), preferred_element_type=jnp.float32)
+
+
+def lane_cat(parts):
+    return jnp.concatenate(parts, axis=-1)
+
+
+def mask_kernel(meta, live, cot, out):
+    row = iota((BLOCK, cot.shape[1]), 0)
+    for k in range(cot.shape[0] // BLOCK):
+        rows = slice(k * BLOCK, (k + 1) * BLOCK)
+        value = cot[rows, :].astype(jnp.float32)
+        out[rows, :] = jnp.where(row < live[meta[0] + k], value, 0.0).astype(out.dtype)
+
+
+def mask_rows(meta, block_live_rows, cotangent):
+    whole = pl.BlockSpec(cotangent.shape, lambda i, *_: (0, 0))
+    return pl.pallas_call(
+        mask_kernel,
+        grid_spec=pltpu.PrefetchScalarGridSpec(
+            num_scalar_prefetch=2, grid=(1,), in_specs=[whole], out_specs=whole
+        ),
+        out_shape=jax.ShapeDtypeStruct(cotangent.shape, cotangent.dtype),
+        compiler_params=PARAMS,
+        cost_estimate=SMALL,
+        name="mask_rows",
+    )(meta, block_live_rows, cotangent)
+
+
+def rank_major_order(transposed):
+    shape = (8 * LANES, 8 * LANES)
+    near, far = (1, 0) if transposed else (0, 1)
+    a, b = iota(shape, near), iota(shape, far)
+    return ((a % LANES) * 8 + a // LANES == b).astype(jnp.bfloat16)
+
+
+def gather_kernel(adapter, storage, down, up, payload, dbuf, ubuf, dscr, uscr, cols, dsem, usem):
+    blocks = adapter.shape[0]
+    devices = payload.shape[0]
+    group = dbuf.shape[1]
+    per_down, per_up = down.shape[1] // LANES, up.shape[1] // LANES
+    down_rows = 2 * per_down
+
+    def copies(b):
+        slot = storage[adapter[b]]
+        start = pl.multiple_of((slot // group) * group, group)
+        return (
+            slot % group,
+            pltpu.make_async_copy(down.at[pl.ds(start, group), :], dbuf.at[b], dsem.at[b]),
+            pltpu.make_async_copy(up.at[pl.ds(start, group), :], ubuf.at[b], usem.at[b]),
+        )
+
+    def begin(b, carry):
+        _, first, second = copies(b)
+        first.start()
+        second.start()
+        return carry
+
+    lax.fori_loop(0, blocks, begin, 0)
+    order = rank_major_order(False)
+
+    def one(j, carry):
+        wide, narrow = [], []
+        for k in range(2):
+            b = 2 * j + k
+            row, first, second = copies(b)
+            first.wait()
+            second.wait()
+            late = row >= 8
+            line = row % 8
+            value = dbuf[b].astype(jnp.float32)
+            value = jnp.where(late, value[8:], value[:8])
+            for t in range(per_down):
+                dscr[k, 8 * t : 8 * t + 8, :] = value[:, t * LANES : (t + 1) * LANES]
+            wide.append(dscr[k, pl.ds(line, per_down, stride=8), :])
+            value = ubuf[b].astype(jnp.float32)
+            value = jnp.where(late, value[8:], value[:8])
+            for t in range(per_up):
+                uscr[k, 8 * t : 8 * t + 8, :] = value[:, t * LANES : (t + 1) * LANES]
+            narrow.append(uscr[k, pl.ds(line, per_up, stride=8), :])
+        turned = jnp.concatenate(wide, axis=0).T
+        start = pl.multiple_of(j * ADAPTER_RANK, ADAPTER_RANK)
+        for lo in range(8):
+            piece = turned[lo * ADAPTER_RANK : (lo + 1) * ADAPTER_RANK, :]
+            cols[pl.ds(start, ADAPTER_RANK), lo * LANES : (lo + 1) * LANES] = piece.astype(cols.dtype)
+        payload[j, down_rows:, :] = jnp.concatenate(narrow, axis=0).astype(payload.dtype)
+        return carry
+
+    lax.fori_loop(0, devices, one, 0)
+    result = dot_n(cols[...], order).astype(payload.dtype).reshape(devices, ADAPTER_RANK, 8 * LANES)
+    for q in range(8):
+        payload[:, q * ADAPTER_RANK : (q + 1) * ADAPTER_RANK, :] = result[
+            :, :, q * LANES : (q + 1) * LANES
+        ]
+
+
+def gather_rows(padded_block_adapter, adapter_storage_row, down, up, devices):
+    blocks = padded_block_adapter.shape[0]
+    per_down, per_up = down.shape[1] // LANES, up.shape[1] // LANES
+    group = 16
+    rows = 2 * (per_down + per_up)
+    shape = (devices, rows, LANES)
+    return pl.pallas_call(
+        gather_kernel,
+        grid_spec=pltpu.PrefetchScalarGridSpec(
+            num_scalar_prefetch=2,
+            grid=(1,),
+            in_specs=[pl.BlockSpec(memory_space=pl.ANY)] * 2,
+            out_specs=pl.BlockSpec(shape, lambda i, *_: (0, 0, 0)),
+            scratch_shapes=[
+                pltpu.VMEM((blocks, group, down.shape[1]), down.dtype),
+                pltpu.VMEM((blocks, group, up.shape[1]), up.dtype),
+                pltpu.VMEM((2, 8 * per_down, LANES), jnp.float32),
+                pltpu.VMEM((2, 8 * per_up, LANES), jnp.float32),
+                pltpu.VMEM((devices * ADAPTER_RANK, 8 * LANES), jnp.bfloat16),
+                pltpu.SemaphoreType.DMA((blocks,)),
+                pltpu.SemaphoreType.DMA((blocks,)),
+            ],
+        ),
+        out_shape=jax.ShapeDtypeStruct(shape, jnp.bfloat16),
+        compiler_params=PARAMS,
+        cost_estimate=SMALL,
+        name="gather_rows",
+    )(padded_block_adapter, adapter_storage_row, down, up)
+
+
+def adapter_kernel(x, cot, recv, sent, g_out, low_scr, gt_scr):
+    step = pl.program_id(0)
+    devices = recv.shape[0]
+    blocks = x.shape[0] // BLOCK
+    span = x.shape[1]
+    tiles = cot.shape[1] // LANES
+    up_chunk = tiles * ADAPTER_RANK // devices
+    down_rows = recv.shape[1] - blocks * up_chunk
+    per = down_rows // blocks // ADAPTER_RANK
+    here = span // LANES // per
+
+    @pl.when(step == 0)
+    def _():
+        lane = iota((BLOCK, LANES), 1)
+        gather_rank = (iota((LANES, LANES), 0) // 8 == iota((LANES, LANES), 1)).astype(jnp.float32)
+        b_all = recv[:, down_rows:, :].astype(jnp.float32)
+        for k in range(blocks):
+            m = cot[k * BLOCK : (k + 1) * BLOCK, :]
+            b_flat = b_all[:, k * up_chunk : (k + 1) * up_chunk, :].reshape(LANES, LANES)
+            b_flat = b_flat.astype(jnp.bfloat16)
+            total = jnp.zeros((BLOCK, LANES), jnp.float32)
+            for t in range(tiles):
+                part = dot_t(m[:, t * LANES : (t + 1) * LANES], b_flat)
+                total = total + jnp.where(lane % tiles == t, part, 0.0)
+            g = dot_n(total, gather_rank, lax.Precision.HIGHEST).astype(jnp.bfloat16)
+            g_out[k * BLOCK : (k + 1) * BLOCK, :] = g
+            gt_scr[k] = g.astype(jnp.float32).T[:ADAPTER_RANK, :].astype(jnp.bfloat16)
+        low_scr[...] = jnp.zeros_like(low_scr)
+
+    for k in range(blocks):
+        part = x[k * BLOCK : (k + 1) * BLOCK, :]
+        first = k * per * ADAPTER_RANK
+        a = lane_cat(
+            [
+                recv[step * here + j, first + q * ADAPTER_RANK : first + (q + 1) * ADAPTER_RANK, :]
+                for j in range(here)
+                for q in range(per)
+            ]
+        )
+        low_scr[k] += dot_t(part, a)
+        grad = (adapter_scale * dot_n(gt_scr[k], part)).astype(sent.dtype)
+        for j in range(here):
+            for q in range(per):
+                tile = j * per + q
+                sent[
+                    step * here + j, first + q * ADAPTER_RANK : first + (q + 1) * ADAPTER_RANK, :
+                ] = grad[:, tile * LANES : (tile + 1) * LANES]
+
+    @pl.when(step == pl.num_programs(0) - 1)
+    def _():
+        ups = []
+        row = iota((LANES, LANES), 0)
+        spread = (iota((ADAPTER_RANK, LANES), 1) // 8 == iota((ADAPTER_RANK, LANES), 0)).astype(
+            jnp.bfloat16
+        )
+        for k in range(blocks):
+            low8 = dot_n(low_scr[k].astype(jnp.bfloat16), spread).astype(jnp.bfloat16)
+            up = dot_0(low8, cot[k * BLOCK : (k + 1) * BLOCK, :])
+            flat = jnp.zeros((LANES, LANES), jnp.float32)
+            for t in range(tiles):
+                flat = flat + jnp.where(row % tiles == t, up[:, t * LANES : (t + 1) * LANES], 0.0)
+            ups.append((adapter_scale * flat).reshape(devices, up_chunk, LANES))
+        sent[:, down_rows:, :] = jnp.concatenate(ups, axis=1).astype(sent.dtype)
+
+
+def adapter_terms(x, cot, recv):
+    rows, width = x.shape
+    blocks = rows // BLOCK
+    steps = 8
+    whole = pl.BlockSpec(recv.shape, lambda i: (0, 0, 0))
+    return pl.pallas_call(
+        adapter_kernel,
+        grid=(steps,),
+        in_specs=[
+            pl.BlockSpec((rows, width // steps), lambda i: (0, i)),
+            pl.BlockSpec(cot.shape, lambda i: (0, 0)),
+            whole,
+        ],
+        out_specs=[whole, pl.BlockSpec((rows, LANES), lambda i: (0, 0))],
+        out_shape=[
+            jax.ShapeDtypeStruct(recv.shape, jnp.bfloat16),
+            jax.ShapeDtypeStruct((rows, LANES), jnp.bfloat16),
+        ],
+        scratch_shapes=[
+            pltpu.VMEM((blocks, BLOCK, ADAPTER_RANK), jnp.float32),
+            pltpu.VMEM((blocks, ADAPTER_RANK, BLOCK), jnp.bfloat16),
+        ],
+        compiler_params=PARAMS,
+        cost_estimate=SMALL,
+        name="adapter_terms",
+    )(x, cot, recv)
+
+
+def zero_kernel(down, up, zeros, sems):
+    zeros[...] = jnp.zeros_like(zeros)
+    rows = zeros.shape[0]
+    count = down.shape[0] // rows
+    copies = []
+    for i in range(count):
+        part = pl.ds(i * rows, rows)
+        copies.append(pltpu.make_async_copy(zeros, down.at[part, :], sems.at[2 * i]))
+        copies.append(
+            pltpu.make_async_copy(zeros.at[:, : up.shape[1]], up.at[part, :], sems.at[2 * i + 1])
+        )
+    for copy in copies:
+        copy.start()
+    for copy in copies:
+        copy.wait()
+
+
+def zero_grads(after, down_shape, up_shape):
+    rows = 64
+    count = down_shape[0] // rows
+
+    def kernel(after, down, up, zeros, sems):
+        zero_kernel(down, up, zeros, sems)
+
+    return pl.pallas_call(
+        kernel,
+        in_specs=[pl.BlockSpec(memory_space=pl.ANY)],
+        out_specs=[pl.BlockSpec(memory_space=pl.ANY)] * 2,
+        out_shape=[
+            jax.ShapeDtypeStruct(down_shape, jnp.float32),
+            jax.ShapeDtypeStruct(up_shape, jnp.float32),
+        ],
+        scratch_shapes=[
+            pltpu.VMEM((rows, down_shape[1]), jnp.float32),
+            pltpu.SemaphoreType.DMA((2 * count,)),
+        ],
+        compiler_params=PARAMS,
+        cost_estimate=SMALL,
+        name="zero_grads",
+    )(after)
+
+
+def scatter_kernel(
+    adapter, storage, recv, _down, _up, down, up, table, dacc, uacc, dscr, uscr, drow, urow, dsem, usem
+):
+    blocks = adapter.shape[0]
+    devices = recv.shape[0]
+    per_down, per_up = down.shape[1] // LANES, up.shape[1] // LANES
+    down_rows = 2 * per_down
+
+    def mark(i, carry):
+        b = blocks - 1 - i
+        table[storage[adapter[b]]] = b
+        return carry
+
+    lax.fori_loop(0, blocks, mark, 0)
+    dacc[...] = jnp.zeros_like(dacc)
+    uacc[...] = jnp.zeros_like(uacc)
+    value = lane_cat([recv[:, q * ADAPTER_RANK : (q + 1) * ADAPTER_RANK, :] for q in range(8)])
+    value = dot_n(value.reshape(devices * ADAPTER_RANK, 8 * LANES), rank_major_order(True))
+    for j in range(devices):
+        part = value[j * ADAPTER_RANK : (j + 1) * ADAPTER_RANK, :]
+        turned = jnp.concatenate(
+            [part[:, lo * LANES : (lo + 1) * LANES] for lo in range(8)], axis=0
+        ).T
+        narrow = recv[j, down_rows:, :].astype(jnp.float32)
+        for k in range(2):
+            first = table[storage[adapter[2 * j + k]]]
+            dacc[first] += turned[k * per_down : (k + 1) * per_down, :]
+            uacc[first] += narrow[k * per_up : (k + 1) * per_up, :]
+    for g in range(blocks // 8):
+        for i in range(8):
+            dscr[pl.ds(i, per_down, stride=8), :] = dacc[8 * g + i]
+            uscr[pl.ds(i, per_up, stride=8), :] = uacc[8 * g + i]
+        for t in range(per_down):
+            drow[8 * g : 8 * g + 8, t * LANES : (t + 1) * LANES] = dscr[8 * t : 8 * t + 8, :]
+        for t in range(per_up):
+            urow[8 * g : 8 * g + 8, t * LANES : (t + 1) * LANES] = uscr[8 * t : 8 * t + 8, :]
+
+    def copies(b):
+        slot = storage[adapter[b]]
+        return (
+            table[slot] == b,
+            pltpu.make_async_copy(drow.at[pl.ds(b, 1), :], down.at[pl.ds(slot, 1), :], dsem.at[b]),
+            pltpu.make_async_copy(urow.at[pl.ds(b, 1), :], up.at[pl.ds(slot, 1), :], usem.at[b]),
+        )
+
+    def begin(b, carry):
+        mine, first, second = copies(b)
+
+        @pl.when(mine)
+        def _():
+            first.start()
+            second.start()
+
+        return carry
+
+    def end(b, carry):
+        mine, first, second = copies(b)
+
+        @pl.when(mine)
+        def _():
+            first.wait()
+            second.wait()
+
+        return carry
+
+    lax.fori_loop(0, blocks, begin, 0)
+    lax.fori_loop(0, blocks, end, 0)
+
+
+def scatter_rows(padded_block_adapter, adapter_storage_row, recv, down, up):
+    blocks = padded_block_adapter.shape[0]
+    per_down, per_up = down.shape[1] // LANES, up.shape[1] // LANES
+    return pl.pallas_call(
+        scatter_kernel,
+        grid_spec=pltpu.PrefetchScalarGridSpec(
+            num_scalar_prefetch=2,
+            grid=(1,),
+            in_specs=[
+                pl.BlockSpec(recv.shape, lambda i, *_: (0, 0, 0)),
+                pl.BlockSpec(memory_space=pl.ANY),
+                pl.BlockSpec(memory_space=pl.ANY),
+            ],
+            out_specs=[pl.BlockSpec(memory_space=pl.ANY)] * 2,
+            scratch_shapes=[
+                pltpu.SMEM((ADAPTER_GROUP,), jnp.int32),
+                pltpu.VMEM((blocks, per_down, LANES), jnp.float32),
+                pltpu.VMEM((blocks, per_up, LANES), jnp.float32),
+                pltpu.VMEM((8 * per_down, LANES), jnp.float32),
+                pltpu.VMEM((8 * per_up, LANES), jnp.float32),
+                pltpu.VMEM((blocks, per_down * LANES), jnp.float32),
+                pltpu.VMEM((blocks, per_up * LANES), jnp.float32),
+                pltpu.SemaphoreType.DMA((blocks,)),
+                pltpu.SemaphoreType.DMA((blocks,)),
+            ],
+        ),
+        out_shape=[
+            jax.ShapeDtypeStruct(down.shape, down.dtype),
+            jax.ShapeDtypeStruct(up.shape, up.dtype),
+        ],
+        input_output_aliases={3: 0, 4: 1},
+        compiler_params=PARAMS,
+        cost_estimate=SMALL,
+        name="scatter_rows",
+    )(padded_block_adapter, adapter_storage_row, recv, down, up)
+
+
+def far_kernel(cot, left, right, out):
+    step = pl.program_id(0)
+    half = pl.num_programs(0) // 2
+
+    def part(weight):
+        out[...] = dot_t(cot[...], weight[...]).astype(out.dtype)
+
+    pl.when(step < half)(lambda: part(left))
+    pl.when(step >= half)(lambda: part(right))
+
+
+def far_product(cot, left, right):
+    rows, depth = cot.shape
+    width = left.shape[0]
+    tile = 256
+    per = width // tile
+    return pl.pallas_call(
+        far_kernel,
+        grid=(2 * per,),
+        in_specs=[
+            pl.BlockSpec((rows, depth), lambda i: (0, 0)),
+            pl.BlockSpec((tile, depth), lambda i: (jnp.minimum(i, per - 1), 0)),
+            pl.BlockSpec((tile, depth), lambda i: (jnp.maximum(i - per, 0), 0)),
+        ],
+        out_specs=pl.BlockSpec((rows, tile), lambda i: (0, i)),
+        out_shape=jax.ShapeDtypeStruct((rows, 2 * width), jnp.bfloat16),
+        compiler_params=PARAMS,
+        cost_estimate=SMALL,
+        name="far_product",
+    )(cot, left, right)
+
+
+def low_rank_columns(index, per_device, g, recv, width):
+    blocks = g.shape[0] // BLOCK
+    per = per_device * width // LANES
+    parts = []
+    for k in range(blocks):
+        first = (k * per + (index % per_device) * (width // LANES)) * ADAPTER_RANK
+        a = lane_cat(
+            [
+                recv[0, pl.ds(pl.multiple_of(first + q * ADAPTER_RANK, ADAPTER_RANK), ADAPTER_RANK), :]
+                for q in range(width // LANES)
+            ]
+        )
+        parts.append(dot_n(g[k * BLOCK : (k + 1) * BLOCK, :ADAPTER_RANK], a))
+    return adapter_scale * jnp.concatenate(parts, axis=0)
+
+
+def own_columns(meta, at, cot, left, right, g, recv, out, width, columns):
+    rows, depth = cot.shape
+    span = left.shape[0]
+    per_device = columns // span
+
+    def kernel(meta, cot, left, right, g, recv, *rest):
+        step = pl.program_id(0)
+        result = rest[-1]
+        lr = low_rank_columns(meta[at + step], per_device, g, recv, span)
+
+        def part(weight):
+            result[...] = (dot_t(cot[...], weight[...]) + lr).astype(result.dtype)
+
+        pl.when(step == 0)(lambda: part(left))
+        pl.when(step == 1)(lambda: part(right))
+
+    return pl.pallas_call(
+        kernel,
+        grid_spec=pltpu.PrefetchScalarGridSpec(
+            num_scalar_prefetch=1,
+            grid=(2,),
+            in_specs=[
+                pl.BlockSpec((rows, depth), lambda j, m: (0, 0)),
+                pl.BlockSpec((span, depth), lambda j, m: (0, 0)),
+                pl.BlockSpec((span, depth), lambda j, m: (0, 0)),
+                pl.BlockSpec((rows, LANES), lambda j, m: (0, 0)),
+                pl.BlockSpec((1,) + recv.shape[1:], lambda j, m: (m[at + j] // per_device, 0, 0)),
+            ]
+            + ([] if out is None else [pl.BlockSpec(memory_space=pl.ANY)]),
+            out_specs=pl.BlockSpec((rows, span), lambda j, m: (0, m[at + j])),
+        ),
+        out_shape=jax.ShapeDtypeStruct((rows, width), jnp.bfloat16),
+        input_output_aliases={} if out is None else {6: 0},
+        compiler_params=PARAMS,
+        cost_estimate=SMALL,
+        name="own_columns",
+    )(meta, cot, left, right, g, recv, *([] if out is None else [out]))
+
+
+def far_columns(meta, at, far, g, recv, out, columns):
+    rows, both = far.shape
+    span = both // 2
+    per_device = columns // span
+
+    def kernel(meta, far, g, recv, _, result):
+        lr = low_rank_columns(meta[at + pl.program_id(0)], per_device, g, recv, span)
+        result[...] = (far[...].astype(jnp.float32) + lr).astype(result.dtype)
+
+    return pl.pallas_call(
+        kernel,
+        grid_spec=pltpu.PrefetchScalarGridSpec(
+            num_scalar_prefetch=1,
+            grid=(2,),
+            in_specs=[
+                pl.BlockSpec((rows, span), lambda j, m: (0, j)),
+                pl.BlockSpec((rows, LANES), lambda j, m: (0, 0)),
+                pl.BlockSpec((1,) + recv.shape[1:], lambda j, m: (m[at + j] // per_device, 0, 0)),
+                pl.BlockSpec(memory_space=pl.ANY),
+            ],
+            out_specs=pl.BlockSpec((rows, span), lambda j, m: (0, m[at + j])),
+        ),
+        out_shape=jax.ShapeDtypeStruct(out.shape, out.dtype),
+        input_output_aliases={4: 0},
+        compiler_params=PARAMS,
+        cost_estimate=SMALL,
+        name="far_columns",
+    )(meta, far, g, recv, out)
+
+
+def ring_table(devices):
+    chips = devices // 2
+    order = list(range(0, chips, 2)) + list(range(chips - 1, 0, -2))
+    place = {c: i for i, c in enumerate(order)}
+    ring = []
+    for c in range(chips):
+        ring.append((2 * c, 2 * order[(place[c] + 1) % chips]))
+        ring.append((2 * c + 1, 2 * order[(place[c] - 1) % chips] + 1))
+    table = []
+    for part in range(2):
+        for index in range(devices):
+            chip, core = index // 2, index % 2
+            way = 2 * core - 1
+            row = [2 * index, index, index ^ 1]
+            for step in range(1, chips // 2):
+                pair = [order[(place[chip] + sign * way * step) % chips] for sign in (1, -1)]
+                row += [2 * c + part for c in pair] + [2 * c + 1 - part for c in pair]
+            last = order[(place[chip] + chips // 2) % chips]
+            row += [2 * (2 * last + part) + h for h in (core, 1 - core)]
+            row += [2 * (2 * last + 1 - part) + h for h in (core, 1 - core)]
+            table.append(row)
+    return ring, np.array(table, np.int32)
+
+
+def ring_body(
+    inputs,
+    cotangent,
+    frozen_value_weight,
+    adapter_down_weights,
+    adapter_up_weights,
+    padded_block_adapter,
+    block_live_rows,
+    adapter_storage_row,
+    *,
+    devices,
+):
+    chips = devices // 2
+    shard = frozen_value_weight.shape[0]
+    width = inputs.shape[1]
+    index, part = lax.axis_index("fsdp"), lax.axis_index("parts")
+    core = index % 2
+    ring, table = ring_table(devices)
+    meta = lax.dynamic_index_in_dim(jnp.asarray(table), part * devices + index, keepdims=False)
+    cores = [(i, i ^ 1) for i in range(devices)]
+    across = [(0, 1), (1, 0)]
+
+    other_shard = lax.ppermute(frozen_value_weight, "fsdp", cores)
+    masked = mask_rows(meta, block_live_rows, cotangent)
+    far_masked = lax.ppermute(masked, "parts", across)
+    travelling = jnp.where(part == core, frozen_value_weight, other_shard)
+
+    adapter, travelling = after(padded_block_adapter, travelling)
+    payload = gather_rows(
+        adapter, adapter_storage_row, adapter_down_weights, adapter_up_weights, devices
+    )
+    recv = lax.all_to_all(payload, "fsdp", split_axis=0, concat_axis=0, tiled=True)
+
+    pairs, fars = [], []
+    previous = payload
+    for step in range(chips // 2):
+        if step == chips // 2 - 1:
+            travelling = lax.dynamic_slice_in_dim(travelling, core * (shard // 2), shard // 2)
+        travelling = lax.ppermute(travelling, "fsdp", ring)
+        forwarded = lax.ppermute(travelling, "fsdp", cores)
+        pairs.append((travelling, forwarded))
+        product = far_product(far_masked, travelling, forwarded)
+        fars.append(lax.ppermute(product, "parts", across))
+        if step == 0:
+            down, up = zero_grads(product, adapter_down_weights.shape, adapter_up_weights.shape)
+            cot, _, _ = after(masked, product, down)
+            sent, g = adapter_terms(inputs, cot, recv)
+            grads = lax.all_to_all(sent, "fsdp", split_axis=0, concat_axis=0, tiled=True)
+
+    out = own_columns(
+        meta, 1, masked, frozen_value_weight, other_shard, g, recv, None, width, shard
+    )
+    for step in range(chips // 2):
+        out = own_columns(meta, 3 + 4 * step, masked, *pairs[step], g, recv, out, width, shard)
+        out = far_columns(meta, 5 + 4 * step, fars[step], g, recv, out, shard)
+    down_grad, up_grad = scatter_rows(padded_block_adapter, adapter_storage_row, grads, down, up)
+    return (out, down_grad, up_grad)
+
+
+def after(value, *earlier):
+    return lax.optimization_barrier((value,) + earlier)
+
+
+def gather_body(
     inputs,
     cotangent,
     frozen_value_weight,
@@ -91,6 +684,7 @@
 
 
 def solution(mesh):
+    devices = mesh.shape["fsdp"]
     in_specs = (
         P(("parts", "fsdp"), None),
         P(("parts", "fsdp"), None),
@@ -102,4 +696,18 @@
         P("parts"),
     )
     out_specs = (P(("parts", "fsdp"), None), P("parts", "fsdp"), P("parts", "fsdp"))
-    return jax.shard_map(body, mesh=mesh, in_specs=in_specs, out_specs=out_specs, check_vma=False)
+
+    def program(*arrays):
+        shard = arrays[2].shape[0] // devices
+        rows = arrays[0].shape[0] // devices // 2
+        adapter_tiles = arrays[3].shape[1] // devices // LANES
+        fits = rows == 2 * BLOCK and 2 * adapter_tiles == LANES and shard % 512 == 0
+        if mesh.shape["parts"] == 2 and devices % 4 == 0 and fits:
+            body = functools.partial(ring_body, devices=devices)
+        else:
+            body = gather_body
+        return jax.shard_map(
+            body, mesh=mesh, in_specs=in_specs, out_specs=out_specs, check_vma=False
+        )(*arrays)
+
+    return program

time: 193 us -> 144 us (0.75)
  Pallas kernels: 0 us -> 62.4 us
  matrix products: 41.1 us -> 0 us
  waiting for transfers between devices: 77.1 us -> 45.1 us
  local copies, waits for them, and re-layouts: 28.1 us -> 7.12 us
  between operations: 14.2 us -> 0.84 us
  starting transfers between devices: 29.3 us -> 25.9 us
    pallas_call x0 -> x18, Pallas kernels: none -> 62.4 us  [the longest x5 18.2 us: own_columns(): pl.pallas_call(kernel, grid_spec=pltpu.PrefetchScalarGridSpec(num_scalar_...]
    all_to_all x4 -> x2, waiting for transfers between devices: 53.4 us -> 0.01 us  [the longest x1 0.01 us: ring_body(): lax.all_to_all(payload, 'fsdp', split_axis=0, concat_axis=0, tiled=True)]
    ppermute x0 -> x14, waiting for transfers between devices: none -> 45.1 us  [the longest x4 25.9 us: ring_body(): travelling = lax.ppermute(travelling, 'fsdp', ring)]
    dot_general x7 -> x0, matrix products: 41.1 us -> none  [the longest x1 12.4 us: body(): lax.dot_general(masked, lax.all_gather(frozen_value_weight, 'fsdp', axis=...]
    all_gather x1 -> x0, waiting for transfers between devices: 23 us -> none  [body(): lax.all_gather(frozen_value_weight, 'fsdp', axis=0, tiled=True)]
    all_to_all x4 -> x2, starting transfers between devices: 29.2 us -> 10.9 us  [the longest x1 5.92 us: ring_body(): lax.all_to_all(sent, 'fsdp', split_axis=0, concat_axis=0, tiled=True)]
    ppermute x0 -> x14, starting transfers between devices: none -> 15 us  [the longest x4 8.81 us: ring_body(): travelling = lax.ppermute(travelling, 'fsdp', ring)]
    all_to_all x5 -> x0, local copies, waits for them, and re-layouts: 10.8 us -> none  [the longest x3 10.4 us: body(): lax.all_to_all(partial_down_weight, 'fsdp', split_axis=1, concat_axis=0,...]
  transfers between devices with their start and end apart: 5 -> 16, of which waited for: 3 -> 6; matrix products, arithmetic and copies ran while one was open for 27% -> 1% of each run, Pallas kernels for 0% -> 42%
where the time goes in v2:
time: 144 us; the launch traced here: 143 us
  Pallas kernels  62.4 us (43%)
  waiting for transfers between devices  45.1 us (31%)
  starting transfers between devices  25.9 us (18%)
  local copies, waits for them, and re-layouts  7.12 us (5%)
  other arithmetic  1.74 us (1%)
    ppermute x4, waiting for transfers between devices, ring_body(): travelling = lax.ppermute(travelling, 'fsdp', ring)  25.9 us
    pallas_call x5, Pallas kernels, own_columns(): pl.pallas_call(kernel, grid_spec=pltpu.PrefetchScalarGridSpec(num_scalar_...  18.2 us
    pallas_call x4, Pallas kernels, far_product(): pl.pallas_call(far_kernel, grid=(2 * per,), in_specs=[pl.BlockSpec((rows,...  12.5 us
    ppermute x1, waiting for transfers between devices, ring_body(): far_masked = lax.ppermute(masked, 'parts', across)  10.9 us
    ppermute x4, starting transfers between devices, ring_body(): travelling = lax.ppermute(travelling, 'fsdp', ring)  8.81 us
    pallas_call x1, Pallas kernels, gather_rows(): pl.pallas_call(gather_kernel, grid_spec=pltpu.PrefetchScalarGridSpec(num_...  8.35 us
    pallas_call x4, Pallas kernels, far_columns(): pl.pallas_call(kernel, grid_spec=pltpu.PrefetchScalarGridSpec(num_scalar_...  7.69 us
    pallas_call x1, Pallas kernels, zero_grads(): pl.pallas_call(kernel, in_specs=[pl.BlockSpec(memory_space=pl.ANY)], out_...  6.73 us
  transfers between devices with their start and end apart: 16, of which 6 were waited for; matrix products, arithmetic and copies ran while one was open for 1% of the time, Pallas kernels for 42%

profile of v2, /device:TPU:0, one launch (start us, length us, event | category | flops | bytes accessed | tf_op | source)
XLA Modules:
  0.0 143.1 jit_solution(12369154414619473966)
XLA Ops:
  0.6 0.5 collective-permute-start.1
  1.1 2.5 %collective-permute-done.1.right = bf16[512,1024]{1,0:T(8,128)(2,1)S(1)} collective-permute-done((bf16[512,1024]{1,0:T(8,128)(2,1)}, bf16[512,1024]{1,0:T(8,128)(2,1)S(1)}, u32[]{:S(2)}, u32[]{:S(2)}) %collective-permute-start.1) | collective-permute-done | bytes 1048608 | tf_op jit(solution)/shard_map/ppermute | solution.py:571
  3.7 1.7 %broadcast_select_fusion = bf16[512,1024]{1,0:T(8,128)(2,1)S(1)} fusion(bf16[512,1024]{1,0:T(8,128)(2,1)} %left.1, bf16[512,1024]{1,0:T(8,128)(2,1)S(1)} %collective-permute-done.1.right, pred[]{:T(512)S(6)} %eq.5), kind=kLoop, calls=%fused_computation | loop fusion | flops 524288 | bytes 3145729 | tf_op jit(solution)/shard_map/jit(_where)/select_n | solution.py:574
  5.4 3.0 %collective-permute-start.2 = (bf16[512,1024]{1,0:T(8,128)(2,1)S(1)}, bf16[512,1024]{1,0:T(8,128)(2,1)}, u32[]{:S(2)}, u32[]{:S(2)}) collective-permute-start(bf16[512,1024]{1,0:T(8,128)(2,1)S(1)} %broadcast_select_fusion), channel_id=1, source_target_pairs={{0,4},{1,3},{2,0},{3,7},{4,8},{5,1},{6,2},{7,11},{8,12},{9,5},{10,... | collective-permute-start | bytes 3145736 | tf_op jit(solution)/shard_map/ppermute | solution.py:587
  8.4 12.8 %collective-permute-done.2.left = bf16[512,1024]{1,0:T(8,128)(2,1)} collective-permute-done((bf16[512,1024]{1,0:T(8,128)(2,1)S(1)}, bf16[512,1024]{1,0:T(8,128)(2,1)}, u32[]{:S(2)}, u32[]{:S(2)}) %collective-permute-start.2) | collective-permute-done | bytes 1048608 | tf_op jit(solution)/shard_map/ppermute | solution.py:587
  21.2 2.1 %collective-permute-start.3 = (bf16[512,1024]{1,0:T(8,128)(2,1)}, bf16[512,1024]{1,0:T(8,128)(2,1)}, u32[]{:S(2)}, u32[]{:S(2)}) collective-permute-start(bf16[512,1024]{1,0:T(8,128)(2,1)} %collective-permute-done.2.left), channel_id=1, source_target_pairs={{0,4},{1,3},{2,0},{3,7},{4,8},{5,1},{6,2},{7,11},{8,12},{9,5},{10,... | collective-permute-start | bytes 3145736 | tf_op jit(solution)/shard_map/ppermute | solution.py:587
  23.3 13.0 %collective-permute-done.3.left = bf16[512,1024]{1,0:T(8,128)(2,1)} collective-permute-done((bf16[512,1024]{1,0:T(8,128)(2,1)}, bf16[512,1024]{1,0:T(8,128)(2,1)}, u32[]{:S(2)}, u32[]{:S(2)}) %collective-permute-start.3) | collective-permute-done | bytes 1048608 | tf_op jit(solution)/shard_map/ppermute | solution.py:587
  36.3 2.1 %collective-permute-start.4 = (bf16[512,1024]{1,0:T(8,128)(2,1)}, bf16[512,1024]{1,0:T(8,128)(2,1)S(1)}, u32[]{:S(2)}, u32[]{:S(2)}) collective-permute-start(bf16[512,1024]{1,0:T(8,128)(2,1)} %collective-permute-done.3.left), channel_id=1, source_target_pairs={{0,4},{1,3},{2,0},{3,7},{4,8},{5,1},{6,2},{7,11},{8,12},{9,5},{10,... | collective-permute-start | bytes 3145736 | tf_op jit(solution)/shard_map/ppermute | solution.py:587
  38.4 1.2 copy-done.7
  39.6 0.7 copy-done.10
  40.3 0.7 copy-done.12
  41.0 8.4 %gather_rows.1 = bf16[16,144,128]{2,1,0:T(8,128)(2,1)} custom-call(s32[32]{0:T(128)S(1)} %copy-done.12, s32[512]{0:T(512)S(1)} %copy-done.10, bf16[512,8192]{1,0:T(8,128)(2,1)} %down.1, bf16[512,1024]{1,0:T(8,128)(2,1)S(1)} %copy-done.7), custom_call_target="tpu_custom_call" | custom-call | flops 1 | bytes 1 | tf_op jit(solution)/shard_map/gather_rows/pallas_call | solution.py:143
  49.3 4.9 %all-to-all-start = ((bf16[16,144,128]{2,1,0:T(8,128)(2,1)}), bf16[16,144,128]{2,1,0:T(8,128)(2,1)S(1)}, u32[]{:S(2)}, u32[]{:S(2)}) async-start(bf16[16,144,128]{2,1,0:T(8,128)(2,1)} %gather_rows.1), calls=%async_computation | async-start | bytes 1179648 | tf_op jit(solution)/shard_map/all_to_all | solution.py:580
  54.3 0.4 collective-permute-start.8
  54.7 0.7 dynamic-slice_bitcast_fusion.meta
  55.4 0.0 copy-done.9
  55.4 0.6 mask_rows.1.cot
  56.0 0.1 collective-permute-start
  56.1 0.2 collective-permute-start.11
  56.3 0.0 collective-permute-done.4.left
  56.4 0.3 collective-permute-start.9
  56.7 0.8 constant_dynamic-slice_fusion
  57.5 1.7 %collective-permute-start.5 = (bf16[256,1024]{1,0:T(8,128)(2,1)}, bf16[256,1024]{1,0:T(8,128)(2,1)}, u32[]{:S(2)}, u32[]{:S(2)}) collective-permute-start(bf16[256,1024]{1,0:T(8,128)(2,1)} %constant_dynamic-slice_fusion), channel_id=1, source_target_pairs={{0,4},{1,3},{2,0},{3,7},{4,8},{5,1},{6,2},{7,11},{8,12},{9,5},{10,... | collective-permute-start | bytes 1572872 | tf_op jit(solution)/shard_map/ppermute | solution.py:587
  59.2 10.9 %collective-permute-done.cot = bf16[256,1024]{1,0:T(8,128)(2,1)S(1)} collective-permute-done((bf16[256,1024]{1,0:T(8,128)(2,1)S(1)}, bf16[256,1024]{1,0:T(8,128)(2,1)S(1)}, u32[]{:S(2)}, u32[]{:S(2)}) %collective-permute-start) | collective-permute-done | bytes 524320 | tf_op jit(solution)/shard_map/ppermute | solution.py:573
  70.1 0.0 collective-permute-done.8.right
  70.1 3.4 %far_product.5.after = bf16[256,1024]{1,0:T(8,128)(2,1)S(1)} custom-call(bf16[256,1024]{1,0:T(8,128)(2,1)S(1)} %collective-permute-done.cot, bf16[512,1024]{1,0:T(8,128)(2,1)} %collective-permute-done.2.left, bf16[512,1024]{1,0:T(8,128)(2,1)} %collective-permute-done.8.right), custom_call_target="tpu_custom_call" | custom-call | flops 1 | bytes 1 | tf_op jit(solution)/shard_map/far_product/pallas_call | solution.py:424
  73.5 6.7 %zero_grads.1 = (f32[512,8192]{1,0:T(8,128)}, f32[512,1024]{1,0:T(8,128)}) custom-call(bf16[256,1024]{1,0:T(8,128)(2,1)S(1)} %far_product.5.after), custom_call_target="tpu_custom_call" | custom-call | flops 1 | bytes 1 | tf_op jit(solution)/shard_map/zero_grads/pallas_call | solution.py:284
  80.2 0.0 all-to-all-done.recv
  80.3 0.0 copy-start
  80.3 2.2 %copy-done = bf16[256,8192]{1,0:T(8,128)(2,1)S(1)} copy-done((bf16[256,8192]{1,0:T(8,128)(2,1)S(1)}, bf16[256,8192]{1,0:T(8,128)(2,1)}, u32[]{:S(2)}) %copy-start) | copy-done | bytes 4194328
  82.4 4.6 %adapter_terms.1 = (bf16[16,144,128]{2,1,0:T(8,128)(2,1)S(1)}, bf16[256,128]{1,0:T(8,128)(2,1)S(1)}) custom-call(bf16[256,8192]{1,0:T(8,128)(2,1)S(1)} %copy-done, bf16[256,1024]{1,0:T(8,128)(2,1)S(1)} %mask_rows.1.cot, bf16[16,144,128]{2,1,0:T(8,128)(2,1)S(1)} %all-to-all-done.recv), custom_call_target="tpu_custom_call" | custom-call | flops 1 | bytes 1 | tf_op jit(solution)/shard_map/adapter_terms/pallas_call | solution.py:237
  87.0 0.8 copy-done.8
  87.8 5.9 %all-to-all-start.1 = ((bf16[16,144,128]{2,1,0:T(8,128)(2,1)}), bf16[16,144,128]{2,1,0:T(8,128)(2,1)S(1)}, u32[]{:S(2)}, u32[]{:S(2)}) async-start(bf16[16,144,128]{2,1,0:T(8,128)(2,1)} %copy-done.8), calls=%async_computation.1 | async-start | bytes 1179648 | tf_op jit(solution)/shard_map/all_to_all | solution.py:596
  93.8 0.0 copy-start.1
  93.8 0.0 copy-start.3
  93.8 0.0 collective-permute-done.5.left
  93.8 0.5 collective-permute-start.6
  94.3 0.3 collective-permute-start.13
  94.6 0.0 collective-permute-done.11.right
  94.6 3.4 %far_product.7 = bf16[256,1024]{1,0:T(8,128)(2,1)S(1)} custom-call(bf16[256,1024]{1,0:T(8,128)(2,1)S(1)} %collective-permute-done.cot, bf16[512,1024]{1,0:T(8,128)(2,1)} %collective-permute-done.3.left, bf16[512,1024]{1,0:T(8,128)(2,1)} %collective-permute-done.11.right), custom_call_target="tpu_custom_call" | custom-call | flops 1 | bytes 1 | tf_op jit(solution)/shard_map/far_product/pallas_call | solution.py:424
  97.9 1.8 %collective-permute-start.12 = (bf16[256,1024]{1,0:T(8,128)(2,1)S(1)}, bf16[256,1024]{1,0:T(8,128)(2,1)S(1)}, u32[]{:S(2)}, u32[]{:S(2)}) collective-permute-start(bf16[256,1024]{1,0:T(8,128)(2,1)S(1)} %far_product.7), channel_id=1, source_target_pairs={{0,16},{16,0},{1,17},{17,1},{2,18},{18,2},{3,19},{19,3},{4,20},{20... | collective-permute-start | bytes 1572872 | tf_op jit(solution)/shard_map/ppermute | solution.py:591
  99.7 0.0 collective-permute-done.9.right
  99.7 3.2 %far_product.6 = bf16[256,1024]{1,0:T(8,128)(2,1)S(1)} custom-call(bf16[256,1024]{1,0:T(8,128)(2,1)S(1)} %collective-permute-done.cot, bf16[512,1024]{1,0:T(8,128)(2,1)S(1)} %collective-permute-done.4.left, bf16[512,1024]{1,0:T(8,128)(2,1)} %collective-permute-done.9.right), custom_call_target="tpu_custom_call" | custom-call | flops 1 | bytes 1 | tf_op jit(solution)/shard_map/far_product/pallas_call | solution.py:424
  102.9 0.4 collective-permute-start.10
  103.3 0.0 collective-permute-done.6.right
  103.3 2.6 %far_product.4 = bf16[256,512]{1,0:T(8,128)(2,1)} custom-call(bf16[256,1024]{1,0:T(8,128)(2,1)S(1)} %collective-permute-done.cot, bf16[256,1024]{1,0:T(8,128)(2,1)} %collective-permute-done.5.left, bf16[256,1024]{1,0:T(8,128)(2,1)S(1)} %collective-permute-done.6.right), custom_call_target="tpu_custom_call" | custom-call | flops 1 | bytes 1 | tf_op jit(solution)/shard_map/far_product/pallas_call | solution.py:424
  105.9 1.7 %collective-permute-start.7 = (bf16[256,512]{1,0:T(8,128)(2,1)}, bf16[256,512]{1,0:T(8,128)(2,1)}, u32[]{:S(2)}, u32[]{:S(2)}) collective-permute-start(bf16[256,512]{1,0:T(8,128)(2,1)} %far_product.4), channel_id=1, source_target_pairs={{0,16},{16,0},{1,17},{17,1},{2,18},{18,2},{3,19},{19,3},{4,20},{20... | collective-permute-start | bytes 786440 | tf_op jit(solution)/shard_map/ppermute | solution.py:591
  107.6 0.0 copy-done.1
  107.6 2.6 %own_columns.5.rest_0_ = bf16[256,8192]{1,0:T(8,128)(2,1)} custom-call(s32[19]{0:T(128)S(1)} %dynamic-slice_bitcast_fusion.meta, bf16[256,1024]{1,0:T(8,128)(2,1)S(1)} %mask_rows.1.cot, bf16[512,1024]{1,0:T(8,128)(2,1)S(1)} %copy-done.1, bf16[512,1024]{1,0:T(8,128)(2,1)S(1)} %copy-done.3, bf16[256,128]{1,0:T(8,128)(2,1)S(1)} %get-tuple-element.16.g, ...), custom_call_target="tpu_custom_call" | custom-call | flops 1 | bytes 1 | tf_op jit(solution)/shard_map/own_columns/pallas_call | solution.py:472
  110.2 4.2 %own_columns.6._ = bf16[256,8192]{1,0:T(8,128)(2,1)} custom-call(s32[19]{0:T(128)S(1)} %dynamic-slice_bitcast_fusion.meta, bf16[256,1024]{1,0:T(8,128)(2,1)S(1)} %mask_rows.1.cot, bf16[512,1024]{1,0:T(8,128)(2,1)} %collective-permute-done.2.left, bf16[512,1024]{1,0:T(8,128)(2,1)} %collective-permute-done.8.right, ...), custom_call_target="tpu_custom_call", output_to_operand_aliasing={{}: (6, {})} | custom-call | flops 1 | bytes 1 | tf_op jit(solution)/shard_map/own_columns/pallas_call | solution.py:472
  114.4 0.0 collective-permute-done.13.far
  114.4 1.7 %far_columns.4.rest_0_ = bf16[256,8192]{1,0:T(8,128)(2,1)} custom-call(s32[19]{0:T(128)S(1)} %dynamic-slice_bitcast_fusion.meta, bf16[256,1024]{1,0:T(8,128)(2,1)S(1)} %collective-permute-done.13.far, bf16[256,128]{1,0:T(8,128)(2,1)S(1)} %get-tuple-element.16.g, bf16[16,144,128]{2,1,0:T(8,128)(2,1)S(1)} %all-to-all-done.recv, ...), custom_call_target="tpu_custom_call", output_to_operand_aliasing={{}: (4, {})} | custom-call | flops 1 | bytes 1 | tf_op jit(solution)/shard_map/far_columns/pallas_call | solution.py:504
  116.2 4.2 %own_columns.7._ = bf16[256,8192]{1,0:T(8,128)(2,1)} custom-call(s32[19]{0:T(128)S(1)} %dynamic-slice_bitcast_fusion.meta, bf16[256,1024]{1,0:T(8,128)(2,1)S(1)} %mask_rows.1.cot, bf16[512,1024]{1,0:T(8,128)(2,1)} %collective-permute-done.3.left, bf16[512,1024]{1,0:T(8,128)(2,1)} %collective-permute-done.11.right, ...), custom_call_target="tpu_custom_call", output_to_operand_aliasing={{}: (6, {})} | custom-call | flops 1 | bytes 1 | tf_op jit(solution)/shard_map/own_columns/pallas_call | solution.py:472
  120.3 0.1 collective-permute-done.12.far
  120.5 1.7 %far_columns.5.rest_0_ = bf16[256,8192]{1,0:T(8,128)(2,1)} custom-call(s32[19]{0:T(128)S(1)} %dynamic-slice_bitcast_fusion.meta, bf16[256,1024]{1,0:T(8,128)(2,1)S(1)} %collective-permute-done.12.far, bf16[256,128]{1,0:T(8,128)(2,1)S(1)} %get-tuple-element.16.g, bf16[16,144,128]{2,1,0:T(8,128)(2,1)S(1)} %all-to-all-done.recv, ...), custom_call_target="tpu_custom_call", output_to_operand_aliasing={{}: (4, {})} | custom-call | flops 1 | bytes 1 | tf_op jit(solution)/shard_map/far_columns/pallas_call | solution.py:504
  122.2 3.9 %own_columns.8._ = bf16[256,8192]{1,0:T(8,128)(2,1)} custom-call(s32[19]{0:T(128)S(1)} %dynamic-slice_bitcast_fusion.meta, bf16[256,1024]{1,0:T(8,128)(2,1)S(1)} %mask_rows.1.cot, bf16[512,1024]{1,0:T(8,128)(2,1)S(1)} %collective-permute-done.4.left, bf16[512,1024]{1,0:T(8,128)(2,1)} %collective-permute-done.9.right, ...), custom_call_target="tpu_custom_call", output_to_operand_aliasing={{}: (6, {})} | custom-call | flops 1 | bytes 1 | tf_op jit(solution)/shard_map/own_columns/pallas_call | solution.py:472
  126.1 5.6 %collective-permute-done.10.far = bf16[256,1024]{1,0:T(8,128)(2,1)S(1)} collective-permute-done((bf16[256,1024]{1,0:T(8,128)(2,1)S(1)}, bf16[256,1024]{1,0:T(8,128)(2,1)S(1)}, u32[]{:S(2)}, u32[]{:S(2)}) %collective-permute-start.10) | collective-permute-done | bytes 524320 | tf_op jit(solution)/shard_map/ppermute | solution.py:591
  131.7 1.7 %far_columns.6.rest_0_ = bf16[256,8192]{1,0:T(8,128)(2,1)} custom-call(s32[19]{0:T(128)S(1)} %dynamic-slice_bitcast_fusion.meta, bf16[256,1024]{1,0:T(8,128)(2,1)S(1)} %collective-permute-done.10.far, bf16[256,128]{1,0:T(8,128)(2,1)S(1)} %get-tuple-element.16.g, bf16[16,144,128]{2,1,0:T(8,128)(2,1)S(1)} %all-to-all-done.recv, ...), custom_call_target="tpu_custom_call", output_to_operand_aliasing={{}: (4, {})} | custom-call | flops 1 | bytes 1 | tf_op jit(solution)/shard_map/far_columns/pallas_call | solution.py:504
  133.5 0.0 all-to-all-done.1.recv
  133.5 0.0 copy-done.11
  133.5 3.8 %scatter_rows.1 = (f32[512,8192]{1,0:T(8,128)}, f32[512,1024]{1,0:T(8,128)}) custom-call(s32[32]{0:T(128)S(1)} %copy-done.13, s32[512]{0:T(512)S(1)} %copy-done.11, bf16[16,144,128]{2,1,0:T(8,128)(2,1)S(1)} %all-to-all-done.1.recv, f32[512,8192]{1,0:T(8,128)} %get-tuple-element.13._down, ...), custom_call_target="tpu_custom_call", output_to_operand_aliasing={{0}: (3, {}), {1}: (4, {})} | custom-call | flops 1 | bytes 1 | tf_op jit(solution)/shard_map/scatter_rows/pallas_call | solution.py:374
  137.3 3.3 %own_columns.9._ = bf16[256,8192]{1,0:T(8,128)(2,1)} custom-call(s32[19]{0:T(128)S(1)} %dynamic-slice_bitcast_fusion.meta, bf16[256,1024]{1,0:T(8,128)(2,1)S(1)} %mask_rows.1.cot, bf16[256,1024]{1,0:T(8,128)(2,1)} %collective-permute-done.5.left, bf16[256,1024]{1,0:T(8,128)(2,1)S(1)} %copy-done.6, ...), custom_call_target="tpu_custom_call", output_to_operand_aliasing={{}: (6, {})} | custom-call | flops 1 | bytes 1 | tf_op jit(solution)/shard_map/own_columns/pallas_call | solution.py:472
  140.6 0.0 collective-permute-done.7.far
  140.6 2.5 %far_columns.7 = bf16[256,8192]{1,0:T(8,128)(2,1)} custom-call(s32[19]{0:T(128)S(1)} %dynamic-slice_bitcast_fusion.meta, bf16[256,512]{1,0:T(8,128)(2,1)} %collective-permute-done.7.far, bf16[256,128]{1,0:T(8,128)(2,1)S(1)} %get-tuple-element.16.g, bf16[16,144,128]{2,1,0:T(8,128)(2,1)S(1)} %all-to-all-done.recv, ...), custom_call_target="tpu_custom_call", output_to_operand_aliasing={{}: (4, {})} | custom-call | flops 1 | bytes 1 | tf_op jit(solution)/shard_map/far_columns/pallas_call | solution.py:504
  (19 shorter events, 0.0 us)
Async XLA Ops:
  0.6 3.0 %collective-permute-start.1 = (bf16[512,1024]{1,0:T(8,128)(2,1)}, bf16[512,1024]{1,0:T(8,128)(2,1)S(1)}, u32[]{:S(2)}, u32[]{:S(2)}) collective-permute-start(bf16[512,1024]{1,0:T(8,128)(2,1)} %left.1), channel_id=1, source_target_pairs={{0,1},{1,0},{2,3},{3,2},{4,5},{5,4},{6,7},{7,6},{8,9},{9,8},{10,11... | collective-permute-start | bytes 3145736 | tf_op jit(solution)/shard_map/ppermute | solution.py:571
  3.6 45.7 %copy-start.2 = (bf16[512,1024]{1,0:T(8,128)(2,1)}, bf16[512,1024]{1,0:T(8,128)(2,1)S(1)}, u32[]{:S(2)}) copy-start(bf16[512,1024]{1,0:T(8,128)(2,1)S(1)} %collective-permute-done.1.right) | copy-start | bytes 3145732
  3.6 51.7 %copy-start.9 = (bf16[256,1024]{1,0:T(8,128)(2,1)S(1)}, bf16[256,1024]{1,0:T(8,128)(2,1)}, u32[]{:S(2)}) copy-start(bf16[256,1024]{1,0:T(8,128)(2,1)} %cot.1) | copy-start | bytes 1572868
  3.7 51.7 %copy-start.14 = (s32[32]{0:T(128)S(1)}, s32[32]{0:T(128)}, u32[]{:S(2)}) copy-start(s32[32]{0:T(128)} %live.1) | copy-start | bytes 388
  5.4 15.8 %collective-permute-start.2 = (bf16[512,1024]{1,0:T(8,128)(2,1)S(1)}, bf16[512,1024]{1,0:T(8,128)(2,1)}, u32[]{:S(2)}, u32[]{:S(2)}) collective-permute-start(bf16[512,1024]{1,0:T(8,128)(2,1)S(1)} %broadcast_select_fusion), channel_id=1, source_target_pairs={{0,4},{1,3},{2,0},{3,7},{4,8},{5,1},{6,2},{7,11},{8,12},{9,5},{10,... | collective-permute-start | bytes 3145736 | tf_op jit(solution)/shard_map/ppermute | solution.py:587
  21.2 15.1 %collective-permute-start.3 = (bf16[512,1024]{1,0:T(8,128)(2,1)}, bf16[512,1024]{1,0:T(8,128)(2,1)}, u32[]{:S(2)}, u32[]{:S(2)}) collective-permute-start(bf16[512,1024]{1,0:T(8,128)(2,1)} %collective-permute-done.2.left), channel_id=1, source_target_pairs={{0,4},{1,3},{2,0},{3,7},{4,8},{5,1},{6,2},{7,11},{8,12},{9,5},{10,... | collective-permute-start | bytes 3145736 | tf_op jit(solution)/shard_map/ppermute | solution.py:587
  36.3 20.0 %collective-permute-start.4 = (bf16[512,1024]{1,0:T(8,128)(2,1)}, bf16[512,1024]{1,0:T(8,128)(2,1)S(1)}, u32[]{:S(2)}, u32[]{:S(2)}) collective-permute-start(bf16[512,1024]{1,0:T(8,128)(2,1)} %collective-permute-done.3.left), channel_id=1, source_target_pairs={{0,4},{1,3},{2,0},{3,7},{4,8},{5,1},{6,2},{7,11},{8,12},{9,5},{10,... | collective-permute-start | bytes 3145736 | tf_op jit(solution)/shard_map/ppermute | solution.py:587
  38.4 1.2 copy-start.7
  39.6 0.7 copy-start.10
  40.3 0.7 copy-start.12
  49.3 30.9 %all-to-all-start = ((bf16[16,144,128]{2,1,0:T(8,128)(2,1)}), bf16[16,144,128]{2,1,0:T(8,128)(2,1)S(1)}, u32[]{:S(2)}, u32[]{:S(2)}) async-start(bf16[16,144,128]{2,1,0:T(8,128)(2,1)} %gather_rows.1), calls=%async_computation | async-start | bytes 1179648 | tf_op jit(solution)/shard_map/all_to_all | solution.py:580
  54.3 15.8 %collective-permute-start.8 = (bf16[512,1024]{1,0:T(8,128)(2,1)}, bf16[512,1024]{1,0:T(8,128)(2,1)}, u32[]{:S(2)}, u32[]{:S(2)}) collective-permute-start(bf16[512,1024]{1,0:T(8,128)(2,1)} %collective-permute-done.2.left), channel_id=1, source_target_pairs={{0,1},{1,0},{2,3},{3,2},{4,5},{5,4},{6,7},{7,6},{8,9},{9,8},{10,11... | collective-permute-start | bytes 3145736 | tf_op jit(solution)/shard_map/ppermute | solution.py:588
  56.0 14.1 %collective-permute-start = (bf16[256,1024]{1,0:T(8,128)(2,1)S(1)}, bf16[256,1024]{1,0:T(8,128)(2,1)S(1)}, u32[]{:S(2)}, u32[]{:S(2)}) collective-permute-start(bf16[256,1024]{1,0:T(8,128)(2,1)S(1)} %mask_rows.1.cot), channel_id=1, source_target_pairs={{0,16},{16,0},{1,17},{17,1},{2,18},{18,2},{3,19},{19,3},{4,20},{20... | collective-permute-start | bytes 1572872 | tf_op jit(solution)/shard_map/ppermute | solution.py:573
  56.1 38.4 %collective-permute-start.11 = (bf16[512,1024]{1,0:T(8,128)(2,1)}, bf16[512,1024]{1,0:T(8,128)(2,1)}, u32[]{:S(2)}, u32[]{:S(2)}) collective-permute-start(bf16[512,1024]{1,0:T(8,128)(2,1)} %collective-permute-done.3.left), channel_id=1, source_target_pairs={{0,1},{1,0},{2,3},{3,2},{4,5},{5,4},{6,7},{7,6},{8,9},{9,8},{10,11... | collective-permute-start | bytes 3145736 | tf_op jit(solution)/shard_map/ppermute | solution.py:588
  56.4 43.4 %collective-permute-start.9 = (bf16[512,1024]{1,0:T(8,128)(2,1)S(1)}, bf16[512,1024]{1,0:T(8,128)(2,1)}, u32[]{:S(2)}, u32[]{:S(2)}) collective-permute-start(bf16[512,1024]{1,0:T(8,128)(2,1)S(1)} %collective-permute-done.4.left), channel_id=1, source_target_pairs={{0,1},{1,0},{2,3},{3,2},{4,5},{5,4},{6,7},{7,6},{8,9},{9,8},{10,11... | collective-permute-start | bytes 3145736 | tf_op jit(solution)/shard_map/ppermute | solution.py:588
  57.5 36.3 %collective-permute-start.5 = (bf16[256,1024]{1,0:T(8,128)(2,1)}, bf16[256,1024]{1,0:T(8,128)(2,1)}, u32[]{:S(2)}, u32[]{:S(2)}) collective-permute-start(bf16[256,1024]{1,0:T(8,128)(2,1)} %constant_dynamic-slice_fusion), channel_id=1, source_target_pairs={{0,4},{1,3},{2,0},{3,7},{4,8},{5,1},{6,2},{7,11},{8,12},{9,5},{10,... | collective-permute-start | bytes 1572872 | tf_op jit(solution)/shard_map/ppermute | solution.py:587
  73.5 6.7 %copy-start.4 = (bf16[256,1024]{1,0:T(8,128)(2,1)}, bf16[256,1024]{1,0:T(8,128)(2,1)S(1)}, u32[]{:S(2)}) copy-start(bf16[256,1024]{1,0:T(8,128)(2,1)S(1)} %far_product.5.after) | copy-start | bytes 1572868
  80.3 2.2 %copy-start = (bf16[256,8192]{1,0:T(8,128)(2,1)S(1)}, bf16[256,8192]{1,0:T(8,128)(2,1)}, u32[]{:S(2)}) copy-start(bf16[256,8192]{1,0:T(8,128)(2,1)} %x.1) | copy-start | bytes 12582916
  87.0 0.8 copy-start.8
  87.8 45.6 %all-to-all-start.1 = ((bf16[16,144,128]{2,1,0:T(8,128)(2,1)}), bf16[16,144,128]{2,1,0:T(8,128)(2,1)S(1)}, u32[]{:S(2)}, u32[]{:S(2)}) async-start(bf16[16,144,128]{2,1,0:T(8,128)(2,1)} %copy-done.8), calls=%async_computation.1 | async-start | bytes 1179648 | tf_op jit(solution)/shard_map/all_to_all | solution.py:596
  93.8 13.8 %copy-start.1 = (bf16[512,1024]{1,0:T(8,128)(2,1)S(1)}, bf16[512,1024]{1,0:T(8,128)(2,1)}, u32[]{:S(2)}) copy-start(bf16[512,1024]{1,0:T(8,128)(2,1)} %left.1) | copy-start | bytes 3145732
  93.8 13.8 %copy-start.3 = (bf16[512,1024]{1,0:T(8,128)(2,1)S(1)}, bf16[512,1024]{1,0:T(8,128)(2,1)}, u32[]{:S(2)}) copy-start(bf16[512,1024]{1,0:T(8,128)(2,1)} %copy-done.2) | copy-start | bytes 3145732
  93.8 9.5 %collective-permute-start.6 = (bf16[256,1024]{1,0:T(8,128)(2,1)}, bf16[256,1024]{1,0:T(8,128)(2,1)S(1)}, u32[]{:S(2)}, u32[]{:S(2)}) collective-permute-start(bf16[256,1024]{1,0:T(8,128)(2,1)} %collective-permute-done.5.left), channel_id=1, source_target_pairs={{0,1},{1,0},{2,3},{3,2},{4,5},{5,4},{6,7},{7,6},{8,9},{9,8},{10,11... | collective-permute-start | bytes 1572872 | tf_op jit(solution)/shard_map/ppermute | solution.py:588
  94.3 20.2 %collective-permute-start.13 = (bf16[256,1024]{1,0:T(8,128)(2,1)}, bf16[256,1024]{1,0:T(8,128)(2,1)S(1)}, u32[]{:S(2)}, u32[]{:S(2)}) collective-permute-start(bf16[256,1024]{1,0:T(8,128)(2,1)} %copy-done.4), channel_id=1, source_target_pairs={{0,16},{16,0},{1,17},{17,1},{2,18},{18,2},{3,19},{19,3},{4,20},{20... | collective-permute-start | bytes 1572872 | tf_op jit(solution)/shard_map/ppermute | solution.py:591
  97.9 22.6 %collective-permute-start.12 = (bf16[256,1024]{1,0:T(8,128)(2,1)S(1)}, bf16[256,1024]{1,0:T(8,128)(2,1)S(1)}, u32[]{:S(2)}, u32[]{:S(2)}) collective-permute-start(bf16[256,1024]{1,0:T(8,128)(2,1)S(1)} %far_product.7), channel_id=1, source_target_pairs={{0,16},{16,0},{1,17},{17,1},{2,18},{18,2},{3,19},{19,3},{4,20},{20... | collective-permute-start | bytes 1572872 | tf_op jit(solution)/shard_map/ppermute | solution.py:591
  102.9 28.8 %collective-permute-start.10 = (bf16[256,1024]{1,0:T(8,128)(2,1)S(1)}, bf16[256,1024]{1,0:T(8,128)(2,1)S(1)}, u32[]{:S(2)}, u32[]{:S(2)}) collective-permute-start(bf16[256,1024]{1,0:T(8,128)(2,1)S(1)} %far_product.6), channel_id=1, source_target_pairs={{0,16},{16,0},{1,17},{17,1},{2,18},{18,2},{3,19},{19,3},{4,20},{20... | collective-permute-start | bytes 1572872 | tf_op jit(solution)/shard_map/ppermute | solution.py:591
  103.3 7.0 %copy-start.5 = (bf16[256,1024]{1,0:T(8,128)(2,1)}, bf16[256,1024]{1,0:T(8,128)(2,1)S(1)}, u32[]{:S(2)}) copy-start(bf16[256,1024]{1,0:T(8,128)(2,1)S(1)} %collective-permute-done.6.right) | copy-start | bytes 1572868
  105.9 34.7 %collective-permute-start.7 = (bf16[256,512]{1,0:T(8,128)(2,1)}, bf16[256,512]{1,0:T(8,128)(2,1)}, u32[]{:S(2)}, u32[]{:S(2)}) collective-permute-start(bf16[256,512]{1,0:T(8,128)(2,1)} %far_product.4), channel_id=1, source_target_pairs={{0,16},{16,0},{1,17},{17,1},{2,18},{18,2},{3,19},{19,3},{4,20},{20... | collective-permute-start | bytes 786440 | tf_op jit(solution)/shard_map/ppermute | solution.py:591
  126.1 7.4 %copy-start.11 = (s32[512]{0:T(512)S(1)}, s32[512]{0:T(512)}, u32[]{:S(2)}) copy-start(s32[512]{0:T(512)} %storage.3) | copy-start | bytes 6148
  126.1 7.4 %copy-start.13 = (s32[32]{0:T(128)S(1)}, s32[32]{0:T(128)}, u32[]{:S(2)}) copy-start(s32[32]{0:T(128)} %adapter.2) | copy-start | bytes 388
  133.5 3.8 %copy-start.6 = (bf16[256,1024]{1,0:T(8,128)(2,1)S(1)}, bf16[256,1024]{1,0:T(8,128)(2,1)}, u32[]{:S(2)}) copy-start(bf16[256,1024]{1,0:T(8,128)(2,1)} %copy-done.5) | copy-start | bytes 1572868

commit v3 on v2

v3 whole, which is shorter than its diff:
```python
import functools

import jax
import jax.numpy as jnp
import numpy as np
from jax import lax
from jax.experimental import pallas as pl
from jax.experimental.pallas import tpu as pltpu
from jax.sharding import PartitionSpec as P

ADAPTER_RANK = 16
ADAPTER_GROUP = 512
BLOCK = 128
LANES = 128
MIB = 1024 * 1024
ZERO_ROWS = 64
PARAMS = pltpu.CompilerParams(vmem_limit_bytes=16 * MIB)
WIDE_PARAMS = pltpu.CompilerParams(vmem_limit_bytes=24 * MIB)
IN_VMEM = pl.BlockSpec(memory_space=pltpu.VMEM)
IN_SMEM = pl.BlockSpec(memory_space=pltpu.SMEM)
IN_HBM = pl.BlockSpec(memory_space=pltpu.HBM)
SMALL = pl.CostEstimate(flops=1, bytes_accessed=1, transcendentals=0)

adapter_scale = 2.0


def slot_lookup(padded_block_adapter, adapter_storage_row):
    matches = padded_block_adapter[:, None] == jnp.arange(ADAPTER_GROUP, dtype=jnp.int32)[None, :]
    return jnp.sum(jnp.where(matches, adapter_storage_row[None, :], 0), axis=1)


def iota(shape, axis):
    return lax.broadcasted_iota(jnp.int32, shape, axis)


def dot_t(a, b):
    return lax.dot_general(a, b, (((1,), (1,)), ((), ())), preferred_element_type=jnp.float32)


def dot_n(a, b, precision=None):
    return lax.dot_general(
        a, b, (((1,), (0,)), ((), ())), precision=precision, preferred_element_type=jnp.float32
    )


def dot_0(a, b):
    return lax.dot_general(a, b, (((0,), (0,)), ((), ())), preferred_element_type=jnp.float32)


def lane_cat(parts):
    return jnp.concatenate(parts, axis=-1)


def mask_kernel(meta, live, cot, out):
    row = iota((BLOCK, cot.shape[1]), 0)
    for k in range(cot.shape[0] // BLOCK):
        rows = slice(k * BLOCK, (k + 1) * BLOCK)
        value = cot[rows, :].astype(jnp.float32)
        out[rows, :] = jnp.where(row < live[meta[0] + k], value, 0.0).astype(out.dtype)


def mask_rows(meta, block_live_rows, cotangent):
    return pl.pallas_call(
        mask_kernel,
        in_specs=[IN_SMEM, IN_SMEM, IN_VMEM],
        out_specs=IN_VMEM,
        out_shape=jax.ShapeDtypeStruct(cotangent.shape, cotangent.dtype),
        compiler_params=PARAMS,
        cost_estimate=SMALL,
        name="mask_rows",
    )(meta, block_live_rows, cotangent)


def rank_major_order(transposed):
    shape = (8 * LANES, 8 * LANES)
    near, far = (1, 0) if transposed else (0, 1)
    a, b = iota(shape, near), iota(shape, far)
    return ((a % LANES) * 8 + a // LANES == b).astype(jnp.bfloat16)


def zero_copies(zeros, target, sems, first, rows):
    part = zeros if target.shape[1] == zeros.shape[1] else zeros.at[:, : target.shape[1]]
    return [
        pltpu.make_async_copy(part, target.at[pl.ds(start, ZERO_ROWS), :], sems.at[i])
        for i, start in enumerate(range(first, first + rows, ZERO_ROWS))
    ]


def gather_kernel(
    adapter, storage, down, up, payload, grads, dbuf, ubuf, dscr, uscr, cols, zeros, dsem, usem, zsem
):
    blocks = adapter.shape[0]
    devices = payload.shape[0]
    group = dbuf.shape[1]
    per_down, per_up = down.shape[1] // LANES, up.shape[1] // LANES
    down_rows = 2 * per_down

    def copies(b):
        slot = storage[adapter[b]]
        start = pl.multiple_of((slot // group) * group, group)
        return (
            slot % group,
            pltpu.make_async_copy(down.at[pl.ds(start, group), :], dbuf.at[b], dsem.at[b]),
            pltpu.make_async_copy(up.at[pl.ds(start, group), :], ubuf.at[b], usem.at[b]),
        )

    def begin(b, carry):
        _, first, second = copies(b)
        first.start()
        second.start()
        return carry

    lax.fori_loop(0, blocks, begin, 0)
    zeros[...] = jnp.zeros_like(zeros)
    fills = zero_copies(zeros, grads, zsem, 0, grads.shape[0] // 2)
    for copy in fills:
        copy.start()
    order = rank_major_order(False)

    def one(j, carry):
        wide, narrow = [], []
        for k in range(2):
            b = 2 * j + k
            row, first, second = copies(b)
            first.wait()
            second.wait()
            late = row >= 8
            line = row % 8
            value = dbuf[b].astype(jnp.float32)
            value = jnp.where(late, value[8:], value[:8])
            for t in range(per_down):
                dscr[k, 8 * t : 8 * t + 8, :] = value[:, t * LANES : (t + 1) * LANES]
            wide.append(dscr[k, pl.ds(line, per_down, stride=8), :])
            value = ubuf[b].astype(jnp.float32)
            value = jnp.where(late, value[8:], value[:8])
            for t in range(per_up):
                uscr[k, 8 * t : 8 * t + 8, :] = value[:, t * LANES : (t + 1) * LANES]
            narrow.append(uscr[k, pl.ds(line, per_up, stride=8), :])
        turned = jnp.concatenate(wide, axis=0).T
        start = pl.multiple_of(j * ADAPTER_RANK, ADAPTER_RANK)
        for lo in range(8):
            piece = turned[lo * ADAPTER_RANK : (lo + 1) * ADAPTER_RANK, :]
            cols[pl.ds(start, ADAPTER_RANK), lo * LANES : (lo + 1) * LANES] = piece.astype(cols.dtype)
        payload[j, down_rows:, :] = jnp.concatenate(narrow, axis=0).astype(payload.dtype)
        return carry

    lax.fori_loop(0, devices, one, 0)
    result = dot_n(cols[...], order).astype(payload.dtype).reshape(devices, ADAPTER_RANK, 8 * LANES)
    for q in range(8):
        payload[:, q * ADAPTER_RANK : (q + 1) * ADAPTER_RANK, :] = result[
            :, :, q * LANES : (q + 1) * LANES
        ]
    for copy in fills:
        copy.wait()


def gather_rows(padded_block_adapter, adapter_storage_row, down, up, devices):
    blocks = padded_block_adapter.shape[0]
    per_down, per_up = down.shape[1] // LANES, up.shape[1] // LANES
    group = 16
    rows = 2 * (per_down + per_up)
    shape = (devices, rows, LANES)
    return pl.pallas_call(
        gather_kernel,
        in_specs=[IN_SMEM, IN_SMEM, IN_HBM, IN_HBM],
        out_specs=[IN_VMEM, IN_HBM],
        out_shape=[
            jax.ShapeDtypeStruct(shape, jnp.bfloat16),
            jax.ShapeDtypeStruct(down.shape, jnp.float32),
        ],
        scratch_shapes=[
            pltpu.VMEM((blocks, group, down.shape[1]), down.dtype),
            pltpu.VMEM((blocks, group, up.shape[1]), up.dtype),
            pltpu.VMEM((2, 8 * per_down, LANES), jnp.float32),
            pltpu.VMEM((2, 8 * per_up, LANES), jnp.float32),
            pltpu.VMEM((devices * ADAPTER_RANK, 8 * LANES), jnp.bfloat16),
            pltpu.VMEM((ZERO_ROWS, down.shape[1]), jnp.float32),
            pltpu.SemaphoreType.DMA((blocks,)),
            pltpu.SemaphoreType.DMA((blocks,)),
            pltpu.SemaphoreType.DMA((down.shape[0] // 2 // ZERO_ROWS,)),
        ],
        compiler_params=WIDE_PARAMS,
        cost_estimate=SMALL,
        name="gather_rows",
    )(padded_block_adapter, adapter_storage_row, down, up)


def adapter_kernel(x, cot, recv, _, sent, g_out, grads, up_grads, xbuf, zeros, xsem, zsem, usem):
    devices = recv.shape[0]
    blocks = x.shape[0] // BLOCK
    steps = xbuf.shape[0]
    span = xbuf.shape[2]
    tiles = cot.shape[1] // LANES
    up_chunk = tiles * ADAPTER_RANK // devices
    down_rows = recv.shape[1] - blocks * up_chunk
    per = down_rows // blocks // ADAPTER_RANK
    here = span // LANES // per

    loads = [
        pltpu.make_async_copy(x.at[:, i * span : (i + 1) * span], xbuf.at[i], xsem.at[i])
        for i in range(steps)
    ]
    for copy in loads:
        copy.start()
    zeros[...] = jnp.zeros_like(zeros)
    half = grads.shape[0] // 2
    fills = zero_copies(zeros, grads, zsem, half, half)
    fills += zero_copies(zeros, up_grads, usem, 0, up_grads.shape[0])
    for copy in fills:
        copy.start()

    lane = iota((BLOCK, LANES), 1)
    gather_rank = (iota((LANES, LANES), 0) // 8 == iota((LANES, LANES), 1)).astype(jnp.float32)
    b_all = recv[:, down_rows:, :].astype(jnp.float32)
    turned = []
    for k in range(blocks):
        m = cot[k * BLOCK : (k + 1) * BLOCK, :]
        b_flat = b_all[:, k * up_chunk : (k + 1) * up_chunk, :].reshape(LANES, LANES)
        b_flat = b_flat.astype(jnp.bfloat16)
        total = jnp.zeros((BLOCK, LANES), jnp.float32)
        for t in range(tiles):
            part = dot_t(m[:, t * LANES : (t + 1) * LANES], b_flat)
            total = total + jnp.where(lane % tiles == t, part, 0.0)
        g = dot_n(total, gather_rank, lax.Precision.HIGHEST).astype(jnp.bfloat16)
        g_out[k * BLOCK : (k + 1) * BLOCK, :] = g
        turned.append(g.astype(jnp.float32).T[:ADAPTER_RANK, :].astype(jnp.bfloat16))

    lows = [jnp.zeros((BLOCK, ADAPTER_RANK), jnp.float32) for _ in range(blocks)]
    for i in range(steps):
        loads[i].wait()
        for k in range(blocks):
            part = xbuf[i, k * BLOCK : (k + 1) * BLOCK, :]
            first = k * per * ADAPTER_RANK
            spots = [
                (i * here + j, first + q * ADAPTER_RANK) for j in range(here) for q in range(per)
            ]
            a = lane_cat([recv[j, at : at + ADAPTER_RANK, :] for j, at in spots])
            lows[k] = lows[k] + dot_t(part, a)
            grad = (adapter_scale * dot_n(turned[k], part)).astype(sent.dtype)
            for tile, (j, at) in enumerate(spots):
                sent[j, at : at + ADAPTER_RANK, :] = grad[:, tile * LANES : (tile + 1) * LANES]

    ups = []
    row = iota((LANES, LANES), 0)
    spread = (iota((ADAPTER_RANK, LANES), 1) // 8 == iota((ADAPTER_RANK, LANES), 0)).astype(
        jnp.bfloat16
    )
    for k in range(blocks):
        low8 = dot_n(lows[k].astype(jnp.bfloat16), spread).astype(jnp.bfloat16)
        up = dot_0(low8, cot[k * BLOCK : (k + 1) * BLOCK, :])
        flat = jnp.zeros((LANES, LANES), jnp.float32)
        for t in range(tiles):
            flat = flat + jnp.where(row % tiles == t, up[:, t * LANES : (t + 1) * LANES], 0.0)
        ups.append((adapter_scale * flat).reshape(devices, up_chunk, LANES))
    sent[:, down_rows:, :] = jnp.concatenate(ups, axis=1).astype(sent.dtype)
    for copy in fills:
        copy.wait()


def adapter_terms(x, cot, recv, grads, up_shape):
    rows, width = x.shape
    steps = 8
    return pl.pallas_call(
        adapter_kernel,
        in_specs=[IN_HBM, IN_VMEM, IN_VMEM, IN_HBM],
        out_specs=[IN_VMEM, IN_VMEM, IN_HBM, IN_HBM],
        out_shape=[
            jax.ShapeDtypeStruct(recv.shape, jnp.bfloat16),
            jax.ShapeDtypeStruct((rows, LANES), jnp.bfloat16),
            jax.ShapeDtypeStruct(grads.shape, grads.dtype),
            jax.ShapeDtypeStruct(up_shape, jnp.float32),
        ],
        input_output_aliases={3: 2},
        scratch_shapes=[
            pltpu.VMEM((steps, rows, width // steps), x.dtype),
            pltpu.VMEM((ZERO_ROWS, grads.shape[1]), jnp.float32),
            pltpu.SemaphoreType.DMA((steps,)),
            pltpu.SemaphoreType.DMA((grads.shape[0] // 2 // ZERO_ROWS,)),
            pltpu.SemaphoreType.DMA((up_shape[0] // ZERO_ROWS,)),
        ],
        compiler_params=PARAMS,
        cost_estimate=SMALL,
        name="adapter_terms",
    )(x, cot, recv, grads)


def scatter_kernel(
    adapter, storage, recv, _down, _up, down, up, table, dacc, uacc, dscr, uscr, drow, urow, dsem, usem
):
    blocks = adapter.shape[0]
    devices = recv.shape[0]
    per_down, per_up = down.shape[1] // LANES, up.shape[1] // LANES
    down_rows = 2 * per_down

    def mark(i, carry):
        b = blocks - 1 - i
        table[storage[adapter[b]]] = b
        return carry

    lax.fori_loop(0, blocks, mark, 0)
    dacc[...] = jnp.zeros_like(dacc)
    uacc[...] = jnp.zeros_like(uacc)
    value = lane_cat([recv[:, q * ADAPTER_RANK : (q + 1) * ADAPTER_RANK, :] for q in range(8)])
    value = dot_n(value.reshape(devices * ADAPTER_RANK, 8 * LANES), rank_major_order(True))
    for j in range(devices):
        part = value[j * ADAPTER_RANK : (j + 1) * ADAPTER_RANK, :]
        turned = jnp.concatenate(
            [part[:, lo * LANES : (lo + 1) * LANES] for lo in range(8)], axis=0
        ).T
        narrow = recv[j, down_rows:, :].astype(jnp.float32)
        for k in range(2):
            first = table[storage[adapter[2 * j + k]]]
            dacc[first] += turned[k * per_down : (k + 1) * per_down, :]
            uacc[first] += narrow[k * per_up : (k + 1) * per_up, :]
    for g in range(blocks // 8):
        for i in range(8):
            dscr[pl.ds(i, per_down, stride=8), :] = dacc[8 * g + i]
            uscr[pl.ds(i, per_up, stride=8), :] = uacc[8 * g + i]
        for t in range(per_down):
            drow[8 * g : 8 * g + 8, t * LANES : (t + 1) * LANES] = dscr[8 * t : 8 * t + 8, :]
        for t in range(per_up):
            urow[8 * g : 8 * g + 8, t * LANES : (t + 1) * LANES] = uscr[8 * t : 8 * t + 8, :]

    def copies(b):
        slot = storage[adapter[b]]
        return (
            table[slot] == b,
            pltpu.make_async_copy(drow.at[pl.ds(b, 1), :], down.at[pl.ds(slot, 1), :], dsem.at[b]),
            pltpu.make_async_copy(urow.at[pl.ds(b, 1), :], up.at[pl.ds(slot, 1), :], usem.at[b]),
        )

    def begin(b, carry):
        mine, first, second = copies(b)

        @pl.when(mine)
        def _():
            first.start()
            second.start()

        return carry

    def end(b, carry):
        mine, first, second = copies(b)

        @pl.when(mine)
        def _():
            first.wait()
            second.wait()

        return carry

    lax.fori_loop(0, blocks, begin, 0)
    lax.fori_loop(0, blocks, end, 0)


def scatter_rows(padded_block_adapter, adapter_storage_row, recv, down, up):
    blocks = padded_block_adapter.shape[0]
    per_down, per_up = down.shape[1] // LANES, up.shape[1] // LANES
    return pl.pallas_call(
        scatter_kernel,
        in_specs=[IN_SMEM, IN_SMEM, IN_VMEM, IN_HBM, IN_HBM],
        out_specs=[IN_HBM, IN_HBM],
        scratch_shapes=[
            pltpu.SMEM((ADAPTER_GROUP,), jnp.int32),
            pltpu.VMEM((blocks, per_down, LANES), jnp.float32),
            pltpu.VMEM((blocks, per_up, LANES), jnp.float32),
            pltpu.VMEM((8 * per_down, LANES), jnp.float32),
            pltpu.VMEM((8 * per_up, LANES), jnp.float32),
            pltpu.VMEM((blocks, per_down * LANES), jnp.float32),
            pltpu.VMEM((blocks, per_up * LANES), jnp.float32),
            pltpu.SemaphoreType.DMA((blocks,)),
            pltpu.SemaphoreType.DMA((blocks,)),
        ],
        out_shape=[
            jax.ShapeDtypeStruct(down.shape, down.dtype),
            jax.ShapeDtypeStruct(up.shape, up.dtype),
        ],
        input_output_aliases={3: 0, 4: 1},
        compiler_params=PARAMS,
        cost_estimate=SMALL,
        name="scatter_rows",
    )(padded_block_adapter, adapter_storage_row, recv, down, up)


def far_kernel(count, *refs):
    weight = refs[count][...]
    for cot, out in zip(refs[:count], refs[count + 1 :]):
        out[...] = dot_t(cot[...], weight).astype(out.dtype)


def far_products(cots, weight):
    shape = jax.ShapeDtypeStruct((cots[0].shape[0], weight.shape[0]), jnp.bfloat16)
    return pl.pallas_call(
        functools.partial(far_kernel, len(cots)),
        in_specs=[IN_VMEM] * (len(cots) + 1),
        out_specs=[IN_VMEM] * len(cots),
        out_shape=[shape] * len(cots),
        compiler_params=PARAMS,
        cost_estimate=SMALL,
        name="far_products",
    )(*cots, weight)


def finish(meta, at, cot, weights, received, g, recv, out, width, columns):
    rows = cot.shape[0]
    span = weights[0].shape[0] if weights else received[0].shape[1]
    per_device = columns // span
    count = len(weights) + len(received)
    per = columns // LANES

    def kernel(meta, cot, g, recv, *rest):
        sources = rest[:count]
        result, buffer, sems = rest[-3:]
        copies = []
        for i in range(count):
            index = meta[at + i]
            device, inner = index // per_device, (index % per_device) * (span // LANES)
            parts = []
            for k in range(rows // BLOCK):
                tiles = []
                for q in range(span // LANES):
                    first = pl.multiple_of((k * per + inner + q) * ADAPTER_RANK, ADAPTER_RANK)
                    tiles.append(recv[device, pl.ds(first, ADAPTER_RANK), :])
                ours = g[k * BLOCK : (k + 1) * BLOCK, :ADAPTER_RANK]
                parts.append(dot_n(ours, lane_cat(tiles)))
            value = adapter_scale * jnp.concatenate(parts, axis=0)
            if i < len(weights):
                value = value + dot_t(cot[...], sources[i][...])
            else:
                value = value + sources[i][...].astype(jnp.float32)
            buffer[i] = value.astype(buffer.dtype)
            start = pl.multiple_of(index * span, span)
            copies.append(
                pltpu.make_async_copy(buffer.at[i], result.at[:, pl.ds(start, span)], sems.at[i])
            )
            copies[-1].start()
        for copy in copies:
            copy.wait()

    return pl.pallas_call(
        kernel,
        in_specs=[IN_SMEM] + [IN_VMEM] * (3 + count) + ([] if out is None else [IN_HBM]),
        out_specs=IN_HBM,
        out_shape=jax.ShapeDtypeStruct((rows, width), jnp.bfloat16),
        input_output_aliases={} if out is None else {4 + count: 0},
        scratch_shapes=[
            pltpu.VMEM((count, rows, span), jnp.bfloat16),
            pltpu.SemaphoreType.DMA((count,)),
        ],
        compiler_params=PARAMS,
        cost_estimate=SMALL,
        name="finish",
    )(meta, cot, g, recv, *weights, *received, *([] if out is None else [out]))


def ring_table(devices):
    chips = devices // 2
    order = list(range(0, chips, 2)) + list(range(chips - 1, 0, -2))
    place = {c: i for i, c in enumerate(order)}
    ring = []
    for c in range(chips):
        ring.append((2 * c, 2 * order[(place[c] + 1) % chips]))
        ring.append((2 * c + 1, 2 * order[(place[c] - 1) % chips] + 1))
    table = []
    for part in range(2):
        for index in range(devices):
            chip, core = index // 2, index % 2
            way = 2 * core - 1
            row = [2 * index, index, index ^ 1]
            for step in range(1, chips // 2):
                near, far = [order[(place[chip] + sign * way * step) % chips] for sign in (1, -1)]
                row += [2 * near + part, 2 * far + part, 2 * near + 1 - part, 2 * far + 1 - part]
            last = order[(place[chip] + chips // 2) % chips]
            for p in (part, 1 - part):
                row += [2 * (2 * last + p) + core, 2 * (2 * last + p) + 1 - core]
            table.append(row)
    return ring, np.array(table, np.int32)


def ring_body(
    inputs,
    cotangent,
    frozen_value_weight,
    adapter_down_weights,
    adapter_up_weights,
    padded_block_adapter,
    block_live_rows,
    adapter_storage_row,
    *,
    devices,
):
    steps = devices // 4
    shard = frozen_value_weight.shape[0]
    width = inputs.shape[1]
    index, part = lax.axis_index("fsdp"), lax.axis_index("parts")
    core = index % 2
    ring, table = ring_table(devices)
    meta = lax.dynamic_index_in_dim(jnp.asarray(table), part * devices + index, keepdims=False)
    cores = [(i, i ^ 1) for i in range(devices)]
    across = [(0, 1), (1, 0)]
    diagonal = [(p * devices + i, (1 - p) * devices + (i ^ 1)) for p in range(2) for i in range(devices)]

    def cross(products):
        return (
            lax.ppermute(products[0], "fsdp", cores),
            lax.ppermute(products[1], "parts", across),
            lax.ppermute(products[2], ("parts", "fsdp"), diagonal),
        )

    other_shard = lax.ppermute(frozen_value_weight, "fsdp", cores)
    masked = mask_rows(meta, block_live_rows, cotangent)
    core_masked = lax.ppermute(masked, "fsdp", cores)
    far_masked = lax.ppermute(masked, "parts", across)
    diagonal_masked = lax.ppermute(far_masked, "fsdp", cores)
    adapter, _ = after(padded_block_adapter, masked)
    payload, grads = gather_rows(
        adapter, adapter_storage_row, adapter_down_weights, adapter_up_weights, devices
    )
    shards, _ = after((frozen_value_weight, other_shard), payload)
    travelling = jnp.where(part == core, *shards)
    recv = lax.all_to_all(payload, "fsdp", split_axis=0, concat_axis=0, tiled=True)

    pieces, received = [], []
    placed = payload
    out = None
    for step in range(steps):
        travelling, _ = after(travelling, placed)
        if step == steps - 1:
            travelling = lax.dynamic_slice_in_dim(travelling, core * (shard // 2), shard // 2)
        travelling = lax.ppermute(travelling, "fsdp", ring)
        placed = payload if out is None else out
        pieces.append(travelling)
        cots = (core_masked, far_masked, diagonal_masked)
        if step > 0:
            cots, _ = after(cots, out)
        products = far_products(cots, travelling)
        received.append(cross(products))
        if step == 0:
            new, _ = after(recv, products[0])
            sent, g, grads, up_grads = adapter_terms(
                inputs, masked, new, grads, adapter_up_weights.shape
            )
            sums = lax.all_to_all(sent, "fsdp", split_axis=0, concat_axis=0, tiled=True)
            out = finish(
                meta, 1, masked, shards, (), g, recv, None, width, shard
            )
        else:
            out, _ = after(out, products[0])
            at = 4 * step - 1
            out = finish(
                meta, at, masked, pieces[step - 1 : step], received[step - 1], g, recv, out, width, shard
            )
        if step == 1:
            sums, _ = after(sums, out)
            down_grad, up_grad = scatter_rows(
                padded_block_adapter, adapter_storage_row, sums, grads, up_grads
            )
    at = 4 * steps - 1
    out = finish(meta, at, masked, pieces[-1:], (), g, recv, out, width, shard)
    out = finish(meta, at + 1, masked, (), received[-1], g, recv, out, width, shard)
    return (out, down_grad, up_grad)


def after(value, *earlier):
    return lax.optimization_barrier((value,) + earlier)


def gather_body(
    inputs,
    cotangent,
    frozen_value_weight,
    adapter_down_weights,
    adapter_up_weights,
    padded_block_adapter,
    block_live_rows,
    adapter_storage_row,
):
    hidden_width = inputs.shape[1]
    kv_width = cotangent.shape[1]
    token_rows = inputs.shape[0]
    block_count = token_rows // BLOCK
    first_block = lax.axis_index("fsdp") * block_count
    live_rows = lax.dynamic_slice_in_dim(block_live_rows, first_block, block_count)
    positions = jnp.arange(BLOCK, dtype=jnp.int32)
    live_mask = positions[None, :] < live_rows[:, None]
    blocked_cot = cotangent.reshape(block_count, BLOCK, kv_width)
    masked_blocks = jnp.where(live_mask[:, :, None], blocked_cot, jnp.zeros_like(blocked_cot))
    masked = masked_blocks.reshape(token_rows, kv_width)
    block_storage_row = slot_lookup(padded_block_adapter, adapter_storage_row)
    down_weight_rows = jnp.take(adapter_down_weights, block_storage_row, axis=0)
    up_weight_rows = jnp.take(adapter_up_weights, block_storage_row, axis=0)
    down_mine, up_mine = (
        lax.all_to_all(down_weight_rows, "fsdp", split_axis=0, concat_axis=1, tiled=True),
        lax.all_to_all(up_weight_rows, "fsdp", split_axis=0, concat_axis=1, tiled=True),
    )
    frozen_gradient = lax.dot_general(
        masked,
        lax.all_gather(frozen_value_weight, "fsdp", axis=0, tiled=True),
        (((1,), (1,)), ((), ())),
        preferred_element_type=jnp.float32,
    )
    down_weight_matrix = down_mine.reshape(block_count, hidden_width, ADAPTER_RANK)
    up_weight_matrix = up_mine.reshape(block_count, ADAPTER_RANK, kv_width)
    blocked_in = inputs.reshape(block_count, BLOCK, hidden_width)
    rank_projection = jnp.einsum(
        "kbd,kdr->kbr", blocked_in, down_weight_matrix, preferred_element_type=jnp.float32
    ).astype(jnp.bfloat16)
    rank_space_gradient = jnp.einsum(
        "kbv,krv->kbr", masked_blocks, up_weight_matrix, preferred_element_type=jnp.float32
    ).astype(jnp.bfloat16)
    adapter_gradient_term = adapter_scale * jnp.einsum(
        "kbr,kdr->kbd", rank_space_gradient, down_weight_matrix, preferred_element_type=jnp.float32
    )
    input_gradient = (
        frozen_gradient + adapter_gradient_term.reshape(token_rows, hidden_width)
    ).astype(jnp.bfloat16)
    partial_down_weight = adapter_scale * jnp.einsum(
        "kbd,kbr->kdr", blocked_in, rank_space_gradient, preferred_element_type=jnp.float32
    )
    partial_up_weight = adapter_scale * jnp.einsum(
        "kbr,kbv->krv", rank_projection, masked_blocks, preferred_element_type=jnp.float32
    )
    partial_down_weight = partial_down_weight.reshape(block_count, hidden_width * ADAPTER_RANK)
    partial_up_weight = partial_up_weight.reshape(block_count, ADAPTER_RANK * kv_width)
    recv_down, recv_up = (
        lax.all_to_all(partial_down_weight, "fsdp", split_axis=1, concat_axis=0, tiled=True),
        lax.all_to_all(partial_up_weight, "fsdp", split_axis=1, concat_axis=0, tiled=True),
    )
    onehot = (
        jnp.arange(ADAPTER_GROUP, dtype=jnp.int32)[:, None] == block_storage_row[None, :]
    ).astype(jnp.float32)
    highest_precision = lax.Precision.HIGHEST
    down_grad = jnp.dot(
        onehot, recv_down, precision=highest_precision, preferred_element_type=jnp.float32
    )
    up_grad = jnp.dot(
        onehot, recv_up, precision=highest_precision, preferred_element_type=jnp.float32
    )
    return (input_gradient, down_grad, up_grad)


def solution(mesh):
    devices = mesh.shape["fsdp"]
    in_specs = (
        P(("parts", "fsdp"), None),
        P(("parts", "fsdp"), None),
        P("fsdp", None),
        P("parts", "fsdp"),
        P("parts", "fsdp"),
        P("parts"),
        P("parts"),
        P("parts"),
    )
    out_specs = (P(("parts", "fsdp"), None), P("parts", "fsdp"), P("parts", "fsdp"))

    def program(*arrays):
        shard = arrays[2].shape[0] // devices
        rows = arrays[0].shape[0] // devices // 2
        adapter_tiles = arrays[3].shape[1] // devices // LANES
        fits = rows == 2 * BLOCK and 2 * adapter_tiles == LANES and shard % 512 == 0
        if mesh.shape["parts"] == 2 and devices % 4 == 0 and fits:
            body = functools.partial(ring_body, devices=devices)
        else:
            body = gather_body
        return jax.shard_map(
            body, mesh=mesh, in_specs=in_specs, out_specs=out_specs, check_vma=False
        )(*arrays)

    return program
```

time: 144 us -> 127 us (0.88)
  Pallas kernels: 62.4 us -> 42.8 us
  waiting for transfers between devices: 45.1 us -> 30.4 us
  local copies, waits for them, and re-layouts: 7.12 us -> 17.8 us
  starting transfers between devices: 25.9 us -> 31.9 us
    pallas_call x18 -> x14, Pallas kernels: 62.4 us -> 42.8 us  [the longest x6 14.6 us: finish(): pl.pallas_call(kernel, in_specs=[IN_SMEM] + [IN_VMEM] * (3 + count) + ([]...]
    ppermute x4, waiting for transfers between devices: 25.9 us -> 10.9 us  [ring_body(): travelling = lax.ppermute(travelling, 'fsdp', ring)]
    ppermute x8 -> x14, waiting for transfers between devices: 5.8 us -> 19.5 us  [the longest x4 10.5 us: cross(): lax.ppermute(products[2], ('parts', 'fsdp'), diagonal)]
    ppermute x1, waiting for transfers between devices: 10.9 us -> 0.01 us  [ring_body(): far_masked = lax.ppermute(masked, 'parts', across)]
    unnamed x30 -> x42, local copies, waits for them, and re-layouts: 5.6 us -> 15.3 us
    ppermute x4, starting transfers between devices: 8.81 us -> 12 us  [ring_body(): travelling = lax.ppermute(travelling, 'fsdp', ring)]
    ppermute x8 -> x14, starting transfers between devices: 5.63 us -> 8.76 us  [the longest x4 5.95 us: cross(): lax.ppermute(products[1], 'parts', across)]
    ppermute x1, waiting for transfers between devices: 2.5 us -> 0.01 us  [ring_body(): other_shard = lax.ppermute(frozen_value_weight, 'fsdp', cores)]
  transfers between devices with their start and end apart: 16 -> 22, of which waited for: 6 -> 8; matrix products, arithmetic and copies ran while one was open for 1% -> 2% of each run, Pallas kernels for 42% -> 33%
where the time goes in v3:
time: 127 us; the launch traced here: 125 us
  Pallas kernels  42.8 us (34%)
  starting transfers between devices  31.9 us (25%)
  waiting for transfers between devices  30.4 us (24%)
  local copies, waits for them, and re-layouts  17.8 us (14%)
    unnamed x42, local copies, waits for them, and re-layouts  15.3 us
    pallas_call x6, Pallas kernels, finish(): pl.pallas_call(kernel, in_specs=[IN_SMEM] + [IN_VMEM] * (3 + count) + ([]...  14.6 us
    ppermute x4, starting transfers between devices, ring_body(): travelling = lax.ppermute(travelling, 'fsdp', ring)  12 us
    ppermute x4, waiting for transfers between devices, ring_body(): travelling = lax.ppermute(travelling, 'fsdp', ring)  10.9 us
    ppermute x4, waiting for transfers between devices, cross(): lax.ppermute(products[2], ('parts', 'fsdp'), diagonal)  10.5 us
    pallas_call x4, Pallas kernels, far_products(): pl.pallas_call(functools.partial(far_kernel, len(cots)), in_specs=[IN_VME...  9.79 us
    pallas_call x1, Pallas kernels, gather_rows(): pl.pallas_call(gather_kernel, in_specs=[IN_SMEM, IN_SMEM, IN_HBM, IN_HBM]...  9.15 us
    ppermute x4, waiting for transfers between devices, cross(): lax.ppermute(products[1], 'parts', across)  6.83 us
  transfers between devices with their start and end apart: 22, of which 8 were waited for; matrix products, arithmetic and copies ran while one was open for 2% of the time, Pallas kernels for 33%

profile of v3, /device:TPU:0, one launch (start us, length us, event | category | flops | bytes accessed | tf_op | source)
XLA Modules:
  0.0 125.3 jit_solution(18361814101705945179)
XLA Ops:
  0.6 0.5 collective-permute-start.3
  1.1 0.7 dynamic-slice_bitcast_fusion.meta
  1.8 1.0 copy-done.8
  2.9 0.7 copy-done.17
  3.5 0.6 mask_rows.1.cot
  4.2 0.0 copy-start
  4.2 3.4 %copy-done = bf16[512,8192]{1,0:T(8,128)(2,1)S(1)} copy-done((bf16[512,8192]{1,0:T(8,128)(2,1)S(1)}, bf16[512,8192]{1,0:T(8,128)(2,1)}, u32[]{:S(2)}) %copy-start) | copy-done | bytes 8388632
  7.6 1.2 copy-done.6
  8.8 0.7 copy-done.13
  9.5 0.7 copy-done.15
  10.1 9.2 %gather_rows.1 = (bf16[16,144,128]{2,1,0:T(8,128)(2,1)}, f32[512,8192]{1,0:T(8,128)}) custom-call(s32[32]{0:T(128)S(1)} %copy-done.15, s32[512]{0:T(512)S(1)} %copy-done.13, bf16[512,8192]{1,0:T(8,128)(2,1)S(1)} %copy-done, bf16[512,1024]{1,0:T(8,128)(2,1)S(1)} %copy-done.6), custom_call_target="tpu_custom_call" | custom-call | flops 1 | bytes 1 | tf_op jit(solution)/shard_map/gather_rows/pallas_call | solution.py:163
  19.3 0.0 copy-start.4
  19.3 1.2 broadcast_select_fusion
  20.5 2.6 %collective-permute-start.4 = (bf16[512,1024]{1,0:T(8,128)(2,1)}, bf16[512,1024]{1,0:T(8,128)(2,1)}, u32[]{:S(2)}, u32[]{:S(2)}) collective-permute-start(bf16[512,1024]{1,0:T(8,128)(2,1)} %broadcast_select_fusion), channel_id=1, source_target_pairs={{0,4},{1,3},{2,0},{3,7},{4,8},{5,1},{6,2},{7,11},{8,12},{9,5},{10,... | collective-permute-start | bytes 3145736 | tf_op jit(solution)/shard_map/ppermute | solution.py:530
  23.1 4.9 %all-to-all-start = ((bf16[16,144,128]{2,1,0:T(8,128)(2,1)}), bf16[16,144,128]{2,1,0:T(8,128)(2,1)S(1)}, u32[]{:S(2)}, u32[]{:S(2)}) async-start(bf16[16,144,128]{2,1,0:T(8,128)(2,1)} %get-tuple-element.45), calls=%async_computation | async-start | bytes 1179648 | tf_op jit(solution)/shard_map/all_to_all | solution.py:521
  28.1 1.6 %collective-permute-start.1 = (bf16[256,1024]{1,0:T(8,128)(2,1)S(1)}, bf16[256,1024]{1,0:T(8,128)(2,1)S(1)}, u32[]{:S(2)}, u32[]{:S(2)}) collective-permute-start(bf16[256,1024]{1,0:T(8,128)(2,1)S(1)} %mask_rows.1.cot), channel_id=1, source_target_pairs={{0,16},{16,0},{1,17},{17,1},{2,18},{18,2},{3,19},{19,3},{4,20},{20... | collective-permute-start | bytes 1572872 | tf_op jit(solution)/shard_map/ppermute | solution.py:513
  29.6 10.9 %collective-permute-done.4.refs_3_.rest_0_ = bf16[512,1024]{1,0:T(8,128)(2,1)} collective-permute-done((bf16[512,1024]{1,0:T(8,128)(2,1)}, bf16[512,1024]{1,0:T(8,128)(2,1)}, u32[]{:S(2)}, u32[]{:S(2)}) %collective-permute-start.4) | collective-permute-done | bytes 1048608 | tf_op jit(solution)/shard_map/ppermute | solution.py:530
  40.5 4.9 %collective-permute-start.5 = (bf16[512,1024]{1,0:T(8,128)(2,1)}, bf16[512,1024]{1,0:T(8,128)(2,1)}, u32[]{:S(2)}, u32[]{:S(2)}) collective-permute-start(bf16[512,1024]{1,0:T(8,128)(2,1)} %collective-permute-done.4.refs_3_.rest_0_), channel_id=1, source_target_pairs={{0,4},{1,3},{2,0},{3,7},{4,8},{5,1},{6,2},{7,11},{8,12},{9,5},{10,... | collective-permute-start | bytes 3145736 | tf_op jit(solution)/shard_map/ppermute | solution.py:530
  45.4 0.0 collective-permute-start
  45.4 0.5 collective-permute-start.2
  45.9 1.4 %collective-permute-done.refs_0_ = bf16[256,1024]{1,0:T(8,128)(2,1)S(1)} collective-permute-done((bf16[256,1024]{1,0:T(8,128)(2,1)S(1)}, bf16[256,1024]{1,0:T(8,128)(2,1)S(1)}, u32[]{:S(2)}, u32[]{:S(2)}) %collective-permute-start) | collective-permute-done | bytes 524320 | tf_op jit(solution)/shard_map/ppermute | solution.py:512
  47.3 0.7 collective-permute-done.2.refs_2_
  48.0 2.2 %far_products.4 = (bf16[256,512]{1,0:T(8,128)(2,1)S(1)}, bf16[256,512]{1,0:T(8,128)(2,1)S(1)}, bf16[256,512]{1,0:T(8,128)(2,1)S(1)}) custom-call(bf16[256,1024]{1,0:T(8,128)(2,1)S(1)} %collective-permute-done.refs_0_, bf16[256,1024]{1,0:T(8,128)(2,1)S(1)} %collective-permute-done.1.refs_1_, bf16[256,1024]{1,0:T(8,128)(2,1)S(1)} %collective-permute-done.2.refs_2_, ...), custom_call_target="tpu_custom_call" | custom-call | flops 1 | bytes 1 | tf_op jit(solution)/shard_map/far_products/pallas_call | solution.py:393
  50.3 0.7 copy-done.18
  51.0 0.7 copy-done.19
  51.7 0.7 copy-done.20
  52.4 2.2 %copy-done.1 = bf16[256,8192]{1,0:T(8,128)(2,1)S(1)} copy-done((bf16[256,8192]{1,0:T(8,128)(2,1)S(1)}, bf16[256,8192]{1,0:T(8,128)(2,1)}, u32[]{:S(2)}) %copy-start.1) | copy-done | bytes 4194328
  54.6 4.8 %adapter_terms.1 = (bf16[16,144,128]{2,1,0:T(8,128)(2,1)S(1)}, bf16[256,128]{1,0:T(8,128)(2,1)S(1)}, f32[512,8192]{1,0:T(8,128)}, f32[512,1024]{1,0:T(8,128)}) custom-call(bf16[256,8192]{1,0:T(8,128)(2,1)S(1)} %copy-done.1, bf16[256,1024]{1,0:T(8,128)(2,1)S(1)} %mask_rows.1.cot, ...), custom_call_target="tpu_custom_call", output_to_operand_aliasing={{2}: (3, {})} | custom-call | flops 1 | bytes 1 | tf_op jit(solution)/shard_map/adapter_terms/pallas_call | solution.py:263
  59.5 2.2 %finish.6.rest_4_ = bf16[256,8192]{1,0:T(8,128)(2,1)} custom-call(s32[19]{0:T(128)S(1)} %dynamic-slice_bitcast_fusion.meta, bf16[256,1024]{1,0:T(8,128)(2,1)S(1)} %mask_rows.1.cot, bf16[256,128]{1,0:T(8,128)(2,1)S(1)} %get-tuple-element.52.g, bf16[16,144,128]{2,1,0:T(8,128)(2,1)S(1)} %all-to-all-done.recv, bf16[512,1024]{1,0:T(8,128)(2,1)S(1)} %copy-done.3, ...), custom_call_target="tpu_custom_call" | custom-call | flops 1 | bytes 1 | tf_op jit(solution)/shard_map/finish/pallas_call | solution.py:440
  61.7 0.0 collective-permute-done.5.refs_3_.rest_0_
  61.7 2.4 %collective-permute-start.12 = (bf16[512,1024]{1,0:T(8,128)(2,1)}, bf16[512,1024]{1,0:T(8,128)(2,1)}, u32[]{:S(2)}, u32[]{:S(2)}) collective-permute-start(bf16[512,1024]{1,0:T(8,128)(2,1)} %collective-permute-done.5.refs_3_.rest_0_), channel_id=1, source_target_pairs={{0,4},{1,3},{2,0},{3,7},{4,8},{5,1},{6,2},{7,11},{8,12},{9,5},{10,... | collective-permute-start | bytes 3145736 | tf_op jit(solution)/shard_map/ppermute | solution.py:530
  64.1 4.2 %all-to-all-start.1 = ((bf16[16,144,128]{2,1,0:T(8,128)(2,1)}), bf16[16,144,128]{2,1,0:T(8,128)(2,1)S(1)}, u32[]{:S(2)}, u32[]{:S(2)}) async-start(bf16[16,144,128]{2,1,0:T(8,128)(2,1)} %copy-done.7), calls=%async_computation.1 | async-start | bytes 1179648 | tf_op jit(solution)/shard_map/all_to_all | solution.py:543
  68.4 0.4 collective-permute-start.9
  68.8 1.5 %collective-permute-start.10 = (bf16[256,512]{1,0:T(8,128)(2,1)}, bf16[256,512]{1,0:T(8,128)(2,1)}, u32[]{:S(2)}, u32[]{:S(2)}) collective-permute-start(bf16[256,512]{1,0:T(8,128)(2,1)} %copy-done.19), channel_id=1, source_target_pairs={{0,16},{16,0},{1,17},{17,1},{2,18},{18,2},{3,19},{19,3},{4,20},{20... | collective-permute-start | bytes 786440 | tf_op jit(solution)/shard_map/ppermute | solution.py:506
  70.3 0.0 collective-permute-start.11
  70.3 3.0 %far_products.5 = (bf16[256,512]{1,0:T(8,128)(2,1)S(1)}, bf16[256,512]{1,0:T(8,128)(2,1)S(1)}, bf16[256,512]{1,0:T(8,128)(2,1)}) custom-call(bf16[256,1024]{1,0:T(8,128)(2,1)S(1)} %collective-permute-done.refs_0_, bf16[256,1024]{1,0:T(8,128)(2,1)S(1)} %collective-permute-done.1.refs_1_, bf16[256,1024]{1,0:T(8,128)(2,1)S(1)} %collective-permute-done.2.refs_2_, ...), custom_call_target="tpu_custom_call" | custom-call | flops 1 | bytes 1 | tf_op jit(solution)/shard_map/far_products/pallas_call | solution.py:393
  73.3 5.0 %collective-permute-done.10.rest_2_ = bf16[256,512]{1,0:T(8,128)(2,1)} collective-permute-done((bf16[256,512]{1,0:T(8,128)(2,1)}, bf16[256,512]{1,0:T(8,128)(2,1)}, u32[]{:S(2)}, u32[]{:S(2)}) %collective-permute-start.10) | collective-permute-done | bytes 262176 | tf_op jit(solution)/shard_map/ppermute | solution.py:506
  78.2 4.1 %collective-permute-done.11.rest_3_ = bf16[256,512]{1,0:T(8,128)(2,1)} collective-permute-done((bf16[256,512]{1,0:T(8,128)(2,1)}, bf16[256,512]{1,0:T(8,128)(2,1)}, u32[]{:S(2)}, u32[]{:S(2)}) %collective-permute-start.11) | collective-permute-done | bytes 262176 | tf_op jit(solution)/shard_map/ppermute | solution.py:507
  82.3 3.0 %finish.7.rest_4_ = bf16[256,8192]{1,0:T(8,128)(2,1)} custom-call(s32[19]{0:T(128)S(1)} %dynamic-slice_bitcast_fusion.meta, bf16[256,1024]{1,0:T(8,128)(2,1)S(1)} %mask_rows.1.cot, bf16[256,128]{1,0:T(8,128)(2,1)S(1)} %get-tuple-element.52.g, bf16[16,144,128]{2,1,0:T(8,128)(2,1)S(1)} %all-to-all-done.recv, ...), custom_call_target="tpu_custom_call", output_to_operand_aliasing={{}: (8, {})} | custom-call | flops 1 | bytes 1 | tf_op jit(solution)/shard_map/finish/pallas_call | solution.py:440
  85.3 0.0 collective-permute-done.12.refs_3_.rest_0_
  85.3 1.9 %constant_dynamic-slice_fusion = bf16[256,1024]{1,0:T(8,128)(2,1)} fusion(bf16[512,1024]{1,0:T(8,128)(2,1)} %collective-permute-done.12.refs_3_.rest_0_, s32[]{:T(128)S(6)} %select_n.26), kind=kLoop, calls=%fused_computation.2 | loop fusion | bytes 1048580 | tf_op jit(solution)/shard_map/dynamic_slice | solution.py:529
  87.2 2.1 %collective-permute-start.13 = (bf16[256,1024]{1,0:T(8,128)(2,1)}, bf16[256,1024]{1,0:T(8,128)(2,1)}, u32[]{:S(2)}, u32[]{:S(2)}) collective-permute-start(bf16[256,1024]{1,0:T(8,128)(2,1)} %constant_dynamic-slice_fusion), channel_id=1, source_target_pairs={{0,4},{1,3},{2,0},{3,7},{4,8},{5,1},{6,2},{7,11},{8,12},{9,5},{10,... | collective-permute-start | bytes 1572872 | tf_op jit(solution)/shard_map/ppermute | solution.py:530
  89.2 0.3 collective-permute-start.6
  89.5 1.5 %collective-permute-start.7 = (bf16[256,512]{1,0:T(8,128)(2,1)S(1)}, bf16[256,512]{1,0:T(8,128)(2,1)S(1)}, u32[]{:S(2)}, u32[]{:S(2)}) collective-permute-start(bf16[256,512]{1,0:T(8,128)(2,1)S(1)} %get-tuple-element.58), channel_id=1, source_target_pairs={{0,16},{16,0},{1,17},{17,1},{2,18},{18,2},{3,19},{19,3},{4,20},{20... | collective-permute-start | bytes 786440 | tf_op jit(solution)/shard_map/ppermute | solution.py:506
  91.0 0.1 collective-permute-start.8
  91.1 2.9 %far_products.6 = (bf16[256,512]{1,0:T(8,128)(2,1)}, bf16[256,512]{1,0:T(8,128)(2,1)}, bf16[256,512]{1,0:T(8,128)(2,1)}) custom-call(bf16[256,1024]{1,0:T(8,128)(2,1)S(1)} %collective-permute-done.refs_0_, bf16[256,1024]{1,0:T(8,128)(2,1)S(1)} %collective-permute-done.1.refs_1_, bf16[256,1024]{1,0:T(8,128)(2,1)S(1)} %collective-permute-done.2.refs_2_, ...), custom_call_target="tpu_custom_call" | custom-call | flops 1 | bytes 1 | tf_op jit(solution)/shard_map/far_products/pallas_call | solution.py:393
  94.0 0.6 collective-permute-start.17
  94.6 0.7 copy-done.9
  95.3 1.5 %collective-permute-start.18 = (bf16[256,512]{1,0:T(8,128)(2,1)}, bf16[256,512]{1,0:T(8,128)(2,1)}, u32[]{:S(2)}, u32[]{:S(2)}) collective-permute-start(bf16[256,512]{1,0:T(8,128)(2,1)} %get-tuple-element.76), channel_id=1, source_target_pairs={{0,16},{16,0},{1,17},{17,1},{2,18},{18,2},{3,19},{19,3},{4,20},{20... | collective-permute-start | bytes 786440 | tf_op jit(solution)/shard_map/ppermute | solution.py:506
  96.8 1.8 %collective-permute-done.7.rest_2_ = bf16[256,512]{1,0:T(8,128)(2,1)S(1)} collective-permute-done((bf16[256,512]{1,0:T(8,128)(2,1)S(1)}, bf16[256,512]{1,0:T(8,128)(2,1)S(1)}, u32[]{:S(2)}, u32[]{:S(2)}) %collective-permute-start.7) | collective-permute-done | bytes 262176 | tf_op jit(solution)/shard_map/ppermute | solution.py:506
  98.7 0.7 copy-done.11
  99.4 4.0 %collective-permute-done.8.rest_3_ = bf16[256,512]{1,0:T(8,128)(2,1)} collective-permute-done((bf16[256,512]{1,0:T(8,128)(2,1)}, bf16[256,512]{1,0:T(8,128)(2,1)}, u32[]{:S(2)}, u32[]{:S(2)}) %collective-permute-start.8) | collective-permute-done | bytes 262176 | tf_op jit(solution)/shard_map/ppermute | solution.py:507
  103.4 0.9 copy-done.10
  104.4 0.9 copy-done.12
  105.3 2.8 %finish.8.rest_4_ = bf16[256,8192]{1,0:T(8,128)(2,1)} custom-call(s32[19]{0:T(128)S(1)} %dynamic-slice_bitcast_fusion.meta, bf16[256,1024]{1,0:T(8,128)(2,1)S(1)} %mask_rows.1.cot, bf16[256,128]{1,0:T(8,128)(2,1)S(1)} %get-tuple-element.52.g, bf16[16,144,128]{2,1,0:T(8,128)(2,1)S(1)} %all-to-all-done.recv, ...), custom_call_target="tpu_custom_call", output_to_operand_aliasing={{}: (8, {})} | custom-call | flops 1 | bytes 1 | tf_op jit(solution)/shard_map/finish/pallas_call | solution.py:440
  108.2 1.7 %far_products.7 = (bf16[256,256]{1,0:T(8,128)(2,1)S(1)}, bf16[256,256]{1,0:T(8,128)(2,1)S(1)}, bf16[256,256]{1,0:T(8,128)(2,1)S(1)}) custom-call(bf16[256,1024]{1,0:T(8,128)(2,1)S(1)} %collective-permute-done.refs_0_, bf16[256,1024]{1,0:T(8,128)(2,1)S(1)} %collective-permute-done.1.refs_1_, bf16[256,1024]{1,0:T(8,128)(2,1)S(1)} %collective-permute-done.2.refs_2_, ...), custom_call_target="tpu_custom_call" | custom-call | flops 1 | bytes 1 | tf_op jit(solution)/shard_map/far_products/pallas_call | solution.py:393
  109.8 0.9 collective-permute-start.14
  110.7 1.5 %collective-permute-start.15 = (bf16[256,256]{1,0:T(8,128)(2,1)S(1)}, bf16[256,256]{1,0:T(8,128)(2,1)S(1)}, u32[]{:S(2)}, u32[]{:S(2)}) collective-permute-start(bf16[256,256]{1,0:T(8,128)(2,1)S(1)} %get-tuple-element.74), channel_id=1, source_target_pairs={{0,16},{16,0},{1,17},{17,1},{2,18},{18,2},{3,19},{19,3},{4,20},{20... | collective-permute-start | bytes 393224 | tf_op jit(solution)/shard_map/ppermute | solution.py:506
  112.2 0.0 collective-permute-done.17.rest_1_
  112.2 2.4 %collective-permute-done.19.rest_3_ = bf16[256,512]{1,0:T(8,128)(2,1)} collective-permute-done((bf16[256,512]{1,0:T(8,128)(2,1)}, bf16[256,512]{1,0:T(8,128)(2,1)}, u32[]{:S(2)}, u32[]{:S(2)}) %collective-permute-start.19) | collective-permute-done | bytes 262176 | tf_op jit(solution)/shard_map/ppermute | solution.py:507
  114.7 3.0 %finish.9.rest_1_ = bf16[256,8192]{1,0:T(8,128)(2,1)} custom-call(s32[19]{0:T(128)S(1)} %dynamic-slice_bitcast_fusion.meta, bf16[256,1024]{1,0:T(8,128)(2,1)S(1)} %mask_rows.1.cot, bf16[256,128]{1,0:T(8,128)(2,1)S(1)} %get-tuple-element.52.g, bf16[16,144,128]{2,1,0:T(8,128)(2,1)S(1)} %all-to-all-done.recv, ...), custom_call_target="tpu_custom_call", output_to_operand_aliasing={{}: (8, {})} | custom-call | flops 1 | bytes 1 | tf_op jit(solution)/shard_map/finish/pallas_call | solution.py:440
  117.6 3.8 %scatter_rows.1 = (f32[512,8192]{1,0:T(8,128)}, f32[512,1024]{1,0:T(8,128)}) custom-call(s32[32]{0:T(128)S(1)} %copy-done.16, s32[512]{0:T(512)S(1)} %copy-done.14, bf16[16,144,128]{2,1,0:T(8,128)(2,1)S(1)} %all-to-all-done.1.recv, f32[512,8192]{1,0:T(8,128)} %get-tuple-element.81._down, ...), custom_call_target="tpu_custom_call", output_to_operand_aliasing={{0}: (3, {}), {1}: (4, {})} | custom-call | flops 1 | bytes 1 | tf_op jit(solution)/shard_map/scatter_rows/pallas_call | solution.py:359
  121.5 2.1 %finish.10.rest_3_ = bf16[256,8192]{1,0:T(8,128)(2,1)} custom-call(s32[19]{0:T(128)S(1)} %dynamic-slice_bitcast_fusion.meta, bf16[256,1024]{1,0:T(8,128)(2,1)S(1)} %mask_rows.1.cot, bf16[256,128]{1,0:T(8,128)(2,1)S(1)} %get-tuple-element.52.g, bf16[16,144,128]{2,1,0:T(8,128)(2,1)S(1)} %all-to-all-done.recv, ...), custom_call_target="tpu_custom_call", output_to_operand_aliasing={{}: (5, {})} | custom-call | flops 1 | bytes 1 | tf_op jit(solution)/shard_map/finish/pallas_call | solution.py:440
  123.6 1.5 %finish.11 = bf16[256,8192]{1,0:T(8,128)(2,1)} custom-call(s32[19]{0:T(128)S(1)} %dynamic-slice_bitcast_fusion.meta, bf16[256,1024]{1,0:T(8,128)(2,1)S(1)} %mask_rows.1.cot, bf16[256,128]{1,0:T(8,128)(2,1)S(1)} %get-tuple-element.52.g, bf16[16,144,128]{2,1,0:T(8,128)(2,1)S(1)} %all-to-all-done.recv, ...), custom_call_target="tpu_custom_call", output_to_operand_aliasing={{}: (7, {})} | custom-call | flops 1 | bytes 1 | tf_op jit(solution)/shard_map/finish/pallas_call | solution.py:440
  (39 shorter events, 0.1 us)
Async XLA Ops:
  0.6 18.7 %collective-permute-start.3 = (bf16[512,1024]{1,0:T(8,128)(2,1)}, bf16[512,1024]{1,0:T(8,128)(2,1)S(1)}, u32[]{:S(2)}, u32[]{:S(2)}) collective-permute-start(bf16[512,1024]{1,0:T(8,128)(2,1)} %rest_0_), channel_id=1, source_target_pairs={{0,1},{1,0},{2,3},{3,2},{4,5},{5,4},{6,7},{7,6},{8,9},{9,8},{10,11... | collective-permute-start | bytes 3145736 | tf_op jit(solution)/shard_map/ppermute | solution.py:510
  1.8 1.0 copy-start.8
  2.9 0.7 copy-start.17
  4.2 3.4 %copy-start = (bf16[512,8192]{1,0:T(8,128)(2,1)S(1)}, bf16[512,8192]{1,0:T(8,128)(2,1)}, u32[]{:S(2)}) copy-start(bf16[512,8192]{1,0:T(8,128)(2,1)} %down.1) | copy-start | bytes 25165828
  7.6 1.2 copy-start.6
  8.8 0.7 copy-start.13
  9.5 0.7 copy-start.15
  10.1 9.2 %copy-start.2 = (bf16[512,1024]{1,0:T(8,128)(2,1)S(1)}, bf16[512,1024]{1,0:T(8,128)(2,1)}, u32[]{:S(2)}) copy-start(bf16[512,1024]{1,0:T(8,128)(2,1)} %rest_0_) | copy-start | bytes 3145732
  19.3 26.1 %copy-start.4 = (bf16[512,1024]{1,0:T(8,128)(2,1)}, bf16[512,1024]{1,0:T(8,128)(2,1)S(1)}, u32[]{:S(2)}) copy-start(bf16[512,1024]{1,0:T(8,128)(2,1)S(1)} %collective-permute-done.3.rest_1_) | copy-start | bytes 3145732
  20.5 20.0 %collective-permute-start.4 = (bf16[512,1024]{1,0:T(8,128)(2,1)}, bf16[512,1024]{1,0:T(8,128)(2,1)}, u32[]{:S(2)}, u32[]{:S(2)}) collective-permute-start(bf16[512,1024]{1,0:T(8,128)(2,1)} %broadcast_select_fusion), channel_id=1, source_target_pairs={{0,4},{1,3},{2,0},{3,7},{4,8},{5,1},{6,2},{7,11},{8,12},{9,5},{10,... | collective-permute-start | bytes 3145736 | tf_op jit(solution)/shard_map/ppermute | solution.py:530
  23.1 29.3 %all-to-all-start = ((bf16[16,144,128]{2,1,0:T(8,128)(2,1)}), bf16[16,144,128]{2,1,0:T(8,128)(2,1)S(1)}, u32[]{:S(2)}, u32[]{:S(2)}) async-start(bf16[16,144,128]{2,1,0:T(8,128)(2,1)} %get-tuple-element.45), calls=%async_computation | async-start | bytes 1179648 | tf_op jit(solution)/shard_map/all_to_all | solution.py:521
  28.1 17.3 %collective-permute-start.1 = (bf16[256,1024]{1,0:T(8,128)(2,1)S(1)}, bf16[256,1024]{1,0:T(8,128)(2,1)S(1)}, u32[]{:S(2)}, u32[]{:S(2)}) collective-permute-start(bf16[256,1024]{1,0:T(8,128)(2,1)S(1)} %mask_rows.1.cot), channel_id=1, source_target_pairs={{0,16},{16,0},{1,17},{17,1},{2,18},{18,2},{3,19},{19,3},{4,20},{20... | collective-permute-start | bytes 1572872 | tf_op jit(solution)/shard_map/ppermute | solution.py:513
  40.5 21.2 %collective-permute-start.5 = (bf16[512,1024]{1,0:T(8,128)(2,1)}, bf16[512,1024]{1,0:T(8,128)(2,1)}, u32[]{:S(2)}, u32[]{:S(2)}) collective-permute-start(bf16[512,1024]{1,0:T(8,128)(2,1)} %collective-permute-done.4.refs_3_.rest_0_), channel_id=1, source_target_pairs={{0,4},{1,3},{2,0},{3,7},{4,8},{5,1},{6,2},{7,11},{8,12},{9,5},{10,... | collective-permute-start | bytes 3145736 | tf_op jit(solution)/shard_map/ppermute | solution.py:530
  45.4 1.9 %collective-permute-start = (bf16[256,1024]{1,0:T(8,128)(2,1)S(1)}, bf16[256,1024]{1,0:T(8,128)(2,1)S(1)}, u32[]{:S(2)}, u32[]{:S(2)}) collective-permute-start(bf16[256,1024]{1,0:T(8,128)(2,1)S(1)} %mask_rows.1.cot), channel_id=1, source_target_pairs={{0,1},{1,0},{2,3},{3,2},{4,5},{5,4},{6,7},{7,6},{8,9},{9,8},{10,11... | collective-permute-start | bytes 1572872 | tf_op jit(solution)/shard_map/ppermute | solution.py:512
  45.4 2.6 %collective-permute-start.2 = (bf16[256,1024]{1,0:T(8,128)(2,1)S(1)}, bf16[256,1024]{1,0:T(8,128)(2,1)S(1)}, u32[]{:S(2)}, u32[]{:S(2)}) collective-permute-start(bf16[256,1024]{1,0:T(8,128)(2,1)S(1)} %collective-permute-done.1.refs_1_), channel_id=1, source_target_pairs={{0,1},{1,0},{2,3},{3,2},{4,5},{5,4},{6,7},{7,6},{8,9},{9,8},{10,11... | collective-permute-start | bytes 1572872 | tf_op jit(solution)/shard_map/ppermute | solution.py:514
  50.3 0.7 copy-start.18
  51.0 0.7 copy-start.19
  51.7 0.7 copy-start.20
  52.4 2.2 %copy-start.1 = (bf16[256,8192]{1,0:T(8,128)(2,1)S(1)}, bf16[256,8192]{1,0:T(8,128)(2,1)}, u32[]{:S(2)}) copy-start(bf16[256,8192]{1,0:T(8,128)(2,1)} %x.1) | copy-start | bytes 12582916
  54.6 4.9 %copy-start.3 = (bf16[512,1024]{1,0:T(8,128)(2,1)S(1)}, bf16[512,1024]{1,0:T(8,128)(2,1)}, u32[]{:S(2)}) copy-start(bf16[512,1024]{1,0:T(8,128)(2,1)} %rest_0_) | copy-start | bytes 3145732
  54.6 4.9 %copy-start.5 = (bf16[512,1024]{1,0:T(8,128)(2,1)S(1)}, bf16[512,1024]{1,0:T(8,128)(2,1)}, u32[]{:S(2)}) copy-start(bf16[512,1024]{1,0:T(8,128)(2,1)} %copy-done.4) | copy-start | bytes 3145732
  59.5 4.7 %copy-start.7 = (bf16[16,144,128]{2,1,0:T(8,128)(2,1)}, bf16[16,144,128]{2,1,0:T(8,128)(2,1)S(1)}, u32[]{:S(2)}) copy-start(bf16[16,144,128]{2,1,0:T(8,128)(2,1)S(1)} %get-tuple-element.79) | copy-start | bytes 1769476
  61.7 23.6 %collective-permute-start.12 = (bf16[512,1024]{1,0:T(8,128)(2,1)}, bf16[512,1024]{1,0:T(8,128)(2,1)}, u32[]{:S(2)}, u32[]{:S(2)}) collective-permute-start(bf16[512,1024]{1,0:T(8,128)(2,1)} %collective-permute-done.5.refs_3_.rest_0_), channel_id=1, source_target_pairs={{0,4},{1,3},{2,0},{3,7},{4,8},{5,1},{6,2},{7,11},{8,12},{9,5},{10,... | collective-permute-start | bytes 3145736 | tf_op jit(solution)/shard_map/ppermute | solution.py:530
  64.1 35.3 %all-to-all-start.1 = ((bf16[16,144,128]{2,1,0:T(8,128)(2,1)}), bf16[16,144,128]{2,1,0:T(8,128)(2,1)S(1)}, u32[]{:S(2)}, u32[]{:S(2)}) async-start(bf16[16,144,128]{2,1,0:T(8,128)(2,1)} %copy-done.7), calls=%async_computation.1 | async-start | bytes 1179648 | tf_op jit(solution)/shard_map/all_to_all | solution.py:543
  68.4 4.9 %collective-permute-start.9 = (bf16[256,512]{1,0:T(8,128)(2,1)}, bf16[256,512]{1,0:T(8,128)(2,1)}, u32[]{:S(2)}, u32[]{:S(2)}) collective-permute-start(bf16[256,512]{1,0:T(8,128)(2,1)} %copy-done.20), channel_id=1, source_target_pairs={{0,1},{1,0},{2,3},{3,2},{4,5},{5,4},{6,7},{7,6},{8,9},{9,8},{10,11... | collective-permute-start | bytes 786440 | tf_op jit(solution)/shard_map/ppermute | solution.py:505
  68.8 9.5 %collective-permute-start.10 = (bf16[256,512]{1,0:T(8,128)(2,1)}, bf16[256,512]{1,0:T(8,128)(2,1)}, u32[]{:S(2)}, u32[]{:S(2)}) collective-permute-start(bf16[256,512]{1,0:T(8,128)(2,1)} %copy-done.19), channel_id=1, source_target_pairs={{0,16},{16,0},{1,17},{17,1},{2,18},{18,2},{3,19},{19,3},{4,20},{20... | collective-permute-start | bytes 786440 | tf_op jit(solution)/shard_map/ppermute | solution.py:506
  70.3 12.0 %collective-permute-start.11 = (bf16[256,512]{1,0:T(8,128)(2,1)}, bf16[256,512]{1,0:T(8,128)(2,1)}, u32[]{:S(2)}, u32[]{:S(2)}) collective-permute-start(bf16[256,512]{1,0:T(8,128)(2,1)} %copy-done.18), channel_id=1, source_target_pairs={{0,17},{1,16},{2,19},{3,18},{4,21},{5,20},{6,23},{7,22},{8,25},{9,... | collective-permute-start | bytes 786440 | tf_op jit(solution)/shard_map/ppermute | solution.py:507
  87.2 21.0 %collective-permute-start.13 = (bf16[256,1024]{1,0:T(8,128)(2,1)}, bf16[256,1024]{1,0:T(8,128)(2,1)}, u32[]{:S(2)}, u32[]{:S(2)}) collective-permute-start(bf16[256,1024]{1,0:T(8,128)(2,1)} %constant_dynamic-slice_fusion), channel_id=1, source_target_pairs={{0,4},{1,3},{2,0},{3,7},{4,8},{5,1},{6,2},{7,11},{8,12},{9,5},{10,... | collective-permute-start | bytes 1572872 | tf_op jit(solution)/shard_map/ppermute | solution.py:530
  89.2 5.4 %collective-permute-start.6 = (bf16[256,512]{1,0:T(8,128)(2,1)S(1)}, bf16[256,512]{1,0:T(8,128)(2,1)S(1)}, u32[]{:S(2)}, u32[]{:S(2)}) collective-permute-start(bf16[256,512]{1,0:T(8,128)(2,1)S(1)} %get-tuple-element.57), channel_id=1, source_target_pairs={{0,1},{1,0},{2,3},{3,2},{4,5},{5,4},{6,7},{7,6},{8,9},{9,8},{10,11... | collective-permute-start | bytes 786440 | tf_op jit(solution)/shard_map/ppermute | solution.py:505
  89.5 9.1 %collective-permute-start.7 = (bf16[256,512]{1,0:T(8,128)(2,1)S(1)}, bf16[256,512]{1,0:T(8,128)(2,1)S(1)}, u32[]{:S(2)}, u32[]{:S(2)}) collective-permute-start(bf16[256,512]{1,0:T(8,128)(2,1)S(1)} %get-tuple-element.58), channel_id=1, source_target_pairs={{0,16},{16,0},{1,17},{17,1},{2,18},{18,2},{3,19},{19,3},{4,20},{20... | collective-permute-start | bytes 786440 | tf_op jit(solution)/shard_map/ppermute | solution.py:506
  91.0 12.4 %collective-permute-start.8 = (bf16[256,512]{1,0:T(8,128)(2,1)}, bf16[256,512]{1,0:T(8,128)(2,1)}, u32[]{:S(2)}, u32[]{:S(2)}) collective-permute-start(bf16[256,512]{1,0:T(8,128)(2,1)} %get-tuple-element.59), channel_id=1, source_target_pairs={{0,17},{1,16},{2,19},{3,18},{4,21},{5,20},{6,23},{7,22},{8,25},{9,... | collective-permute-start | bytes 786440 | tf_op jit(solution)/shard_map/ppermute | solution.py:507
  94.0 18.1 %collective-permute-start.17 = (bf16[256,512]{1,0:T(8,128)(2,1)}, bf16[256,512]{1,0:T(8,128)(2,1)}, u32[]{:S(2)}, u32[]{:S(2)}) collective-permute-start(bf16[256,512]{1,0:T(8,128)(2,1)} %get-tuple-element.67), channel_id=1, source_target_pairs={{0,1},{1,0},{2,3},{3,2},{4,5},{5,4},{6,7},{7,6},{8,9},{9,8},{10,11... | collective-permute-start | bytes 786440 | tf_op jit(solution)/shard_map/ppermute | solution.py:505
  94.6 0.7 copy-start.9
  95.3 16.9 %collective-permute-start.18 = (bf16[256,512]{1,0:T(8,128)(2,1)}, bf16[256,512]{1,0:T(8,128)(2,1)}, u32[]{:S(2)}, u32[]{:S(2)}) collective-permute-start(bf16[256,512]{1,0:T(8,128)(2,1)} %get-tuple-element.76), channel_id=1, source_target_pairs={{0,16},{16,0},{1,17},{17,1},{2,18},{18,2},{3,19},{19,3},{4,20},{20... | collective-permute-start | bytes 786440 | tf_op jit(solution)/shard_map/ppermute | solution.py:506
  98.7 0.7 copy-start.11
  99.4 15.3 %collective-permute-start.19 = (bf16[256,512]{1,0:T(8,128)(2,1)}, bf16[256,512]{1,0:T(8,128)(2,1)}, u32[]{:S(2)}, u32[]{:S(2)}) collective-permute-start(bf16[256,512]{1,0:T(8,128)(2,1)} %get-tuple-element.77), channel_id=1, source_target_pairs={{0,17},{1,16},{2,19},{3,18},{4,21},{5,20},{6,23},{7,22},{8,25},{9,... | collective-permute-start | bytes 786440 | tf_op jit(solution)/shard_map/ppermute | solution.py:507
  103.4 0.9 copy-start.10
  104.4 0.9 copy-start.12
  109.8 13.8 %collective-permute-start.14 = (bf16[256,256]{1,0:T(8,128)(2,1)S(1)}, bf16[256,256]{1,0:T(8,128)(2,1)S(1)}, u32[]{:S(2)}, u32[]{:S(2)}) collective-permute-start(bf16[256,256]{1,0:T(8,128)(2,1)S(1)} %get-tuple-element.73), channel_id=1, source_target_pairs={{0,1},{1,0},{2,3},{3,2},{4,5},{5,4},{6,7},{7,6},{8,9},{9,8},{10,11... | collective-permute-start | bytes 393224 | tf_op jit(solution)/shard_map/ppermute | solution.py:505
  110.7 12.9 %collective-permute-start.15 = (bf16[256,256]{1,0:T(8,128)(2,1)S(1)}, bf16[256,256]{1,0:T(8,128)(2,1)S(1)}, u32[]{:S(2)}, u32[]{:S(2)}) collective-permute-start(bf16[256,256]{1,0:T(8,128)(2,1)S(1)} %get-tuple-element.74), channel_id=1, source_target_pairs={{0,16},{16,0},{1,17},{17,1},{2,18},{18,2},{3,19},{19,3},{4,20},{20... | collective-permute-start | bytes 393224 | tf_op jit(solution)/shard_map/ppermute | solution.py:506
  112.2 5.4 %copy-start.14 = (s32[512]{0:T(512)S(1)}, s32[512]{0:T(512)}, u32[]{:S(2)}) copy-start(s32[512]{0:T(512)} %storage.3) | copy-start | bytes 6148
  112.2 5.5 %copy-start.16 = (s32[32]{0:T(128)S(1)}, s32[32]{0:T(128)}, u32[]{:S(2)}) copy-start(s32[32]{0:T(128)} %adapter.2) | copy-start | bytes 388
  112.2 11.4 %collective-permute-start.16 = (bf16[256,256]{1,0:T(8,128)(2,1)S(1)}, bf16[256,256]{1,0:T(8,128)(2,1)S(1)}, u32[]{:S(2)}, u32[]{:S(2)}) collective-permute-start(bf16[256,256]{1,0:T(8,128)(2,1)S(1)} %get-tuple-element.75), channel_id=1, source_target_pairs={{0,17},{1,16},{2,19},{3,18},{4,21},{5,20},{6,23},{7,22},{8,25},{9,... | collective-permute-start | bytes 393224 | tf_op jit(solution)/shard_map/ppermute | solution.py:507

commit v4 on v3

--- a/solution.py
+++ b/solution.py
@@ -29,6 +29,14 @@
     return jnp.sum(jnp.where(matches, adapter_storage_row[None, :], 0), axis=1)
 
 
+def in_hbm(value):
+    return pltpu.with_memory_space_constraint(value, pltpu.HBM)
+
+
+def table_row(table):
+    return lax.axis_index("parts") * (table.shape[0] // 2) + lax.axis_index("fsdp")
+
+
 def iota(shape, axis):
     return lax.broadcasted_iota(jnp.int32, shape, axis)
 
@@ -51,15 +59,16 @@
     return jnp.concatenate(parts, axis=-1)
 
 
-def mask_kernel(meta, live, cot, out):
+def mask_kernel(table, live, cot, out):
+    first = table[table_row(table), 0]
     row = iota((BLOCK, cot.shape[1]), 0)
     for k in range(cot.shape[0] // BLOCK):
         rows = slice(k * BLOCK, (k + 1) * BLOCK)
         value = cot[rows, :].astype(jnp.float32)
-        out[rows, :] = jnp.where(row < live[meta[0] + k], value, 0.0).astype(out.dtype)
-
-
-def mask_rows(meta, block_live_rows, cotangent):
+        out[rows, :] = jnp.where(row < live[first + k], value, 0.0).astype(out.dtype)
+
+
+def mask_rows(table, block_live_rows, cotangent):
     return pl.pallas_call(
         mask_kernel,
         in_specs=[IN_SMEM, IN_SMEM, IN_VMEM],
@@ -68,7 +77,7 @@
         compiler_params=PARAMS,
         cost_estimate=SMALL,
         name="mask_rows",
-    )(meta, block_live_rows, cotangent)
+    )(in_hbm(table), in_hbm(block_live_rows), in_hbm(cotangent))
 
 
 def rank_major_order(transposed):
@@ -78,19 +87,11 @@
     return ((a % LANES) * 8 + a // LANES == b).astype(jnp.bfloat16)
 
 
-def zero_copies(zeros, target, sems, first, rows):
-    part = zeros if target.shape[1] == zeros.shape[1] else zeros.at[:, : target.shape[1]]
-    return [
-        pltpu.make_async_copy(part, target.at[pl.ds(start, ZERO_ROWS), :], sems.at[i])
-        for i, start in enumerate(range(first, first + rows, ZERO_ROWS))
-    ]
-
-
 def gather_kernel(
-    adapter, storage, down, up, payload, grads, dbuf, ubuf, dscr, uscr, cols, zeros, dsem, usem, zsem
+    adapter, storage, down, up, result, dbuf, ubuf, dscr, uscr, cols, payload, dsem, usem, rsem
 ):
     blocks = adapter.shape[0]
-    devices = payload.shape[0]
+    devices = result.shape[0]
     group = dbuf.shape[1]
     per_down, per_up = down.shape[1] // LANES, up.shape[1] // LANES
     down_rows = 2 * per_down
@@ -111,10 +112,6 @@
         return carry
 
     lax.fori_loop(0, blocks, begin, 0)
-    zeros[...] = jnp.zeros_like(zeros)
-    fills = zero_copies(zeros, grads, zsem, 0, grads.shape[0] // 2)
-    for copy in fills:
-        copy.start()
     order = rank_major_order(False)
 
     def one(j, carry):
@@ -145,13 +142,14 @@
         return carry
 
     lax.fori_loop(0, devices, one, 0)
-    result = dot_n(cols[...], order).astype(payload.dtype).reshape(devices, ADAPTER_RANK, 8 * LANES)
+    value = dot_n(cols[...], order).astype(payload.dtype).reshape(devices, ADAPTER_RANK, 8 * LANES)
     for q in range(8):
-        payload[:, q * ADAPTER_RANK : (q + 1) * ADAPTER_RANK, :] = result[
+        payload[:, q * ADAPTER_RANK : (q + 1) * ADAPTER_RANK, :] = value[
             :, :, q * LANES : (q + 1) * LANES
         ]
-    for copy in fills:
-        copy.wait()
+    copy = pltpu.make_async_copy(payload, result, rsem)
+    copy.start()
+    copy.wait()
 
 
 def gather_rows(padded_block_adapter, adapter_storage_row, down, up, devices):
@@ -163,29 +161,26 @@
     return pl.pallas_call(
         gather_kernel,
         in_specs=[IN_SMEM, IN_SMEM, IN_HBM, IN_HBM],
-        out_specs=[IN_VMEM, IN_HBM],
-        out_shape=[
-            jax.ShapeDtypeStruct(shape, jnp.bfloat16),
-            jax.ShapeDtypeStruct(down.shape, jnp.float32),
-        ],
+        out_specs=IN_HBM,
+        out_shape=jax.ShapeDtypeStruct(shape, jnp.bfloat16),
         scratch_shapes=[
             pltpu.VMEM((blocks, group, down.shape[1]), down.dtype),
             pltpu.VMEM((blocks, group, up.shape[1]), up.dtype),
             pltpu.VMEM((2, 8 * per_down, LANES), jnp.float32),
             pltpu.VMEM((2, 8 * per_up, LANES), jnp.float32),
             pltpu.VMEM((devices * ADAPTER_RANK, 8 * LANES), jnp.bfloat16),
-            pltpu.VMEM((ZERO_ROWS, down.shape[1]), jnp.float32),
+            pltpu.VMEM(shape, jnp.bfloat16),
             pltpu.SemaphoreType.DMA((blocks,)),
             pltpu.SemaphoreType.DMA((blocks,)),
-            pltpu.SemaphoreType.DMA((down.shape[0] // 2 // ZERO_ROWS,)),
+            pltpu.SemaphoreType.DMA,
         ],
         compiler_params=WIDE_PARAMS,
         cost_estimate=SMALL,
         name="gather_rows",
-    )(padded_block_adapter, adapter_storage_row, down, up)
-
-
-def adapter_kernel(x, cot, recv, _, sent, g_out, grads, up_grads, xbuf, zeros, xsem, zsem, usem):
+    )(in_hbm(padded_block_adapter), in_hbm(adapter_storage_row), in_hbm(down), in_hbm(up))
+
+
+def adapter_kernel(x, cot, recv, result, g_out, xbuf, sent, xsem, rsem):
     devices = recv.shape[0]
     blocks = x.shape[0] // BLOCK
     steps = xbuf.shape[0]
@@ -202,13 +197,6 @@
     ]
     for copy in loads:
         copy.start()
-    zeros[...] = jnp.zeros_like(zeros)
-    half = grads.shape[0] // 2
-    fills = zero_copies(zeros, grads, zsem, half, half)
-    fills += zero_copies(zeros, up_grads, usem, 0, up_grads.shape[0])
-    for copy in fills:
-        copy.start()
-
     lane = iota((BLOCK, LANES), 1)
     gather_rank = (iota((LANES, LANES), 0) // 8 == iota((LANES, LANES), 1)).astype(jnp.float32)
     b_all = recv[:, down_rows:, :].astype(jnp.float32)
@@ -225,6 +213,7 @@
         g_out[k * BLOCK : (k + 1) * BLOCK, :] = g
         turned.append(g.astype(jnp.float32).T[:ADAPTER_RANK, :].astype(jnp.bfloat16))
 
+    stores = []
     lows = [jnp.zeros((BLOCK, ADAPTER_RANK), jnp.float32) for _ in range(blocks)]
     for i in range(steps):
         loads[i].wait()
@@ -239,6 +228,9 @@
             grad = (adapter_scale * dot_n(turned[k], part)).astype(sent.dtype)
             for tile, (j, at) in enumerate(spots):
                 sent[j, at : at + ADAPTER_RANK, :] = grad[:, tile * LANES : (tile + 1) * LANES]
+        part = (pl.ds(i * here, here), pl.ds(0, down_rows), slice(None))
+        stores.append(pltpu.make_async_copy(sent.at[part], result.at[part], rsem.at[i]))
+        stores[-1].start()
 
     ups = []
     row = iota((LANES, LANES), 0)
@@ -253,35 +245,69 @@
             flat = flat + jnp.where(row % tiles == t, up[:, t * LANES : (t + 1) * LANES], 0.0)
         ups.append((adapter_scale * flat).reshape(devices, up_chunk, LANES))
     sent[:, down_rows:, :] = jnp.concatenate(ups, axis=1).astype(sent.dtype)
-    for copy in fills:
+    part = (slice(None), pl.ds(down_rows, sent.shape[1] - down_rows), slice(None))
+    stores.append(pltpu.make_async_copy(sent.at[part], result.at[part], rsem.at[steps]))
+    stores[-1].start()
+    for copy in stores:
         copy.wait()
 
 
-def adapter_terms(x, cot, recv, grads, up_shape):
+def adapter_terms(x, cot, recv):
     rows, width = x.shape
     steps = 8
     return pl.pallas_call(
         adapter_kernel,
-        in_specs=[IN_HBM, IN_VMEM, IN_VMEM, IN_HBM],
-        out_specs=[IN_VMEM, IN_VMEM, IN_HBM, IN_HBM],
+        in_specs=[IN_HBM, IN_VMEM, IN_VMEM],
+        out_specs=[IN_HBM, IN_VMEM],
         out_shape=[
             jax.ShapeDtypeStruct(recv.shape, jnp.bfloat16),
             jax.ShapeDtypeStruct((rows, LANES), jnp.bfloat16),
-            jax.ShapeDtypeStruct(grads.shape, grads.dtype),
-            jax.ShapeDtypeStruct(up_shape, jnp.float32),
         ],
-        input_output_aliases={3: 2},
         scratch_shapes=[
             pltpu.VMEM((steps, rows, width // steps), x.dtype),
-            pltpu.VMEM((ZERO_ROWS, grads.shape[1]), jnp.float32),
+            pltpu.VMEM(recv.shape, jnp.bfloat16),
             pltpu.SemaphoreType.DMA((steps,)),
-            pltpu.SemaphoreType.DMA((grads.shape[0] // 2 // ZERO_ROWS,)),
-            pltpu.SemaphoreType.DMA((up_shape[0] // ZERO_ROWS,)),
+            pltpu.SemaphoreType.DMA((steps + 1,)),
         ],
         compiler_params=PARAMS,
         cost_estimate=SMALL,
         name="adapter_terms",
-    )(x, cot, recv, grads)
+    )(in_hbm(x), cot, recv)
+
+
+def zero_kernel(_, down, up, zeros, dsem, usem):
+    zeros[...] = jnp.zeros_like(zeros)
+    copies = []
+    for i in range(down.shape[0] // ZERO_ROWS):
+        rows = pl.ds(i * ZERO_ROWS, ZERO_ROWS)
+        part = zeros.at[:, : up.shape[1]]
+        copies.append(pltpu.make_async_copy(zeros, down.at[rows, :], dsem.at[i]))
+        copies.append(pltpu.make_async_copy(part, up.at[rows, :], usem.at[i]))
+    for copy in copies:
+        copy.start()
+    for copy in copies:
+        copy.wait()
+
+
+def zero_grads(earlier, down_shape, up_shape):
+    count = down_shape[0] // ZERO_ROWS
+    return pl.pallas_call(
+        zero_kernel,
+        in_specs=[pl.BlockSpec(memory_space=pl.ANY)],
+        out_specs=[IN_HBM, IN_HBM],
+        out_shape=[
+            jax.ShapeDtypeStruct(down_shape, jnp.float32),
+            jax.ShapeDtypeStruct(up_shape, jnp.float32),
+        ],
+        scratch_shapes=[
+            pltpu.VMEM((ZERO_ROWS, down_shape[1]), jnp.float32),
+            pltpu.SemaphoreType.DMA((count,)),
+            pltpu.SemaphoreType.DMA((count,)),
+        ],
+        compiler_params=PARAMS,
+        cost_estimate=SMALL,
+        name="zero_grads",
+    )(earlier)
 
 
 def scatter_kernel(
@@ -379,41 +405,103 @@
         compiler_params=PARAMS,
         cost_estimate=SMALL,
         name="scatter_rows",
-    )(padded_block_adapter, adapter_storage_row, recv, down, up)
+    )(in_hbm(padded_block_adapter), in_hbm(adapter_storage_row), recv, down, up)
+
+
+def pick_kernel(own, other, out, sem):
+    mine = lax.axis_index("parts") == lax.axis_index("fsdp") % 2
+
+    @pl.when(mine)
+    def _():
+        copy = pltpu.make_async_copy(own, out, sem)
+        copy.start()
+        copy.wait()
+
+    @pl.when(jnp.logical_not(mine))
+    def _():
+        copy = pltpu.make_async_copy(other, out, sem)
+        copy.start()
+        copy.wait()
+
+
+def pick(own, other):
+    return pl.pallas_call(
+        pick_kernel,
+        in_specs=[pl.BlockSpec(memory_space=pl.ANY)] * 2,
+        out_specs=IN_VMEM,
+        out_shape=jax.ShapeDtypeStruct(own.shape, own.dtype),
+        scratch_shapes=[pltpu.SemaphoreType.DMA],
+        compiler_params=PARAMS,
+        cost_estimate=SMALL,
+        name="pick",
+    )(in_hbm(own), other)
 
 
 def far_kernel(count, *refs):
-    weight = refs[count][...]
-    for cot, out in zip(refs[:count], refs[count + 1 :]):
-        out[...] = dot_t(cot[...], weight).astype(out.dtype)
+    cots, weight, outs = refs[:count], refs[count], refs[count + 1 : 2 * count + 1]
+    wbuf, buffer, wsem, sems = refs[2 * count + 1 :]
+    tile = wbuf.shape[1]
+    loads = [
+        pltpu.make_async_copy(weight.at[i * tile : (i + 1) * tile, :], wbuf.at[i], wsem.at[i])
+        for i in range(wbuf.shape[0])
+    ]
+    for copy in loads:
+        copy.start()
+    stores = [pltpu.make_async_copy(buffer.at[n], outs[n], sems.at[n]) for n in range(count)]
+    for i, load in enumerate(loads):
+        load.wait()
+        for n, cot in enumerate(cots):
+            value = dot_t(cot[...], wbuf[i]).astype(buffer.dtype)
+            buffer[n, :, i * tile : (i + 1) * tile] = value
+            if i == len(loads) - 1:
+                stores[n].start()
+    for copy in stores:
+        copy.wait()
 
 
 def far_products(cots, weight):
-    shape = jax.ShapeDtypeStruct((cots[0].shape[0], weight.shape[0]), jnp.bfloat16)
+    count, rows, tile = len(cots), cots[0].shape[0], 256
+    span, depth = weight.shape
+    shape = jax.ShapeDtypeStruct((rows, span), jnp.bfloat16)
     return pl.pallas_call(
-        functools.partial(far_kernel, len(cots)),
-        in_specs=[IN_VMEM] * (len(cots) + 1),
-        out_specs=[IN_VMEM] * len(cots),
-        out_shape=[shape] * len(cots),
+        functools.partial(far_kernel, count),
+        in_specs=[IN_VMEM] * count + [pl.BlockSpec(memory_space=pl.ANY)],
+        out_specs=[IN_HBM] * count,
+        out_shape=[shape] * count,
+        scratch_shapes=[
+            pltpu.VMEM((span // tile, tile, depth), weight.dtype),
+            pltpu.VMEM((count, rows, span), jnp.bfloat16),
+            pltpu.SemaphoreType.DMA((span // tile,)),
+            pltpu.SemaphoreType.DMA((count,)),
+        ],
         compiler_params=PARAMS,
         cost_estimate=SMALL,
         name="far_products",
-    )(*cots, weight)
-
-
-def finish(meta, at, cot, weights, received, g, recv, out, width, columns):
+    )(*cots, in_hbm(weight))
+
+
+def finish(table, at, cot, weights, received, g, recv, out, width, columns):
     rows = cot.shape[0]
-    span = weights[0].shape[0] if weights else received[0].shape[1]
-    per_device = columns // span
-    count = len(weights) + len(received)
+    spans = [w.shape[0] for w in weights] + [r.shape[1] for r in received]
+    count = len(spans)
+    sources = [in_hbm(source) for source in (*weights, *received)]
     per = columns // LANES
 
-    def kernel(meta, cot, g, recv, *rest):
-        sources = rest[:count]
-        result, buffer, sems = rest[-3:]
+    def kernel(table, cot, g, recv, *rest):
+        mine = table_row(table)
+        given = rest[:count]
+        result = rest[-4 - count]
+        buffer, sems, loaded = rest[-3 - count], rest[-2 - count], rest[-1 - count : -1]
+        load_sems = rest[-1]
+        loads = [
+            pltpu.make_async_copy(given[i], loaded[i], load_sems.at[i]) for i in range(count)
+        ]
+        for load in loads:
+            load.start()
         copies = []
         for i in range(count):
-            index = meta[at + i]
+            index, span = table[mine, at[i]], spans[i]
+            per_device = columns // span
             device, inner = index // per_device, (index % per_device) * (span // LANES)
             parts = []
             for k in range(rows // BLOCK):
@@ -424,14 +512,17 @@
                 ours = g[k * BLOCK : (k + 1) * BLOCK, :ADAPTER_RANK]
                 parts.append(dot_n(ours, lane_cat(tiles)))
             value = adapter_scale * jnp.concatenate(parts, axis=0)
+            loads[i].wait()
             if i < len(weights):
-                value = value + dot_t(cot[...], sources[i][...])
+                value = value + dot_t(cot[...], loaded[i][...])
             else:
-                value = value + sources[i][...].astype(jnp.float32)
-            buffer[i] = value.astype(buffer.dtype)
+                value = value + loaded[i][...].astype(jnp.float32)
+            buffer[i, :, :span] = value.astype(buffer.dtype)
             start = pl.multiple_of(index * span, span)
             copies.append(
-                pltpu.make_async_copy(buffer.at[i], result.at[:, pl.ds(start, span)], sems.at[i])
+                pltpu.make_async_copy(
+                    buffer.at[i, :, :span], result.at[:, pl.ds(start, span)], sems.at[i]
+                )
             )
             copies[-1].start()
         for copy in copies:
@@ -439,18 +530,23 @@
 
     return pl.pallas_call(
         kernel,
-        in_specs=[IN_SMEM] + [IN_VMEM] * (3 + count) + ([] if out is None else [IN_HBM]),
+        in_specs=[IN_SMEM]
+        + [IN_VMEM] * 3
+        + [pl.BlockSpec(memory_space=pl.ANY)] * count
+        + ([] if out is None else [IN_HBM]),
         out_specs=IN_HBM,
         out_shape=jax.ShapeDtypeStruct((rows, width), jnp.bfloat16),
         input_output_aliases={} if out is None else {4 + count: 0},
         scratch_shapes=[
-            pltpu.VMEM((count, rows, span), jnp.bfloat16),
+            pltpu.VMEM((count, rows, max(spans)), jnp.bfloat16),
             pltpu.SemaphoreType.DMA((count,)),
-        ],
-        compiler_params=PARAMS,
+        ]
+        + [pltpu.VMEM(source.shape, source.dtype) for source in sources]
+        + [pltpu.SemaphoreType.DMA((count,))],
+        compiler_params=WIDE_PARAMS,
         cost_estimate=SMALL,
         name="finish",
-    )(meta, cot, g, recv, *weights, *received, *([] if out is None else [out]))
+    )(in_hbm(table), cot, g, recv, *sources, *([] if out is None else [out]))
 
 
 def ring_table(devices):
@@ -492,10 +588,9 @@
     steps = devices // 4
     shard = frozen_value_weight.shape[0]
     width = inputs.shape[1]
-    index, part = lax.axis_index("fsdp"), lax.axis_index("parts")
-    core = index % 2
+    core = lax.axis_index("fsdp") % 2
     ring, table = ring_table(devices)
-    meta = lax.dynamic_index_in_dim(jnp.asarray(table), part * devices + index, keepdims=False)
+    table = jnp.asarray(table)
     cores = [(i, i ^ 1) for i in range(devices)]
     across = [(0, 1), (1, 0)]
     diagonal = [(p * devices + i, (1 - p) * devices + (i ^ 1)) for p in range(2) for i in range(devices)]
@@ -508,56 +603,60 @@
         )
 
     other_shard = lax.ppermute(frozen_value_weight, "fsdp", cores)
-    masked = mask_rows(meta, block_live_rows, cotangent)
+    masked = mask_rows(table, block_live_rows, cotangent)
     core_masked = lax.ppermute(masked, "fsdp", cores)
     far_masked = lax.ppermute(masked, "parts", across)
+    travelling = pick(frozen_value_weight, other_shard)
+    adapter, _, _ = after(padded_block_adapter, masked, travelling)
+    payload = gather_rows(
+        adapter, adapter_storage_row, adapter_down_weights, adapter_up_weights, devices
+    )
+    recv = lax.all_to_all(payload, "fsdp", split_axis=0, concat_axis=0, tiled=True)
+    far_masked, _ = after(far_masked, payload)
     diagonal_masked = lax.ppermute(far_masked, "fsdp", cores)
-    adapter, _ = after(padded_block_adapter, masked)
-    payload, grads = gather_rows(
-        adapter, adapter_storage_row, adapter_down_weights, adapter_up_weights, devices
-    )
-    shards, _ = after((frozen_value_weight, other_shard), payload)
-    travelling = jnp.where(part == core, *shards)
-    recv = lax.all_to_all(payload, "fsdp", split_axis=0, concat_axis=0, tiled=True)
-
+    cots = (core_masked, far_masked, diagonal_masked)
+
+    travelling = lax.ppermute(travelling, "fsdp", ring)
+
+    firsts = [3 + 4 * step for step in range(steps)]
     pieces, received = [], []
-    placed = payload
-    out = None
     for step in range(steps):
-        travelling, _ = after(travelling, placed)
-        if step == steps - 1:
-            travelling = lax.dynamic_slice_in_dim(travelling, core * (shard // 2), shard // 2)
-        travelling = lax.ppermute(travelling, "fsdp", ring)
-        placed = payload if out is None else out
+        if step == 0:
+            travelling, cots, _ = after(travelling, cots, payload)
+        elif step == 1:
+            travelling, sent, grads, received[0] = after(travelling, sent, grads, received[0])
+            sums = lax.all_to_all(sent, "fsdp", split_axis=0, concat_axis=0, tiled=True)
+        elif step < steps - 1:
+            travelling, out, received[step - 1] = after(travelling, out, received[step - 1])
         pieces.append(travelling)
-        cots = (core_masked, far_masked, diagonal_masked)
-        if step > 0:
-            cots, _ = after(cots, out)
-        products = far_products(cots, travelling)
+        if step < steps - 1:
+            if step == steps - 2:
+                travelling = lax.dynamic_slice_in_dim(travelling, core * (shard // 2), shard // 2)
+            travelling = lax.ppermute(travelling, "fsdp", ring)
+        products = far_products(cots, pieces[step])
         received.append(cross(products))
         if step == 0:
-            new, _ = after(recv, products[0])
-            sent, g, grads, up_grads = adapter_terms(
-                inputs, masked, new, grads, adapter_up_weights.shape
+            grads = zero_grads(products[0], adapter_down_weights.shape, adapter_up_weights.shape)
+            recv, _ = after(recv, grads)
+            sent, g = adapter_terms(inputs, masked, recv)
+        if step == steps - 2 - 1:
+            cot, _ = after(masked, products[0])
+            weights = (frozen_value_weight, other_shard, *pieces)
+            at = [1, 2] + firsts[: step + 1] + [firsts[0] + i for i in range(1, 4)]
+            out = finish(table, at, cot, weights, received[0], g, recv, None, width, shard)
+        if step == steps - 2:
+            sums, _ = after(sums, products)
+            down_grad, up_grad = scatter_rows(
+                padded_block_adapter, adapter_storage_row, sums, *grads
             )
-            sums = lax.all_to_all(sent, "fsdp", split_axis=0, concat_axis=0, tiled=True)
-            out = finish(
-                meta, 1, masked, shards, (), g, recv, None, width, shard
-            )
-        else:
-            out, _ = after(out, products[0])
-            at = 4 * step - 1
-            out = finish(
-                meta, at, masked, pieces[step - 1 : step], received[step - 1], g, recv, out, width, shard
-            )
-        if step == 1:
-            sums, _ = after(sums, out)
-            down_grad, up_grad = scatter_rows(
-                padded_block_adapter, adapter_storage_row, sums, grads, up_grads
-            )
-    at = 4 * steps - 1
-    out = finish(meta, at, masked, pieces[-1:], (), g, recv, out, width, shard)
-    out = finish(meta, at + 1, masked, (), received[-1], g, recv, out, width, shard)
+            travelling, up_grad = after(travelling, up_grad)
+    g, _ = after(g, products)
+    at = firsts[-2:] + [first + i for first in firsts[1:-2] for i in range(1, 4)]
+    early = sum(received[1:-2], ())
+    out = finish(table, at, masked, pieces[-2:], early, g, recv, out, width, shard)
+    at = [first + i for first in firsts[-2:] for i in range(1, 4)]
+    late = sum(received[-2:], ())
+    out = finish(table, at, masked, (), late, g, recv, out, width, shard)
     return (out, down_grad, up_grad)
 
 

time: 127 us -> 106 us (0.83)
  waiting for transfers between devices: 30.4 us -> 13.5 us
  local copies, waits for them, and re-layouts: 17.8 us -> 3.34 us
  Pallas kernels: 42.8 us -> 53.5 us
  starting transfers between devices: 31.9 us -> 33.6 us
    unnamed x42 -> x10, local copies, waits for them, and re-layouts: 15.3 us -> 1.47 us
    pallas_call x11 -> x10, Pallas kernels: 29.2 us -> 40.4 us  [the longest x3 13.8 us: finish(): pl.pallas_call(kernel, in_specs=[IN_SMEM] + [IN_VMEM] * 3 + [pl.BlockSpec...]
    ppermute x4, waiting for transfers between devices: 10.9 us -> 0.75 us  [ring_body(): travelling = lax.ppermute(travelling, 'fsdp', ring)]
    ppermute x4, waiting for transfers between devices: 10.5 us -> 5.86 us  [cross(): lax.ppermute(products[2], ('parts', 'fsdp'), diagonal)]
    ppermute x4, waiting for transfers between devices: 6.83 us -> 4.95 us  [cross(): lax.ppermute(products[1], 'parts', across)]
    all_to_all x1, waiting for transfers between devices: 0.01 us -> 1.75 us  [ring_body(): lax.all_to_all(payload, 'fsdp', split_axis=0, concat_axis=0, tiled=True)]
    all_to_all x1, starting transfers between devices: 4.23 us -> 5.63 us  [ring_body(): sums = lax.all_to_all(sent, 'fsdp', split_axis=0, concat_axis=0, tiled=True)]
    ppermute x1, waiting for transfers between devices: 1.39 us -> 0.01 us  [ring_body(): core_masked = lax.ppermute(masked, 'fsdp', cores)]
  transfers between devices with their start and end apart: 22 -> 22, of which waited for: 8 -> 7; matrix products, arithmetic and copies ran while one was open for 2% -> 2% of each run, Pallas kernels for 33% -> 47%
where the time goes in v4:
time: 106 us; the launch traced here: 105 us
  Pallas kernels  53.5 us (50%)
  starting transfers between devices  33.6 us (32%)
  waiting for transfers between devices  13.5 us (13%)
  local copies, waits for them, and re-layouts  3.34 us (3%)
    pallas_call x3, Pallas kernels, finish(): pl.pallas_call(kernel, in_specs=[IN_SMEM] + [IN_VMEM] * 3 + [pl.BlockSpec...  13.8 us
    pallas_call x4, Pallas kernels, far_products(): pl.pallas_call(functools.partial(far_kernel, count), in_specs=[IN_VMEM] *...  12.6 us
    ppermute x4, starting transfers between devices, ring_body(): travelling = lax.ppermute(travelling, 'fsdp', ring)  10.8 us
    pallas_call x1, Pallas kernels, gather_rows(): pl.pallas_call(gather_kernel, in_specs=[IN_SMEM, IN_SMEM, IN_HBM, IN_HBM]...  8.03 us
    pallas_call x1, Pallas kernels, zero_grads(): pl.pallas_call(zero_kernel, in_specs=[pl.BlockSpec(memory_space=pl.ANY)],...  6.7 us
    ppermute x4, starting transfers between devices, cross(): lax.ppermute(products[1], 'parts', across)  6.08 us
    all_to_all x1, starting transfers between devices, ring_body(): lax.all_to_all(payload, 'fsdp', split_axis=0, concat_axis=0, tiled=True)  5.9 us
    ppermute x4, waiting for transfers between devices, cross(): lax.ppermute(products[2], ('parts', 'fsdp'), diagonal)  5.86 us
  transfers between devices with their start and end apart: 22, of which 7 were waited for; matrix products, arithmetic and copies ran while one was open for 2% of the time, Pallas kernels for 47%

profile of v4, /device:TPU:0, one launch (start us, length us, event | category | flops | bytes accessed | tf_op | source)
XLA Modules:
  0.0 105.0 jit_solution(15158565347577845486)
XLA Ops:
  0.6 0.5 collective-permute-start
  1.1 1.2 %mask_rows.1.cot = bf16[256,1024]{1,0:T(8,128)(2,1)S(1)} custom-call(s32[32,19]{1,0:T(8,128)} %constant.24.clone.table, s32[32]{0:T(128)} %live.1, bf16[256,1024]{1,0:T(8,128)(2,1)} %cot.1), custom_call_target="tpu_custom_call" | custom-call | flops 1 | bytes 1 | tf_op jit(solution)/shard_map/mask_rows/pallas_call | solution.py:72
  2.3 2.6 %collective-permute-start.3 = (bf16[256,1024]{1,0:T(8,128)(2,1)S(1)}, bf16[256,1024]{1,0:T(8,128)(2,1)S(1)}, u32[]{:S(2)}, u32[]{:S(2)}) collective-permute-start(bf16[256,1024]{1,0:T(8,128)(2,1)S(1)} %mask_rows.1.cot), channel_id=1, source_target_pairs={{0,16},{16,0},{1,17},{17,1},{2,18},{18,2},{3,19},{19,3},{4,20},{20... | collective-permute-start | bytes 1572872 | tf_op jit(solution)/shard_map/ppermute | solution.py:608
  4.9 0.0 collective-permute-done.other.rest_1_
  4.9 2.6 %pick.1 = bf16[512,1024]{1,0:T(8,128)(2,1)} custom-call(bf16[512,1024]{1,0:T(8,128)(2,1)} %rest_0_.1, bf16[512,1024]{1,0:T(8,128)(2,1)S(1)} %collective-permute-done.other.rest_1_), custom_call_target="tpu_custom_call" | custom-call | flops 1 | bytes 1 | tf_op jit(solution)/shard_map/pick/pallas_call | solution.py:428
  7.5 0.0 copy-done
  7.5 1.8 %collective-permute-start.1 = (bf16[512,1024]{1,0:T(8,128)(2,1)}, bf16[512,1024]{1,0:T(8,128)(2,1)}, u32[]{:S(2)}, u32[]{:S(2)}) collective-permute-start(bf16[512,1024]{1,0:T(8,128)(2,1)} %pick.1), channel_id=1, source_target_pairs={{0,4},{1,3},{2,0},{3,7},{4,8},{5,1},{6,2},{7,11},{8,12},{9,5},{10,... | collective-permute-start | bytes 3145736 | tf_op jit(solution)/shard_map/ppermute | solution.py:619
  9.2 0.0 collective-permute-start.2
  9.2 8.0 %gather_rows.1 = bf16[16,144,128]{2,1,0:T(8,128)(2,1)} custom-call(s32[32]{0:T(128)} %adapter.2, s32[512]{0:T(512)} %storage.3, bf16[512,8192]{1,0:T(8,128)(2,1)} %down.1, bf16[512,1024]{1,0:T(8,128)(2,1)} %up.1), custom_call_target="tpu_custom_call" | custom-call | flops 1 | bytes 1 | tf_op jit(solution)/shard_map/gather_rows/pallas_call | solution.py:161
  17.3 0.2 collective-permute-done.3.refs_1_
  17.5 0.4 collective-permute-start.4
  17.9 5.9 %all-to-all-start = ((bf16[16,144,128]{2,1,0:T(8,128)(2,1)}), bf16[16,144,128]{2,1,0:T(8,128)(2,1)S(1)}, u32[]{:S(2)}, u32[]{:S(2)}) async-start(bf16[16,144,128]{2,1,0:T(8,128)(2,1)} %gather_rows.1), calls=%async_computation | async-start | bytes 1179648 | tf_op jit(solution)/shard_map/all_to_all | solution.py:614
  23.8 0.0 collective-permute-done.2.refs_0_
  23.8 0.0 collective-permute-done.4.refs_2_
  23.8 0.0 collective-permute-done.1.refs_3_.rest_2_
  23.8 2.0 %collective-permute-start.5 = (bf16[512,1024]{1,0:T(8,128)(2,1)}, bf16[512,1024]{1,0:T(8,128)(2,1)}, u32[]{:S(2)}, u32[]{:S(2)}) collective-permute-start(bf16[512,1024]{1,0:T(8,128)(2,1)} %collective-permute-done.1.refs_3_.rest_2_), channel_id=1, source_target_pairs={{0,4},{1,3},{2,0},{3,7},{4,8},{5,1},{6,2},{7,11},{8,12},{9,5},{10,... | collective-permute-start | bytes 3145736 | tf_op jit(solution)/shard_map/ppermute | solution.py:635
  25.8 3.3 %far_products.4 = (bf16[256,512]{1,0:T(8,128)(2,1)S(1)}, bf16[256,512]{1,0:T(8,128)(2,1)S(1)}, bf16[256,512]{1,0:T(8,128)(2,1)S(1)}) custom-call(bf16[256,1024]{1,0:T(8,128)(2,1)S(1)} %collective-permute-done.2.refs_0_, bf16[256,1024]{1,0:T(8,128)(2,1)S(1)} %collective-permute-done.3.refs_1_, bf16[256,1024]{1,0:T(8,128)(2,1)S(1)} %collective-permute-done.4.refs_2_, ...), custom_call_target="tpu_custom_call" | custom-call | flops 1 | bytes 1 | tf_op jit(solution)/shard_map/far_products/pallas_call | solution.py:466
  29.1 0.1 collective-permute-start.6
  29.1 1.6 %collective-permute-start.7 = (bf16[256,512]{1,0:T(8,128)(2,1)S(1)}, bf16[256,512]{1,0:T(8,128)(2,1)}, u32[]{:S(2)}, u32[]{:S(2)}) collective-permute-start(bf16[256,512]{1,0:T(8,128)(2,1)S(1)} %get-tuple-element.57), channel_id=1, source_target_pairs={{0,16},{16,0},{1,17},{17,1},{2,18},{18,2},{3,19},{19,3},{4,20},{20... | collective-permute-start | bytes 786440 | tf_op jit(solution)/shard_map/ppermute | solution.py:601
  30.7 0.3 collective-permute-start.8
  31.0 6.7 %zero_grads.1 = (f32[512,8192]{1,0:T(8,128)}, f32[512,1024]{1,0:T(8,128)}) custom-call(bf16[256,512]{1,0:T(8,128)(2,1)S(1)} %get-tuple-element.51._), custom_call_target="tpu_custom_call" | custom-call | flops 1 | bytes 1 | tf_op jit(solution)/shard_map/zero_grads/pallas_call | solution.py:294
  37.7 1.8 %all-to-all-done.recv = bf16[16,144,128]{2,1,0:T(8,128)(2,1)S(1)} async-done(((bf16[16,144,128]{2,1,0:T(8,128)(2,1)}), bf16[16,144,128]{2,1,0:T(8,128)(2,1)S(1)}, u32[]{:S(2)}, u32[]{:S(2)}) %all-to-all-start) | async-done | bytes 589856 | tf_op jit(solution)/shard_map/all_to_all | solution.py:614
  39.5 4.6 %adapter_terms.1 = (bf16[16,144,128]{2,1,0:T(8,128)(2,1)S(1)}, bf16[256,128]{1,0:T(8,128)(2,1)S(1)}) custom-call(bf16[256,8192]{1,0:T(8,128)(2,1)} %x.1, bf16[256,1024]{1,0:T(8,128)(2,1)S(1)} %mask_rows.1.cot, bf16[16,144,128]{2,1,0:T(8,128)(2,1)S(1)} %all-to-all-done.recv), custom_call_target="tpu_custom_call" | custom-call | flops 1 | bytes 1 | tf_op jit(solution)/shard_map/adapter_terms/pallas_call | solution.py:258
  44.1 0.0 copy-start.1
  44.1 0.8 copy-done.1
  44.9 0.0 collective-permute-done.6.rest_4_
  44.9 0.0 collective-permute-done.7.rest_5_
  44.9 0.0 collective-permute-done.8.rest_6_
  44.9 0.7 collective-permute-done.5.refs_3_.rest_3_
  45.7 4.9 %collective-permute-start.9 = (bf16[512,1024]{1,0:T(8,128)(2,1)}, bf16[512,1024]{1,0:T(8,128)(2,1)}, u32[]{:S(2)}, u32[]{:S(2)}) collective-permute-start(bf16[512,1024]{1,0:T(8,128)(2,1)} %collective-permute-done.5.refs_3_.rest_3_), channel_id=1, source_target_pairs={{0,4},{1,3},{2,0},{3,7},{4,8},{5,1},{6,2},{7,11},{8,12},{9,5},{10,... | collective-permute-start | bytes 3145736 | tf_op jit(solution)/shard_map/ppermute | solution.py:635
  50.6 5.6 %all-to-all-start.1 = ((bf16[16,144,128]{2,1,0:T(8,128)(2,1)}), bf16[16,144,128]{2,1,0:T(8,128)(2,1)S(1)}, u32[]{:S(2)}, u32[]{:S(2)}) async-start(bf16[16,144,128]{2,1,0:T(8,128)(2,1)} %copy-done.1), calls=%async_computation.1 | async-start | bytes 1179648 | tf_op jit(solution)/shard_map/all_to_all | solution.py:628
  56.2 3.3 %far_products.5 = (bf16[256,512]{1,0:T(8,128)(2,1)}, bf16[256,512]{1,0:T(8,128)(2,1)}, bf16[256,512]{1,0:T(8,128)(2,1)}) custom-call(bf16[256,1024]{1,0:T(8,128)(2,1)S(1)} %collective-permute-done.2.refs_0_, bf16[256,1024]{1,0:T(8,128)(2,1)S(1)} %collective-permute-done.3.refs_1_, bf16[256,1024]{1,0:T(8,128)(2,1)S(1)} %collective-permute-done.4.refs_2_, ...), custom_call_target="tpu_custom_call" | custom-call | flops 1 | bytes 1 | tf_op jit(solution)/shard_map/far_products/pallas_call | solution.py:466
  59.5 0.5 collective-permute-start.10
  59.9 1.5 %collective-permute-start.11 = (bf16[256,512]{1,0:T(8,128)(2,1)}, bf16[256,512]{1,0:T(8,128)(2,1)}, u32[]{:S(2)}, u32[]{:S(2)}) collective-permute-start(bf16[256,512]{1,0:T(8,128)(2,1)} %get-tuple-element.65), channel_id=1, source_target_pairs={{0,16},{16,0},{1,17},{17,1},{2,18},{18,2},{3,19},{19,3},{4,20},{20... | collective-permute-start | bytes 786440 | tf_op jit(solution)/shard_map/ppermute | solution.py:601
  61.5 0.0 collective-permute-start.12
  61.5 5.7 %finish.3.rest_5_ = bf16[256,8192]{1,0:T(8,128)(2,1)} custom-call(s32[32,19]{1,0:T(8,128)} %constant.24.clone.table, bf16[256,1024]{1,0:T(8,128)(2,1)S(1)} %mask_rows.1.cot, bf16[256,128]{1,0:T(8,128)(2,1)S(1)} %get-tuple-element.80.g, bf16[16,144,128]{2,1,0:T(8,128)(2,1)S(1)} %all-to-all-done.recv, bf16[512,1024]{1,0:T(8,128)(2,1)} %rest_0_.1, ...), custom_call_target="tpu_custom_call" | custom-call | flops 1 | bytes 1 | tf_op jit(solution)/shard_map/finish/pallas_call | solution.py:531
  67.1 0.0 collective-permute-done.10.rest_2_
  67.2 2.3 %collective-permute-done.11.rest_3_ = bf16[256,512]{1,0:T(8,128)(2,1)} collective-permute-done((bf16[256,512]{1,0:T(8,128)(2,1)}, bf16[256,512]{1,0:T(8,128)(2,1)}, u32[]{:S(2)}, u32[]{:S(2)}) %collective-permute-start.11) | collective-permute-done | bytes 262176 | tf_op jit(solution)/shard_map/ppermute | solution.py:601
  69.4 4.0 %collective-permute-done.12.rest_4_ = bf16[256,512]{1,0:T(8,128)(2,1)} collective-permute-done((bf16[256,512]{1,0:T(8,128)(2,1)}, bf16[256,512]{1,0:T(8,128)(2,1)}, u32[]{:S(2)}, u32[]{:S(2)}) %collective-permute-start.12) | collective-permute-done | bytes 262176 | tf_op jit(solution)/shard_map/ppermute | solution.py:602
  73.4 0.0 collective-permute-done.9.refs_3_.rest_0_
  73.4 1.9 %constant_dynamic-slice_fusion = bf16[256,1024]{1,0:T(8,128)(2,1)} fusion(bf16[512,1024]{1,0:T(8,128)(2,1)} %collective-permute-done.9.refs_3_.rest_0_, s32[]{:T(128)S(6)} %select_n.11), kind=kLoop, calls=%fused_computation | loop fusion | bytes 1048580 | tf_op jit(solution)/shard_map/dynamic_slice | solution.py:634
  75.2 2.2 %collective-permute-start.13 = (bf16[256,1024]{1,0:T(8,128)(2,1)}, bf16[256,1024]{1,0:T(8,128)(2,1)}, u32[]{:S(2)}, u32[]{:S(2)}) collective-permute-start(bf16[256,1024]{1,0:T(8,128)(2,1)} %constant_dynamic-slice_fusion), channel_id=1, source_target_pairs={{0,4},{1,3},{2,0},{3,7},{4,8},{5,1},{6,2},{7,11},{8,12},{9,5},{10,... | collective-permute-start | bytes 1572872 | tf_op jit(solution)/shard_map/ppermute | solution.py:635
  77.4 3.3 %far_products.6 = (bf16[256,512]{1,0:T(8,128)(2,1)}, bf16[256,512]{1,0:T(8,128)(2,1)}, bf16[256,512]{1,0:T(8,128)(2,1)}) custom-call(bf16[256,1024]{1,0:T(8,128)(2,1)S(1)} %collective-permute-done.2.refs_0_, bf16[256,1024]{1,0:T(8,128)(2,1)S(1)} %collective-permute-done.3.refs_1_, bf16[256,1024]{1,0:T(8,128)(2,1)S(1)} %collective-permute-done.4.refs_2_, ...), custom_call_target="tpu_custom_call" | custom-call | flops 1 | bytes 1 | tf_op jit(solution)/shard_map/far_products/pallas_call | solution.py:466
  80.7 0.1 collective-permute-start.14
  80.9 1.5 %collective-permute-start.15 = (bf16[256,512]{1,0:T(8,128)(2,1)}, bf16[256,512]{1,0:T(8,128)(2,1)}, u32[]{:S(2)}, u32[]{:S(2)}) collective-permute-start(bf16[256,512]{1,0:T(8,128)(2,1)} %get-tuple-element.70), channel_id=1, source_target_pairs={{0,16},{16,0},{1,17},{17,1},{2,18},{18,2},{3,19},{19,3},{4,20},{20... | collective-permute-start | bytes 786440 | tf_op jit(solution)/shard_map/ppermute | solution.py:601
  82.4 0.3 collective-permute-start.16
  82.7 0.0 all-to-all-done.1.recv
  82.7 3.9 %scatter_rows.1 = (f32[512,8192]{1,0:T(8,128)}, f32[512,1024]{1,0:T(8,128)}) custom-call(s32[32]{0:T(128)} %adapter.2, s32[512]{0:T(512)} %storage.3, bf16[16,144,128]{2,1,0:T(8,128)(2,1)S(1)} %all-to-all-done.1.recv, f32[512,8192]{1,0:T(8,128)} %get-tuple-element.73._down, ...), custom_call_target="tpu_custom_call", output_to_operand_aliasing={{0}: (3, {}), {1}: (4, {})} | custom-call | flops 1 | bytes 1 | tf_op jit(solution)/shard_map/scatter_rows/pallas_call | solution.py:385
  86.6 0.0 collective-permute-done.13.refs_3_.rest_1_
  86.6 2.8 %far_products.7 = (bf16[256,256]{1,0:T(8,128)(2,1)S(1)}, bf16[256,256]{1,0:T(8,128)(2,1)S(1)}, bf16[256,256]{1,0:T(8,128)(2,1)S(1)}) custom-call(bf16[256,1024]{1,0:T(8,128)(2,1)S(1)} %collective-permute-done.2.refs_0_, bf16[256,1024]{1,0:T(8,128)(2,1)S(1)} %collective-permute-done.3.refs_1_, bf16[256,1024]{1,0:T(8,128)(2,1)S(1)} %collective-permute-done.4.refs_2_, ...), custom_call_target="tpu_custom_call" | custom-call | flops 1 | bytes 1 | tf_op jit(solution)/shard_map/far_products/pallas_call | solution.py:466
  89.4 0.4 collective-permute-start.17
  89.9 1.5 %collective-permute-start.18 = (bf16[256,256]{1,0:T(8,128)(2,1)S(1)}, bf16[256,256]{1,0:T(8,128)(2,1)S(1)}, u32[]{:S(2)}, u32[]{:S(2)}) collective-permute-start(bf16[256,256]{1,0:T(8,128)(2,1)S(1)} %get-tuple-element.78), channel_id=1, source_target_pairs={{0,16},{16,0},{1,17},{17,1},{2,18},{18,2},{3,19},{19,3},{4,20},{20... | collective-permute-start | bytes 393224 | tf_op jit(solution)/shard_map/ppermute | solution.py:601
  91.3 0.0 collective-permute-done.14.rest_0_
  91.3 0.0 collective-permute-start.19
  91.4 4.5 %finish.4.rest_6_ = bf16[256,8192]{1,0:T(8,128)(2,1)} custom-call(s32[32,19]{1,0:T(8,128)} %constant.24.clone.table, bf16[256,1024]{1,0:T(8,128)(2,1)S(1)} %mask_rows.1.cot, bf16[256,128]{1,0:T(8,128)(2,1)S(1)} %get-tuple-element.80.g, bf16[16,144,128]{2,1,0:T(8,128)(2,1)S(1)} %all-to-all-done.recv, ...), custom_call_target="tpu_custom_call", output_to_operand_aliasing={{}: (9, {})} | custom-call | flops 1 | bytes 1 | tf_op jit(solution)/shard_map/finish/pallas_call | solution.py:531
  95.9 0.0 collective-permute-done.15.rest_1_
  95.9 0.0 collective-permute-done.16.rest_2_
  95.9 0.0 collective-permute-done.17.rest_3_
  95.9 0.0 copy-start.2
  95.9 2.7 %collective-permute-done.18.rest_4_ = bf16[256,256]{1,0:T(8,128)(2,1)S(1)} collective-permute-done((bf16[256,256]{1,0:T(8,128)(2,1)S(1)}, bf16[256,256]{1,0:T(8,128)(2,1)S(1)}, u32[]{:S(2)}, u32[]{:S(2)}) %collective-permute-start.18) | collective-permute-done | bytes 131104 | tf_op jit(solution)/shard_map/ppermute | solution.py:601
  98.6 1.9 %collective-permute-done.19.rest_5_ = bf16[256,256]{1,0:T(8,128)(2,1)S(1)} collective-permute-done((bf16[256,256]{1,0:T(8,128)(2,1)S(1)}, bf16[256,256]{1,0:T(8,128)(2,1)S(1)}, u32[]{:S(2)}, u32[]{:S(2)}) %collective-permute-start.19) | collective-permute-done | bytes 131104 | tf_op jit(solution)/shard_map/ppermute | solution.py:602
  100.5 0.0 copy-done.3
  100.5 0.6 copy-done.4
  101.2 3.7 %finish.5 = bf16[256,8192]{1,0:T(8,128)(2,1)} custom-call(s32[32,19]{1,0:T(8,128)} %constant.24.clone.table, bf16[256,1024]{1,0:T(8,128)(2,1)S(1)} %mask_rows.1.cot, bf16[256,128]{1,0:T(8,128)(2,1)S(1)} %get-tuple-element.80.g, bf16[16,144,128]{2,1,0:T(8,128)(2,1)S(1)} %all-to-all-done.recv, ...), custom_call_target="tpu_custom_call", output_to_operand_aliasing={{}: (10, {})} | custom-call | flops 1 | bytes 1 | tf_op jit(solution)/shard_map/finish/pallas_call | solution.py:531
  (4 shorter events, 0.0 us)
Async XLA Ops:
  0.6 4.3 %collective-permute-start = (bf16[512,1024]{1,0:T(8,128)(2,1)}, bf16[512,1024]{1,0:T(8,128)(2,1)S(1)}, u32[]{:S(2)}, u32[]{:S(2)}) collective-permute-start(bf16[512,1024]{1,0:T(8,128)(2,1)} %rest_0_.1), channel_id=1, source_target_pairs={{0,1},{1,0},{2,3},{3,2},{4,5},{5,4},{6,7},{7,6},{8,9},{9,8},{10,11... | collective-permute-start | bytes 3145736 | tf_op jit(solution)/shard_map/ppermute | solution.py:605
  2.3 15.2 %collective-permute-start.3 = (bf16[256,1024]{1,0:T(8,128)(2,1)S(1)}, bf16[256,1024]{1,0:T(8,128)(2,1)S(1)}, u32[]{:S(2)}, u32[]{:S(2)}) collective-permute-start(bf16[256,1024]{1,0:T(8,128)(2,1)S(1)} %mask_rows.1.cot), channel_id=1, source_target_pairs={{0,16},{16,0},{1,17},{17,1},{2,18},{18,2},{3,19},{19,3},{4,20},{20... | collective-permute-start | bytes 1572872 | tf_op jit(solution)/shard_map/ppermute | solution.py:608
  4.9 2.6 %copy-start = (bf16[512,1024]{1,0:T(8,128)(2,1)}, bf16[512,1024]{1,0:T(8,128)(2,1)S(1)}, u32[]{:S(2)}) copy-start(bf16[512,1024]{1,0:T(8,128)(2,1)S(1)} %collective-permute-done.other.rest_1_) | copy-start | bytes 3145732
  7.5 16.3 %collective-permute-start.1 = (bf16[512,1024]{1,0:T(8,128)(2,1)}, bf16[512,1024]{1,0:T(8,128)(2,1)}, u32[]{:S(2)}, u32[]{:S(2)}) collective-permute-start(bf16[512,1024]{1,0:T(8,128)(2,1)} %pick.1), channel_id=1, source_target_pairs={{0,4},{1,3},{2,0},{3,7},{4,8},{5,1},{6,2},{7,11},{8,12},{9,5},{10,... | collective-permute-start | bytes 3145736 | tf_op jit(solution)/shard_map/ppermute | solution.py:619
  9.2 14.5 %collective-permute-start.2 = (bf16[256,1024]{1,0:T(8,128)(2,1)S(1)}, bf16[256,1024]{1,0:T(8,128)(2,1)S(1)}, u32[]{:S(2)}, u32[]{:S(2)}) collective-permute-start(bf16[256,1024]{1,0:T(8,128)(2,1)S(1)} %mask_rows.1.cot), channel_id=1, source_target_pairs={{0,1},{1,0},{2,3},{3,2},{4,5},{5,4},{6,7},{7,6},{8,9},{9,8},{10,11... | collective-permute-start | bytes 1572872 | tf_op jit(solution)/shard_map/ppermute | solution.py:607
  17.5 6.3 %collective-permute-start.4 = (bf16[256,1024]{1,0:T(8,128)(2,1)S(1)}, bf16[256,1024]{1,0:T(8,128)(2,1)S(1)}, u32[]{:S(2)}, u32[]{:S(2)}) collective-permute-start(bf16[256,1024]{1,0:T(8,128)(2,1)S(1)} %collective-permute-done.3.refs_1_), channel_id=1, source_target_pairs={{0,1},{1,0},{2,3},{3,2},{4,5},{5,4},{6,7},{7,6},{8,9},{9,8},{10,11... | collective-permute-start | bytes 1572872 | tf_op jit(solution)/shard_map/ppermute | solution.py:616
  17.9 21.6 %all-to-all-start = ((bf16[16,144,128]{2,1,0:T(8,128)(2,1)}), bf16[16,144,128]{2,1,0:T(8,128)(2,1)S(1)}, u32[]{:S(2)}, u32[]{:S(2)}) async-start(bf16[16,144,128]{2,1,0:T(8,128)(2,1)} %gather_rows.1), calls=%async_computation | async-start | bytes 1179648 | tf_op jit(solution)/shard_map/all_to_all | solution.py:614
  23.8 21.9 %collective-permute-start.5 = (bf16[512,1024]{1,0:T(8,128)(2,1)}, bf16[512,1024]{1,0:T(8,128)(2,1)}, u32[]{:S(2)}, u32[]{:S(2)}) collective-permute-start(bf16[512,1024]{1,0:T(8,128)(2,1)} %collective-permute-done.1.refs_3_.rest_2_), channel_id=1, source_target_pairs={{0,4},{1,3},{2,0},{3,7},{4,8},{5,1},{6,2},{7,11},{8,12},{9,5},{10,... | collective-permute-start | bytes 3145736 | tf_op jit(solution)/shard_map/ppermute | solution.py:635
  29.1 15.9 %collective-permute-start.6 = (bf16[256,512]{1,0:T(8,128)(2,1)S(1)}, bf16[256,512]{1,0:T(8,128)(2,1)}, u32[]{:S(2)}, u32[]{:S(2)}) collective-permute-start(bf16[256,512]{1,0:T(8,128)(2,1)S(1)} %get-tuple-element.51._), channel_id=1, source_target_pairs={{0,1},{1,0},{2,3},{3,2},{4,5},{5,4},{6,7},{7,6},{8,9},{9,8},{10,11... | collective-permute-start | bytes 786440 | tf_op jit(solution)/shard_map/ppermute | solution.py:600
  29.1 15.8 %collective-permute-start.7 = (bf16[256,512]{1,0:T(8,128)(2,1)S(1)}, bf16[256,512]{1,0:T(8,128)(2,1)}, u32[]{:S(2)}, u32[]{:S(2)}) collective-permute-start(bf16[256,512]{1,0:T(8,128)(2,1)S(1)} %get-tuple-element.57), channel_id=1, source_target_pairs={{0,16},{16,0},{1,17},{17,1},{2,18},{18,2},{3,19},{19,3},{4,20},{20... | collective-permute-start | bytes 786440 | tf_op jit(solution)/shard_map/ppermute | solution.py:601
  30.7 14.2 %collective-permute-start.8 = (bf16[256,512]{1,0:T(8,128)(2,1)S(1)}, bf16[256,512]{1,0:T(8,128)(2,1)}, u32[]{:S(2)}, u32[]{:S(2)}) collective-permute-start(bf16[256,512]{1,0:T(8,128)(2,1)S(1)} %get-tuple-element.58), channel_id=1, source_target_pairs={{0,17},{1,16},{2,19},{3,18},{4,21},{5,20},{6,23},{7,22},{8,25},{9,... | collective-permute-start | bytes 786440 | tf_op jit(solution)/shard_map/ppermute | solution.py:602
  44.1 0.8 copy-start.1
  45.7 27.7 %collective-permute-start.9 = (bf16[512,1024]{1,0:T(8,128)(2,1)}, bf16[512,1024]{1,0:T(8,128)(2,1)}, u32[]{:S(2)}, u32[]{:S(2)}) collective-permute-start(bf16[512,1024]{1,0:T(8,128)(2,1)} %collective-permute-done.5.refs_3_.rest_3_), channel_id=1, source_target_pairs={{0,4},{1,3},{2,0},{3,7},{4,8},{5,1},{6,2},{7,11},{8,12},{9,5},{10,... | collective-permute-start | bytes 3145736 | tf_op jit(solution)/shard_map/ppermute | solution.py:635
  50.6 32.1 %all-to-all-start.1 = ((bf16[16,144,128]{2,1,0:T(8,128)(2,1)}), bf16[16,144,128]{2,1,0:T(8,128)(2,1)S(1)}, u32[]{:S(2)}, u32[]{:S(2)}) async-start(bf16[16,144,128]{2,1,0:T(8,128)(2,1)} %copy-done.1), calls=%async_computation.1 | async-start | bytes 1179648 | tf_op jit(solution)/shard_map/all_to_all | solution.py:628
  59.5 7.7 %collective-permute-start.10 = (bf16[256,512]{1,0:T(8,128)(2,1)}, bf16[256,512]{1,0:T(8,128)(2,1)}, u32[]{:S(2)}, u32[]{:S(2)}) collective-permute-start(bf16[256,512]{1,0:T(8,128)(2,1)} %get-tuple-element.60), channel_id=1, source_target_pairs={{0,1},{1,0},{2,3},{3,2},{4,5},{5,4},{6,7},{7,6},{8,9},{9,8},{10,11... | collective-permute-start | bytes 786440 | tf_op jit(solution)/shard_map/ppermute | solution.py:600
  59.9 9.5 %collective-permute-start.11 = (bf16[256,512]{1,0:T(8,128)(2,1)}, bf16[256,512]{1,0:T(8,128)(2,1)}, u32[]{:S(2)}, u32[]{:S(2)}) collective-permute-start(bf16[256,512]{1,0:T(8,128)(2,1)} %get-tuple-element.65), channel_id=1, source_target_pairs={{0,16},{16,0},{1,17},{17,1},{2,18},{18,2},{3,19},{19,3},{4,20},{20... | collective-permute-start | bytes 786440 | tf_op jit(solution)/shard_map/ppermute | solution.py:601
  61.5 11.9 %collective-permute-start.12 = (bf16[256,512]{1,0:T(8,128)(2,1)}, bf16[256,512]{1,0:T(8,128)(2,1)}, u32[]{:S(2)}, u32[]{:S(2)}) collective-permute-start(bf16[256,512]{1,0:T(8,128)(2,1)} %get-tuple-element.66), channel_id=1, source_target_pairs={{0,17},{1,16},{2,19},{3,18},{4,21},{5,20},{6,23},{7,22},{8,25},{9,... | collective-permute-start | bytes 786440 | tf_op jit(solution)/shard_map/ppermute | solution.py:602
  75.2 11.4 %collective-permute-start.13 = (bf16[256,1024]{1,0:T(8,128)(2,1)}, bf16[256,1024]{1,0:T(8,128)(2,1)}, u32[]{:S(2)}, u32[]{:S(2)}) collective-permute-start(bf16[256,1024]{1,0:T(8,128)(2,1)} %constant_dynamic-slice_fusion), channel_id=1, source_target_pairs={{0,4},{1,3},{2,0},{3,7},{4,8},{5,1},{6,2},{7,11},{8,12},{9,5},{10,... | collective-permute-start | bytes 1572872 | tf_op jit(solution)/shard_map/ppermute | solution.py:635
  80.7 10.6 %collective-permute-start.14 = (bf16[256,512]{1,0:T(8,128)(2,1)}, bf16[256,512]{1,0:T(8,128)(2,1)}, u32[]{:S(2)}, u32[]{:S(2)}) collective-permute-start(bf16[256,512]{1,0:T(8,128)(2,1)} %get-tuple-element.69), channel_id=1, source_target_pairs={{0,1},{1,0},{2,3},{3,2},{4,5},{5,4},{6,7},{7,6},{8,9},{9,8},{10,11... | collective-permute-start | bytes 786440 | tf_op jit(solution)/shard_map/ppermute | solution.py:600
  80.9 15.0 %collective-permute-start.15 = (bf16[256,512]{1,0:T(8,128)(2,1)}, bf16[256,512]{1,0:T(8,128)(2,1)}, u32[]{:S(2)}, u32[]{:S(2)}) collective-permute-start(bf16[256,512]{1,0:T(8,128)(2,1)} %get-tuple-element.70), channel_id=1, source_target_pairs={{0,16},{16,0},{1,17},{17,1},{2,18},{18,2},{3,19},{19,3},{4,20},{20... | collective-permute-start | bytes 786440 | tf_op jit(solution)/shard_map/ppermute | solution.py:601
  82.4 13.5 %collective-permute-start.16 = (bf16[256,512]{1,0:T(8,128)(2,1)}, bf16[256,512]{1,0:T(8,128)(2,1)}, u32[]{:S(2)}, u32[]{:S(2)}) collective-permute-start(bf16[256,512]{1,0:T(8,128)(2,1)} %get-tuple-element.71), channel_id=1, source_target_pairs={{0,17},{1,16},{2,19},{3,18},{4,21},{5,20},{6,23},{7,22},{8,25},{9,... | collective-permute-start | bytes 786440 | tf_op jit(solution)/shard_map/ppermute | solution.py:602
  89.4 6.5 %collective-permute-start.17 = (bf16[256,256]{1,0:T(8,128)(2,1)S(1)}, bf16[256,256]{1,0:T(8,128)(2,1)S(1)}, u32[]{:S(2)}, u32[]{:S(2)}) collective-permute-start(bf16[256,256]{1,0:T(8,128)(2,1)S(1)} %get-tuple-element.77), channel_id=1, source_target_pairs={{0,1},{1,0},{2,3},{3,2},{4,5},{5,4},{6,7},{7,6},{8,9},{9,8},{10,11... | collective-permute-start | bytes 393224 | tf_op jit(solution)/shard_map/ppermute | solution.py:600
  89.9 8.8 %collective-permute-start.18 = (bf16[256,256]{1,0:T(8,128)(2,1)S(1)}, bf16[256,256]{1,0:T(8,128)(2,1)S(1)}, u32[]{:S(2)}, u32[]{:S(2)}) collective-permute-start(bf16[256,256]{1,0:T(8,128)(2,1)S(1)} %get-tuple-element.78), channel_id=1, source_target_pairs={{0,16},{16,0},{1,17},{17,1},{2,18},{18,2},{3,19},{19,3},{4,20},{20... | collective-permute-start | bytes 393224 | tf_op jit(solution)/shard_map/ppermute | solution.py:601
  91.3 9.2 %collective-permute-start.19 = (bf16[256,256]{1,0:T(8,128)(2,1)S(1)}, bf16[256,256]{1,0:T(8,128)(2,1)S(1)}, u32[]{:S(2)}, u32[]{:S(2)}) collective-permute-start(bf16[256,256]{1,0:T(8,128)(2,1)S(1)} %get-tuple-element.79), channel_id=1, source_target_pairs={{0,17},{1,16},{2,19},{3,18},{4,21},{5,20},{6,23},{7,22},{8,25},{9,... | collective-permute-start | bytes 393224 | tf_op jit(solution)/shard_map/ppermute | solution.py:602
  95.9 4.6 %copy-start.2 = (bf16[256,256]{1,0:T(8,128)(2,1)}, bf16[256,256]{1,0:T(8,128)(2,1)S(1)}, u32[]{:S(2)}) copy-start(bf16[256,256]{1,0:T(8,128)(2,1)S(1)} %collective-permute-done.17.rest_3_) | copy-start | bytes 393220
  98.6 1.9 %copy-start.3 = (bf16[256,256]{1,0:T(8,128)(2,1)}, bf16[256,256]{1,0:T(8,128)(2,1)S(1)}, u32[]{:S(2)}) copy-start(bf16[256,256]{1,0:T(8,128)(2,1)S(1)} %collective-permute-done.18.rest_4_) | copy-start | bytes 393220
  100.5 0.6 copy-start.4

commit v5 on v4

--- a/solution.py
+++ b/solution.py
@@ -2,7 +2,6 @@
 
 import jax
 import jax.numpy as jnp
-import numpy as np
 from jax import lax
 from jax.experimental import pallas as pl
 from jax.experimental.pallas import tpu as pltpu
@@ -20,6 +19,7 @@
 IN_SMEM = pl.BlockSpec(memory_space=pltpu.SMEM)
 IN_HBM = pl.BlockSpec(memory_space=pltpu.HBM)
 SMALL = pl.CostEstimate(flops=1, bytes_accessed=1, transcendentals=0)
+LONGER = pl.CostEstimate(flops=5_000_000_000, bytes_accessed=1, transcendentals=0)
 
 adapter_scale = 2.0
 
@@ -33,8 +33,30 @@
     return pltpu.with_memory_space_constraint(value, pltpu.HBM)
 
 
-def table_row(table):
-    return lax.axis_index("parts") * (table.shape[0] // 2) + lax.axis_index("fsdp")
+def as_it_is(value):
+    return value
+
+
+def column_blocks(devices):
+    index, part = lax.axis_index("fsdp"), lax.axis_index("parts")
+    chips = devices // 2
+    chip, core = lax.div(index, 2), lax.rem(index, 2)
+    way = 2 * core - 1
+    odd = lax.rem(chip, 2) == 1
+    place = jnp.where(odd, chips - lax.div(chip + 1, 2), lax.div(chip, 2))
+
+    def at(steps):
+        position = lax.rem(place + steps + chips, chips)
+        return jnp.where(position < chips // 2, 2 * position, 2 * (chips - position) - 1)
+
+    blocks = [index, index + 1 - 2 * core]
+    for step in range(1, chips // 2):
+        near, far = at(way * step), at(-way * step)
+        blocks += [2 * near + part, 2 * far + part, 2 * near + 1 - part, 2 * far + 1 - part]
+    last = at(chips // 2)
+    for p in (part, 1 - part):
+        blocks += [2 * (2 * last + p) + core, 2 * (2 * last + p) + 1 - core]
+    return blocks
 
 
 def iota(shape, axis):
@@ -59,8 +81,8 @@
     return jnp.concatenate(parts, axis=-1)
 
 
-def mask_kernel(table, live, cot, out):
-    first = table[table_row(table), 0]
+def mask_kernel(live, cot, out):
+    first = lax.axis_index("fsdp") * (cot.shape[0] // BLOCK)
     row = iota((BLOCK, cot.shape[1]), 0)
     for k in range(cot.shape[0] // BLOCK):
         rows = slice(k * BLOCK, (k + 1) * BLOCK)
@@ -68,22 +90,21 @@
         out[rows, :] = jnp.where(row < live[first + k], value, 0.0).astype(out.dtype)
 
 
-def mask_rows(table, block_live_rows, cotangent):
+def mask_rows(block_live_rows, cotangent):
     return pl.pallas_call(
         mask_kernel,
-        in_specs=[IN_SMEM, IN_SMEM, IN_VMEM],
+        in_specs=[IN_SMEM, IN_VMEM],
         out_specs=IN_VMEM,
         out_shape=jax.ShapeDtypeStruct(cotangent.shape, cotangent.dtype),
         compiler_params=PARAMS,
         cost_estimate=SMALL,
         name="mask_rows",
-    )(in_hbm(table), in_hbm(block_live_rows), in_hbm(cotangent))
-
-
-def rank_major_order(transposed):
+    )(in_hbm(block_live_rows), in_hbm(cotangent))
+
+
+def rank_major_order():
     shape = (8 * LANES, 8 * LANES)
-    near, far = (1, 0) if transposed else (0, 1)
-    a, b = iota(shape, near), iota(shape, far)
+    a, b = iota(shape, 0), iota(shape, 1)
     return ((a % LANES) * 8 + a // LANES == b).astype(jnp.bfloat16)
 
 
@@ -101,26 +122,25 @@
         start = pl.multiple_of((slot // group) * group, group)
         return (
             slot % group,
+            start,
             pltpu.make_async_copy(down.at[pl.ds(start, group), :], dbuf.at[b], dsem.at[b]),
-            pltpu.make_async_copy(up.at[pl.ds(start, group), :], ubuf.at[b], usem.at[b]),
         )
 
     def begin(b, carry):
-        _, first, second = copies(b)
-        first.start()
-        second.start()
+        copies(b)[2].start()
         return carry
 
+    ups = pltpu.make_async_copy(up, ubuf, usem)
+    ups.start()
     lax.fori_loop(0, blocks, begin, 0)
-    order = rank_major_order(False)
+    order = rank_major_order()
 
     def one(j, carry):
         wide, narrow = [], []
         for k in range(2):
             b = 2 * j + k
-            row, first, second = copies(b)
-            first.wait()
-            second.wait()
+            row, start, copy = copies(b)
+            copy.wait()
             late = row >= 8
             line = row % 8
             value = dbuf[b].astype(jnp.float32)
@@ -128,7 +148,7 @@
             for t in range(per_down):
                 dscr[k, 8 * t : 8 * t + 8, :] = value[:, t * LANES : (t + 1) * LANES]
             wide.append(dscr[k, pl.ds(line, per_down, stride=8), :])
-            value = ubuf[b].astype(jnp.float32)
+            value = ubuf[pl.ds(start, group), :].astype(jnp.float32)
             value = jnp.where(late, value[8:], value[:8])
             for t in range(per_up):
                 uscr[k, 8 * t : 8 * t + 8, :] = value[:, t * LANES : (t + 1) * LANES]
@@ -141,15 +161,25 @@
         payload[j, down_rows:, :] = jnp.concatenate(narrow, axis=0).astype(payload.dtype)
         return carry
 
-    lax.fori_loop(0, devices, one, 0)
-    value = dot_n(cols[...], order).astype(payload.dtype).reshape(devices, ADAPTER_RANK, 8 * LANES)
-    for q in range(8):
-        payload[:, q * ADAPTER_RANK : (q + 1) * ADAPTER_RANK, :] = value[
-            :, :, q * LANES : (q + 1) * LANES
-        ]
-    copy = pltpu.make_async_copy(payload, result, rsem)
-    copy.start()
-    copy.wait()
+    ups.wait()
+    stores = []
+    parts = 2
+    count = devices // parts
+    for h in range(parts):
+        lax.fori_loop(h * count, h * count + count, one, 0)
+        rows = slice(h * count * ADAPTER_RANK, (h + 1) * count * ADAPTER_RANK)
+        value = dot_n(cols[rows, :], order).astype(payload.dtype)
+        value = value.reshape(count, ADAPTER_RANK, 8 * LANES)
+        here = slice(h * count, h * count + count)
+        for q in range(8):
+            payload[here, q * ADAPTER_RANK : (q + 1) * ADAPTER_RANK, :] = value[
+                :, :, q * LANES : (q + 1) * LANES
+            ]
+        part = pl.ds(h * count, count)
+        stores.append(pltpu.make_async_copy(payload.at[part], result.at[part], rsem.at[h]))
+        stores[-1].start()
+    for copy in stores:
+        copy.wait()
 
 
 def gather_rows(padded_block_adapter, adapter_storage_row, down, up, devices):
@@ -165,14 +195,14 @@
         out_shape=jax.ShapeDtypeStruct(shape, jnp.bfloat16),
         scratch_shapes=[
             pltpu.VMEM((blocks, group, down.shape[1]), down.dtype),
-            pltpu.VMEM((blocks, group, up.shape[1]), up.dtype),
+            pltpu.VMEM(up.shape, up.dtype),
             pltpu.VMEM((2, 8 * per_down, LANES), jnp.float32),
             pltpu.VMEM((2, 8 * per_up, LANES), jnp.float32),
             pltpu.VMEM((devices * ADAPTER_RANK, 8 * LANES), jnp.bfloat16),
             pltpu.VMEM(shape, jnp.bfloat16),
             pltpu.SemaphoreType.DMA((blocks,)),
-            pltpu.SemaphoreType.DMA((blocks,)),
             pltpu.SemaphoreType.DMA,
+            pltpu.SemaphoreType.DMA((2,)),
         ],
         compiler_params=WIDE_PARAMS,
         cost_estimate=SMALL,
@@ -210,6 +240,7 @@
             part = dot_t(m[:, t * LANES : (t + 1) * LANES], b_flat)
             total = total + jnp.where(lane % tiles == t, part, 0.0)
         g = dot_n(total, gather_rank, lax.Precision.HIGHEST).astype(jnp.bfloat16)
+        g = (adapter_scale * g.astype(jnp.float32)).astype(jnp.bfloat16)
         g_out[k * BLOCK : (k + 1) * BLOCK, :] = g
         turned.append(g.astype(jnp.float32).T[:ADAPTER_RANK, :].astype(jnp.bfloat16))
 
@@ -225,7 +256,7 @@
             ]
             a = lane_cat([recv[j, at : at + ADAPTER_RANK, :] for j, at in spots])
             lows[k] = lows[k] + dot_t(part, a)
-            grad = (adapter_scale * dot_n(turned[k], part)).astype(sent.dtype)
+            grad = dot_n(turned[k], part).astype(sent.dtype)
             for tile, (j, at) in enumerate(spots):
                 sent[j, at : at + ADAPTER_RANK, :] = grad[:, tile * LANES : (tile + 1) * LANES]
         part = (pl.ds(i * here, here), pl.ds(0, down_rows), slice(None))
@@ -260,7 +291,7 @@
         in_specs=[IN_HBM, IN_VMEM, IN_VMEM],
         out_specs=[IN_HBM, IN_VMEM],
         out_shape=[
-            jax.ShapeDtypeStruct(recv.shape, jnp.bfloat16),
+            pltpu.HBM(recv.shape, jnp.bfloat16),
             jax.ShapeDtypeStruct((rows, LANES), jnp.bfloat16),
         ],
         scratch_shapes=[
@@ -307,7 +338,7 @@
         compiler_params=PARAMS,
         cost_estimate=SMALL,
         name="zero_grads",
-    )(earlier)
+    )(in_hbm(earlier))
 
 
 def scatter_kernel(
@@ -326,18 +357,59 @@
     lax.fori_loop(0, blocks, mark, 0)
     dacc[...] = jnp.zeros_like(dacc)
     uacc[...] = jnp.zeros_like(uacc)
-    value = lane_cat([recv[:, q * ADAPTER_RANK : (q + 1) * ADAPTER_RANK, :] for q in range(8)])
-    value = dot_n(value.reshape(devices * ADAPTER_RANK, 8 * LANES), rank_major_order(True))
+    count = 8 * per_down
+    a, b = iota((count, count), 0), iota((count, count), 1)
+    order = ((b % per_down) * 8 + b // per_down == a).astype(jnp.bfloat16)
+    values = []
+    for k in range(2):
+        tiles = [
+            recv[:, q * ADAPTER_RANK : (q + 1) * ADAPTER_RANK, :] for q in range(4 * k, 4 * k + 4)
+        ]
+        values.append(dot_n(lane_cat(tiles).reshape(devices * ADAPTER_RANK, count), order))
+    lower = iota((ADAPTER_RANK, LANES), 1) < per_down
     for j in range(devices):
-        part = value[j * ADAPTER_RANK : (j + 1) * ADAPTER_RANK, :]
-        turned = jnp.concatenate(
-            [part[:, lo * LANES : (lo + 1) * LANES] for lo in range(8)], axis=0
-        ).T
+        rows = []
+        for t in range(4):
+            first, second = [
+                value[j * ADAPTER_RANK : (j + 1) * ADAPTER_RANK, t * LANES : (t + 1) * LANES]
+                for value in values
+            ]
+            rows.append(jnp.where(lower, first, pltpu.roll(second, per_down, 1)))
+            rows.append(jnp.where(lower, pltpu.roll(first, per_down, 1), second))
+        turned = jnp.concatenate(rows, axis=0).T
         narrow = recv[j, down_rows:, :].astype(jnp.float32)
         for k in range(2):
             first = table[storage[adapter[2 * j + k]]]
             dacc[first] += turned[k * per_down : (k + 1) * per_down, :]
             uacc[first] += narrow[k * per_up : (k + 1) * per_up, :]
+    def copies(b):
+        slot = storage[adapter[b]]
+        return (
+            table[slot] == b,
+            pltpu.make_async_copy(drow.at[pl.ds(b, 1), :], down.at[pl.ds(slot, 1), :], dsem.at[b]),
+            pltpu.make_async_copy(urow.at[pl.ds(b, 1), :], up.at[pl.ds(slot, 1), :], usem.at[b]),
+        )
+
+    def begin(b, carry):
+        mine, first, second = copies(b)
+
+        @pl.when(mine)
+        def _():
+            first.start()
+            second.start()
+
+        return carry
+
+    def end(b, carry):
+        mine, first, second = copies(b)
+
+        @pl.when(mine)
+        def _():
+            first.wait()
+            second.wait()
+
+        return carry
+
     for g in range(blocks // 8):
         for i in range(8):
             dscr[pl.ds(i, per_down, stride=8), :] = dacc[8 * g + i]
@@ -346,36 +418,7 @@
             drow[8 * g : 8 * g + 8, t * LANES : (t + 1) * LANES] = dscr[8 * t : 8 * t + 8, :]
         for t in range(per_up):
             urow[8 * g : 8 * g + 8, t * LANES : (t + 1) * LANES] = uscr[8 * t : 8 * t + 8, :]
-
-    def copies(b):
-        slot = storage[adapter[b]]
-        return (
-            table[slot] == b,
-            pltpu.make_async_copy(drow.at[pl.ds(b, 1), :], down.at[pl.ds(slot, 1), :], dsem.at[b]),
-            pltpu.make_async_copy(urow.at[pl.ds(b, 1), :], up.at[pl.ds(slot, 1), :], usem.at[b]),
-        )
-
-    def begin(b, carry):
-        mine, first, second = copies(b)
-
-        @pl.when(mine)
-        def _():
-            first.start()
-            second.start()
-
-        return carry
-
-    def end(b, carry):
-        mine, first, second = copies(b)
-
-        @pl.when(mine)
-        def _():
-            first.wait()
-            second.wait()
-
-        return carry
-
-    lax.fori_loop(0, blocks, begin, 0)
+        lax.fori_loop(8 * g, 8 * g + 8, begin, 0)
     lax.fori_loop(0, blocks, end, 0)
 
 
@@ -437,9 +480,9 @@
     )(in_hbm(own), other)
 
 
-def far_kernel(count, *refs):
+def far_kernel(count, handed, *refs):
     cots, weight, outs = refs[:count], refs[count], refs[count + 1 : 2 * count + 1]
-    wbuf, buffer, wsem, sems = refs[2 * count + 1 :]
+    wbuf, buffer, wsem, sems, hsem = refs[2 * count + 1 + handed :]
     tile = wbuf.shape[1]
     loads = [
         pltpu.make_async_copy(weight.at[i * tile : (i + 1) * tile, :], wbuf.at[i], wsem.at[i])
@@ -455,40 +498,47 @@
             buffer[n, :, i * tile : (i + 1) * tile] = value
             if i == len(loads) - 1:
                 stores[n].start()
+    if handed:
+        core = lax.axis_index("fsdp") % 2
+        copy = pltpu.make_async_copy(wbuf.at[core], refs[2 * count + 1], hsem)
+        copy.start()
+        copy.wait()
     for copy in stores:
         copy.wait()
 
 
-def far_products(cots, weight):
+def far_products(cots, weight, pin=in_hbm, handed=False):
     count, rows, tile = len(cots), cots[0].shape[0], 256
     span, depth = weight.shape
-    shape = jax.ShapeDtypeStruct((rows, span), jnp.bfloat16)
+    shape = pltpu.HBM((rows, span), jnp.bfloat16)
+    half = [pltpu.HBM((tile, depth), weight.dtype)] if handed else []
     return pl.pallas_call(
-        functools.partial(far_kernel, count),
+        functools.partial(far_kernel, count, len(half)),
         in_specs=[IN_VMEM] * count + [pl.BlockSpec(memory_space=pl.ANY)],
-        out_specs=[IN_HBM] * count,
-        out_shape=[shape] * count,
+        out_specs=[IN_HBM] * (count + len(half)),
+        out_shape=[shape] * count + half,
         scratch_shapes=[
             pltpu.VMEM((span // tile, tile, depth), weight.dtype),
             pltpu.VMEM((count, rows, span), jnp.bfloat16),
             pltpu.SemaphoreType.DMA((span // tile,)),
             pltpu.SemaphoreType.DMA((count,)),
+            pltpu.SemaphoreType.DMA,
         ],
         compiler_params=PARAMS,
         cost_estimate=SMALL,
         name="far_products",
-    )(*cots, in_hbm(weight))
-
-
-def finish(table, at, cot, weights, received, g, recv, out, width, columns):
+    )(*cots, pin(weight))
+
+
+def finish(devices, at, cot, weights, received, g, recv, out, width, columns, pin=in_hbm, cost=SMALL):
     rows = cot.shape[0]
     spans = [w.shape[0] for w in weights] + [r.shape[1] for r in received]
     count = len(spans)
-    sources = [in_hbm(source) for source in (*weights, *received)]
+    sources = [pin(source) for source in (*weights, *received)]
     per = columns // LANES
 
-    def kernel(table, cot, g, recv, *rest):
-        mine = table_row(table)
+    def kernel(cot, g, recv, *rest):
+        where = column_blocks(devices)
         given = rest[:count]
         result = rest[-4 - count]
         buffer, sems, loaded = rest[-3 - count], rest[-2 - count], rest[-1 - count : -1]
@@ -500,7 +550,7 @@
             load.start()
         copies = []
         for i in range(count):
-            index, span = table[mine, at[i]], spans[i]
+            index, span = where[at[i]], spans[i]
             per_device = columns // span
             device, inner = index // per_device, (index % per_device) * (span // LANES)
             parts = []
@@ -511,7 +561,7 @@
                     tiles.append(recv[device, pl.ds(first, ADAPTER_RANK), :])
                 ours = g[k * BLOCK : (k + 1) * BLOCK, :ADAPTER_RANK]
                 parts.append(dot_n(ours, lane_cat(tiles)))
-            value = adapter_scale * jnp.concatenate(parts, axis=0)
+            value = jnp.concatenate(parts, axis=0)
             loads[i].wait()
             if i < len(weights):
                 value = value + dot_t(cot[...], loaded[i][...])
@@ -530,13 +580,12 @@
 
     return pl.pallas_call(
         kernel,
-        in_specs=[IN_SMEM]
-        + [IN_VMEM] * 3
+        in_specs=[IN_VMEM] * 3
         + [pl.BlockSpec(memory_space=pl.ANY)] * count
         + ([] if out is None else [IN_HBM]),
         out_specs=IN_HBM,
         out_shape=jax.ShapeDtypeStruct((rows, width), jnp.bfloat16),
-        input_output_aliases={} if out is None else {4 + count: 0},
+        input_output_aliases={} if out is None else {3 + count: 0},
         scratch_shapes=[
             pltpu.VMEM((count, rows, max(spans)), jnp.bfloat16),
             pltpu.SemaphoreType.DMA((count,)),
@@ -544,12 +593,12 @@
         + [pltpu.VMEM(source.shape, source.dtype) for source in sources]
         + [pltpu.SemaphoreType.DMA((count,))],
         compiler_params=WIDE_PARAMS,
-        cost_estimate=SMALL,
+        cost_estimate=cost,
         name="finish",
-    )(in_hbm(table), cot, g, recv, *sources, *([] if out is None else [out]))
-
-
-def ring_table(devices):
+    )(cot, g, recv, *sources, *([] if out is None else [out]))
+
+
+def ring_pairs(devices):
     chips = devices // 2
     order = list(range(0, chips, 2)) + list(range(chips - 1, 0, -2))
     place = {c: i for i, c in enumerate(order)}
@@ -557,20 +606,7 @@
     for c in range(chips):
         ring.append((2 * c, 2 * order[(place[c] + 1) % chips]))
         ring.append((2 * c + 1, 2 * order[(place[c] - 1) % chips] + 1))
-    table = []
-    for part in range(2):
-        for index in range(devices):
-            chip, core = index // 2, index % 2
-            way = 2 * core - 1
-            row = [2 * index, index, index ^ 1]
-            for step in range(1, chips // 2):
-                near, far = [order[(place[chip] + sign * way * step) % chips] for sign in (1, -1)]
-                row += [2 * near + part, 2 * far + part, 2 * near + 1 - part, 2 * far + 1 - part]
-            last = order[(place[chip] + chips // 2) % chips]
-            for p in (part, 1 - part):
-                row += [2 * (2 * last + p) + core, 2 * (2 * last + p) + 1 - core]
-            table.append(row)
-    return ring, np.array(table, np.int32)
+    return ring
 
 
 def ring_body(
@@ -588,9 +624,7 @@
     steps = devices // 4
     shard = frozen_value_weight.shape[0]
     width = inputs.shape[1]
-    core = lax.axis_index("fsdp") % 2
-    ring, table = ring_table(devices)
-    table = jnp.asarray(table)
+    ring = ring_pairs(devices)
     cores = [(i, i ^ 1) for i in range(devices)]
     across = [(0, 1), (1, 0)]
     diagonal = [(p * devices + i, (1 - p) * devices + (i ^ 1)) for p in range(2) for i in range(devices)]
@@ -603,7 +637,7 @@
         )
 
     other_shard = lax.ppermute(frozen_value_weight, "fsdp", cores)
-    masked = mask_rows(table, block_live_rows, cotangent)
+    masked = mask_rows(block_live_rows, cotangent)
     core_masked = lax.ppermute(masked, "fsdp", cores)
     far_masked = lax.ppermute(masked, "parts", across)
     travelling = pick(frozen_value_weight, other_shard)
@@ -618,45 +652,59 @@
 
     travelling = lax.ppermute(travelling, "fsdp", ring)
 
-    firsts = [3 + 4 * step for step in range(steps)]
+    firsts = [2 + 4 * step for step in range(steps)]
     pieces, received = [], []
     for step in range(steps):
         if step == 0:
             travelling, cots, _ = after(travelling, cots, payload)
         elif step == 1:
-            travelling, sent, grads, received[0] = after(travelling, sent, grads, received[0])
-            sums = lax.all_to_all(sent, "fsdp", split_axis=0, concat_axis=0, tiled=True)
-        elif step < steps - 1:
-            travelling, out, received[step - 1] = after(travelling, out, received[step - 1])
+            travelling, sent, out, grads, received[0] = after(
+                travelling, sent, out, grads, received[0]
+            )
         pieces.append(travelling)
-        if step < steps - 1:
-            if step == steps - 2:
-                travelling = lax.dynamic_slice_in_dim(travelling, core * (shard // 2), shard // 2)
+        if step < steps - 2:
             travelling = lax.ppermute(travelling, "fsdp", ring)
-        products = far_products(cots, pieces[step])
+        pin = as_it_is if step >= steps - 2 else in_hbm
+        products = far_products(cots, pieces[step], pin, step == steps - 2)
+        if step == steps - 2:
+            *products, travelling = products
+            travelling, products, out, received[-1] = after(
+                travelling, products, out, received[-1]
+            )
+            travelling = lax.ppermute(travelling, "fsdp", ring)
+        if step == steps - 1:
+            products, received[-1] = after(products, received[-1])
         received.append(cross(products))
         if step == 0:
             grads = zero_grads(products[0], adapter_down_weights.shape, adapter_up_weights.shape)
             recv, _ = after(recv, grads)
             sent, g = adapter_terms(inputs, masked, recv)
-        if step == steps - 2 - 1:
+            weights = (frozen_value_weight, other_shard)
+            out = finish(devices, [0, 1], masked, weights, (), g, recv, None, width, shard)
+        if step == steps - 3:
             cot, _ = after(masked, products[0])
-            weights = (frozen_value_weight, other_shard, *pieces)
-            at = [1, 2] + firsts[: step + 1] + [firsts[0] + i for i in range(1, 4)]
-            out = finish(table, at, cot, weights, received[0], g, recv, None, width, shard)
+            at = firsts[: step + 1] + [firsts[0] + i for i in range(1, 4)]
+            out = finish(devices, at, cot, pieces[:2], received[0], g, recv, out, width, shard)
+            sent, out = after(sent, out)
+            sums = lax.all_to_all(sent, "fsdp", split_axis=0, concat_axis=0, tiled=True)
+            travelling, out = after(travelling, out)
         if step == steps - 2:
-            sums, _ = after(sums, products)
-            down_grad, up_grad = scatter_rows(
-                padded_block_adapter, adapter_storage_row, sums, *grads
-            )
-            travelling, up_grad = after(travelling, up_grad)
-    g, _ = after(g, products)
-    at = firsts[-2:] + [first + i for first in firsts[1:-2] for i in range(1, 4)]
-    early = sum(received[1:-2], ())
-    out = finish(table, at, masked, pieces[-2:], early, g, recv, out, width, shard)
-    at = [first + i for first in firsts[-2:] for i in range(1, 4)]
-    late = sum(received[-2:], ())
-    out = finish(table, at, masked, (), late, g, recv, out, width, shard)
+            out, _ = after(out, products)
+            at = [firsts[step]] + [first + i for first in firsts[1:step] for i in range(1, 4)]
+            early = sum(received[1:step], ())
+            piece = pieces[step : step + 1]
+            out = finish(devices, at, masked, piece, early, g, recv, out, width, shard)
+            travelling, out = after(travelling, out)
+    at = firsts[-1:] + [firsts[-2] + i for i in range(1, 4)]
+    piece = pieces[-1:]
+    out = finish(
+        devices, at, masked, piece, received[-2], g, recv, out, width, shard, as_it_is, LONGER
+    )
+    sums, out = after(sums, out)
+    down_grad, up_grad = scatter_rows(padded_block_adapter, adapter_storage_row, sums, *grads)
+    out, up_grad = after(out, up_grad)
+    at = [firsts[-1] + i for i in range(1, 4)]
+    out = finish(devices, at, masked, (), received[-1], g, recv, out, width, shard, as_it_is)
     return (out, down_grad, up_grad)
 
 

time: 106 us -> 98 us (0.925)
  the two profiles are of different devices: /device:TPU:0 before, /device:TPU:13 now
where the time goes in v5:
time: 98 us; the launch traced here: 97.5 us
  Pallas kernels  50.4 us (51%)
  starting transfers between devices  31.6 us (32%)
  waiting for transfers between devices  14.2 us (14%)
  between operations  1.07 us (1%)
    pallas_call x5, Pallas kernels, finish(): pl.pallas_call(kernel, in_specs=[IN_VMEM] * 3 + [pl.BlockSpec(memory_spac...  13.3 us
    pallas_call x4, Pallas kernels, far_products(): pl.pallas_call(functools.partial(far_kernel, count, len(half)), in_specs=...  11.5 us
    ppermute x4, waiting for transfers between devices, ring_body(): travelling = lax.ppermute(travelling, 'fsdp', ring)  10.3 us
    pallas_call x1, Pallas kernels, gather_rows(): pl.pallas_call(gather_kernel, in_specs=[IN_SMEM, IN_SMEM, IN_HBM, IN_HBM]...  7.74 us
    pallas_call x1, Pallas kernels, zero_grads(): pl.pallas_call(zero_kernel, in_specs=[pl.BlockSpec(memory_space=pl.ANY)],...  6.7 us
    all_to_all x1, starting transfers between devices, ring_body(): lax.all_to_all(payload, 'fsdp', split_axis=0, concat_axis=0, tiled=True)  5.99 us
    ppermute x4, starting transfers between devices, ring_body(): travelling = lax.ppermute(travelling, 'fsdp', ring)  5.84 us
    all_to_all x1, starting transfers between devices, ring_body(): sums = lax.all_to_all(sent, 'fsdp', split_axis=0, concat_axis=0, tiled=True)  5.82 us
  transfers between devices with their start and end apart: 22, of which 6 were waited for; matrix products, arithmetic and copies ran while one was open for 0% of the time, Pallas kernels for 50%

profile of v5, /device:TPU:13, one launch (start us, length us, event | category | flops | bytes accessed | tf_op | source)
XLA Modules:
  0.0 97.5 jit_solution(5137089312023885715)
XLA Ops:
  0.6 0.7 collective-permute-start
  1.4 1.1 %mask_rows.1.cot = bf16[256,1024]{1,0:T(8,128)(2,1)S(1)} custom-call(s32[32]{0:T(128)} %live.1, bf16[256,1024]{1,0:T(8,128)(2,1)} %cot.1), custom_call_target="tpu_custom_call" | custom-call | flops 1 | bytes 1 | tf_op jit(solution)/shard_map/mask_rows/pallas_call | solution.py:94
  2.5 1.3 %collective-permute-start.3 = (bf16[256,1024]{1,0:T(8,128)(2,1)S(1)}, bf16[256,1024]{1,0:T(8,128)(2,1)S(1)}, u32[]{:S(2)}, u32[]{:S(2)}) collective-permute-start(bf16[256,1024]{1,0:T(8,128)(2,1)S(1)} %mask_rows.1.cot), channel_id=1, source_target_pairs={{0,16},{16,0},{1,17},{17,1},{2,18},{18,2},{3,19},{19,3},{4,20},{20... | collective-permute-start | bytes 1572872 | tf_op jit(solution)/shard_map/ppermute | solution.py:642
  3.8 0.1 collective-permute-done.other.rest_1_
  3.9 1.1 %pick.1 = bf16[512,1024]{1,0:T(8,128)(2,1)} custom-call(bf16[512,1024]{1,0:T(8,128)(2,1)} %rest_0_.1, bf16[512,1024]{1,0:T(8,128)(2,1)S(1)} %collective-permute-done.other.rest_1_), custom_call_target="tpu_custom_call" | custom-call | flops 1 | bytes 1 | tf_op jit(solution)/shard_map/pick/pallas_call | solution.py:471
  5.0 0.2 copy-done
  5.2 1.3 %collective-permute-start.1 = (bf16[512,1024]{1,0:T(8,128)(2,1)}, bf16[512,1024]{1,0:T(8,128)(2,1)}, u32[]{:S(2)}, u32[]{:S(2)}) collective-permute-start(bf16[512,1024]{1,0:T(8,128)(2,1)} %pick.1), channel_id=1, source_target_pairs={{0,4},{1,3},{2,0},{3,7},{4,8},{5,1},{6,2},{7,11},{8,12},{9,5},{10,... | collective-permute-start | bytes 3145736 | tf_op jit(solution)/shard_map/ppermute | solution.py:653
  6.5 0.9 collective-permute-start.2
  7.3 7.7 %gather_rows.1 = bf16[16,144,128]{2,1,0:T(8,128)(2,1)} custom-call(s32[32]{0:T(128)} %adapter.2, s32[512]{0:T(512)} %storage.3, bf16[512,8192]{1,0:T(8,128)(2,1)} %down.1, bf16[512,1024]{1,0:T(8,128)(2,1)} %up.1), custom_call_target="tpu_custom_call" | custom-call | flops 1 | bytes 1 | tf_op jit(solution)/shard_map/gather_rows/pallas_call | solution.py:191
  15.1 1.1 %collective-permute-done.3.refs_1_ = bf16[256,1024]{1,0:T(8,128)(2,1)S(1)} collective-permute-done((bf16[256,1024]{1,0:T(8,128)(2,1)S(1)}, bf16[256,1024]{1,0:T(8,128)(2,1)S(1)}, u32[]{:S(2)}, u32[]{:S(2)}) %collective-permute-start.3) | collective-permute-done | bytes 524320 | tf_op jit(solution)/shard_map/ppermute | solution.py:642
  16.2 0.7 collective-permute-start.4
  16.9 6.0 %all-to-all-start = ((bf16[16,144,128]{2,1,0:T(8,128)(2,1)}), bf16[16,144,128]{2,1,0:T(8,128)(2,1)S(1)}, u32[]{:S(2)}, u32[]{:S(2)}) async-start(bf16[16,144,128]{2,1,0:T(8,128)(2,1)} %gather_rows.1), calls=%async_computation | async-start | bytes 1179648 | tf_op jit(solution)/shard_map/all_to_all | solution.py:648
  22.9 0.0 collective-permute-done.2.refs_0_
  22.9 0.0 collective-permute-done.4.refs_2_
  22.9 0.0 collective-permute-done.1.refs_3_.rest_0_
  23.0 1.2 %collective-permute-start.5 = (bf16[512,1024]{1,0:T(8,128)(2,1)}, bf16[512,1024]{1,0:T(8,128)(2,1)}, u32[]{:S(2)}, u32[]{:S(2)}) collective-permute-start(bf16[512,1024]{1,0:T(8,128)(2,1)} %collective-permute-done.1.refs_3_.rest_0_), channel_id=1, source_target_pairs={{0,4},{1,3},{2,0},{3,7},{4,8},{5,1},{6,2},{7,11},{8,12},{9,5},{10,... | collective-permute-start | bytes 3145736 | tf_op jit(solution)/shard_map/ppermute | solution.py:666
  24.2 3.4 %far_products.4 = (bf16[256,512]{1,0:T(8,128)(2,1)}, bf16[256,512]{1,0:T(8,128)(2,1)}, bf16[256,512]{1,0:T(8,128)(2,1)}) custom-call(bf16[256,1024]{1,0:T(8,128)(2,1)S(1)} %collective-permute-done.2.refs_0_, bf16[256,1024]{1,0:T(8,128)(2,1)S(1)} %collective-permute-done.3.refs_1_, bf16[256,1024]{1,0:T(8,128)(2,1)S(1)} %collective-permute-done.4.refs_2_, ...), custom_call_target="tpu_custom_call" | custom-call | flops 1 | bytes 1 | tf_op jit(solution)/shard_map/far_products/pallas_call | solution.py:515
  27.6 1.3 %collective-permute-start.7 = (bf16[256,512]{1,0:T(8,128)(2,1)}, bf16[256,512]{1,0:T(8,128)(2,1)S(1)}, u32[]{:S(2)}, u32[]{:S(2)}) collective-permute-start(bf16[256,512]{1,0:T(8,128)(2,1)} %get-tuple-element.75), channel_id=1, source_target_pairs={{0,16},{16,0},{1,17},{17,1},{2,18},{18,2},{3,19},{19,3},{4,20},{20... | collective-permute-start | bytes 786440 | tf_op jit(solution)/shard_map/ppermute | solution.py:635
  28.8 0.2 collective-permute-start.8
  29.0 0.5 collective-permute-start.6
  29.5 6.7 %zero_grads.1 = (f32[512,8192]{1,0:T(8,128)}, f32[512,1024]{1,0:T(8,128)}) custom-call(bf16[256,512]{1,0:T(8,128)(2,1)} %get-tuple-element.69._), custom_call_target="tpu_custom_call" | custom-call | flops 1 | bytes 1 | tf_op jit(solution)/shard_map/zero_grads/pallas_call | solution.py:325
  36.2 2.2 %all-to-all-done.recv = bf16[16,144,128]{2,1,0:T(8,128)(2,1)S(1)} async-done(((bf16[16,144,128]{2,1,0:T(8,128)(2,1)}), bf16[16,144,128]{2,1,0:T(8,128)(2,1)S(1)}, u32[]{:S(2)}, u32[]{:S(2)}) %all-to-all-start) | async-done | bytes 589856 | tf_op jit(solution)/shard_map/all_to_all | solution.py:648
  38.4 5.0 %adapter_terms.1 = (bf16[16,144,128]{2,1,0:T(8,128)(2,1)}, bf16[256,128]{1,0:T(8,128)(2,1)S(1)}) custom-call(bf16[256,8192]{1,0:T(8,128)(2,1)} %x.1, bf16[256,1024]{1,0:T(8,128)(2,1)S(1)} %mask_rows.1.cot, bf16[16,144,128]{2,1,0:T(8,128)(2,1)S(1)} %all-to-all-done.recv), custom_call_target="tpu_custom_call" | custom-call | flops 1 | bytes 1 | tf_op jit(solution)/shard_map/adapter_terms/pallas_call | solution.py:289
  43.4 2.9 %finish.5.rest_5_ = bf16[256,8192]{1,0:T(8,128)(2,1)} custom-call(bf16[256,1024]{1,0:T(8,128)(2,1)S(1)} %mask_rows.1.cot, bf16[256,128]{1,0:T(8,128)(2,1)S(1)} %get-tuple-element.73.g, bf16[16,144,128]{2,1,0:T(8,128)(2,1)S(1)} %all-to-all-done.recv, bf16[512,1024]{1,0:T(8,128)(2,1)} %rest_0_.1, bf16[512,1024]{1,0:T(8,128)(2,1)} %copy-done), custom_call_target="tpu_custom_call" | custom-call | flops 1 | bytes 1 | tf_op jit(solution)/shard_map/finish/pallas_call | solution.py:581
  46.3 0.0 collective-permute-done.7.rest_3_
  46.3 0.0 copy-start.1
  46.3 0.0 collective-permute-done.8.rest_4_
  46.4 0.0 copy-start.2
  46.4 0.0 collective-permute-done.6.rest_2_
  46.4 0.0 copy-start.3
  46.4 1.2 %collective-permute-done.5.refs_3_.rest_1_ = bf16[512,1024]{1,0:T(8,128)(2,1)} collective-permute-done((bf16[512,1024]{1,0:T(8,128)(2,1)}, bf16[512,1024]{1,0:T(8,128)(2,1)}, u32[]{:S(2)}, u32[]{:S(2)}) %collective-permute-start.5) | collective-permute-done | bytes 1048608 | tf_op jit(solution)/shard_map/ppermute | solution.py:666
  47.6 1.9 %collective-permute-start.9 = (bf16[512,1024]{1,0:T(8,128)(2,1)}, bf16[512,1024]{1,0:T(8,128)(2,1)}, u32[]{:S(2)}, u32[]{:S(2)}) collective-permute-start(bf16[512,1024]{1,0:T(8,128)(2,1)} %collective-permute-done.5.refs_3_.rest_1_), channel_id=1, source_target_pairs={{0,4},{1,3},{2,0},{3,7},{4,8},{5,1},{6,2},{7,11},{8,12},{9,5},{10,... | collective-permute-start | bytes 3145736 | tf_op jit(solution)/shard_map/ppermute | solution.py:666
  49.5 3.3 %far_products.5 = (bf16[256,512]{1,0:T(8,128)(2,1)}, bf16[256,512]{1,0:T(8,128)(2,1)}, bf16[256,512]{1,0:T(8,128)(2,1)}) custom-call(bf16[256,1024]{1,0:T(8,128)(2,1)S(1)} %collective-permute-done.2.refs_0_, bf16[256,1024]{1,0:T(8,128)(2,1)S(1)} %collective-permute-done.3.refs_1_, bf16[256,1024]{1,0:T(8,128)(2,1)S(1)} %collective-permute-done.4.refs_2_, ...), custom_call_target="tpu_custom_call" | custom-call | flops 1 | bytes 1 | tf_op jit(solution)/shard_map/far_products/pallas_call | solution.py:515
  52.9 1.3 %collective-permute-start.11 = (bf16[256,512]{1,0:T(8,128)(2,1)}, bf16[256,512]{1,0:T(8,128)(2,1)}, u32[]{:S(2)}, u32[]{:S(2)}) collective-permute-start(bf16[256,512]{1,0:T(8,128)(2,1)} %get-tuple-element.92), channel_id=1, source_target_pairs={{0,16},{16,0},{1,17},{17,1},{2,18},{18,2},{3,19},{19,3},{4,20},{20... | collective-permute-start | bytes 786440 | tf_op jit(solution)/shard_map/ppermute | solution.py:635
  54.1 0.9 collective-permute-start.12
  55.1 0.0 collective-permute-start.10
  55.1 0.0 copy-done.3
  55.1 3.6 %finish.6.rest_4_ = bf16[256,8192]{1,0:T(8,128)(2,1)} custom-call(bf16[256,1024]{1,0:T(8,128)(2,1)S(1)} %mask_rows.1.cot, bf16[256,128]{1,0:T(8,128)(2,1)S(1)} %get-tuple-element.73.g, bf16[16,144,128]{2,1,0:T(8,128)(2,1)S(1)} %all-to-all-done.recv, bf16[512,1024]{1,0:T(8,128)(2,1)} %collective-permute-done.1.refs_3_.rest_0_, ...), custom_call_target="tpu_custom_call", output_to_operand_aliasing={{}: (8, {})} | custom-call | flops 1 | bytes 1 | tf_op jit(solution)/shard_map/finish/pallas_call | solution.py:581
  58.7 5.8 %all-to-all-start.1 = ((bf16[16,144,128]{2,1,0:T(8,128)(2,1)}), bf16[16,144,128]{2,1,0:T(8,128)(2,1)S(1)}, u32[]{:S(2)}, u32[]{:S(2)}) async-start(bf16[16,144,128]{2,1,0:T(8,128)(2,1)} %get-tuple-element.110), calls=%async_computation.1 | async-start | bytes 1179648 | tf_op jit(solution)/shard_map/all_to_all | solution.py:689
  64.5 0.0 collective-permute-done.9.refs_3_.rest_0_
  64.5 3.4 %far_products.6 = (bf16[256,512]{1,0:T(8,128)(2,1)}, bf16[256,512]{1,0:T(8,128)(2,1)}, bf16[256,512]{1,0:T(8,128)(2,1)}, bf16[256,1024]{1,0:T(8,128)(2,1)}) custom-call(bf16[256,1024]{1,0:T(8,128)(2,1)S(1)} %collective-permute-done.2.refs_0_, bf16[256,1024]{1,0:T(8,128)(2,1)S(1)} %collective-permute-done.3.refs_1_, ...), custom_call_target="tpu_custom_call" | custom-call | flops 1 | bytes 1 | tf_op jit(solution)/shard_map/far_products/pallas_call | solution.py:515
  67.9 0.0 collective-permute-done.11.rest_2_
  67.9 0.0 collective-permute-done.12.rest_3_
  67.9 0.0 collective-permute-done.10.rest_1_
  67.9 1.4 %collective-permute-start.13 = (bf16[256,1024]{1,0:T(8,128)(2,1)}, bf16[256,1024]{1,0:T(8,128)(2,1)S(1)}, u32[]{:S(2)}, u32[]{:S(2)}) collective-permute-start(bf16[256,1024]{1,0:T(8,128)(2,1)} %get-tuple-element.94), channel_id=1, source_target_pairs={{0,4},{1,3},{2,0},{3,7},{4,8},{5,1},{6,2},{7,11},{8,12},{9,5},{10,... | collective-permute-start | bytes 1572872 | tf_op jit(solution)/shard_map/ppermute | solution.py:674
  69.3 0.0 collective-permute-start.14
  69.3 1.2 %collective-permute-start.15 = (bf16[256,512]{1,0:T(8,128)(2,1)}, bf16[256,512]{1,0:T(8,128)(2,1)S(1)}, u32[]{:S(2)}, u32[]{:S(2)}) collective-permute-start(bf16[256,512]{1,0:T(8,128)(2,1)} %get-tuple-element.100), channel_id=1, source_target_pairs={{0,16},{16,0},{1,17},{17,1},{2,18},{18,2},{3,19},{19,3},{4,20},{20... | collective-permute-start | bytes 786440 | tf_op jit(solution)/shard_map/ppermute | solution.py:635
  70.5 0.9 collective-permute-start.16
  71.5 3.0 %finish.7.rest_4_ = bf16[256,8192]{1,0:T(8,128)(2,1)} custom-call(bf16[256,1024]{1,0:T(8,128)(2,1)S(1)} %mask_rows.1.cot, bf16[256,128]{1,0:T(8,128)(2,1)S(1)} %get-tuple-element.73.g, bf16[16,144,128]{2,1,0:T(8,128)(2,1)S(1)} %all-to-all-done.recv, bf16[512,1024]{1,0:T(8,128)(2,1)} %collective-permute-done.9.refs_3_.rest_0_, ...), custom_call_target="tpu_custom_call", output_to_operand_aliasing={{}: (7, {})} | custom-call | flops 1 | bytes 1 | tf_op jit(solution)/shard_map/finish/pallas_call | solution.py:581
  74.5 9.0 %collective-permute-done.13.refs_3_.rest_0_ = bf16[256,1024]{1,0:T(8,128)(2,1)S(1)} collective-permute-done((bf16[256,1024]{1,0:T(8,128)(2,1)}, bf16[256,1024]{1,0:T(8,128)(2,1)S(1)}, u32[]{:S(2)}, u32[]{:S(2)}) %collective-permute-start.13) | collective-permute-done | bytes 524320 | tf_op jit(solution)/shard_map/ppermute | solution.py:674
  83.6 1.4 %far_products.7 = (bf16[256,256]{1,0:T(8,128)(2,1)}, bf16[256,256]{1,0:T(8,128)(2,1)}, bf16[256,256]{1,0:T(8,128)(2,1)}) custom-call(bf16[256,1024]{1,0:T(8,128)(2,1)S(1)} %collective-permute-done.2.refs_0_, bf16[256,1024]{1,0:T(8,128)(2,1)S(1)} %collective-permute-done.3.refs_1_, bf16[256,1024]{1,0:T(8,128)(2,1)S(1)} %collective-permute-done.4.refs_2_, ...), custom_call_target="tpu_custom_call" | custom-call | flops 1 | bytes 1 | tf_op jit(solution)/shard_map/far_products/pallas_call | solution.py:515
  84.9 0.0 collective-permute-done.14.rest_1_
  85.0 0.0 collective-permute-done.15.rest_2_
  85.0 0.0 collective-permute-done.16.rest_3_
  85.0 2.4 %collective-permute-start.17 = (bf16[256,256]{1,0:T(8,128)(2,1)}, bf16[256,256]{1,0:T(8,128)(2,1)S(1)}, u32[]{:S(2)}, u32[]{:S(2)}) collective-permute-start(bf16[256,256]{1,0:T(8,128)(2,1)} %get-tuple-element.107), channel_id=1, source_target_pairs={{0,1},{1,0},{2,3},{3,2},{4,5},{5,4},{6,7},{7,6},{8,9},{9,8},{10,11... | collective-permute-start | bytes 393224 | tf_op jit(solution)/shard_map/ppermute | solution.py:634
  87.3 1.2 %collective-permute-start.18 = (bf16[256,256]{1,0:T(8,128)(2,1)}, bf16[256,256]{1,0:T(8,128)(2,1)S(1)}, u32[]{:S(2)}, u32[]{:S(2)}) collective-permute-start(bf16[256,256]{1,0:T(8,128)(2,1)} %get-tuple-element.108), channel_id=1, source_target_pairs={{0,16},{16,0},{1,17},{17,1},{2,18},{18,2},{3,19},{19,3},{4,20},{20... | collective-permute-start | bytes 393224 | tf_op jit(solution)/shard_map/ppermute | solution.py:635
  88.6 0.5 collective-permute-start.19
  89.1 2.1 %finish.8.rest_3_ = bf16[256,8192]{1,0:T(8,128)(2,1)} custom-call(bf16[256,1024]{1,0:T(8,128)(2,1)S(1)} %mask_rows.1.cot, bf16[256,128]{1,0:T(8,128)(2,1)S(1)} %get-tuple-element.73.g, bf16[16,144,128]{2,1,0:T(8,128)(2,1)S(1)} %all-to-all-done.recv, bf16[256,1024]{1,0:T(8,128)(2,1)S(1)} %collective-permute-done.13.refs_3_.rest_0_, ...), custom_call_target="tpu_custom_call", output_to_operand_aliasing={{}: (7, {})} | custom-call | flops 5000000000 | bytes 1 | tf_op jit(solution)/shard_map/finish/pallas_call | solution.py:581
  91.1 0.0 all-to-all-done.1.recv
  91.1 4.0 %scatter_rows.1 = (f32[512,8192]{1,0:T(8,128)}, f32[512,1024]{1,0:T(8,128)}) custom-call(s32[32]{0:T(128)} %adapter.2, s32[512]{0:T(512)} %storage.3, bf16[16,144,128]{2,1,0:T(8,128)(2,1)S(1)} %all-to-all-done.1.recv, f32[512,8192]{1,0:T(8,128)} %get-tuple-element.117._down, ...), custom_call_target="tpu_custom_call", output_to_operand_aliasing={{0}: (3, {}), {1}: (4, {})} | custom-call | flops 1 | bytes 1 | tf_op jit(solution)/shard_map/scatter_rows/pallas_call | solution.py:428
  95.2 0.0 collective-permute-done.17.rest_0_
  95.2 0.0 collective-permute-done.18.rest_1_
  95.2 0.4 collective-permute-done.19.rest_2_
  95.6 1.7 %finish.9 = bf16[256,8192]{1,0:T(8,128)(2,1)} custom-call(bf16[256,1024]{1,0:T(8,128)(2,1)S(1)} %mask_rows.1.cot, bf16[256,128]{1,0:T(8,128)(2,1)S(1)} %get-tuple-element.73.g, bf16[16,144,128]{2,1,0:T(8,128)(2,1)S(1)} %all-to-all-done.recv, bf16[256,256]{1,0:T(8,128)(2,1)S(1)} %collective-permute-done.17.rest_0_, ...), custom_call_target="tpu_custom_call", output_to_operand_aliasing={{}: (6, {})} | custom-call | flops 1 | bytes 1 | tf_op jit(solution)/shard_map/finish/pallas_call | solution.py:581
  (3 shorter events, 0.0 us)
Async XLA Ops:
  0.6 3.2 %collective-permute-start = (bf16[512,1024]{1,0:T(8,128)(2,1)}, bf16[512,1024]{1,0:T(8,128)(2,1)S(1)}, u32[]{:S(2)}, u32[]{:S(2)}) collective-permute-start(bf16[512,1024]{1,0:T(8,128)(2,1)} %rest_0_.1), channel_id=1, source_target_pairs={{0,1},{1,0},{2,3},{3,2},{4,5},{5,4},{6,7},{7,6},{8,9},{9,8},{10,11... | collective-permute-start | bytes 3145736 | tf_op jit(solution)/shard_map/ppermute | solution.py:639
  2.5 13.7 %collective-permute-start.3 = (bf16[256,1024]{1,0:T(8,128)(2,1)S(1)}, bf16[256,1024]{1,0:T(8,128)(2,1)S(1)}, u32[]{:S(2)}, u32[]{:S(2)}) collective-permute-start(bf16[256,1024]{1,0:T(8,128)(2,1)S(1)} %mask_rows.1.cot), channel_id=1, source_target_pairs={{0,16},{16,0},{1,17},{17,1},{2,18},{18,2},{3,19},{19,3},{4,20},{20... | collective-permute-start | bytes 1572872 | tf_op jit(solution)/shard_map/ppermute | solution.py:642
  3.9 1.3 %copy-start = (bf16[512,1024]{1,0:T(8,128)(2,1)}, bf16[512,1024]{1,0:T(8,128)(2,1)S(1)}, u32[]{:S(2)}) copy-start(bf16[512,1024]{1,0:T(8,128)(2,1)S(1)} %collective-permute-done.other.rest_1_) | copy-start | bytes 3145732
  5.2 17.8 %collective-permute-start.1 = (bf16[512,1024]{1,0:T(8,128)(2,1)}, bf16[512,1024]{1,0:T(8,128)(2,1)}, u32[]{:S(2)}, u32[]{:S(2)}) collective-permute-start(bf16[512,1024]{1,0:T(8,128)(2,1)} %pick.1), channel_id=1, source_target_pairs={{0,4},{1,3},{2,0},{3,7},{4,8},{5,1},{6,2},{7,11},{8,12},{9,5},{10,... | collective-permute-start | bytes 3145736 | tf_op jit(solution)/shard_map/ppermute | solution.py:653
  6.5 16.4 %collective-permute-start.2 = (bf16[256,1024]{1,0:T(8,128)(2,1)S(1)}, bf16[256,1024]{1,0:T(8,128)(2,1)S(1)}, u32[]{:S(2)}, u32[]{:S(2)}) collective-permute-start(bf16[256,1024]{1,0:T(8,128)(2,1)S(1)} %mask_rows.1.cot), channel_id=1, source_target_pairs={{0,1},{1,0},{2,3},{3,2},{4,5},{5,4},{6,7},{7,6},{8,9},{9,8},{10,11... | collective-permute-start | bytes 1572872 | tf_op jit(solution)/shard_map/ppermute | solution.py:641
  16.2 6.7 %collective-permute-start.4 = (bf16[256,1024]{1,0:T(8,128)(2,1)S(1)}, bf16[256,1024]{1,0:T(8,128)(2,1)S(1)}, u32[]{:S(2)}, u32[]{:S(2)}) collective-permute-start(bf16[256,1024]{1,0:T(8,128)(2,1)S(1)} %collective-permute-done.3.refs_1_), channel_id=1, source_target_pairs={{0,1},{1,0},{2,3},{3,2},{4,5},{5,4},{6,7},{7,6},{8,9},{9,8},{10,11... | collective-permute-start | bytes 1572872 | tf_op jit(solution)/shard_map/ppermute | solution.py:650
  16.9 21.5 %all-to-all-start = ((bf16[16,144,128]{2,1,0:T(8,128)(2,1)}), bf16[16,144,128]{2,1,0:T(8,128)(2,1)S(1)}, u32[]{:S(2)}, u32[]{:S(2)}) async-start(bf16[16,144,128]{2,1,0:T(8,128)(2,1)} %gather_rows.1), calls=%async_computation | async-start | bytes 1179648 | tf_op jit(solution)/shard_map/all_to_all | solution.py:648
  23.0 24.7 %collective-permute-start.5 = (bf16[512,1024]{1,0:T(8,128)(2,1)}, bf16[512,1024]{1,0:T(8,128)(2,1)}, u32[]{:S(2)}, u32[]{:S(2)}) collective-permute-start(bf16[512,1024]{1,0:T(8,128)(2,1)} %collective-permute-done.1.refs_3_.rest_0_), channel_id=1, source_target_pairs={{0,4},{1,3},{2,0},{3,7},{4,8},{5,1},{6,2},{7,11},{8,12},{9,5},{10,... | collective-permute-start | bytes 3145736 | tf_op jit(solution)/shard_map/ppermute | solution.py:666
  27.6 18.8 %collective-permute-start.7 = (bf16[256,512]{1,0:T(8,128)(2,1)}, bf16[256,512]{1,0:T(8,128)(2,1)S(1)}, u32[]{:S(2)}, u32[]{:S(2)}) collective-permute-start(bf16[256,512]{1,0:T(8,128)(2,1)} %get-tuple-element.75), channel_id=1, source_target_pairs={{0,16},{16,0},{1,17},{17,1},{2,18},{18,2},{3,19},{19,3},{4,20},{20... | collective-permute-start | bytes 786440 | tf_op jit(solution)/shard_map/ppermute | solution.py:635
  28.8 17.5 %collective-permute-start.8 = (bf16[256,512]{1,0:T(8,128)(2,1)}, bf16[256,512]{1,0:T(8,128)(2,1)S(1)}, u32[]{:S(2)}, u32[]{:S(2)}) collective-permute-start(bf16[256,512]{1,0:T(8,128)(2,1)} %get-tuple-element.76), channel_id=1, source_target_pairs={{0,17},{1,16},{2,19},{3,18},{4,21},{5,20},{6,23},{7,22},{8,25},{9,... | collective-permute-start | bytes 786440 | tf_op jit(solution)/shard_map/ppermute | solution.py:636
  29.0 17.4 %collective-permute-start.6 = (bf16[256,512]{1,0:T(8,128)(2,1)}, bf16[256,512]{1,0:T(8,128)(2,1)S(1)}, u32[]{:S(2)}, u32[]{:S(2)}) collective-permute-start(bf16[256,512]{1,0:T(8,128)(2,1)} %get-tuple-element.69._), channel_id=1, source_target_pairs={{0,1},{1,0},{2,3},{3,2},{4,5},{5,4},{6,7},{7,6},{8,9},{9,8},{10,11... | collective-permute-start | bytes 786440 | tf_op jit(solution)/shard_map/ppermute | solution.py:634
  46.3 8.7 %copy-start.1 = (bf16[256,512]{1,0:T(8,128)(2,1)}, bf16[256,512]{1,0:T(8,128)(2,1)S(1)}, u32[]{:S(2)}) copy-start(bf16[256,512]{1,0:T(8,128)(2,1)S(1)} %collective-permute-done.7.rest_3_) | copy-start | bytes 786436
  46.4 8.7 %copy-start.2 = (bf16[256,512]{1,0:T(8,128)(2,1)}, bf16[256,512]{1,0:T(8,128)(2,1)S(1)}, u32[]{:S(2)}) copy-start(bf16[256,512]{1,0:T(8,128)(2,1)S(1)} %collective-permute-done.8.rest_4_) | copy-start | bytes 786436
  46.4 8.7 %copy-start.3 = (bf16[256,512]{1,0:T(8,128)(2,1)}, bf16[256,512]{1,0:T(8,128)(2,1)S(1)}, u32[]{:S(2)}) copy-start(bf16[256,512]{1,0:T(8,128)(2,1)S(1)} %collective-permute-done.6.rest_2_) | copy-start | bytes 786436
  47.6 16.9 %collective-permute-start.9 = (bf16[512,1024]{1,0:T(8,128)(2,1)}, bf16[512,1024]{1,0:T(8,128)(2,1)}, u32[]{:S(2)}, u32[]{:S(2)}) collective-permute-start(bf16[512,1024]{1,0:T(8,128)(2,1)} %collective-permute-done.5.refs_3_.rest_1_), channel_id=1, source_target_pairs={{0,4},{1,3},{2,0},{3,7},{4,8},{5,1},{6,2},{7,11},{8,12},{9,5},{10,... | collective-permute-start | bytes 3145736 | tf_op jit(solution)/shard_map/ppermute | solution.py:666
  52.9 15.0 %collective-permute-start.11 = (bf16[256,512]{1,0:T(8,128)(2,1)}, bf16[256,512]{1,0:T(8,128)(2,1)}, u32[]{:S(2)}, u32[]{:S(2)}) collective-permute-start(bf16[256,512]{1,0:T(8,128)(2,1)} %get-tuple-element.92), channel_id=1, source_target_pairs={{0,16},{16,0},{1,17},{17,1},{2,18},{18,2},{3,19},{19,3},{4,20},{20... | collective-permute-start | bytes 786440 | tf_op jit(solution)/shard_map/ppermute | solution.py:635
  54.1 13.8 %collective-permute-start.12 = (bf16[256,512]{1,0:T(8,128)(2,1)}, bf16[256,512]{1,0:T(8,128)(2,1)}, u32[]{:S(2)}, u32[]{:S(2)}) collective-permute-start(bf16[256,512]{1,0:T(8,128)(2,1)} %get-tuple-element.93), channel_id=1, source_target_pairs={{0,17},{1,16},{2,19},{3,18},{4,21},{5,20},{6,23},{7,22},{8,25},{9,... | collective-permute-start | bytes 786440 | tf_op jit(solution)/shard_map/ppermute | solution.py:636
  55.1 12.9 %collective-permute-start.10 = (bf16[256,512]{1,0:T(8,128)(2,1)}, bf16[256,512]{1,0:T(8,128)(2,1)}, u32[]{:S(2)}, u32[]{:S(2)}) collective-permute-start(bf16[256,512]{1,0:T(8,128)(2,1)} %get-tuple-element.79), channel_id=1, source_target_pairs={{0,1},{1,0},{2,3},{3,2},{4,5},{5,4},{6,7},{7,6},{8,9},{9,8},{10,11... | collective-permute-start | bytes 786440 | tf_op jit(solution)/shard_map/ppermute | solution.py:634
  58.7 32.5 %all-to-all-start.1 = ((bf16[16,144,128]{2,1,0:T(8,128)(2,1)}), bf16[16,144,128]{2,1,0:T(8,128)(2,1)S(1)}, u32[]{:S(2)}, u32[]{:S(2)}) async-start(bf16[16,144,128]{2,1,0:T(8,128)(2,1)} %get-tuple-element.110), calls=%async_computation.1 | async-start | bytes 1179648 | tf_op jit(solution)/shard_map/all_to_all | solution.py:689
  67.9 15.6 %collective-permute-start.13 = (bf16[256,1024]{1,0:T(8,128)(2,1)}, bf16[256,1024]{1,0:T(8,128)(2,1)S(1)}, u32[]{:S(2)}, u32[]{:S(2)}) collective-permute-start(bf16[256,1024]{1,0:T(8,128)(2,1)} %get-tuple-element.94), channel_id=1, source_target_pairs={{0,4},{1,3},{2,0},{3,7},{4,8},{5,1},{6,2},{7,11},{8,12},{9,5},{10,... | collective-permute-start | bytes 1572872 | tf_op jit(solution)/shard_map/ppermute | solution.py:674
  69.3 15.6 %collective-permute-start.14 = (bf16[256,512]{1,0:T(8,128)(2,1)}, bf16[256,512]{1,0:T(8,128)(2,1)S(1)}, u32[]{:S(2)}, u32[]{:S(2)}) collective-permute-start(bf16[256,512]{1,0:T(8,128)(2,1)} %get-tuple-element.99), channel_id=1, source_target_pairs={{0,1},{1,0},{2,3},{3,2},{4,5},{5,4},{6,7},{7,6},{8,9},{9,8},{10,11... | collective-permute-start | bytes 786440 | tf_op jit(solution)/shard_map/ppermute | solution.py:634
  69.3 15.6 %collective-permute-start.15 = (bf16[256,512]{1,0:T(8,128)(2,1)}, bf16[256,512]{1,0:T(8,128)(2,1)S(1)}, u32[]{:S(2)}, u32[]{:S(2)}) collective-permute-start(bf16[256,512]{1,0:T(8,128)(2,1)} %get-tuple-element.100), channel_id=1, source_target_pairs={{0,16},{16,0},{1,17},{17,1},{2,18},{18,2},{3,19},{19,3},{4,20},{20... | collective-permute-start | bytes 786440 | tf_op jit(solution)/shard_map/ppermute | solution.py:635
  70.5 14.4 %collective-permute-start.16 = (bf16[256,512]{1,0:T(8,128)(2,1)}, bf16[256,512]{1,0:T(8,128)(2,1)S(1)}, u32[]{:S(2)}, u32[]{:S(2)}) collective-permute-start(bf16[256,512]{1,0:T(8,128)(2,1)} %get-tuple-element.101), channel_id=1, source_target_pairs={{0,17},{1,16},{2,19},{3,18},{4,21},{5,20},{6,23},{7,22},{8,25},{9,... | collective-permute-start | bytes 786440 | tf_op jit(solution)/shard_map/ppermute | solution.py:636
  85.0 10.2 %collective-permute-start.17 = (bf16[256,256]{1,0:T(8,128)(2,1)}, bf16[256,256]{1,0:T(8,128)(2,1)S(1)}, u32[]{:S(2)}, u32[]{:S(2)}) collective-permute-start(bf16[256,256]{1,0:T(8,128)(2,1)} %get-tuple-element.107), channel_id=1, source_target_pairs={{0,1},{1,0},{2,3},{3,2},{4,5},{5,4},{6,7},{7,6},{8,9},{9,8},{10,11... | collective-permute-start | bytes 393224 | tf_op jit(solution)/shard_map/ppermute | solution.py:634
  87.3 7.8 %collective-permute-start.18 = (bf16[256,256]{1,0:T(8,128)(2,1)}, bf16[256,256]{1,0:T(8,128)(2,1)S(1)}, u32[]{:S(2)}, u32[]{:S(2)}) collective-permute-start(bf16[256,256]{1,0:T(8,128)(2,1)} %get-tuple-element.108), channel_id=1, source_target_pairs={{0,16},{16,0},{1,17},{17,1},{2,18},{18,2},{3,19},{19,3},{4,20},{20... | collective-permute-start | bytes 393224 | tf_op jit(solution)/shard_map/ppermute | solution.py:635
  88.6 7.0 %collective-permute-start.19 = (bf16[256,256]{1,0:T(8,128)(2,1)}, bf16[256,256]{1,0:T(8,128)(2,1)S(1)}, u32[]{:S(2)}, u32[]{:S(2)}) collective-permute-start(bf16[256,256]{1,0:T(8,128)(2,1)} %get-tuple-element.109), channel_id=1, source_target_pairs={{0,17},{1,16},{2,19},{3,18},{4,21},{5,20},{6,23},{7,22},{8,25},{9,... | collective-permute-start | bytes 393224 | tf_op jit(solution)/shard_map/ppermute | solution.py:636

commit v6 on v5

--- a/solution.py
+++ b/solution.py
@@ -19,7 +19,7 @@
 IN_SMEM = pl.BlockSpec(memory_space=pltpu.SMEM)
 IN_HBM = pl.BlockSpec(memory_space=pltpu.HBM)
 SMALL = pl.CostEstimate(flops=1, bytes_accessed=1, transcendentals=0)
-LONGER = pl.CostEstimate(flops=5_000_000_000, bytes_accessed=1, transcendentals=0)
+LONGER = pl.CostEstimate(flops=10_000_000_000, bytes_accessed=1, transcendentals=0)
 
 adapter_scale = 2.0
 
@@ -41,7 +41,7 @@
     index, part = lax.axis_index("fsdp"), lax.axis_index("parts")
     chips = devices // 2
     chip, core = lax.div(index, 2), lax.rem(index, 2)
-    way = 2 * core - 1
+    way = jnp.where(core == part, -1, 1)
     odd = lax.rem(chip, 2) == 1
     place = jnp.where(odd, chips - lax.div(chip + 1, 2), lax.div(chip, 2))
 
@@ -52,10 +52,10 @@
     blocks = [index, index + 1 - 2 * core]
     for step in range(1, chips // 2):
         near, far = at(way * step), at(-way * step)
-        blocks += [2 * near + part, 2 * far + part, 2 * near + 1 - part, 2 * far + 1 - part]
+        blocks += [2 * near + core, 2 * far + 1 - core, 2 * far + core, 2 * near + 1 - core]
     last = at(chips // 2)
     for p in (part, 1 - part):
-        blocks += [2 * (2 * last + p) + core, 2 * (2 * last + p) + 1 - core]
+        blocks += [2 * (2 * last + core) + p, 2 * (2 * last + 1 - core) + p]
     return blocks
 
 
@@ -342,19 +342,19 @@
 
 
 def scatter_kernel(
-    adapter, storage, recv, _down, _up, down, up, table, dacc, uacc, dscr, uscr, drow, urow, dsem, usem
+    adapter_hbm, storage_hbm, recv, _down, _up, down, up, adapter, storage, isem, table, dacc, uacc, dscr, uscr, drow, urow, dsem, usem
 ):
-    blocks = adapter.shape[0]
+    blocks = adapter_hbm.shape[0]
     devices = recv.shape[0]
     per_down, per_up = down.shape[1] // LANES, up.shape[1] // LANES
     down_rows = 2 * per_down
 
-    def mark(i, carry):
-        b = blocks - 1 - i
-        table[storage[adapter[b]]] = b
-        return carry
-
-    lax.fori_loop(0, blocks, mark, 0)
+    indices = [
+        pltpu.make_async_copy(adapter_hbm, adapter, isem.at[0]),
+        pltpu.make_async_copy(storage_hbm, storage, isem.at[1]),
+    ]
+    for copy in indices:
+        copy.start()
     dacc[...] = jnp.zeros_like(dacc)
     uacc[...] = jnp.zeros_like(uacc)
     count = 8 * per_down
@@ -366,6 +366,15 @@
             recv[:, q * ADAPTER_RANK : (q + 1) * ADAPTER_RANK, :] for q in range(4 * k, 4 * k + 4)
         ]
         values.append(dot_n(lane_cat(tiles).reshape(devices * ADAPTER_RANK, count), order))
+    for copy in indices:
+        copy.wait()
+
+    def mark(i, carry):
+        b = blocks - 1 - i
+        table[storage[adapter[b]]] = b
+        return carry
+
+    lax.fori_loop(0, blocks, mark, 0)
     lower = iota((ADAPTER_RANK, LANES), 1) < per_down
     for j in range(devices):
         rows = []
@@ -427,9 +436,12 @@
     per_down, per_up = down.shape[1] // LANES, up.shape[1] // LANES
     return pl.pallas_call(
         scatter_kernel,
-        in_specs=[IN_SMEM, IN_SMEM, IN_VMEM, IN_HBM, IN_HBM],
+        in_specs=[IN_HBM, IN_HBM, IN_VMEM, IN_HBM, IN_HBM],
         out_specs=[IN_HBM, IN_HBM],
         scratch_shapes=[
+            pltpu.SMEM((blocks,), jnp.int32),
+            pltpu.SMEM(adapter_storage_row.shape, jnp.int32),
+            pltpu.SemaphoreType.DMA((2,)),
             pltpu.SMEM((ADAPTER_GROUP,), jnp.int32),
             pltpu.VMEM((blocks, per_down, LANES), jnp.float32),
             pltpu.VMEM((blocks, per_up, LANES), jnp.float32),
@@ -451,35 +463,6 @@
     )(in_hbm(padded_block_adapter), in_hbm(adapter_storage_row), recv, down, up)
 
 
-def pick_kernel(own, other, out, sem):
-    mine = lax.axis_index("parts") == lax.axis_index("fsdp") % 2
-
-    @pl.when(mine)
-    def _():
-        copy = pltpu.make_async_copy(own, out, sem)
-        copy.start()
-        copy.wait()
-
-    @pl.when(jnp.logical_not(mine))
-    def _():
-        copy = pltpu.make_async_copy(other, out, sem)
-        copy.start()
-        copy.wait()
-
-
-def pick(own, other):
-    return pl.pallas_call(
-        pick_kernel,
-        in_specs=[pl.BlockSpec(memory_space=pl.ANY)] * 2,
-        out_specs=IN_VMEM,
-        out_shape=jax.ShapeDtypeStruct(own.shape, own.dtype),
-        scratch_shapes=[pltpu.SemaphoreType.DMA],
-        compiler_params=PARAMS,
-        cost_estimate=SMALL,
-        name="pick",
-    )(in_hbm(own), other)
-
-
 def far_kernel(count, handed, *refs):
     cots, weight, outs = refs[:count], refs[count], refs[count + 1 : 2 * count + 1]
     wbuf, buffer, wsem, sems, hsem = refs[2 * count + 1 + handed :]
@@ -499,8 +482,7 @@
             if i == len(loads) - 1:
                 stores[n].start()
     if handed:
-        core = lax.axis_index("fsdp") % 2
-        copy = pltpu.make_async_copy(wbuf.at[core], refs[2 * count + 1], hsem)
+        copy = pltpu.make_async_copy(wbuf.at[lax.axis_index("parts")], refs[2 * count + 1], hsem)
         copy.start()
         copy.wait()
     for copy in stores:
@@ -601,12 +583,13 @@
 def ring_pairs(devices):
     chips = devices // 2
     order = list(range(0, chips, 2)) + list(range(chips - 1, 0, -2))
-    place = {c: i for i, c in enumerate(order)}
-    ring = []
-    for c in range(chips):
-        ring.append((2 * c, 2 * order[(place[c] + 1) % chips]))
-        ring.append((2 * c + 1, 2 * order[(place[c] - 1) % chips] + 1))
-    return ring
+    pairs = []
+    for part in range(2):
+        for i, chip in enumerate(order):
+            for core in range(2):
+                other = order[(i + (1 if core == part else -1)) % chips]
+                pairs.append((part * devices + 2 * chip + core, part * devices + 2 * other + core))
+    return pairs
 
 
 def ring_body(
@@ -640,30 +623,28 @@
     masked = mask_rows(block_live_rows, cotangent)
     core_masked = lax.ppermute(masked, "fsdp", cores)
     far_masked = lax.ppermute(masked, "parts", across)
-    travelling = pick(frozen_value_weight, other_shard)
-    adapter, _, _ = after(padded_block_adapter, masked, travelling)
+    adapter, _ = after(padded_block_adapter, masked)
     payload = gather_rows(
         adapter, adapter_storage_row, adapter_down_weights, adapter_up_weights, devices
     )
     recv = lax.all_to_all(payload, "fsdp", split_axis=0, concat_axis=0, tiled=True)
-    far_masked, _ = after(far_masked, payload)
-    diagonal_masked = lax.ppermute(far_masked, "fsdp", cores)
-    cots = (core_masked, far_masked, diagonal_masked)
-
-    travelling = lax.ppermute(travelling, "fsdp", ring)
+
+    travelling = lax.ppermute(frozen_value_weight, ("parts", "fsdp"), ring)
 
     firsts = [2 + 4 * step for step in range(steps)]
     pieces, received = [], []
     for step in range(steps):
         if step == 0:
-            travelling, cots, _ = after(travelling, cots, payload)
+            travelling, far_masked, _ = after(travelling, far_masked, payload)
+            diagonal_masked = lax.ppermute(far_masked, "fsdp", cores)
+            cots = (core_masked, far_masked, diagonal_masked)
         elif step == 1:
             travelling, sent, out, grads, received[0] = after(
                 travelling, sent, out, grads, received[0]
             )
         pieces.append(travelling)
         if step < steps - 2:
-            travelling = lax.ppermute(travelling, "fsdp", ring)
+            travelling = lax.ppermute(travelling, ("parts", "fsdp"), ring)
         pin = as_it_is if step >= steps - 2 else in_hbm
         products = far_products(cots, pieces[step], pin, step == steps - 2)
         if step == steps - 2:
@@ -671,9 +652,9 @@
             travelling, products, out, received[-1] = after(
                 travelling, products, out, received[-1]
             )
-            travelling = lax.ppermute(travelling, "fsdp", ring)
-        if step == steps - 1:
-            products, received[-1] = after(products, received[-1])
+            travelling = lax.ppermute(travelling, ("parts", "fsdp"), ring)
+            sent, products = after(sent, products)
+            sums = lax.all_to_all(sent, "fsdp", split_axis=0, concat_axis=0, tiled=True)
         received.append(cross(products))
         if step == 0:
             grads = zero_grads(products[0], adapter_down_weights.shape, adapter_up_weights.shape)
@@ -685,8 +666,6 @@
             cot, _ = after(masked, products[0])
             at = firsts[: step + 1] + [firsts[0] + i for i in range(1, 4)]
             out = finish(devices, at, cot, pieces[:2], received[0], g, recv, out, width, shard)
-            sent, out = after(sent, out)
-            sums = lax.all_to_all(sent, "fsdp", split_axis=0, concat_axis=0, tiled=True)
             travelling, out = after(travelling, out)
         if step == steps - 2:
             out, _ = after(out, products)
@@ -700,11 +679,10 @@
     out = finish(
         devices, at, masked, piece, received[-2], g, recv, out, width, shard, as_it_is, LONGER
     )
+    at = [firsts[-1] + i for i in range(1, 4)]
+    out = finish(devices, at, masked, (), received[-1], g, recv, out, width, shard, as_it_is)
     sums, out = after(sums, out)
     down_grad, up_grad = scatter_rows(padded_block_adapter, adapter_storage_row, sums, *grads)
-    out, up_grad = after(out, up_grad)
-    at = [firsts[-1] + i for i in range(1, 4)]
-    out = finish(devices, at, masked, (), received[-1], g, recv, out, width, shard, as_it_is)
     return (out, down_grad, up_grad)
 
 

time: 98 us -> 92.3 us (0.942)
  the two profiles are of different devices: /device:TPU:13 before, /device:TPU:0 now
where the time goes in v6:
time: 92.3 us; the launch traced here: 91.4 us
  Pallas kernels  50 us (54%)
  starting transfers between devices  29.7 us (32%)
  waiting for transfers between devices  9.73 us (11%)
  between operations  1.03 us (1%)
  local copies, waits for them, and re-layouts  0.99 us (1%)
    pallas_call x5, Pallas kernels, finish(): pl.pallas_call(kernel, in_specs=[IN_VMEM] * 3 + [pl.BlockSpec(memory_spac...  14.2 us
    pallas_call x4, Pallas kernels, far_products(): pl.pallas_call(functools.partial(far_kernel, count, len(half)), in_specs=...  11.5 us
    pallas_call x1, Pallas kernels, gather_rows(): pl.pallas_call(gather_kernel, in_specs=[IN_SMEM, IN_SMEM, IN_HBM, IN_HBM]...  7.88 us
    pallas_call x1, Pallas kernels, zero_grads(): pl.pallas_call(zero_kernel, in_specs=[pl.BlockSpec(memory_space=pl.ANY)],...  6.7 us
    all_to_all x1, starting transfers between devices, ring_body(): sums = lax.all_to_all(sent, 'fsdp', split_axis=0, concat_axis=0, tiled=True)  5.56 us
    ppermute x3, starting transfers between devices, ring_body(): travelling = lax.ppermute(travelling, ('parts', 'fsdp'), ring)  5.4 us
    all_to_all x1, starting transfers between devices, ring_body(): lax.all_to_all(payload, 'fsdp', split_axis=0, concat_axis=0, tiled=True)  5 us
    pallas_call x1, Pallas kernels, adapter_terms(): pl.pallas_call(adapter_kernel, in_specs=[IN_HBM, IN_VMEM, IN_VMEM], out_s...  4.97 us
  transfers between devices with their start and end apart: 22, of which 6 were waited for; matrix products, arithmetic and copies ran while one was open for 0% of the time, Pallas kernels for 51%

profile of v6, /device:TPU:0, one launch (start us, length us, event | category | flops | bytes accessed | tf_op | source)
XLA Modules:
  0.0 91.4 jit_solution(18275097410270345194)
XLA Ops:
  0.6 3.1 %collective-permute-start = (bf16[512,1024]{1,0:T(8,128)(2,1)}, bf16[512,1024]{1,0:T(8,128)(2,1)}, u32[]{:S(2)}, u32[]{:S(2)}) collective-permute-start(bf16[512,1024]{1,0:T(8,128)(2,1)} %rest_0_.1), channel_id=1, source_target_pairs={{0,4},{1,3},{4,8},{5,1},{8,12},{9,5},{12,14},{13,9},{14,10},{15,13... | collective-permute-start | bytes 3145736 | tf_op jit(solution)/shard_map/ppermute | solution.py:632
  3.7 1.1 %mask_rows.1.cot = bf16[256,1024]{1,0:T(8,128)(2,1)S(1)} custom-call(s32[32]{0:T(128)} %live.1, bf16[256,1024]{1,0:T(8,128)(2,1)} %cot.1), custom_call_target="tpu_custom_call" | custom-call | flops 1 | bytes 1 | tf_op jit(solution)/shard_map/mask_rows/pallas_call | solution.py:94
  4.9 1.5 %collective-permute-start.1 = (bf16[256,1024]{1,0:T(8,128)(2,1)S(1)}, bf16[256,1024]{1,0:T(8,128)(2,1)S(1)}, u32[]{:S(2)}, u32[]{:S(2)}) collective-permute-start(bf16[256,1024]{1,0:T(8,128)(2,1)S(1)} %mask_rows.1.cot), channel_id=1, source_target_pairs={{0,16},{16,0},{1,17},{17,1},{2,18},{18,2},{3,19},{19,3},{4,20},{20... | collective-permute-start | bytes 1572872 | tf_op jit(solution)/shard_map/ppermute | solution.py:625
  6.4 7.9 %gather_rows.1 = bf16[16,144,128]{2,1,0:T(8,128)(2,1)} custom-call(s32[32]{0:T(128)} %adapter_hbm.1, s32[512]{0:T(512)} %storage_hbm.1, bf16[512,8192]{1,0:T(8,128)(2,1)} %down.1, bf16[512,1024]{1,0:T(8,128)(2,1)} %up.1), custom_call_target="tpu_custom_call" | custom-call | flops 1 | bytes 1 | tf_op jit(solution)/shard_map/gather_rows/pallas_call | solution.py:191
  14.2 5.0 %all-to-all-start = ((bf16[16,144,128]{2,1,0:T(8,128)(2,1)}), bf16[16,144,128]{2,1,0:T(8,128)(2,1)S(1)}, u32[]{:S(2)}, u32[]{:S(2)}) async-start(bf16[16,144,128]{2,1,0:T(8,128)(2,1)} %gather_rows.1), calls=%async_computation | async-start | bytes 1179648 | tf_op jit(solution)/shard_map/all_to_all | solution.py:630
  19.3 0.4 collective-permute-start.5
  19.7 0.0 collective-permute-done.1.refs_1_
  19.7 0.0 collective-permute-done.refs_3_.rest_0_
  19.7 1.7 %collective-permute-start.2 = (bf16[512,1024]{1,0:T(8,128)(2,1)}, bf16[512,1024]{1,0:T(8,128)(2,1)}, u32[]{:S(2)}, u32[]{:S(2)}) collective-permute-start(bf16[512,1024]{1,0:T(8,128)(2,1)} %collective-permute-done.refs_3_.rest_0_), channel_id=1, source_target_pairs={{0,4},{1,3},{4,8},{5,1},{8,12},{9,5},{12,14},{13,9},{14,10},{15,13... | collective-permute-start | bytes 3145736 | tf_op jit(solution)/shard_map/ppermute | solution.py:647
  21.3 0.1 collective-permute-start.3
  21.4 0.4 collective-permute-start.4
  21.9 1.4 %collective-permute-done.3.refs_0_ = bf16[256,1024]{1,0:T(8,128)(2,1)S(1)} collective-permute-done((bf16[256,1024]{1,0:T(8,128)(2,1)S(1)}, bf16[256,1024]{1,0:T(8,128)(2,1)S(1)}, u32[]{:S(2)}, u32[]{:S(2)}) %collective-permute-start.3) | collective-permute-done | bytes 524320 | tf_op jit(solution)/shard_map/ppermute | solution.py:624
  23.3 0.7 collective-permute-done.4.refs_2_
  24.0 3.3 %far_products.4 = (bf16[256,512]{1,0:T(8,128)(2,1)}, bf16[256,512]{1,0:T(8,128)(2,1)}, bf16[256,512]{1,0:T(8,128)(2,1)}) custom-call(bf16[256,1024]{1,0:T(8,128)(2,1)S(1)} %collective-permute-done.3.refs_0_, bf16[256,1024]{1,0:T(8,128)(2,1)S(1)} %collective-permute-done.1.refs_1_, bf16[256,1024]{1,0:T(8,128)(2,1)S(1)} %collective-permute-done.4.refs_2_, ...), custom_call_target="tpu_custom_call" | custom-call | flops 1 | bytes 1 | tf_op jit(solution)/shard_map/far_products/pallas_call | solution.py:497
  27.3 0.5 collective-permute-start.7
  27.8 1.0 %collective-permute-start.8 = (bf16[256,512]{1,0:T(8,128)(2,1)}, bf16[256,512]{1,0:T(8,128)(2,1)S(1)}, u32[]{:S(2)}, u32[]{:S(2)}) collective-permute-start(bf16[256,512]{1,0:T(8,128)(2,1)} %get-tuple-element.64), channel_id=1, source_target_pairs={{0,17},{1,16},{2,19},{3,18},{4,21},{5,20},{6,23},{7,22},{8,25},{9,... | collective-permute-start | bytes 786440 | tf_op jit(solution)/shard_map/ppermute | solution.py:619
  28.8 0.7 collective-permute-start.6
  29.5 6.7 %zero_grads.1 = (f32[512,8192]{1,0:T(8,128)}, f32[512,1024]{1,0:T(8,128)}) custom-call(bf16[256,512]{1,0:T(8,128)(2,1)} %get-tuple-element.57._), custom_call_target="tpu_custom_call" | custom-call | flops 1 | bytes 1 | tf_op jit(solution)/shard_map/zero_grads/pallas_call | solution.py:325
  36.2 0.0 all-to-all-done.recv
  36.2 5.0 %adapter_terms.1 = (bf16[16,144,128]{2,1,0:T(8,128)(2,1)}, bf16[256,128]{1,0:T(8,128)(2,1)S(1)}) custom-call(bf16[256,8192]{1,0:T(8,128)(2,1)} %x.1, bf16[256,1024]{1,0:T(8,128)(2,1)S(1)} %mask_rows.1.cot, bf16[16,144,128]{2,1,0:T(8,128)(2,1)S(1)} %all-to-all-done.recv), custom_call_target="tpu_custom_call" | custom-call | flops 1 | bytes 1 | tf_op jit(solution)/shard_map/adapter_terms/pallas_call | solution.py:289
  41.2 0.0 collective-permute-done.5.rest_1_
  41.2 2.9 %finish.5.rest_5_ = bf16[256,8192]{1,0:T(8,128)(2,1)} custom-call(bf16[256,1024]{1,0:T(8,128)(2,1)S(1)} %mask_rows.1.cot, bf16[256,128]{1,0:T(8,128)(2,1)S(1)} %get-tuple-element.62.g, bf16[16,144,128]{2,1,0:T(8,128)(2,1)S(1)} %all-to-all-done.recv, bf16[512,1024]{1,0:T(8,128)(2,1)} %rest_0_.1, bf16[512,1024]{1,0:T(8,128)(2,1)} %collective-permute-done.5.rest_1_), custom_call_target="tpu_custom_call" | custom-call | flops 1 | bytes 1 | tf_op jit(solution)/shard_map/finish/pallas_call | solution.py:563
  44.1 0.0 collective-permute-done.7.rest_3_
  44.1 0.0 copy-start.1
  44.2 0.0 collective-permute-done.8.rest_4_
  44.2 0.0 copy-start.2
  44.2 0.0 collective-permute-done.6.rest_2_
  44.2 0.0 copy-start.3
  44.2 0.0 collective-permute-done.2.refs_3_.rest_1_
  44.2 1.8 %collective-permute-start.9 = (bf16[512,1024]{1,0:T(8,128)(2,1)}, bf16[512,1024]{1,0:T(8,128)(2,1)S(1)}, u32[]{:S(2)}, u32[]{:S(2)}) collective-permute-start(bf16[512,1024]{1,0:T(8,128)(2,1)} %collective-permute-done.2.refs_3_.rest_1_), channel_id=1, source_target_pairs={{0,4},{1,3},{4,8},{5,1},{8,12},{9,5},{12,14},{13,9},{14,10},{15,13... | collective-permute-start | bytes 3145736 | tf_op jit(solution)/shard_map/ppermute | solution.py:647
  46.0 3.3 %far_products.5 = (bf16[256,512]{1,0:T(8,128)(2,1)}, bf16[256,512]{1,0:T(8,128)(2,1)}, bf16[256,512]{1,0:T(8,128)(2,1)}) custom-call(bf16[256,1024]{1,0:T(8,128)(2,1)S(1)} %collective-permute-done.3.refs_0_, bf16[256,1024]{1,0:T(8,128)(2,1)S(1)} %collective-permute-done.1.refs_1_, bf16[256,1024]{1,0:T(8,128)(2,1)S(1)} %collective-permute-done.4.refs_2_, ...), custom_call_target="tpu_custom_call" | custom-call | flops 1 | bytes 1 | tf_op jit(solution)/shard_map/far_products/pallas_call | solution.py:497
  49.4 0.2 collective-permute-start.11
  49.6 0.5 collective-permute-start.12
  50.1 1.5 %collective-permute-start.10 = (bf16[256,512]{1,0:T(8,128)(2,1)}, bf16[256,512]{1,0:T(8,128)(2,1)}, u32[]{:S(2)}, u32[]{:S(2)}) collective-permute-start(bf16[256,512]{1,0:T(8,128)(2,1)} %get-tuple-element.67), channel_id=1, source_target_pairs={{0,1},{1,0},{2,3},{3,2},{4,5},{5,4},{6,7},{7,6},{8,9},{9,8},{10,11... | collective-permute-start | bytes 786440 | tf_op jit(solution)/shard_map/ppermute | solution.py:617
  51.6 0.0 copy-done.1
  51.6 0.0 copy-done.2
  51.6 3.6 %finish.6.rest_4_ = bf16[256,8192]{1,0:T(8,128)(2,1)} custom-call(bf16[256,1024]{1,0:T(8,128)(2,1)S(1)} %mask_rows.1.cot, bf16[256,128]{1,0:T(8,128)(2,1)S(1)} %get-tuple-element.62.g, bf16[16,144,128]{2,1,0:T(8,128)(2,1)S(1)} %all-to-all-done.recv, bf16[512,1024]{1,0:T(8,128)(2,1)} %collective-permute-done.refs_3_.rest_0_, ...), custom_call_target="tpu_custom_call", output_to_operand_aliasing={{}: (8, {})} | custom-call | flops 1 | bytes 1 | tf_op jit(solution)/shard_map/finish/pallas_call | solution.py:563
  55.2 4.1 %collective-permute-done.9.refs_3_.rest_0_ = bf16[512,1024]{1,0:T(8,128)(2,1)S(1)} collective-permute-done((bf16[512,1024]{1,0:T(8,128)(2,1)}, bf16[512,1024]{1,0:T(8,128)(2,1)S(1)}, u32[]{:S(2)}, u32[]{:S(2)}) %collective-permute-start.9) | collective-permute-done | bytes 1048608 | tf_op jit(solution)/shard_map/ppermute | solution.py:647
  59.3 2.5 %far_products.6 = (bf16[256,512]{1,0:T(8,128)(2,1)}, bf16[256,512]{1,0:T(8,128)(2,1)}, bf16[256,512]{1,0:T(8,128)(2,1)}, bf16[256,1024]{1,0:T(8,128)(2,1)}) custom-call(bf16[256,1024]{1,0:T(8,128)(2,1)S(1)} %collective-permute-done.3.refs_0_, bf16[256,1024]{1,0:T(8,128)(2,1)S(1)} %collective-permute-done.1.refs_1_, ...), custom_call_target="tpu_custom_call" | custom-call | flops 1 | bytes 1 | tf_op jit(solution)/shard_map/far_products/pallas_call | solution.py:497
  61.7 1.0 %copy-done = bf16[512,1024]{1,0:T(8,128)(2,1)} copy-done((bf16[512,1024]{1,0:T(8,128)(2,1)}, bf16[512,1024]{1,0:T(8,128)(2,1)S(1)}, u32[]{:S(2)}) %copy-start) | copy-done | bytes 1048600
  62.7 0.0 collective-permute-done.11.rest_2_
  62.7 0.0 collective-permute-done.12.rest_3_
  62.7 0.0 collective-permute-done.10.rest_1_
  62.7 1.9 %collective-permute-start.13 = (bf16[256,1024]{1,0:T(8,128)(2,1)}, bf16[256,1024]{1,0:T(8,128)(2,1)}, u32[]{:S(2)}, u32[]{:S(2)}) collective-permute-start(bf16[256,1024]{1,0:T(8,128)(2,1)} %get-tuple-element.85), channel_id=1, source_target_pairs={{0,4},{1,3},{4,8},{5,1},{8,12},{9,5},{12,14},{13,9},{14,10},{15,13... | collective-permute-start | bytes 1572872 | tf_op jit(solution)/shard_map/ppermute | solution.py:655
  64.6 0.0 collective-permute-start.17
  64.6 0.9 collective-permute-start.18
  65.5 1.0 %collective-permute-start.19 = (bf16[256,512]{1,0:T(8,128)(2,1)}, bf16[256,512]{1,0:T(8,128)(2,1)}, u32[]{:S(2)}, u32[]{:S(2)}) collective-permute-start(bf16[256,512]{1,0:T(8,128)(2,1)} %get-tuple-element.92), channel_id=1, source_target_pairs={{0,17},{1,16},{2,19},{3,18},{4,21},{5,20},{6,23},{7,22},{8,25},{9,... | collective-permute-start | bytes 786440 | tf_op jit(solution)/shard_map/ppermute | solution.py:619
  66.5 5.6 %all-to-all-start.1 = ((bf16[16,144,128]{2,1,0:T(8,128)(2,1)}), bf16[16,144,128]{2,1,0:T(8,128)(2,1)S(1)}, u32[]{:S(2)}, u32[]{:S(2)}) async-start(bf16[16,144,128]{2,1,0:T(8,128)(2,1)} %get-tuple-element.84), calls=%async_computation.1 | async-start | bytes 1179648 | tf_op jit(solution)/shard_map/all_to_all | solution.py:657
  72.1 3.1 %finish.7.rest_4_ = bf16[256,8192]{1,0:T(8,128)(2,1)} custom-call(bf16[256,1024]{1,0:T(8,128)(2,1)S(1)} %mask_rows.1.cot, bf16[256,128]{1,0:T(8,128)(2,1)S(1)} %get-tuple-element.62.g, bf16[16,144,128]{2,1,0:T(8,128)(2,1)S(1)} %all-to-all-done.recv, bf16[512,1024]{1,0:T(8,128)(2,1)} %copy-done, ...), custom_call_target="tpu_custom_call", output_to_operand_aliasing={{}: (7, {})} | custom-call | flops 1 | bytes 1 | tf_op jit(solution)/shard_map/finish/pallas_call | solution.py:563
  75.2 0.0 collective-permute-done.13.refs_3_.rest_0_
  75.2 2.4 %far_products.7 = (bf16[256,256]{1,0:T(8,128)(2,1)}, bf16[256,256]{1,0:T(8,128)(2,1)}, bf16[256,256]{1,0:T(8,128)(2,1)}) custom-call(bf16[256,1024]{1,0:T(8,128)(2,1)S(1)} %collective-permute-done.3.refs_0_, bf16[256,1024]{1,0:T(8,128)(2,1)S(1)} %collective-permute-done.1.refs_1_, bf16[256,1024]{1,0:T(8,128)(2,1)S(1)} %collective-permute-done.4.refs_2_, ...), custom_call_target="tpu_custom_call" | custom-call | flops 1 | bytes 1 | tf_op jit(solution)/shard_map/far_products/pallas_call | solution.py:497
  77.6 0.5 collective-permute-start.14
  78.0 0.3 collective-permute-start.15
  78.4 0.0 collective-permute-done.17.rest_1_
  78.4 1.2 %collective-permute-start.16 = (bf16[256,256]{1,0:T(8,128)(2,1)}, bf16[256,256]{1,0:T(8,128)(2,1)S(1)}, u32[]{:S(2)}, u32[]{:S(2)}) collective-permute-start(bf16[256,256]{1,0:T(8,128)(2,1)} %get-tuple-element.97), channel_id=1, source_target_pairs={{0,17},{1,16},{2,19},{3,18},{4,21},{5,20},{6,23},{7,22},{8,25},{9,... | collective-permute-start | bytes 393224 | tf_op jit(solution)/shard_map/ppermute | solution.py:619
  79.5 0.0 collective-permute-done.18.rest_2_
  79.5 0.0 collective-permute-done.19.rest_3_
  79.5 2.9 %finish.8.rest_3_ = bf16[256,8192]{1,0:T(8,128)(2,1)} custom-call(bf16[256,1024]{1,0:T(8,128)(2,1)S(1)} %mask_rows.1.cot, bf16[256,128]{1,0:T(8,128)(2,1)S(1)} %get-tuple-element.62.g, bf16[16,144,128]{2,1,0:T(8,128)(2,1)S(1)} %all-to-all-done.recv, bf16[256,1024]{1,0:T(8,128)(2,1)} %collective-permute-done.13.refs_3_.rest_0_, ...), custom_call_target="tpu_custom_call", output_to_operand_aliasing={{}: (7, {})} | custom-call | flops 10000000000 | bytes 1 | tf_op jit(solution)/shard_map/finish/pallas_call | solution.py:563
  82.4 0.0 collective-permute-done.14.rest_0_
  82.5 2.1 %collective-permute-done.15.rest_1_ = bf16[256,256]{1,0:T(8,128)(2,1)S(1)} collective-permute-done((bf16[256,256]{1,0:T(8,128)(2,1)}, bf16[256,256]{1,0:T(8,128)(2,1)S(1)}, u32[]{:S(2)}, u32[]{:S(2)}) %collective-permute-start.15) | collective-permute-done | bytes 131104 | tf_op jit(solution)/shard_map/ppermute | solution.py:618
  84.6 1.2 %collective-permute-done.16.rest_2_ = bf16[256,256]{1,0:T(8,128)(2,1)S(1)} collective-permute-done((bf16[256,256]{1,0:T(8,128)(2,1)}, bf16[256,256]{1,0:T(8,128)(2,1)S(1)}, u32[]{:S(2)}, u32[]{:S(2)}) %collective-permute-start.16) | collective-permute-done | bytes 131104 | tf_op jit(solution)/shard_map/ppermute | solution.py:619
  85.7 1.7 %finish.9 = bf16[256,8192]{1,0:T(8,128)(2,1)} custom-call(bf16[256,1024]{1,0:T(8,128)(2,1)S(1)} %mask_rows.1.cot, bf16[256,128]{1,0:T(8,128)(2,1)S(1)} %get-tuple-element.62.g, bf16[16,144,128]{2,1,0:T(8,128)(2,1)S(1)} %all-to-all-done.recv, bf16[256,256]{1,0:T(8,128)(2,1)S(1)} %collective-permute-done.14.rest_0_, ...), custom_call_target="tpu_custom_call", output_to_operand_aliasing={{}: (6, {})} | custom-call | flops 1 | bytes 1 | tf_op jit(solution)/shard_map/finish/pallas_call | solution.py:563
  87.5 0.1 all-to-all-done.1.recv
  87.6 3.6 %scatter_rows.1 = (f32[512,8192]{1,0:T(8,128)}, f32[512,1024]{1,0:T(8,128)}) custom-call(s32[32]{0:T(128)} %adapter_hbm.1, s32[512]{0:T(512)} %storage_hbm.1, bf16[16,144,128]{2,1,0:T(8,128)(2,1)S(1)} %all-to-all-done.1.recv, f32[512,8192]{1,0:T(8,128)} %get-tuple-element.101._down, ...), custom_call_target="tpu_custom_call", output_to_operand_aliasing={{0}: (3, {}), {1}: (4, {})} | custom-call | flops 1 | bytes 1 | tf_op jit(solution)/shard_map/scatter_rows/pallas_call | solution.py:437
  (2 shorter events, 0.0 us)
Async XLA Ops:
  0.6 19.0 %collective-permute-start = (bf16[512,1024]{1,0:T(8,128)(2,1)}, bf16[512,1024]{1,0:T(8,128)(2,1)}, u32[]{:S(2)}, u32[]{:S(2)}) collective-permute-start(bf16[512,1024]{1,0:T(8,128)(2,1)} %rest_0_.1), channel_id=1, source_target_pairs={{0,4},{1,3},{4,8},{5,1},{8,12},{9,5},{12,14},{13,9},{14,10},{15,13... | collective-permute-start | bytes 3145736 | tf_op jit(solution)/shard_map/ppermute | solution.py:632
  4.9 14.8 %collective-permute-start.1 = (bf16[256,1024]{1,0:T(8,128)(2,1)S(1)}, bf16[256,1024]{1,0:T(8,128)(2,1)S(1)}, u32[]{:S(2)}, u32[]{:S(2)}) collective-permute-start(bf16[256,1024]{1,0:T(8,128)(2,1)S(1)} %mask_rows.1.cot), channel_id=1, source_target_pairs={{0,16},{16,0},{1,17},{17,1},{2,18},{18,2},{3,19},{19,3},{4,20},{20... | collective-permute-start | bytes 1572872 | tf_op jit(solution)/shard_map/ppermute | solution.py:625
  14.2 22.0 %all-to-all-start = ((bf16[16,144,128]{2,1,0:T(8,128)(2,1)}), bf16[16,144,128]{2,1,0:T(8,128)(2,1)S(1)}, u32[]{:S(2)}, u32[]{:S(2)}) async-start(bf16[16,144,128]{2,1,0:T(8,128)(2,1)} %gather_rows.1), calls=%async_computation | async-start | bytes 1179648 | tf_op jit(solution)/shard_map/all_to_all | solution.py:630
  19.3 22.0 %collective-permute-start.5 = (bf16[512,1024]{1,0:T(8,128)(2,1)}, bf16[512,1024]{1,0:T(8,128)(2,1)}, u32[]{:S(2)}, u32[]{:S(2)}) collective-permute-start(bf16[512,1024]{1,0:T(8,128)(2,1)} %rest_0_.1), channel_id=1, source_target_pairs={{0,1},{1,0},{2,3},{3,2},{4,5},{5,4},{6,7},{7,6},{8,9},{9,8},{10,11... | collective-permute-start | bytes 3145736 | tf_op jit(solution)/shard_map/ppermute | solution.py:622
  19.7 24.5 %collective-permute-start.2 = (bf16[512,1024]{1,0:T(8,128)(2,1)}, bf16[512,1024]{1,0:T(8,128)(2,1)}, u32[]{:S(2)}, u32[]{:S(2)}) collective-permute-start(bf16[512,1024]{1,0:T(8,128)(2,1)} %collective-permute-done.refs_3_.rest_0_), channel_id=1, source_target_pairs={{0,4},{1,3},{4,8},{5,1},{8,12},{9,5},{12,14},{13,9},{14,10},{15,13... | collective-permute-start | bytes 3145736 | tf_op jit(solution)/shard_map/ppermute | solution.py:647
  21.3 1.9 %collective-permute-start.3 = (bf16[256,1024]{1,0:T(8,128)(2,1)S(1)}, bf16[256,1024]{1,0:T(8,128)(2,1)S(1)}, u32[]{:S(2)}, u32[]{:S(2)}) collective-permute-start(bf16[256,1024]{1,0:T(8,128)(2,1)S(1)} %mask_rows.1.cot), channel_id=1, source_target_pairs={{0,1},{1,0},{2,3},{3,2},{4,5},{5,4},{6,7},{7,6},{8,9},{9,8},{10,11... | collective-permute-start | bytes 1572872 | tf_op jit(solution)/shard_map/ppermute | solution.py:624
  21.4 2.6 %collective-permute-start.4 = (bf16[256,1024]{1,0:T(8,128)(2,1)S(1)}, bf16[256,1024]{1,0:T(8,128)(2,1)S(1)}, u32[]{:S(2)}, u32[]{:S(2)}) collective-permute-start(bf16[256,1024]{1,0:T(8,128)(2,1)S(1)} %collective-permute-done.1.refs_1_), channel_id=1, source_target_pairs={{0,1},{1,0},{2,3},{3,2},{4,5},{5,4},{6,7},{7,6},{8,9},{9,8},{10,11... | collective-permute-start | bytes 1572872 | tf_op jit(solution)/shard_map/ppermute | solution.py:639
  27.3 16.8 %collective-permute-start.7 = (bf16[256,512]{1,0:T(8,128)(2,1)}, bf16[256,512]{1,0:T(8,128)(2,1)S(1)}, u32[]{:S(2)}, u32[]{:S(2)}) collective-permute-start(bf16[256,512]{1,0:T(8,128)(2,1)} %get-tuple-element.63), channel_id=1, source_target_pairs={{0,16},{16,0},{1,17},{17,1},{2,18},{18,2},{3,19},{19,3},{4,20},{20... | collective-permute-start | bytes 786440 | tf_op jit(solution)/shard_map/ppermute | solution.py:618
  27.8 16.4 %collective-permute-start.8 = (bf16[256,512]{1,0:T(8,128)(2,1)}, bf16[256,512]{1,0:T(8,128)(2,1)S(1)}, u32[]{:S(2)}, u32[]{:S(2)}) collective-permute-start(bf16[256,512]{1,0:T(8,128)(2,1)} %get-tuple-element.64), channel_id=1, source_target_pairs={{0,17},{1,16},{2,19},{3,18},{4,21},{5,20},{6,23},{7,22},{8,25},{9,... | collective-permute-start | bytes 786440 | tf_op jit(solution)/shard_map/ppermute | solution.py:619
  28.8 15.3 %collective-permute-start.6 = (bf16[256,512]{1,0:T(8,128)(2,1)}, bf16[256,512]{1,0:T(8,128)(2,1)S(1)}, u32[]{:S(2)}, u32[]{:S(2)}) collective-permute-start(bf16[256,512]{1,0:T(8,128)(2,1)} %get-tuple-element.57._), channel_id=1, source_target_pairs={{0,1},{1,0},{2,3},{3,2},{4,5},{5,4},{6,7},{7,6},{8,9},{9,8},{10,11... | collective-permute-start | bytes 786440 | tf_op jit(solution)/shard_map/ppermute | solution.py:617
  44.1 7.4 %copy-start.1 = (bf16[256,512]{1,0:T(8,128)(2,1)}, bf16[256,512]{1,0:T(8,128)(2,1)S(1)}, u32[]{:S(2)}) copy-start(bf16[256,512]{1,0:T(8,128)(2,1)S(1)} %collective-permute-done.7.rest_3_) | copy-start | bytes 786436
  44.2 7.4 %copy-start.2 = (bf16[256,512]{1,0:T(8,128)(2,1)}, bf16[256,512]{1,0:T(8,128)(2,1)S(1)}, u32[]{:S(2)}) copy-start(bf16[256,512]{1,0:T(8,128)(2,1)S(1)} %collective-permute-done.8.rest_4_) | copy-start | bytes 786436
  44.2 7.4 %copy-start.3 = (bf16[256,512]{1,0:T(8,128)(2,1)}, bf16[256,512]{1,0:T(8,128)(2,1)S(1)}, u32[]{:S(2)}) copy-start(bf16[256,512]{1,0:T(8,128)(2,1)S(1)} %collective-permute-done.6.rest_2_) | copy-start | bytes 786436
  44.2 15.1 %collective-permute-start.9 = (bf16[512,1024]{1,0:T(8,128)(2,1)}, bf16[512,1024]{1,0:T(8,128)(2,1)S(1)}, u32[]{:S(2)}, u32[]{:S(2)}) collective-permute-start(bf16[512,1024]{1,0:T(8,128)(2,1)} %collective-permute-done.2.refs_3_.rest_1_), channel_id=1, source_target_pairs={{0,4},{1,3},{4,8},{5,1},{8,12},{9,5},{12,14},{13,9},{14,10},{15,13... | collective-permute-start | bytes 3145736 | tf_op jit(solution)/shard_map/ppermute | solution.py:647
  49.4 13.4 %collective-permute-start.11 = (bf16[256,512]{1,0:T(8,128)(2,1)}, bf16[256,512]{1,0:T(8,128)(2,1)}, u32[]{:S(2)}, u32[]{:S(2)}) collective-permute-start(bf16[256,512]{1,0:T(8,128)(2,1)} %get-tuple-element.79), channel_id=1, source_target_pairs={{0,16},{16,0},{1,17},{17,1},{2,18},{18,2},{3,19},{19,3},{4,20},{20... | collective-permute-start | bytes 786440 | tf_op jit(solution)/shard_map/ppermute | solution.py:618
  49.6 13.2 %collective-permute-start.12 = (bf16[256,512]{1,0:T(8,128)(2,1)}, bf16[256,512]{1,0:T(8,128)(2,1)}, u32[]{:S(2)}, u32[]{:S(2)}) collective-permute-start(bf16[256,512]{1,0:T(8,128)(2,1)} %get-tuple-element.80), channel_id=1, source_target_pairs={{0,17},{1,16},{2,19},{3,18},{4,21},{5,20},{6,23},{7,22},{8,25},{9,... | collective-permute-start | bytes 786440 | tf_op jit(solution)/shard_map/ppermute | solution.py:619
  50.1 12.7 %collective-permute-start.10 = (bf16[256,512]{1,0:T(8,128)(2,1)}, bf16[256,512]{1,0:T(8,128)(2,1)}, u32[]{:S(2)}, u32[]{:S(2)}) collective-permute-start(bf16[256,512]{1,0:T(8,128)(2,1)} %get-tuple-element.67), channel_id=1, source_target_pairs={{0,1},{1,0},{2,3},{3,2},{4,5},{5,4},{6,7},{7,6},{8,9},{9,8},{10,11... | collective-permute-start | bytes 786440 | tf_op jit(solution)/shard_map/ppermute | solution.py:617
  61.7 1.0 %copy-start = (bf16[512,1024]{1,0:T(8,128)(2,1)}, bf16[512,1024]{1,0:T(8,128)(2,1)S(1)}, u32[]{:S(2)}) copy-start(bf16[512,1024]{1,0:T(8,128)(2,1)S(1)} %collective-permute-done.9.refs_3_.rest_0_) | copy-start | bytes 3145732
  62.7 12.4 %collective-permute-start.13 = (bf16[256,1024]{1,0:T(8,128)(2,1)}, bf16[256,1024]{1,0:T(8,128)(2,1)}, u32[]{:S(2)}, u32[]{:S(2)}) collective-permute-start(bf16[256,1024]{1,0:T(8,128)(2,1)} %get-tuple-element.85), channel_id=1, source_target_pairs={{0,4},{1,3},{4,8},{5,1},{8,12},{9,5},{12,14},{13,9},{14,10},{15,13... | collective-permute-start | bytes 1572872 | tf_op jit(solution)/shard_map/ppermute | solution.py:655
  64.6 13.7 %collective-permute-start.17 = (bf16[256,512]{1,0:T(8,128)(2,1)}, bf16[256,512]{1,0:T(8,128)(2,1)}, u32[]{:S(2)}, u32[]{:S(2)}) collective-permute-start(bf16[256,512]{1,0:T(8,128)(2,1)} %get-tuple-element.90), channel_id=1, source_target_pairs={{0,1},{1,0},{2,3},{3,2},{4,5},{5,4},{6,7},{7,6},{8,9},{9,8},{10,11... | collective-permute-start | bytes 786440 | tf_op jit(solution)/shard_map/ppermute | solution.py:617
  64.6 14.9 %collective-permute-start.18 = (bf16[256,512]{1,0:T(8,128)(2,1)}, bf16[256,512]{1,0:T(8,128)(2,1)}, u32[]{:S(2)}, u32[]{:S(2)}) collective-permute-start(bf16[256,512]{1,0:T(8,128)(2,1)} %get-tuple-element.91), channel_id=1, source_target_pairs={{0,16},{16,0},{1,17},{17,1},{2,18},{18,2},{3,19},{19,3},{4,20},{20... | collective-permute-start | bytes 786440 | tf_op jit(solution)/shard_map/ppermute | solution.py:618
  65.5 14.0 %collective-permute-start.19 = (bf16[256,512]{1,0:T(8,128)(2,1)}, bf16[256,512]{1,0:T(8,128)(2,1)}, u32[]{:S(2)}, u32[]{:S(2)}) collective-permute-start(bf16[256,512]{1,0:T(8,128)(2,1)} %get-tuple-element.92), channel_id=1, source_target_pairs={{0,17},{1,16},{2,19},{3,18},{4,21},{5,20},{6,23},{7,22},{8,25},{9,... | collective-permute-start | bytes 786440 | tf_op jit(solution)/shard_map/ppermute | solution.py:619
  66.5 21.1 %all-to-all-start.1 = ((bf16[16,144,128]{2,1,0:T(8,128)(2,1)}), bf16[16,144,128]{2,1,0:T(8,128)(2,1)S(1)}, u32[]{:S(2)}, u32[]{:S(2)}) async-start(bf16[16,144,128]{2,1,0:T(8,128)(2,1)} %get-tuple-element.84), calls=%async_computation.1 | async-start | bytes 1179648 | tf_op jit(solution)/shard_map/all_to_all | solution.py:657
  77.6 4.9 %collective-permute-start.14 = (bf16[256,256]{1,0:T(8,128)(2,1)}, bf16[256,256]{1,0:T(8,128)(2,1)S(1)}, u32[]{:S(2)}, u32[]{:S(2)}) collective-permute-start(bf16[256,256]{1,0:T(8,128)(2,1)} %get-tuple-element.95), channel_id=1, source_target_pairs={{0,1},{1,0},{2,3},{3,2},{4,5},{5,4},{6,7},{7,6},{8,9},{9,8},{10,11... | collective-permute-start | bytes 393224 | tf_op jit(solution)/shard_map/ppermute | solution.py:617
  78.0 6.6 %collective-permute-start.15 = (bf16[256,256]{1,0:T(8,128)(2,1)}, bf16[256,256]{1,0:T(8,128)(2,1)S(1)}, u32[]{:S(2)}, u32[]{:S(2)}) collective-permute-start(bf16[256,256]{1,0:T(8,128)(2,1)} %get-tuple-element.96), channel_id=1, source_target_pairs={{0,16},{16,0},{1,17},{17,1},{2,18},{18,2},{3,19},{19,3},{4,20},{20... | collective-permute-start | bytes 393224 | tf_op jit(solution)/shard_map/ppermute | solution.py:618
  78.4 7.4 %collective-permute-start.16 = (bf16[256,256]{1,0:T(8,128)(2,1)}, bf16[256,256]{1,0:T(8,128)(2,1)S(1)}, u32[]{:S(2)}, u32[]{:S(2)}) collective-permute-start(bf16[256,256]{1,0:T(8,128)(2,1)} %get-tuple-element.97), channel_id=1, source_target_pairs={{0,17},{1,16},{2,19},{3,18},{4,21},{5,20},{6,23},{7,22},{8,25},{9,... | collective-permute-start | bytes 393224 | tf_op jit(solution)/shard_map/ppermute | solution.py:619

commit v7 on v6

--- a/solution.py
+++ b/solution.py
@@ -465,7 +465,7 @@
 
 def far_kernel(count, handed, *refs):
     cots, weight, outs = refs[:count], refs[count], refs[count + 1 : 2 * count + 1]
-    wbuf, buffer, wsem, sems, hsem = refs[2 * count + 1 + handed :]
+    wbuf, wsem, sems, hsem, *buffers = refs[2 * count + 1 + handed :]
     tile = wbuf.shape[1]
     loads = [
         pltpu.make_async_copy(weight.at[i * tile : (i + 1) * tile, :], wbuf.at[i], wsem.at[i])
@@ -473,12 +473,12 @@
     ]
     for copy in loads:
         copy.start()
-    stores = [pltpu.make_async_copy(buffer.at[n], outs[n], sems.at[n]) for n in range(count)]
+    stores = [pltpu.make_async_copy(buffers[n], outs[n], sems.at[n]) for n in range(count)]
     for i, load in enumerate(loads):
         load.wait()
         for n, cot in enumerate(cots):
-            value = dot_t(cot[...], wbuf[i]).astype(buffer.dtype)
-            buffer[n, :, i * tile : (i + 1) * tile] = value
+            value = dot_t(cot[...], wbuf[i]).astype(buffers[n].dtype)
+            buffers[n][:, i * tile : (i + 1) * tile] = value
             if i == len(loads) - 1:
                 stores[n].start()
     if handed:
@@ -489,23 +489,25 @@
         copy.wait()
 
 
-def far_products(cots, weight, pin=in_hbm, handed=False):
+def far_products(cots, weight, pin=in_hbm, handed=False, owned=False):
     count, rows, tile = len(cots), cots[0].shape[0], 256
     span, depth = weight.shape
-    shape = pltpu.HBM((rows, span), jnp.bfloat16)
+    types = [jnp.bfloat16] * count
+    if owned:
+        types[-1] = jnp.float32
     half = [pltpu.HBM((tile, depth), weight.dtype)] if handed else []
     return pl.pallas_call(
         functools.partial(far_kernel, count, len(half)),
         in_specs=[IN_VMEM] * count + [pl.BlockSpec(memory_space=pl.ANY)],
         out_specs=[IN_HBM] * (count + len(half)),
-        out_shape=[shape] * count + half,
+        out_shape=[pltpu.HBM((rows, span), kind) for kind in types] + half,
         scratch_shapes=[
             pltpu.VMEM((span // tile, tile, depth), weight.dtype),
-            pltpu.VMEM((count, rows, span), jnp.bfloat16),
             pltpu.SemaphoreType.DMA((span // tile,)),
             pltpu.SemaphoreType.DMA((count,)),
             pltpu.SemaphoreType.DMA,
-        ],
+        ]
+        + [pltpu.VMEM((rows, span), kind) for kind in types],
         compiler_params=PARAMS,
         cost_estimate=SMALL,
         name="far_products",
@@ -646,15 +648,20 @@
         if step < steps - 2:
             travelling = lax.ppermute(travelling, ("parts", "fsdp"), ring)
         pin = as_it_is if step >= steps - 2 else in_hbm
-        products = far_products(cots, pieces[step], pin, step == steps - 2)
+        owned = step >= steps - 2
+        if owned:
+            cots = (*cots[:3], masked)
+        products = far_products(cots, pieces[step], pin, step == steps - 2, owned)
         if step == steps - 2:
-            *products, travelling = products
+            *products, own, travelling = products
             travelling, products, out, received[-1] = after(
                 travelling, products, out, received[-1]
             )
             travelling = lax.ppermute(travelling, ("parts", "fsdp"), ring)
             sent, products = after(sent, products)
             sums = lax.all_to_all(sent, "fsdp", split_axis=0, concat_axis=0, tiled=True)
+        if step == steps - 1:
+            *products, last_own = products
         received.append(cross(products))
         if step == 0:
             grads = zero_grads(products[0], adapter_down_weights.shape, adapter_up_weights.shape)
@@ -670,15 +677,12 @@
         if step == steps - 2:
             out, _ = after(out, products)
             at = [firsts[step]] + [first + i for first in firsts[1:step] for i in range(1, 4)]
-            early = sum(received[1:step], ())
-            piece = pieces[step : step + 1]
-            out = finish(devices, at, masked, piece, early, g, recv, out, width, shard)
+            early = (own, *sum(received[1:step], ()))
+            out = finish(devices, at, masked, (), early, g, recv, out, width, shard)
             travelling, out = after(travelling, out)
     at = firsts[-1:] + [firsts[-2] + i for i in range(1, 4)]
-    piece = pieces[-1:]
-    out = finish(
-        devices, at, masked, piece, received[-2], g, recv, out, width, shard, as_it_is, LONGER
-    )
+    late = (last_own, *received[-2])
+    out = finish(devices, at, masked, (), late, g, recv, out, width, shard, in_hbm, LONGER)
     at = [firsts[-1] + i for i in range(1, 4)]
     out = finish(devices, at, masked, (), received[-1], g, recv, out, width, shard, as_it_is)
     sums, out = after(sums, out)

time: 92.3 us -> 91.2 us (0.988)
  local copies, waits for them, and re-layouts: 0.99 us -> 0.01 us
    ppermute x4, starting transfers between devices: 3.67 us -> 2.27 us  [cross(): lax.ppermute(products[2], ('parts', 'fsdp'), diagonal)]
    unnamed x8 -> x6, local copies, waits for them, and re-layouts: 0.99 us -> 0.01 us
    pallas_call x5, Pallas kernels: 14.2 us -> 13.2 us  [finish(): pl.pallas_call(kernel, in_specs=[IN_VMEM] * 3 + [pl.BlockSpec(memory_spac...]
where the time goes in v7:
time: 91.2 us; the launch traced here: 90.4 us
  Pallas kernels  49.3 us (54%)
  starting transfers between devices  29.6 us (32%)
  waiting for transfers between devices  10.5 us (12%)
  between operations  1.04 us (1%)
    pallas_call x5, Pallas kernels, finish(): pl.pallas_call(kernel, in_specs=[IN_VMEM] * 3 + [pl.BlockSpec(memory_spac...  13.2 us
    pallas_call x4, Pallas kernels, far_products(): pl.pallas_call(functools.partial(far_kernel, count, len(half)), in_specs=...  12 us
    pallas_call x1, Pallas kernels, gather_rows(): pl.pallas_call(gather_kernel, in_specs=[IN_SMEM, IN_SMEM, IN_HBM, IN_HBM]...  7.68 us
    pallas_call x1, Pallas kernels, zero_grads(): pl.pallas_call(zero_kernel, in_specs=[pl.BlockSpec(memory_space=pl.ANY)],...  6.7 us
    all_to_all x1, starting transfers between devices, ring_body(): sums = lax.all_to_all(sent, 'fsdp', split_axis=0, concat_axis=0, tiled=True)  5.39 us
    ppermute x3, starting transfers between devices, ring_body(): travelling = lax.ppermute(travelling, ('parts', 'fsdp'), ring)  5.36 us
    all_to_all x1, starting transfers between devices, ring_body(): lax.all_to_all(payload, 'fsdp', split_axis=0, concat_axis=0, tiled=True)  5 us
    pallas_call x1, Pallas kernels, adapter_terms(): pl.pallas_call(adapter_kernel, in_specs=[IN_HBM, IN_VMEM, IN_VMEM], out_s...  4.98 us
  transfers between devices with their start and end apart: 22, of which 6 were waited for; matrix products, arithmetic and copies ran while one was open for 0% of the time, Pallas kernels for 51%

profile of v7, /device:TPU:0, one launch (start us, length us, event | category | flops | bytes accessed | tf_op | source)
XLA Modules:
  0.0 90.4 jit_solution(2699098482272807861)
XLA Ops:
  0.6 3.1 %collective-permute-start = (bf16[512,1024]{1,0:T(8,128)(2,1)}, bf16[512,1024]{1,0:T(8,128)(2,1)}, u32[]{:S(2)}, u32[]{:S(2)}) collective-permute-start(bf16[512,1024]{1,0:T(8,128)(2,1)} %rest_0_.1), channel_id=1, source_target_pairs={{0,4},{1,3},{4,8},{5,1},{8,12},{9,5},{12,14},{13,9},{14,10},{15,13... | collective-permute-start | bytes 3145736 | tf_op jit(solution)/shard_map/ppermute | solution.py:634
  3.7 1.1 %mask_rows.1.cot.refs_3_ = bf16[256,1024]{1,0:T(8,128)(2,1)S(1)} custom-call(s32[32]{0:T(128)} %live.1, bf16[256,1024]{1,0:T(8,128)(2,1)} %cot.1), custom_call_target="tpu_custom_call" | custom-call | flops 1 | bytes 1 | tf_op jit(solution)/shard_map/mask_rows/pallas_call | solution.py:94
  4.9 1.5 %collective-permute-start.1 = (bf16[256,1024]{1,0:T(8,128)(2,1)S(1)}, bf16[256,1024]{1,0:T(8,128)(2,1)S(1)}, u32[]{:S(2)}, u32[]{:S(2)}) collective-permute-start(bf16[256,1024]{1,0:T(8,128)(2,1)S(1)} %mask_rows.1.cot.refs_3_), channel_id=1, source_target_pairs={{0,16},{16,0},{1,17},{17,1},{2,18},{18,2},{3,19},{19,3},{4,20},{20... | collective-permute-start | bytes 1572872 | tf_op jit(solution)/shard_map/ppermute | solution.py:627
  6.4 7.7 %gather_rows.1 = bf16[16,144,128]{2,1,0:T(8,128)(2,1)} custom-call(s32[32]{0:T(128)} %adapter_hbm.1, s32[512]{0:T(512)} %storage_hbm.1, bf16[512,8192]{1,0:T(8,128)(2,1)} %down.1, bf16[512,1024]{1,0:T(8,128)(2,1)} %up.1), custom_call_target="tpu_custom_call" | custom-call | flops 1 | bytes 1 | tf_op jit(solution)/shard_map/gather_rows/pallas_call | solution.py:191
  14.1 5.0 %all-to-all-start = ((bf16[16,144,128]{2,1,0:T(8,128)(2,1)}), bf16[16,144,128]{2,1,0:T(8,128)(2,1)S(1)}, u32[]{:S(2)}, u32[]{:S(2)}) async-start(bf16[16,144,128]{2,1,0:T(8,128)(2,1)} %gather_rows.1), calls=%async_computation | async-start | bytes 1179648 | tf_op jit(solution)/shard_map/all_to_all | solution.py:632
  19.1 0.4 collective-permute-start.5
  19.5 0.0 collective-permute-done.1.refs_1_
  19.5 0.0 collective-permute-done.refs_3_.rest_0_
  19.5 1.7 %collective-permute-start.2 = (bf16[512,1024]{1,0:T(8,128)(2,1)}, bf16[512,1024]{1,0:T(8,128)(2,1)}, u32[]{:S(2)}, u32[]{:S(2)}) collective-permute-start(bf16[512,1024]{1,0:T(8,128)(2,1)} %collective-permute-done.refs_3_.rest_0_), channel_id=1, source_target_pairs={{0,4},{1,3},{4,8},{5,1},{8,12},{9,5},{12,14},{13,9},{14,10},{15,13... | collective-permute-start | bytes 3145736 | tf_op jit(solution)/shard_map/ppermute | solution.py:649
  21.1 0.1 collective-permute-start.3
  21.2 0.4 collective-permute-start.4
  21.7 1.4 %collective-permute-done.3.refs_0_ = bf16[256,1024]{1,0:T(8,128)(2,1)S(1)} collective-permute-done((bf16[256,1024]{1,0:T(8,128)(2,1)S(1)}, bf16[256,1024]{1,0:T(8,128)(2,1)S(1)}, u32[]{:S(2)}, u32[]{:S(2)}) %collective-permute-start.3) | collective-permute-done | bytes 524320 | tf_op jit(solution)/shard_map/ppermute | solution.py:626
  23.1 0.7 collective-permute-done.4.refs_2_
  23.8 3.3 %far_products.4 = (bf16[256,512]{1,0:T(8,128)(2,1)}, bf16[256,512]{1,0:T(8,128)(2,1)}, bf16[256,512]{1,0:T(8,128)(2,1)}) custom-call(bf16[256,1024]{1,0:T(8,128)(2,1)S(1)} %collective-permute-done.3.refs_0_, bf16[256,1024]{1,0:T(8,128)(2,1)S(1)} %collective-permute-done.1.refs_1_, bf16[256,1024]{1,0:T(8,128)(2,1)S(1)} %collective-permute-done.4.refs_2_, ...), custom_call_target="tpu_custom_call" | custom-call | flops 1 | bytes 1 | tf_op jit(solution)/shard_map/far_products/pallas_call | solution.py:499
  27.1 0.6 collective-permute-start.7
  27.7 0.9 %collective-permute-start.8 = (bf16[256,512]{1,0:T(8,128)(2,1)}, bf16[256,512]{1,0:T(8,128)(2,1)S(1)}, u32[]{:S(2)}, u32[]{:S(2)}) collective-permute-start(bf16[256,512]{1,0:T(8,128)(2,1)} %get-tuple-element.66), channel_id=1, source_target_pairs={{0,17},{1,16},{2,19},{3,18},{4,21},{5,20},{6,23},{7,22},{8,25},{9,... | collective-permute-start | bytes 786440 | tf_op jit(solution)/shard_map/ppermute | solution.py:621
  28.7 0.7 collective-permute-start.6
  29.3 6.7 %zero_grads.1 = (f32[512,8192]{1,0:T(8,128)}, f32[512,1024]{1,0:T(8,128)}) custom-call(bf16[256,512]{1,0:T(8,128)(2,1)} %get-tuple-element.59._), custom_call_target="tpu_custom_call" | custom-call | flops 1 | bytes 1 | tf_op jit(solution)/shard_map/zero_grads/pallas_call | solution.py:325
  36.0 0.0 all-to-all-done.recv
  36.1 5.0 %adapter_terms.1 = (bf16[16,144,128]{2,1,0:T(8,128)(2,1)}, bf16[256,128]{1,0:T(8,128)(2,1)S(1)}) custom-call(bf16[256,8192]{1,0:T(8,128)(2,1)} %x.1, bf16[256,1024]{1,0:T(8,128)(2,1)S(1)} %mask_rows.1.cot.refs_3_, bf16[16,144,128]{2,1,0:T(8,128)(2,1)S(1)} %all-to-all-done.recv), custom_call_target="tpu_custom_call" | custom-call | flops 1 | bytes 1 | tf_op jit(solution)/shard_map/adapter_terms/pallas_call | solution.py:289
  41.0 0.0 collective-permute-done.5.rest_1_
  41.0 2.9 %finish.5.rest_5_ = bf16[256,8192]{1,0:T(8,128)(2,1)} custom-call(bf16[256,1024]{1,0:T(8,128)(2,1)S(1)} %mask_rows.1.cot.refs_3_, bf16[256,128]{1,0:T(8,128)(2,1)S(1)} %get-tuple-element.64.g, bf16[16,144,128]{2,1,0:T(8,128)(2,1)S(1)} %all-to-all-done.recv, bf16[512,1024]{1,0:T(8,128)(2,1)} %rest_0_.1, bf16[512,1024]{1,0:T(8,128)(2,1)} %collective-permute-done.5.rest_1_), custom_call_target="tpu_custom_call" | custom-call | flops 1 | bytes 1 | tf_op jit(solution)/shard_map/finish/pallas_call | solution.py:565
  44.0 0.0 collective-permute-done.7.rest_3_
  44.0 0.0 copy-start
  44.0 0.0 collective-permute-done.8.rest_4_
  44.0 0.0 copy-start.1
  44.0 0.0 collective-permute-done.6.rest_2_
  44.0 0.0 copy-start.2
  44.0 0.0 collective-permute-done.2.refs_3_.rest_1_
  44.0 1.8 %collective-permute-start.9 = (bf16[512,1024]{1,0:T(8,128)(2,1)}, bf16[512,1024]{1,0:T(8,128)(2,1)S(1)}, u32[]{:S(2)}, u32[]{:S(2)}) collective-permute-start(bf16[512,1024]{1,0:T(8,128)(2,1)} %collective-permute-done.2.refs_3_.rest_1_), channel_id=1, source_target_pairs={{0,4},{1,3},{4,8},{5,1},{8,12},{9,5},{12,14},{13,9},{14,10},{15,13... | collective-permute-start | bytes 3145736 | tf_op jit(solution)/shard_map/ppermute | solution.py:649
  45.8 3.3 %far_products.5 = (bf16[256,512]{1,0:T(8,128)(2,1)}, bf16[256,512]{1,0:T(8,128)(2,1)}, bf16[256,512]{1,0:T(8,128)(2,1)}) custom-call(bf16[256,1024]{1,0:T(8,128)(2,1)S(1)} %collective-permute-done.3.refs_0_, bf16[256,1024]{1,0:T(8,128)(2,1)S(1)} %collective-permute-done.1.refs_1_, bf16[256,1024]{1,0:T(8,128)(2,1)S(1)} %collective-permute-done.4.refs_2_, ...), custom_call_target="tpu_custom_call" | custom-call | flops 1 | bytes 1 | tf_op jit(solution)/shard_map/far_products/pallas_call | solution.py:499
  49.2 0.3 collective-permute-start.11
  49.5 0.4 collective-permute-start.12
  49.9 1.5 %collective-permute-start.10 = (bf16[256,512]{1,0:T(8,128)(2,1)}, bf16[256,512]{1,0:T(8,128)(2,1)}, u32[]{:S(2)}, u32[]{:S(2)}) collective-permute-start(bf16[256,512]{1,0:T(8,128)(2,1)} %get-tuple-element.69), channel_id=1, source_target_pairs={{0,1},{1,0},{2,3},{3,2},{4,5},{5,4},{6,7},{7,6},{8,9},{9,8},{10,11... | collective-permute-start | bytes 786440 | tf_op jit(solution)/shard_map/ppermute | solution.py:619
  51.4 0.0 copy-done
  51.4 0.0 copy-done.1
  51.4 0.0 copy-done.2
  51.4 3.6 %finish.6.rest_4_ = bf16[256,8192]{1,0:T(8,128)(2,1)} custom-call(bf16[256,1024]{1,0:T(8,128)(2,1)S(1)} %mask_rows.1.cot.refs_3_, bf16[256,128]{1,0:T(8,128)(2,1)S(1)} %get-tuple-element.64.g, bf16[16,144,128]{2,1,0:T(8,128)(2,1)S(1)} %all-to-all-done.recv, bf16[512,1024]{1,0:T(8,128)(2,1)} %collective-permute-done.refs_3_.rest_0_, ...), custom_call_target="tpu_custom_call", output_to_operand_aliasing={{}: (8, {})} | custom-call | flops 1 | bytes 1 | tf_op jit(solution)/shard_map/finish/pallas_call | solution.py:565
  55.0 4.1 %collective-permute-done.9.refs_4_ = bf16[512,1024]{1,0:T(8,128)(2,1)S(1)} collective-permute-done((bf16[512,1024]{1,0:T(8,128)(2,1)}, bf16[512,1024]{1,0:T(8,128)(2,1)S(1)}, u32[]{:S(2)}, u32[]{:S(2)}) %collective-permute-start.9) | collective-permute-done | bytes 1048608 | tf_op jit(solution)/shard_map/ppermute | solution.py:649
  59.1 2.7 %far_products.6 = (bf16[256,512]{1,0:T(8,128)(2,1)}, bf16[256,512]{1,0:T(8,128)(2,1)}, bf16[256,512]{1,0:T(8,128)(2,1)}, f32[256,512]{1,0:T(8,128)}, bf16[256,1024]{1,0:T(8,128)(2,1)}) custom-call(bf16[256,1024]{1,0:T(8,128)(2,1)S(1)} %collective-permute-done.3.refs_0_, bf16[256,1024]{1,0:T(8,128)(2,1)S(1)} %collective-permute-done.1.refs_1_, ...), custom_call_target="tpu_custom_call" | custom-call | flops 1 | bytes 1 | tf_op jit(solution)/shard_map/far_products/pallas_call | solution.py:499
  61.8 0.0 collective-permute-done.11.rest_2_
  61.8 0.0 collective-permute-done.12.rest_3_
  61.8 0.0 collective-permute-done.10.rest_1_
  61.8 1.9 %collective-permute-start.13 = (bf16[256,1024]{1,0:T(8,128)(2,1)}, bf16[256,1024]{1,0:T(8,128)(2,1)}, u32[]{:S(2)}, u32[]{:S(2)}) collective-permute-start(bf16[256,1024]{1,0:T(8,128)(2,1)} %get-tuple-element.87), channel_id=1, source_target_pairs={{0,4},{1,3},{4,8},{5,1},{8,12},{9,5},{12,14},{13,9},{14,10},{15,13... | collective-permute-start | bytes 1572872 | tf_op jit(solution)/shard_map/ppermute | solution.py:660
  63.7 0.7 collective-permute-start.17
  64.3 1.1 %collective-permute-start.18 = (bf16[256,512]{1,0:T(8,128)(2,1)}, bf16[256,512]{1,0:T(8,128)(2,1)}, u32[]{:S(2)}, u32[]{:S(2)}) collective-permute-start(bf16[256,512]{1,0:T(8,128)(2,1)} %get-tuple-element.94), channel_id=1, source_target_pairs={{0,16},{16,0},{1,17},{17,1},{2,18},{18,2},{3,19},{19,3},{4,20},{20... | collective-permute-start | bytes 786440 | tf_op jit(solution)/shard_map/ppermute | solution.py:620
  65.5 0.3 collective-permute-start.19
  65.7 5.4 %all-to-all-start.1 = ((bf16[16,144,128]{2,1,0:T(8,128)(2,1)}), bf16[16,144,128]{2,1,0:T(8,128)(2,1)S(1)}, u32[]{:S(2)}, u32[]{:S(2)}) async-start(bf16[16,144,128]{2,1,0:T(8,128)(2,1)} %get-tuple-element.86), calls=%async_computation.1 | async-start | bytes 1179648 | tf_op jit(solution)/shard_map/all_to_all | solution.py:662
  71.1 2.6 %finish.7.rest_4_ = bf16[256,8192]{1,0:T(8,128)(2,1)} custom-call(bf16[256,1024]{1,0:T(8,128)(2,1)S(1)} %mask_rows.1.cot.refs_3_, bf16[256,128]{1,0:T(8,128)(2,1)S(1)} %get-tuple-element.64.g, bf16[16,144,128]{2,1,0:T(8,128)(2,1)S(1)} %all-to-all-done.recv, f32[256,512]{1,0:T(8,128)} %get-tuple-element.88.rest_0_, ...), custom_call_target="tpu_custom_call", output_to_operand_aliasing={{}: (7, {})} | custom-call | flops 1 | bytes 1 | tf_op jit(solution)/shard_map/finish/pallas_call | solution.py:565
  73.7 0.0 collective-permute-done.13.refs_4_
  73.7 2.6 %far_products.7 = (bf16[256,256]{1,0:T(8,128)(2,1)}, bf16[256,256]{1,0:T(8,128)(2,1)}, bf16[256,256]{1,0:T(8,128)(2,1)}, f32[256,256]{1,0:T(8,128)}) custom-call(bf16[256,1024]{1,0:T(8,128)(2,1)S(1)} %collective-permute-done.3.refs_0_, bf16[256,1024]{1,0:T(8,128)(2,1)S(1)} %collective-permute-done.1.refs_1_, ...), custom_call_target="tpu_custom_call" | custom-call | flops 1 | bytes 1 | tf_op jit(solution)/shard_map/far_products/pallas_call | solution.py:499
  76.3 0.5 collective-permute-start.14
  76.8 0.8 collective-permute-start.15
  77.6 0.0 collective-permute-done.17.rest_1_
  77.6 0.7 collective-permute-start.16
  78.3 0.0 collective-permute-done.18.rest_2_
  78.3 0.0 collective-permute-done.19.rest_3_
  78.3 2.5 %finish.8.rest_3_ = bf16[256,8192]{1,0:T(8,128)(2,1)} custom-call(bf16[256,1024]{1,0:T(8,128)(2,1)S(1)} %mask_rows.1.cot.refs_3_, bf16[256,128]{1,0:T(8,128)(2,1)S(1)} %get-tuple-element.64.g, bf16[16,144,128]{2,1,0:T(8,128)(2,1)S(1)} %all-to-all-done.recv, f32[256,256]{1,0:T(8,128)} %get-tuple-element.101.rest_0_, ...), custom_call_target="tpu_custom_call", output_to_operand_aliasing={{}: (7, {})} | custom-call | flops 10000000000 | bytes 1 | tf_op jit(solution)/shard_map/finish/pallas_call | solution.py:565
  80.7 0.0 collective-permute-done.14.rest_0_
  80.8 2.6 %collective-permute-done.15.rest_1_ = bf16[256,256]{1,0:T(8,128)(2,1)S(1)} collective-permute-done((bf16[256,256]{1,0:T(8,128)(2,1)}, bf16[256,256]{1,0:T(8,128)(2,1)S(1)}, u32[]{:S(2)}, u32[]{:S(2)}) %collective-permute-start.15) | collective-permute-done | bytes 131104 | tf_op jit(solution)/shard_map/ppermute | solution.py:620
  83.4 1.1 %collective-permute-done.16.rest_2_ = bf16[256,256]{1,0:T(8,128)(2,1)S(1)} collective-permute-done((bf16[256,256]{1,0:T(8,128)(2,1)}, bf16[256,256]{1,0:T(8,128)(2,1)S(1)}, u32[]{:S(2)}, u32[]{:S(2)}) %collective-permute-start.16) | collective-permute-done | bytes 131104 | tf_op jit(solution)/shard_map/ppermute | solution.py:621
  84.4 1.7 %finish.9 = bf16[256,8192]{1,0:T(8,128)(2,1)} custom-call(bf16[256,1024]{1,0:T(8,128)(2,1)S(1)} %mask_rows.1.cot.refs_3_, bf16[256,128]{1,0:T(8,128)(2,1)S(1)} %get-tuple-element.64.g, bf16[16,144,128]{2,1,0:T(8,128)(2,1)S(1)} %all-to-all-done.recv, bf16[256,256]{1,0:T(8,128)(2,1)S(1)} %collective-permute-done.14.rest_0_, ...), custom_call_target="tpu_custom_call", output_to_operand_aliasing={{}: (6, {})} | custom-call | flops 1 | bytes 1 | tf_op jit(solution)/shard_map/finish/pallas_call | solution.py:565
  86.2 0.5 all-to-all-done.1.recv
  86.6 3.6 %scatter_rows.1 = (f32[512,8192]{1,0:T(8,128)}, f32[512,1024]{1,0:T(8,128)}) custom-call(s32[32]{0:T(128)} %adapter_hbm.1, s32[512]{0:T(512)} %storage_hbm.1, bf16[16,144,128]{2,1,0:T(8,128)(2,1)S(1)} %all-to-all-done.1.recv, f32[512,8192]{1,0:T(8,128)} %get-tuple-element.105._down, ...), custom_call_target="tpu_custom_call", output_to_operand_aliasing={{0}: (3, {}), {1}: (4, {})} | custom-call | flops 1 | bytes 1 | tf_op jit(solution)/shard_map/scatter_rows/pallas_call | solution.py:437
Async XLA Ops:
  0.6 18.8 %collective-permute-start = (bf16[512,1024]{1,0:T(8,128)(2,1)}, bf16[512,1024]{1,0:T(8,128)(2,1)}, u32[]{:S(2)}, u32[]{:S(2)}) collective-permute-start(bf16[512,1024]{1,0:T(8,128)(2,1)} %rest_0_.1), channel_id=1, source_target_pairs={{0,4},{1,3},{4,8},{5,1},{8,12},{9,5},{12,14},{13,9},{14,10},{15,13... | collective-permute-start | bytes 3145736 | tf_op jit(solution)/shard_map/ppermute | solution.py:634
  4.9 14.6 %collective-permute-start.1 = (bf16[256,1024]{1,0:T(8,128)(2,1)S(1)}, bf16[256,1024]{1,0:T(8,128)(2,1)S(1)}, u32[]{:S(2)}, u32[]{:S(2)}) collective-permute-start(bf16[256,1024]{1,0:T(8,128)(2,1)S(1)} %mask_rows.1.cot.refs_3_), channel_id=1, source_target_pairs={{0,16},{16,0},{1,17},{17,1},{2,18},{18,2},{3,19},{19,3},{4,20},{20... | collective-permute-start | bytes 1572872 | tf_op jit(solution)/shard_map/ppermute | solution.py:627
  14.1 22.0 %all-to-all-start = ((bf16[16,144,128]{2,1,0:T(8,128)(2,1)}), bf16[16,144,128]{2,1,0:T(8,128)(2,1)S(1)}, u32[]{:S(2)}, u32[]{:S(2)}) async-start(bf16[16,144,128]{2,1,0:T(8,128)(2,1)} %gather_rows.1), calls=%async_computation | async-start | bytes 1179648 | tf_op jit(solution)/shard_map/all_to_all | solution.py:632
  19.1 22.0 %collective-permute-start.5 = (bf16[512,1024]{1,0:T(8,128)(2,1)}, bf16[512,1024]{1,0:T(8,128)(2,1)}, u32[]{:S(2)}, u32[]{:S(2)}) collective-permute-start(bf16[512,1024]{1,0:T(8,128)(2,1)} %rest_0_.1), channel_id=1, source_target_pairs={{0,1},{1,0},{2,3},{3,2},{4,5},{5,4},{6,7},{7,6},{8,9},{9,8},{10,11... | collective-permute-start | bytes 3145736 | tf_op jit(solution)/shard_map/ppermute | solution.py:624
  19.5 24.5 %collective-permute-start.2 = (bf16[512,1024]{1,0:T(8,128)(2,1)}, bf16[512,1024]{1,0:T(8,128)(2,1)}, u32[]{:S(2)}, u32[]{:S(2)}) collective-permute-start(bf16[512,1024]{1,0:T(8,128)(2,1)} %collective-permute-done.refs_3_.rest_0_), channel_id=1, source_target_pairs={{0,4},{1,3},{4,8},{5,1},{8,12},{9,5},{12,14},{13,9},{14,10},{15,13... | collective-permute-start | bytes 3145736 | tf_op jit(solution)/shard_map/ppermute | solution.py:649
  21.1 1.9 %collective-permute-start.3 = (bf16[256,1024]{1,0:T(8,128)(2,1)S(1)}, bf16[256,1024]{1,0:T(8,128)(2,1)S(1)}, u32[]{:S(2)}, u32[]{:S(2)}) collective-permute-start(bf16[256,1024]{1,0:T(8,128)(2,1)S(1)} %mask_rows.1.cot.refs_3_), channel_id=1, source_target_pairs={{0,1},{1,0},{2,3},{3,2},{4,5},{5,4},{6,7},{7,6},{8,9},{9,8},{10,11... | collective-permute-start | bytes 1572872 | tf_op jit(solution)/shard_map/ppermute | solution.py:626
  21.2 2.6 %collective-permute-start.4 = (bf16[256,1024]{1,0:T(8,128)(2,1)S(1)}, bf16[256,1024]{1,0:T(8,128)(2,1)S(1)}, u32[]{:S(2)}, u32[]{:S(2)}) collective-permute-start(bf16[256,1024]{1,0:T(8,128)(2,1)S(1)} %collective-permute-done.1.refs_1_), channel_id=1, source_target_pairs={{0,1},{1,0},{2,3},{3,2},{4,5},{5,4},{6,7},{7,6},{8,9},{9,8},{10,11... | collective-permute-start | bytes 1572872 | tf_op jit(solution)/shard_map/ppermute | solution.py:641
  27.1 16.8 %collective-permute-start.7 = (bf16[256,512]{1,0:T(8,128)(2,1)}, bf16[256,512]{1,0:T(8,128)(2,1)S(1)}, u32[]{:S(2)}, u32[]{:S(2)}) collective-permute-start(bf16[256,512]{1,0:T(8,128)(2,1)} %get-tuple-element.65), channel_id=1, source_target_pairs={{0,16},{16,0},{1,17},{17,1},{2,18},{18,2},{3,19},{19,3},{4,20},{20... | collective-permute-start | bytes 786440 | tf_op jit(solution)/shard_map/ppermute | solution.py:620
  27.7 16.3 %collective-permute-start.8 = (bf16[256,512]{1,0:T(8,128)(2,1)}, bf16[256,512]{1,0:T(8,128)(2,1)S(1)}, u32[]{:S(2)}, u32[]{:S(2)}) collective-permute-start(bf16[256,512]{1,0:T(8,128)(2,1)} %get-tuple-element.66), channel_id=1, source_target_pairs={{0,17},{1,16},{2,19},{3,18},{4,21},{5,20},{6,23},{7,22},{8,25},{9,... | collective-permute-start | bytes 786440 | tf_op jit(solution)/shard_map/ppermute | solution.py:621
  28.7 15.3 %collective-permute-start.6 = (bf16[256,512]{1,0:T(8,128)(2,1)}, bf16[256,512]{1,0:T(8,128)(2,1)S(1)}, u32[]{:S(2)}, u32[]{:S(2)}) collective-permute-start(bf16[256,512]{1,0:T(8,128)(2,1)} %get-tuple-element.59._), channel_id=1, source_target_pairs={{0,1},{1,0},{2,3},{3,2},{4,5},{5,4},{6,7},{7,6},{8,9},{9,8},{10,11... | collective-permute-start | bytes 786440 | tf_op jit(solution)/shard_map/ppermute | solution.py:619
  44.0 7.4 %copy-start = (bf16[256,512]{1,0:T(8,128)(2,1)}, bf16[256,512]{1,0:T(8,128)(2,1)S(1)}, u32[]{:S(2)}) copy-start(bf16[256,512]{1,0:T(8,128)(2,1)S(1)} %collective-permute-done.7.rest_3_) | copy-start | bytes 786436
  44.0 7.4 %copy-start.1 = (bf16[256,512]{1,0:T(8,128)(2,1)}, bf16[256,512]{1,0:T(8,128)(2,1)S(1)}, u32[]{:S(2)}) copy-start(bf16[256,512]{1,0:T(8,128)(2,1)S(1)} %collective-permute-done.8.rest_4_) | copy-start | bytes 786436
  44.0 7.4 %copy-start.2 = (bf16[256,512]{1,0:T(8,128)(2,1)}, bf16[256,512]{1,0:T(8,128)(2,1)S(1)}, u32[]{:S(2)}) copy-start(bf16[256,512]{1,0:T(8,128)(2,1)S(1)} %collective-permute-done.6.rest_2_) | copy-start | bytes 786436
  44.0 15.1 %collective-permute-start.9 = (bf16[512,1024]{1,0:T(8,128)(2,1)}, bf16[512,1024]{1,0:T(8,128)(2,1)S(1)}, u32[]{:S(2)}, u32[]{:S(2)}) collective-permute-start(bf16[512,1024]{1,0:T(8,128)(2,1)} %collective-permute-done.2.refs_3_.rest_1_), channel_id=1, source_target_pairs={{0,4},{1,3},{4,8},{5,1},{8,12},{9,5},{12,14},{13,9},{14,10},{15,13... | collective-permute-start | bytes 3145736 | tf_op jit(solution)/shard_map/ppermute | solution.py:649
  49.2 12.6 %collective-permute-start.11 = (bf16[256,512]{1,0:T(8,128)(2,1)}, bf16[256,512]{1,0:T(8,128)(2,1)}, u32[]{:S(2)}, u32[]{:S(2)}) collective-permute-start(bf16[256,512]{1,0:T(8,128)(2,1)} %get-tuple-element.81), channel_id=1, source_target_pairs={{0,16},{16,0},{1,17},{17,1},{2,18},{18,2},{3,19},{19,3},{4,20},{20... | collective-permute-start | bytes 786440 | tf_op jit(solution)/shard_map/ppermute | solution.py:620
  49.5 12.3 %collective-permute-start.12 = (bf16[256,512]{1,0:T(8,128)(2,1)}, bf16[256,512]{1,0:T(8,128)(2,1)}, u32[]{:S(2)}, u32[]{:S(2)}) collective-permute-start(bf16[256,512]{1,0:T(8,128)(2,1)} %get-tuple-element.82), channel_id=1, source_target_pairs={{0,17},{1,16},{2,19},{3,18},{4,21},{5,20},{6,23},{7,22},{8,25},{9,... | collective-permute-start | bytes 786440 | tf_op jit(solution)/shard_map/ppermute | solution.py:621
  49.9 11.9 %collective-permute-start.10 = (bf16[256,512]{1,0:T(8,128)(2,1)}, bf16[256,512]{1,0:T(8,128)(2,1)}, u32[]{:S(2)}, u32[]{:S(2)}) collective-permute-start(bf16[256,512]{1,0:T(8,128)(2,1)} %get-tuple-element.69), channel_id=1, source_target_pairs={{0,1},{1,0},{2,3},{3,2},{4,5},{5,4},{6,7},{7,6},{8,9},{9,8},{10,11... | collective-permute-start | bytes 786440 | tf_op jit(solution)/shard_map/ppermute | solution.py:619
  61.8 11.9 %collective-permute-start.13 = (bf16[256,1024]{1,0:T(8,128)(2,1)}, bf16[256,1024]{1,0:T(8,128)(2,1)}, u32[]{:S(2)}, u32[]{:S(2)}) collective-permute-start(bf16[256,1024]{1,0:T(8,128)(2,1)} %get-tuple-element.87), channel_id=1, source_target_pairs={{0,4},{1,3},{4,8},{5,1},{8,12},{9,5},{12,14},{13,9},{14,10},{15,13... | collective-permute-start | bytes 1572872 | tf_op jit(solution)/shard_map/ppermute | solution.py:660
  63.7 13.9 %collective-permute-start.17 = (bf16[256,512]{1,0:T(8,128)(2,1)}, bf16[256,512]{1,0:T(8,128)(2,1)}, u32[]{:S(2)}, u32[]{:S(2)}) collective-permute-start(bf16[256,512]{1,0:T(8,128)(2,1)} %get-tuple-element.93), channel_id=1, source_target_pairs={{0,1},{1,0},{2,3},{3,2},{4,5},{5,4},{6,7},{7,6},{8,9},{9,8},{10,11... | collective-permute-start | bytes 786440 | tf_op jit(solution)/shard_map/ppermute | solution.py:619
  64.3 13.9 %collective-permute-start.18 = (bf16[256,512]{1,0:T(8,128)(2,1)}, bf16[256,512]{1,0:T(8,128)(2,1)}, u32[]{:S(2)}, u32[]{:S(2)}) collective-permute-start(bf16[256,512]{1,0:T(8,128)(2,1)} %get-tuple-element.94), channel_id=1, source_target_pairs={{0,16},{16,0},{1,17},{17,1},{2,18},{18,2},{3,19},{19,3},{4,20},{20... | collective-permute-start | bytes 786440 | tf_op jit(solution)/shard_map/ppermute | solution.py:620
  65.5 12.8 %collective-permute-start.19 = (bf16[256,512]{1,0:T(8,128)(2,1)}, bf16[256,512]{1,0:T(8,128)(2,1)}, u32[]{:S(2)}, u32[]{:S(2)}) collective-permute-start(bf16[256,512]{1,0:T(8,128)(2,1)} %get-tuple-element.95), channel_id=1, source_target_pairs={{0,17},{1,16},{2,19},{3,18},{4,21},{5,20},{6,23},{7,22},{8,25},{9,... | collective-permute-start | bytes 786440 | tf_op jit(solution)/shard_map/ppermute | solution.py:621
  65.7 20.9 %all-to-all-start.1 = ((bf16[16,144,128]{2,1,0:T(8,128)(2,1)}), bf16[16,144,128]{2,1,0:T(8,128)(2,1)S(1)}, u32[]{:S(2)}, u32[]{:S(2)}) async-start(bf16[16,144,128]{2,1,0:T(8,128)(2,1)} %get-tuple-element.86), calls=%async_computation.1 | async-start | bytes 1179648 | tf_op jit(solution)/shard_map/all_to_all | solution.py:662
  76.3 4.4 %collective-permute-start.14 = (bf16[256,256]{1,0:T(8,128)(2,1)}, bf16[256,256]{1,0:T(8,128)(2,1)S(1)}, u32[]{:S(2)}, u32[]{:S(2)}) collective-permute-start(bf16[256,256]{1,0:T(8,128)(2,1)} %get-tuple-element.98), channel_id=1, source_target_pairs={{0,1},{1,0},{2,3},{3,2},{4,5},{5,4},{6,7},{7,6},{8,9},{9,8},{10,11... | collective-permute-start | bytes 393224 | tf_op jit(solution)/shard_map/ppermute | solution.py:619
  76.8 6.6 %collective-permute-start.15 = (bf16[256,256]{1,0:T(8,128)(2,1)}, bf16[256,256]{1,0:T(8,128)(2,1)S(1)}, u32[]{:S(2)}, u32[]{:S(2)}) collective-permute-start(bf16[256,256]{1,0:T(8,128)(2,1)} %get-tuple-element.99), channel_id=1, source_target_pairs={{0,16},{16,0},{1,17},{17,1},{2,18},{18,2},{3,19},{19,3},{4,20},{20... | collective-permute-start | bytes 393224 | tf_op jit(solution)/shard_map/ppermute | solution.py:620
  77.6 6.9 %collective-permute-start.16 = (bf16[256,256]{1,0:T(8,128)(2,1)}, bf16[256,256]{1,0:T(8,128)(2,1)S(1)}, u32[]{:S(2)}, u32[]{:S(2)}) collective-permute-start(bf16[256,256]{1,0:T(8,128)(2,1)} %get-tuple-element.100), channel_id=1, source_target_pairs={{0,17},{1,16},{2,19},{3,18},{4,21},{5,20},{6,23},{7,22},{8,25},{9,... | collective-permute-start | bytes 393224 | tf_op jit(solution)/shard_map/ppermute | solution.py:621

commit v8 on v7

--- a/solution.py
+++ b/solution.py
@@ -196,8 +196,8 @@
         scratch_shapes=[
             pltpu.VMEM((blocks, group, down.shape[1]), down.dtype),
             pltpu.VMEM(up.shape, up.dtype),
-            pltpu.VMEM((2, 8 * per_down, LANES), jnp.float32),
-            pltpu.VMEM((2, 8 * per_up, LANES), jnp.float32),
+            pltpu.VMEM((2, 8 * per_down + 8, LANES), jnp.float32),
+            pltpu.VMEM((2, 8 * per_up + 8, LANES), jnp.float32),
             pltpu.VMEM((devices * ADAPTER_RANK, 8 * LANES), jnp.bfloat16),
             pltpu.VMEM(shape, jnp.bfloat16),
             pltpu.SemaphoreType.DMA((blocks,)),
@@ -445,8 +445,8 @@
             pltpu.SMEM((ADAPTER_GROUP,), jnp.int32),
             pltpu.VMEM((blocks, per_down, LANES), jnp.float32),
             pltpu.VMEM((blocks, per_up, LANES), jnp.float32),
-            pltpu.VMEM((8 * per_down, LANES), jnp.float32),
-            pltpu.VMEM((8 * per_up, LANES), jnp.float32),
+            pltpu.VMEM((8 * per_down + 8, LANES), jnp.float32),
+            pltpu.VMEM((8 * per_up + 8, LANES), jnp.float32),
             pltpu.VMEM((blocks, per_down * LANES), jnp.float32),
             pltpu.VMEM((blocks, per_up * LANES), jnp.float32),
             pltpu.SemaphoreType.DMA((blocks,)),
@@ -641,9 +641,7 @@
             diagonal_masked = lax.ppermute(far_masked, "fsdp", cores)
             cots = (core_masked, far_masked, diagonal_masked)
         elif step == 1:
-            travelling, sent, out, grads, received[0] = after(
-                travelling, sent, out, grads, received[0]
-            )
+            travelling, sent, grads, received[0] = after(travelling, sent, grads, received[0])
         pieces.append(travelling)
         if step < steps - 2:
             travelling = lax.ppermute(travelling, ("parts", "fsdp"), ring)
@@ -667,12 +665,11 @@
             grads = zero_grads(products[0], adapter_down_weights.shape, adapter_up_weights.shape)
             recv, _ = after(recv, grads)
             sent, g = adapter_terms(inputs, masked, recv)
-            weights = (frozen_value_weight, other_shard)
-            out = finish(devices, [0, 1], masked, weights, (), g, recv, None, width, shard)
         if step == steps - 3:
             cot, _ = after(masked, products[0])
-            at = firsts[: step + 1] + [firsts[0] + i for i in range(1, 4)]
-            out = finish(devices, at, cot, pieces[:2], received[0], g, recv, out, width, shard)
+            at = [0, 1, *firsts[: step + 1]] + [firsts[0] + i for i in range(1, 4)]
+            weights = (frozen_value_weight, other_shard, *pieces[:2])
+            out = finish(devices, at, cot, weights, received[0], g, recv, None, width, shard)
             travelling, out = after(travelling, out)
         if step == steps - 2:
             out, _ = after(out, products)

time: 91.2 us -> 91.3 us (level)
  starting transfers between devices: 29.6 us -> 33 us
  Pallas kernels: 49.3 us -> 47.4 us
  waiting for transfers between devices: 10.5 us -> 9.07 us
    ppermute x3, starting transfers between devices: 5.36 us -> 9.21 us  [ring_body(): travelling = lax.ppermute(travelling, ('parts', 'fsdp'), ring)]
    pallas_call x5 -> x4, Pallas kernels: 13.2 us -> 11.3 us  [finish(): pl.pallas_call(kernel, in_specs=[IN_VMEM] * 3 + [pl.BlockSpec(memory_spac...]
    ppermute x3, waiting for transfers between devices: 4.13 us -> 2.53 us  [ring_body(): travelling = lax.ppermute(travelling, ('parts', 'fsdp'), ring)]
  transfers between devices with their start and end apart: 22 -> 22, of which waited for: 6 -> 7; matrix products, arithmetic and copies ran while one was open for 0% -> 0% of each run, Pallas kernels for 51% -> 48%
where the time goes in v8:
time: 91.3 us; the launch traced here: 90.5 us
  Pallas kernels  47.4 us (52%)
  starting transfers between devices  33 us (36%)
  waiting for transfers between devices  9.07 us (10%)
  between operations  1.05 us (1%)
    pallas_call x4, Pallas kernels, far_products(): pl.pallas_call(functools.partial(far_kernel, count, len(half)), in_specs=...  11.9 us
    pallas_call x4, Pallas kernels, finish(): pl.pallas_call(kernel, in_specs=[IN_VMEM] * 3 + [pl.BlockSpec(memory_spac...  11.3 us
    ppermute x3, starting transfers between devices, ring_body(): travelling = lax.ppermute(travelling, ('parts', 'fsdp'), ring)  9.21 us
    pallas_call x1, Pallas kernels, gather_rows(): pl.pallas_call(gather_kernel, in_specs=[IN_SMEM, IN_SMEM, IN_HBM, IN_HBM]...  7.75 us
    pallas_call x1, Pallas kernels, zero_grads(): pl.pallas_call(zero_kernel, in_specs=[pl.BlockSpec(memory_space=pl.ANY)],...  6.7 us
    all_to_all x1, starting transfers between devices, ring_body(): sums = lax.all_to_all(sent, 'fsdp', split_axis=0, concat_axis=0, tiled=True)  5.55 us
    all_to_all x1, starting transfers between devices, ring_body(): lax.all_to_all(payload, 'fsdp', split_axis=0, concat_axis=0, tiled=True)  5 us
    pallas_call x1, Pallas kernels, adapter_terms(): pl.pallas_call(adapter_kernel, in_specs=[IN_HBM, IN_VMEM, IN_VMEM], out_s...  4.97 us
  transfers between devices with their start and end apart: 22, of which 7 were waited for; matrix products, arithmetic and copies ran while one was open for 0% of the time, Pallas kernels for 48%

profile of v8, /device:TPU:0, one launch (start us, length us, event | category | flops | bytes accessed | tf_op | source)
XLA Modules:
  0.0 90.5 jit_solution(8382149054615207247)
XLA Ops:
  0.6 3.1 %collective-permute-start = (bf16[512,1024]{1,0:T(8,128)(2,1)}, bf16[512,1024]{1,0:T(8,128)(2,1)}, u32[]{:S(2)}, u32[]{:S(2)}) collective-permute-start(bf16[512,1024]{1,0:T(8,128)(2,1)} %rest_0_.1), channel_id=1, source_target_pairs={{0,4},{1,3},{4,8},{5,1},{8,12},{9,5},{12,14},{13,9},{14,10},{15,13... | collective-permute-start | bytes 3145736 | tf_op jit(solution)/shard_map/ppermute | solution.py:634
  3.7 1.1 %mask_rows.1.cot.refs_3_ = bf16[256,1024]{1,0:T(8,128)(2,1)S(1)} custom-call(s32[32]{0:T(128)} %live.1, bf16[256,1024]{1,0:T(8,128)(2,1)} %cot.1), custom_call_target="tpu_custom_call" | custom-call | flops 1 | bytes 1 | tf_op jit(solution)/shard_map/mask_rows/pallas_call | solution.py:94
  4.9 1.5 %collective-permute-start.1 = (bf16[256,1024]{1,0:T(8,128)(2,1)S(1)}, bf16[256,1024]{1,0:T(8,128)(2,1)S(1)}, u32[]{:S(2)}, u32[]{:S(2)}) collective-permute-start(bf16[256,1024]{1,0:T(8,128)(2,1)S(1)} %mask_rows.1.cot.refs_3_), channel_id=1, source_target_pairs={{0,16},{16,0},{1,17},{17,1},{2,18},{18,2},{3,19},{19,3},{4,20},{20... | collective-permute-start | bytes 1572872 | tf_op jit(solution)/shard_map/ppermute | solution.py:627
  6.4 7.8 %gather_rows.1 = bf16[16,144,128]{2,1,0:T(8,128)(2,1)} custom-call(s32[32]{0:T(128)} %adapter_hbm.1, s32[512]{0:T(512)} %storage_hbm.1, bf16[512,8192]{1,0:T(8,128)(2,1)} %down.1, bf16[512,1024]{1,0:T(8,128)(2,1)} %up.1), custom_call_target="tpu_custom_call" | custom-call | flops 1 | bytes 1 | tf_op jit(solution)/shard_map/gather_rows/pallas_call | solution.py:191
  14.1 5.0 %all-to-all-start = ((bf16[16,144,128]{2,1,0:T(8,128)(2,1)}), bf16[16,144,128]{2,1,0:T(8,128)(2,1)S(1)}, u32[]{:S(2)}, u32[]{:S(2)}) async-start(bf16[16,144,128]{2,1,0:T(8,128)(2,1)} %gather_rows.1), calls=%async_computation | async-start | bytes 1179648 | tf_op jit(solution)/shard_map/all_to_all | solution.py:632
  19.1 0.0 collective-permute-done.1.refs_1_
  19.1 0.0 collective-permute-done.refs_3_.rest_2_
  19.1 2.0 %collective-permute-start.2 = (bf16[512,1024]{1,0:T(8,128)(2,1)}, bf16[512,1024]{1,0:T(8,128)(2,1)}, u32[]{:S(2)}, u32[]{:S(2)}) collective-permute-start(bf16[512,1024]{1,0:T(8,128)(2,1)} %collective-permute-done.refs_3_.rest_2_), channel_id=1, source_target_pairs={{0,4},{1,3},{4,8},{5,1},{8,12},{9,5},{12,14},{13,9},{14,10},{15,13... | collective-permute-start | bytes 3145736 | tf_op jit(solution)/shard_map/ppermute | solution.py:647
  21.1 0.0 collective-permute-start.3
  21.1 0.5 collective-permute-start.4
  21.6 1.4 %collective-permute-done.3.refs_0_ = bf16[256,1024]{1,0:T(8,128)(2,1)S(1)} collective-permute-done((bf16[256,1024]{1,0:T(8,128)(2,1)S(1)}, bf16[256,1024]{1,0:T(8,128)(2,1)S(1)}, u32[]{:S(2)}, u32[]{:S(2)}) %collective-permute-start.3) | collective-permute-done | bytes 524320 | tf_op jit(solution)/shard_map/ppermute | solution.py:626
  23.0 0.7 collective-permute-done.4.refs_2_
  23.8 3.3 %far_products.4 = (bf16[256,512]{1,0:T(8,128)(2,1)}, bf16[256,512]{1,0:T(8,128)(2,1)}, bf16[256,512]{1,0:T(8,128)(2,1)}) custom-call(bf16[256,1024]{1,0:T(8,128)(2,1)S(1)} %collective-permute-done.3.refs_0_, bf16[256,1024]{1,0:T(8,128)(2,1)S(1)} %collective-permute-done.1.refs_1_, bf16[256,1024]{1,0:T(8,128)(2,1)S(1)} %collective-permute-done.4.refs_2_, ...), custom_call_target="tpu_custom_call" | custom-call | flops 1 | bytes 1 | tf_op jit(solution)/shard_map/far_products/pallas_call | solution.py:499
  27.1 0.6 collective-permute-start.6
  27.7 0.9 collective-permute-start.7
  28.6 0.7 collective-permute-start.5
  29.3 0.0 collective-permute-start.9
  29.3 6.7 %zero_grads.1 = (f32[512,8192]{1,0:T(8,128)}, f32[512,1024]{1,0:T(8,128)}) custom-call(bf16[256,512]{1,0:T(8,128)(2,1)} %get-tuple-element.58._), custom_call_target="tpu_custom_call" | custom-call | flops 1 | bytes 1 | tf_op jit(solution)/shard_map/zero_grads/pallas_call | solution.py:325
  36.0 0.0 all-to-all-done.recv
  36.0 5.0 %adapter_terms.1 = (bf16[16,144,128]{2,1,0:T(8,128)(2,1)}, bf16[256,128]{1,0:T(8,128)(2,1)S(1)}) custom-call(bf16[256,8192]{1,0:T(8,128)(2,1)} %x.1, bf16[256,1024]{1,0:T(8,128)(2,1)S(1)} %mask_rows.1.cot.refs_3_, bf16[16,144,128]{2,1,0:T(8,128)(2,1)S(1)} %all-to-all-done.recv), custom_call_target="tpu_custom_call" | custom-call | flops 1 | bytes 1 | tf_op jit(solution)/shard_map/adapter_terms/pallas_call | solution.py:289
  41.0 0.0 collective-permute-done.6.rest_5_
  41.0 0.0 copy-start
  41.0 0.0 collective-permute-done.7.rest_6_
  41.0 0.0 copy-start.1
  41.1 0.0 collective-permute-done.5.rest_4_
  41.1 0.0 copy-start.2
  41.1 0.0 collective-permute-done.2.refs_3_.rest_3_
  41.1 4.8 %collective-permute-start.8 = (bf16[512,1024]{1,0:T(8,128)(2,1)}, bf16[512,1024]{1,0:T(8,128)(2,1)S(1)}, u32[]{:S(2)}, u32[]{:S(2)}) collective-permute-start(bf16[512,1024]{1,0:T(8,128)(2,1)} %collective-permute-done.2.refs_3_.rest_3_), channel_id=1, source_target_pairs={{0,4},{1,3},{4,8},{5,1},{8,12},{9,5},{12,14},{13,9},{14,10},{15,13... | collective-permute-start | bytes 3145736 | tf_op jit(solution)/shard_map/ppermute | solution.py:647
  45.9 3.3 %far_products.5 = (bf16[256,512]{1,0:T(8,128)(2,1)}, bf16[256,512]{1,0:T(8,128)(2,1)}, bf16[256,512]{1,0:T(8,128)(2,1)}) custom-call(bf16[256,1024]{1,0:T(8,128)(2,1)S(1)} %collective-permute-done.3.refs_0_, bf16[256,1024]{1,0:T(8,128)(2,1)S(1)} %collective-permute-done.1.refs_1_, bf16[256,1024]{1,0:T(8,128)(2,1)S(1)} %collective-permute-done.4.refs_2_, ...), custom_call_target="tpu_custom_call" | custom-call | flops 1 | bytes 1 | tf_op jit(solution)/shard_map/far_products/pallas_call | solution.py:499
  49.2 0.1 collective-permute-start.11
  49.3 0.1 collective-permute-start.12
  49.4 2.0 %collective-permute-start.10 = (bf16[256,512]{1,0:T(8,128)(2,1)}, bf16[256,512]{1,0:T(8,128)(2,1)}, u32[]{:S(2)}, u32[]{:S(2)}) collective-permute-start(bf16[256,512]{1,0:T(8,128)(2,1)} %get-tuple-element.67), channel_id=1, source_target_pairs={{0,1},{1,0},{2,3},{3,2},{4,5},{5,4},{6,7},{7,6},{8,9},{9,8},{10,11... | collective-permute-start | bytes 786440 | tf_op jit(solution)/shard_map/ppermute | solution.py:619
  51.4 0.0 collective-permute-done.9.rest_1_
  51.4 0.0 copy-done
  51.4 0.0 copy-done.1
  51.4 0.0 copy-done.2
  51.5 4.5 %finish.4.rest_4_ = bf16[256,8192]{1,0:T(8,128)(2,1)} custom-call(bf16[256,1024]{1,0:T(8,128)(2,1)S(1)} %mask_rows.1.cot.refs_3_, bf16[256,128]{1,0:T(8,128)(2,1)S(1)} %get-tuple-element.69.g, bf16[16,144,128]{2,1,0:T(8,128)(2,1)S(1)} %all-to-all-done.recv, bf16[512,1024]{1,0:T(8,128)(2,1)} %rest_0_.1, bf16[512,1024]{1,0:T(8,128)(2,1)} %collective-permute-done.9.rest_1_, ...), custom_call_target="tpu_custom_call" | custom-call | flops 1 | bytes 1 | tf_op jit(solution)/shard_map/finish/pallas_call | solution.py:565
  56.0 2.5 %collective-permute-done.8.refs_4_ = bf16[512,1024]{1,0:T(8,128)(2,1)S(1)} collective-permute-done((bf16[512,1024]{1,0:T(8,128)(2,1)}, bf16[512,1024]{1,0:T(8,128)(2,1)S(1)}, u32[]{:S(2)}, u32[]{:S(2)}) %collective-permute-start.8) | collective-permute-done | bytes 1048608 | tf_op jit(solution)/shard_map/ppermute | solution.py:647
  58.5 2.7 %far_products.6 = (bf16[256,512]{1,0:T(8,128)(2,1)}, bf16[256,512]{1,0:T(8,128)(2,1)}, bf16[256,512]{1,0:T(8,128)(2,1)}, f32[256,512]{1,0:T(8,128)}, bf16[256,1024]{1,0:T(8,128)(2,1)}) custom-call(bf16[256,1024]{1,0:T(8,128)(2,1)S(1)} %collective-permute-done.3.refs_0_, bf16[256,1024]{1,0:T(8,128)(2,1)S(1)} %collective-permute-done.1.refs_1_, ...), custom_call_target="tpu_custom_call" | custom-call | flops 1 | bytes 1 | tf_op jit(solution)/shard_map/far_products/pallas_call | solution.py:499
  61.2 0.0 collective-permute-done.11.rest_2_
  61.2 0.1 collective-permute-done.12.rest_3_
  61.3 0.0 collective-permute-done.10.rest_1_
  61.3 2.4 %collective-permute-start.13 = (bf16[256,1024]{1,0:T(8,128)(2,1)}, bf16[256,1024]{1,0:T(8,128)(2,1)}, u32[]{:S(2)}, u32[]{:S(2)}) collective-permute-start(bf16[256,1024]{1,0:T(8,128)(2,1)} %get-tuple-element.85), channel_id=1, source_target_pairs={{0,4},{1,3},{4,8},{5,1},{8,12},{9,5},{12,14},{13,9},{14,10},{15,13... | collective-permute-start | bytes 1572872 | tf_op jit(solution)/shard_map/ppermute | solution.py:658
  63.8 0.1 collective-permute-start.17
  63.8 1.7 %collective-permute-start.18 = (bf16[256,512]{1,0:T(8,128)(2,1)}, bf16[256,512]{1,0:T(8,128)(2,1)}, u32[]{:S(2)}, u32[]{:S(2)}) collective-permute-start(bf16[256,512]{1,0:T(8,128)(2,1)} %get-tuple-element.92), channel_id=1, source_target_pairs={{0,16},{16,0},{1,17},{17,1},{2,18},{18,2},{3,19},{19,3},{4,20},{20... | collective-permute-start | bytes 786440 | tf_op jit(solution)/shard_map/ppermute | solution.py:620
  65.5 0.1 collective-permute-start.19
  65.6 5.6 %all-to-all-start.1 = ((bf16[16,144,128]{2,1,0:T(8,128)(2,1)}), bf16[16,144,128]{2,1,0:T(8,128)(2,1)S(1)}, u32[]{:S(2)}, u32[]{:S(2)}) async-start(bf16[16,144,128]{2,1,0:T(8,128)(2,1)} %get-tuple-element.84), calls=%async_computation.1 | async-start | bytes 1179648 | tf_op jit(solution)/shard_map/all_to_all | solution.py:660
  71.2 2.6 %finish.5.rest_4_ = bf16[256,8192]{1,0:T(8,128)(2,1)} custom-call(bf16[256,1024]{1,0:T(8,128)(2,1)S(1)} %mask_rows.1.cot.refs_3_, bf16[256,128]{1,0:T(8,128)(2,1)S(1)} %get-tuple-element.69.g, bf16[16,144,128]{2,1,0:T(8,128)(2,1)S(1)} %all-to-all-done.recv, f32[256,512]{1,0:T(8,128)} %get-tuple-element.86.rest_0_, ...), custom_call_target="tpu_custom_call", output_to_operand_aliasing={{}: (7, {})} | custom-call | flops 1 | bytes 1 | tf_op jit(solution)/shard_map/finish/pallas_call | solution.py:565
  73.8 0.0 collective-permute-done.13.refs_4_
  73.8 2.6 %far_products.7 = (bf16[256,256]{1,0:T(8,128)(2,1)}, bf16[256,256]{1,0:T(8,128)(2,1)}, bf16[256,256]{1,0:T(8,128)(2,1)}, f32[256,256]{1,0:T(8,128)}) custom-call(bf16[256,1024]{1,0:T(8,128)(2,1)S(1)} %collective-permute-done.3.refs_0_, bf16[256,1024]{1,0:T(8,128)(2,1)S(1)} %collective-permute-done.1.refs_1_, ...), custom_call_target="tpu_custom_call" | custom-call | flops 1 | bytes 1 | tf_op jit(solution)/shard_map/far_products/pallas_call | solution.py:499
  76.4 0.5 collective-permute-start.14
  76.8 0.8 collective-permute-start.15
  77.6 0.0 collective-permute-done.17.rest_1_
  77.6 0.7 collective-permute-start.16
  78.3 0.0 collective-permute-done.18.rest_2_
  78.3 0.0 collective-permute-done.19.rest_3_
  78.3 2.5 %finish.6.rest_3_ = bf16[256,8192]{1,0:T(8,128)(2,1)} custom-call(bf16[256,1024]{1,0:T(8,128)(2,1)S(1)} %mask_rows.1.cot.refs_3_, bf16[256,128]{1,0:T(8,128)(2,1)S(1)} %get-tuple-element.69.g, bf16[16,144,128]{2,1,0:T(8,128)(2,1)S(1)} %all-to-all-done.recv, f32[256,256]{1,0:T(8,128)} %get-tuple-element.99.rest_0_, ...), custom_call_target="tpu_custom_call", output_to_operand_aliasing={{}: (7, {})} | custom-call | flops 10000000000 | bytes 1 | tf_op jit(solution)/shard_map/finish/pallas_call | solution.py:565
  80.8 0.0 collective-permute-done.14.rest_0_
  80.8 2.6 %collective-permute-done.15.rest_1_ = bf16[256,256]{1,0:T(8,128)(2,1)S(1)} collective-permute-done((bf16[256,256]{1,0:T(8,128)(2,1)}, bf16[256,256]{1,0:T(8,128)(2,1)S(1)}, u32[]{:S(2)}, u32[]{:S(2)}) %collective-permute-start.15) | collective-permute-done | bytes 131104 | tf_op jit(solution)/shard_map/ppermute | solution.py:620
  83.4 1.1 %collective-permute-done.16.rest_2_ = bf16[256,256]{1,0:T(8,128)(2,1)S(1)} collective-permute-done((bf16[256,256]{1,0:T(8,128)(2,1)}, bf16[256,256]{1,0:T(8,128)(2,1)S(1)}, u32[]{:S(2)}, u32[]{:S(2)}) %collective-permute-start.16) | collective-permute-done | bytes 131104 | tf_op jit(solution)/shard_map/ppermute | solution.py:621
  84.5 1.7 %finish.7 = bf16[256,8192]{1,0:T(8,128)(2,1)} custom-call(bf16[256,1024]{1,0:T(8,128)(2,1)S(1)} %mask_rows.1.cot.refs_3_, bf16[256,128]{1,0:T(8,128)(2,1)S(1)} %get-tuple-element.69.g, bf16[16,144,128]{2,1,0:T(8,128)(2,1)S(1)} %all-to-all-done.recv, bf16[256,256]{1,0:T(8,128)(2,1)S(1)} %collective-permute-done.14.rest_0_, ...), custom_call_target="tpu_custom_call", output_to_operand_aliasing={{}: (6, {})} | custom-call | flops 1 | bytes 1 | tf_op jit(solution)/shard_map/finish/pallas_call | solution.py:565
  86.2 0.5 all-to-all-done.1.recv
  86.7 3.7 %scatter_rows.1 = (f32[512,8192]{1,0:T(8,128)}, f32[512,1024]{1,0:T(8,128)}) custom-call(s32[32]{0:T(128)} %adapter_hbm.1, s32[512]{0:T(512)} %storage_hbm.1, bf16[16,144,128]{2,1,0:T(8,128)(2,1)S(1)} %all-to-all-done.1.recv, f32[512,8192]{1,0:T(8,128)} %get-tuple-element.103._down, ...), custom_call_target="tpu_custom_call", output_to_operand_aliasing={{0}: (3, {}), {1}: (4, {})} | custom-call | flops 1 | bytes 1 | tf_op jit(solution)/shard_map/scatter_rows/pallas_call | solution.py:437
Async XLA Ops:
  0.6 18.5 %collective-permute-start = (bf16[512,1024]{1,0:T(8,128)(2,1)}, bf16[512,1024]{1,0:T(8,128)(2,1)}, u32[]{:S(2)}, u32[]{:S(2)}) collective-permute-start(bf16[512,1024]{1,0:T(8,128)(2,1)} %rest_0_.1), channel_id=1, source_target_pairs={{0,4},{1,3},{4,8},{5,1},{8,12},{9,5},{12,14},{13,9},{14,10},{15,13... | collective-permute-start | bytes 3145736 | tf_op jit(solution)/shard_map/ppermute | solution.py:634
  4.9 14.3 %collective-permute-start.1 = (bf16[256,1024]{1,0:T(8,128)(2,1)S(1)}, bf16[256,1024]{1,0:T(8,128)(2,1)S(1)}, u32[]{:S(2)}, u32[]{:S(2)}) collective-permute-start(bf16[256,1024]{1,0:T(8,128)(2,1)S(1)} %mask_rows.1.cot.refs_3_), channel_id=1, source_target_pairs={{0,16},{16,0},{1,17},{17,1},{2,18},{18,2},{3,19},{19,3},{4,20},{20... | collective-permute-start | bytes 1572872 | tf_op jit(solution)/shard_map/ppermute | solution.py:627
  14.1 21.9 %all-to-all-start = ((bf16[16,144,128]{2,1,0:T(8,128)(2,1)}), bf16[16,144,128]{2,1,0:T(8,128)(2,1)S(1)}, u32[]{:S(2)}, u32[]{:S(2)}) async-start(bf16[16,144,128]{2,1,0:T(8,128)(2,1)} %gather_rows.1), calls=%async_computation | async-start | bytes 1179648 | tf_op jit(solution)/shard_map/all_to_all | solution.py:632
  19.1 21.9 %collective-permute-start.2 = (bf16[512,1024]{1,0:T(8,128)(2,1)}, bf16[512,1024]{1,0:T(8,128)(2,1)}, u32[]{:S(2)}, u32[]{:S(2)}) collective-permute-start(bf16[512,1024]{1,0:T(8,128)(2,1)} %collective-permute-done.refs_3_.rest_2_), channel_id=1, source_target_pairs={{0,4},{1,3},{4,8},{5,1},{8,12},{9,5},{12,14},{13,9},{14,10},{15,13... | collective-permute-start | bytes 3145736 | tf_op jit(solution)/shard_map/ppermute | solution.py:647
  21.1 1.9 %collective-permute-start.3 = (bf16[256,1024]{1,0:T(8,128)(2,1)S(1)}, bf16[256,1024]{1,0:T(8,128)(2,1)S(1)}, u32[]{:S(2)}, u32[]{:S(2)}) collective-permute-start(bf16[256,1024]{1,0:T(8,128)(2,1)S(1)} %mask_rows.1.cot.refs_3_), channel_id=1, source_target_pairs={{0,1},{1,0},{2,3},{3,2},{4,5},{5,4},{6,7},{7,6},{8,9},{9,8},{10,11... | collective-permute-start | bytes 1572872 | tf_op jit(solution)/shard_map/ppermute | solution.py:626
  21.1 2.7 %collective-permute-start.4 = (bf16[256,1024]{1,0:T(8,128)(2,1)S(1)}, bf16[256,1024]{1,0:T(8,128)(2,1)S(1)}, u32[]{:S(2)}, u32[]{:S(2)}) collective-permute-start(bf16[256,1024]{1,0:T(8,128)(2,1)S(1)} %collective-permute-done.1.refs_1_), channel_id=1, source_target_pairs={{0,1},{1,0},{2,3},{3,2},{4,5},{5,4},{6,7},{7,6},{8,9},{9,8},{10,11... | collective-permute-start | bytes 1572872 | tf_op jit(solution)/shard_map/ppermute | solution.py:641
  27.1 13.9 %collective-permute-start.6 = (bf16[256,512]{1,0:T(8,128)(2,1)}, bf16[256,512]{1,0:T(8,128)(2,1)S(1)}, u32[]{:S(2)}, u32[]{:S(2)}) collective-permute-start(bf16[256,512]{1,0:T(8,128)(2,1)} %get-tuple-element.63), channel_id=1, source_target_pairs={{0,16},{16,0},{1,17},{17,1},{2,18},{18,2},{3,19},{19,3},{4,20},{20... | collective-permute-start | bytes 786440 | tf_op jit(solution)/shard_map/ppermute | solution.py:620
  27.7 13.3 %collective-permute-start.7 = (bf16[256,512]{1,0:T(8,128)(2,1)}, bf16[256,512]{1,0:T(8,128)(2,1)S(1)}, u32[]{:S(2)}, u32[]{:S(2)}) collective-permute-start(bf16[256,512]{1,0:T(8,128)(2,1)} %get-tuple-element.64), channel_id=1, source_target_pairs={{0,17},{1,16},{2,19},{3,18},{4,21},{5,20},{6,23},{7,22},{8,25},{9,... | collective-permute-start | bytes 786440 | tf_op jit(solution)/shard_map/ppermute | solution.py:621
  28.6 12.4 %collective-permute-start.5 = (bf16[256,512]{1,0:T(8,128)(2,1)}, bf16[256,512]{1,0:T(8,128)(2,1)S(1)}, u32[]{:S(2)}, u32[]{:S(2)}) collective-permute-start(bf16[256,512]{1,0:T(8,128)(2,1)} %get-tuple-element.58._), channel_id=1, source_target_pairs={{0,1},{1,0},{2,3},{3,2},{4,5},{5,4},{6,7},{7,6},{8,9},{9,8},{10,11... | collective-permute-start | bytes 786440 | tf_op jit(solution)/shard_map/ppermute | solution.py:619
  29.3 22.1 %collective-permute-start.9 = (bf16[512,1024]{1,0:T(8,128)(2,1)}, bf16[512,1024]{1,0:T(8,128)(2,1)}, u32[]{:S(2)}, u32[]{:S(2)}) collective-permute-start(bf16[512,1024]{1,0:T(8,128)(2,1)} %rest_0_.1), channel_id=1, source_target_pairs={{0,1},{1,0},{2,3},{3,2},{4,5},{5,4},{6,7},{7,6},{8,9},{9,8},{10,11... | collective-permute-start | bytes 3145736 | tf_op jit(solution)/shard_map/ppermute | solution.py:624
  41.0 10.4 %copy-start = (bf16[256,512]{1,0:T(8,128)(2,1)}, bf16[256,512]{1,0:T(8,128)(2,1)S(1)}, u32[]{:S(2)}) copy-start(bf16[256,512]{1,0:T(8,128)(2,1)S(1)} %collective-permute-done.6.rest_5_) | copy-start | bytes 786436
  41.0 10.4 %copy-start.1 = (bf16[256,512]{1,0:T(8,128)(2,1)}, bf16[256,512]{1,0:T(8,128)(2,1)S(1)}, u32[]{:S(2)}) copy-start(bf16[256,512]{1,0:T(8,128)(2,1)S(1)} %collective-permute-done.7.rest_6_) | copy-start | bytes 786436
  41.1 10.4 %copy-start.2 = (bf16[256,512]{1,0:T(8,128)(2,1)}, bf16[256,512]{1,0:T(8,128)(2,1)S(1)}, u32[]{:S(2)}) copy-start(bf16[256,512]{1,0:T(8,128)(2,1)S(1)} %collective-permute-done.5.rest_4_) | copy-start | bytes 786436
  41.1 17.5 %collective-permute-start.8 = (bf16[512,1024]{1,0:T(8,128)(2,1)}, bf16[512,1024]{1,0:T(8,128)(2,1)S(1)}, u32[]{:S(2)}, u32[]{:S(2)}) collective-permute-start(bf16[512,1024]{1,0:T(8,128)(2,1)} %collective-permute-done.2.refs_3_.rest_3_), channel_id=1, source_target_pairs={{0,4},{1,3},{4,8},{5,1},{8,12},{9,5},{12,14},{13,9},{14,10},{15,13... | collective-permute-start | bytes 3145736 | tf_op jit(solution)/shard_map/ppermute | solution.py:647
  49.2 12.0 %collective-permute-start.11 = (bf16[256,512]{1,0:T(8,128)(2,1)}, bf16[256,512]{1,0:T(8,128)(2,1)}, u32[]{:S(2)}, u32[]{:S(2)}) collective-permute-start(bf16[256,512]{1,0:T(8,128)(2,1)} %get-tuple-element.79), channel_id=1, source_target_pairs={{0,16},{16,0},{1,17},{17,1},{2,18},{18,2},{3,19},{19,3},{4,20},{20... | collective-permute-start | bytes 786440 | tf_op jit(solution)/shard_map/ppermute | solution.py:620
  49.3 12.0 %collective-permute-start.12 = (bf16[256,512]{1,0:T(8,128)(2,1)}, bf16[256,512]{1,0:T(8,128)(2,1)}, u32[]{:S(2)}, u32[]{:S(2)}) collective-permute-start(bf16[256,512]{1,0:T(8,128)(2,1)} %get-tuple-element.80), channel_id=1, source_target_pairs={{0,17},{1,16},{2,19},{3,18},{4,21},{5,20},{6,23},{7,22},{8,25},{9,... | collective-permute-start | bytes 786440 | tf_op jit(solution)/shard_map/ppermute | solution.py:621
  49.4 12.0 %collective-permute-start.10 = (bf16[256,512]{1,0:T(8,128)(2,1)}, bf16[256,512]{1,0:T(8,128)(2,1)}, u32[]{:S(2)}, u32[]{:S(2)}) collective-permute-start(bf16[256,512]{1,0:T(8,128)(2,1)} %get-tuple-element.67), channel_id=1, source_target_pairs={{0,1},{1,0},{2,3},{3,2},{4,5},{5,4},{6,7},{7,6},{8,9},{9,8},{10,11... | collective-permute-start | bytes 786440 | tf_op jit(solution)/shard_map/ppermute | solution.py:619
  61.3 12.4 %collective-permute-start.13 = (bf16[256,1024]{1,0:T(8,128)(2,1)}, bf16[256,1024]{1,0:T(8,128)(2,1)}, u32[]{:S(2)}, u32[]{:S(2)}) collective-permute-start(bf16[256,1024]{1,0:T(8,128)(2,1)} %get-tuple-element.85), channel_id=1, source_target_pairs={{0,4},{1,3},{4,8},{5,1},{8,12},{9,5},{12,14},{13,9},{14,10},{15,13... | collective-permute-start | bytes 1572872 | tf_op jit(solution)/shard_map/ppermute | solution.py:658
  63.8 13.8 %collective-permute-start.17 = (bf16[256,512]{1,0:T(8,128)(2,1)}, bf16[256,512]{1,0:T(8,128)(2,1)}, u32[]{:S(2)}, u32[]{:S(2)}) collective-permute-start(bf16[256,512]{1,0:T(8,128)(2,1)} %get-tuple-element.91), channel_id=1, source_target_pairs={{0,1},{1,0},{2,3},{3,2},{4,5},{5,4},{6,7},{7,6},{8,9},{9,8},{10,11... | collective-permute-start | bytes 786440 | tf_op jit(solution)/shard_map/ppermute | solution.py:619
  63.8 14.5 %collective-permute-start.18 = (bf16[256,512]{1,0:T(8,128)(2,1)}, bf16[256,512]{1,0:T(8,128)(2,1)}, u32[]{:S(2)}, u32[]{:S(2)}) collective-permute-start(bf16[256,512]{1,0:T(8,128)(2,1)} %get-tuple-element.92), channel_id=1, source_target_pairs={{0,16},{16,0},{1,17},{17,1},{2,18},{18,2},{3,19},{19,3},{4,20},{20... | collective-permute-start | bytes 786440 | tf_op jit(solution)/shard_map/ppermute | solution.py:620
  65.5 12.8 %collective-permute-start.19 = (bf16[256,512]{1,0:T(8,128)(2,1)}, bf16[256,512]{1,0:T(8,128)(2,1)}, u32[]{:S(2)}, u32[]{:S(2)}) collective-permute-start(bf16[256,512]{1,0:T(8,128)(2,1)} %get-tuple-element.93), channel_id=1, source_target_pairs={{0,17},{1,16},{2,19},{3,18},{4,21},{5,20},{6,23},{7,22},{8,25},{9,... | collective-permute-start | bytes 786440 | tf_op jit(solution)/shard_map/ppermute | solution.py:621
  65.6 21.1 %all-to-all-start.1 = ((bf16[16,144,128]{2,1,0:T(8,128)(2,1)}), bf16[16,144,128]{2,1,0:T(8,128)(2,1)S(1)}, u32[]{:S(2)}, u32[]{:S(2)}) async-start(bf16[16,144,128]{2,1,0:T(8,128)(2,1)} %get-tuple-element.84), calls=%async_computation.1 | async-start | bytes 1179648 | tf_op jit(solution)/shard_map/all_to_all | solution.py:660
  76.4 4.4 %collective-permute-start.14 = (bf16[256,256]{1,0:T(8,128)(2,1)}, bf16[256,256]{1,0:T(8,128)(2,1)S(1)}, u32[]{:S(2)}, u32[]{:S(2)}) collective-permute-start(bf16[256,256]{1,0:T(8,128)(2,1)} %get-tuple-element.96), channel_id=1, source_target_pairs={{0,1},{1,0},{2,3},{3,2},{4,5},{5,4},{6,7},{7,6},{8,9},{9,8},{10,11... | collective-permute-start | bytes 393224 | tf_op jit(solution)/shard_map/ppermute | solution.py:619
  76.8 6.6 %collective-permute-start.15 = (bf16[256,256]{1,0:T(8,128)(2,1)}, bf16[256,256]{1,0:T(8,128)(2,1)S(1)}, u32[]{:S(2)}, u32[]{:S(2)}) collective-permute-start(bf16[256,256]{1,0:T(8,128)(2,1)} %get-tuple-element.97), channel_id=1, source_target_pairs={{0,16},{16,0},{1,17},{17,1},{2,18},{18,2},{3,19},{19,3},{4,20},{20... | collective-permute-start | bytes 393224 | tf_op jit(solution)/shard_map/ppermute | solution.py:620
  77.6 6.9 %collective-permute-start.16 = (bf16[256,256]{1,0:T(8,128)(2,1)}, bf16[256,256]{1,0:T(8,128)(2,1)S(1)}, u32[]{:S(2)}, u32[]{:S(2)}) collective-permute-start(bf16[256,256]{1,0:T(8,128)(2,1)} %get-tuple-element.98), channel_id=1, source_target_pairs={{0,17},{1,16},{2,19},{3,18},{4,21},{5,20},{6,23},{7,22},{8,25},{9,... | collective-permute-start | bytes 393224 | tf_op jit(solution)/shard_map/ppermute | solution.py:621

commit v9 on v8

--- a/solution.py
+++ b/solution.py
@@ -639,6 +639,8 @@
         if step == 0:
             travelling, far_masked, _ = after(travelling, far_masked, payload)
             diagonal_masked = lax.ppermute(far_masked, "fsdp", cores)
+            grads = zero_grads(payload, adapter_down_weights.shape, adapter_up_weights.shape)
+            (far_masked, grads) = after(far_masked, grads)
             cots = (core_masked, far_masked, diagonal_masked)
         elif step == 1:
             travelling, sent, grads, received[0] = after(travelling, sent, grads, received[0])
@@ -662,8 +664,7 @@
             *products, last_own = products
         received.append(cross(products))
         if step == 0:
-            grads = zero_grads(products[0], adapter_down_weights.shape, adapter_up_weights.shape)
-            recv, _ = after(recv, grads)
+            recv, _ = after(recv, products[0])
             sent, g = adapter_terms(inputs, masked, recv)
         if step == steps - 3:
             cot, _ = after(masked, products[0])

time: 91.3 us -> 91.4 us (level)
  waiting for transfers between devices: 9.07 us -> 14.8 us
  starting transfers between devices: 33 us -> 27.4 us
    ppermute x3, starting transfers between devices: 9.21 us -> 3.85 us  [ring_body(): travelling = lax.ppermute(travelling, ('parts', 'fsdp'), ring)]
    ppermute x4, waiting for transfers between devices: 1.28 us -> 6.17 us  [cross(): lax.ppermute(products[2], ('parts', 'fsdp'), diagonal)]
    ppermute x4, starting transfers between devices: 1.75 us -> 3.35 us  [cross(): lax.ppermute(products[2], ('parts', 'fsdp'), diagonal)]
    ppermute x1, waiting for transfers between devices: 1.4 us -> 0.01 us  [ring_body(): core_masked = lax.ppermute(masked, 'fsdp', cores)]
    ppermute x4, waiting for transfers between devices: 2.61 us -> 3.74 us  [cross(): lax.ppermute(products[1], 'parts', across)]
    ppermute x4, starting transfers between devices: 3.24 us -> 2.25 us  [cross(): lax.ppermute(products[0], 'fsdp', cores)]
    all_to_all x1, waiting for transfers between devices: 0.01 us -> 0.92 us  [ring_body(): lax.all_to_all(payload, 'fsdp', split_axis=0, concat_axis=0, tiled=True)]
  transfers between devices with their start and end apart: 22 -> 22, of which waited for: 7 -> 9; matrix products, arithmetic and copies ran while one was open for 0% -> 0% of each run, Pallas kernels for 48% -> 48%
where the time goes in v9:
time: 91.4 us; the launch traced here: 90.5 us
  Pallas kernels  47.4 us (52%)
  starting transfers between devices  27.4 us (30%)
  waiting for transfers between devices  14.8 us (16%)
  between operations  0.99 us (1%)
    pallas_call x4, Pallas kernels, far_products(): pl.pallas_call(functools.partial(far_kernel, count, len(half)), in_specs=...  11.9 us
    pallas_call x4, Pallas kernels, finish(): pl.pallas_call(kernel, in_specs=[IN_VMEM] * 3 + [pl.BlockSpec(memory_spac...  11.2 us
    pallas_call x1, Pallas kernels, gather_rows(): pl.pallas_call(gather_kernel, in_specs=[IN_SMEM, IN_SMEM, IN_HBM, IN_HBM]...  7.77 us
    pallas_call x1, Pallas kernels, zero_grads(): pl.pallas_call(zero_kernel, in_specs=[pl.BlockSpec(memory_space=pl.ANY)],...  6.7 us
    ppermute x4, waiting for transfers between devices, cross(): lax.ppermute(products[2], ('parts', 'fsdp'), diagonal)  6.17 us
    all_to_all x1, starting transfers between devices, ring_body(): lax.all_to_all(payload, 'fsdp', split_axis=0, concat_axis=0, tiled=True)  5 us
    pallas_call x1, Pallas kernels, adapter_terms(): pl.pallas_call(adapter_kernel, in_specs=[IN_HBM, IN_VMEM, IN_VMEM], out_s...  4.97 us
    all_to_all x1, starting transfers between devices, ring_body(): sums = lax.all_to_all(sent, 'fsdp', split_axis=0, concat_axis=0, tiled=True)  4.89 us
  transfers between devices with their start and end apart: 22, of which 9 were waited for; matrix products, arithmetic and copies ran while one was open for 0% of the time, Pallas kernels for 48%

profile of v9, /device:TPU:0, one launch (start us, length us, event | category | flops | bytes accessed | tf_op | source)
XLA Modules:
  0.0 90.5 jit_solution(13737940896747378217)
XLA Ops:
  0.6 3.1 %collective-permute-start = (bf16[512,1024]{1,0:T(8,128)(2,1)}, bf16[512,1024]{1,0:T(8,128)(2,1)}, u32[]{:S(2)}, u32[]{:S(2)}) collective-permute-start(bf16[512,1024]{1,0:T(8,128)(2,1)} %rest_0_.1), channel_id=1, source_target_pairs={{0,4},{1,3},{4,8},{5,1},{8,12},{9,5},{12,14},{13,9},{14,10},{15,13... | collective-permute-start | bytes 3145736 | tf_op jit(solution)/shard_map/ppermute | solution.py:634
  3.7 1.1 %mask_rows.1.cot.refs_3_ = bf16[256,1024]{1,0:T(8,128)(2,1)S(1)} custom-call(s32[32]{0:T(128)} %live.1, bf16[256,1024]{1,0:T(8,128)(2,1)} %cot.1), custom_call_target="tpu_custom_call" | custom-call | flops 1 | bytes 1 | tf_op jit(solution)/shard_map/mask_rows/pallas_call | solution.py:94
  4.9 1.5 %collective-permute-start.1 = (bf16[256,1024]{1,0:T(8,128)(2,1)S(1)}, bf16[256,1024]{1,0:T(8,128)(2,1)S(1)}, u32[]{:S(2)}, u32[]{:S(2)}) collective-permute-start(bf16[256,1024]{1,0:T(8,128)(2,1)S(1)} %mask_rows.1.cot.refs_3_), channel_id=1, source_target_pairs={{0,16},{16,0},{1,17},{17,1},{2,18},{18,2},{3,19},{19,3},{4,20},{20... | collective-permute-start | bytes 1572872 | tf_op jit(solution)/shard_map/ppermute | solution.py:627
  6.4 7.8 %gather_rows.1._ = bf16[16,144,128]{2,1,0:T(8,128)(2,1)} custom-call(s32[32]{0:T(128)} %adapter_hbm.1, s32[512]{0:T(512)} %storage_hbm.1, bf16[512,8192]{1,0:T(8,128)(2,1)} %down.1, bf16[512,1024]{1,0:T(8,128)(2,1)} %up.1), custom_call_target="tpu_custom_call" | custom-call | flops 1 | bytes 1 | tf_op jit(solution)/shard_map/gather_rows/pallas_call | solution.py:191
  14.1 5.0 %all-to-all-start = ((bf16[16,144,128]{2,1,0:T(8,128)(2,1)}), bf16[16,144,128]{2,1,0:T(8,128)(2,1)S(1)}, u32[]{:S(2)}, u32[]{:S(2)}) async-start(bf16[16,144,128]{2,1,0:T(8,128)(2,1)} %gather_rows.1._), calls=%async_computation | async-start | bytes 1179648 | tf_op jit(solution)/shard_map/all_to_all | solution.py:632
  19.1 0.0 collective-permute-done.1.refs_1_
  19.2 0.0 collective-permute-done.refs_3_.rest_2_
  19.2 2.0 %collective-permute-start.2 = (bf16[512,1024]{1,0:T(8,128)(2,1)}, bf16[512,1024]{1,0:T(8,128)(2,1)}, u32[]{:S(2)}, u32[]{:S(2)}) collective-permute-start(bf16[512,1024]{1,0:T(8,128)(2,1)} %collective-permute-done.refs_3_.rest_2_), channel_id=1, source_target_pairs={{0,4},{1,3},{4,8},{5,1},{8,12},{9,5},{12,14},{13,9},{14,10},{15,13... | collective-permute-start | bytes 3145736 | tf_op jit(solution)/shard_map/ppermute | solution.py:649
  21.1 0.0 collective-permute-start.3
  21.1 0.5 collective-permute-start.4
  21.7 6.7 %zero_grads.1 = (f32[512,8192]{1,0:T(8,128)}, f32[512,1024]{1,0:T(8,128)}) custom-call(bf16[16,144,128]{2,1,0:T(8,128)(2,1)} %gather_rows.1._), custom_call_target="tpu_custom_call" | custom-call | flops 1 | bytes 1 | tf_op jit(solution)/shard_map/zero_grads/pallas_call | solution.py:325
  28.4 0.0 collective-permute-done.3.refs_0_
  28.4 0.0 collective-permute-done.4.refs_2_
  28.4 3.3 %far_products.4 = (bf16[256,512]{1,0:T(8,128)(2,1)}, bf16[256,512]{1,0:T(8,128)(2,1)}, bf16[256,512]{1,0:T(8,128)(2,1)}) custom-call(bf16[256,1024]{1,0:T(8,128)(2,1)S(1)} %collective-permute-done.3.refs_0_, bf16[256,1024]{1,0:T(8,128)(2,1)S(1)} %collective-permute-done.1.refs_1_, bf16[256,1024]{1,0:T(8,128)(2,1)S(1)} %collective-permute-done.4.refs_2_, ...), custom_call_target="tpu_custom_call" | custom-call | flops 1 | bytes 1 | tf_op jit(solution)/shard_map/far_products/pallas_call | solution.py:499
  31.7 0.4 collective-permute-start.6
  32.1 1.0 %collective-permute-start.7 = (bf16[256,512]{1,0:T(8,128)(2,1)}, bf16[256,512]{1,0:T(8,128)(2,1)S(1)}, u32[]{:S(2)}, u32[]{:S(2)}) collective-permute-start(bf16[256,512]{1,0:T(8,128)(2,1)} %get-tuple-element.70), channel_id=1, source_target_pairs={{0,17},{1,16},{2,19},{3,18},{4,21},{5,20},{6,23},{7,22},{8,25},{9,... | collective-permute-start | bytes 786440 | tf_op jit(solution)/shard_map/ppermute | solution.py:621
  33.1 0.8 collective-permute-start.5
  33.9 0.0 collective-permute-start.9
  33.9 0.9 %all-to-all-done.recv = bf16[16,144,128]{2,1,0:T(8,128)(2,1)S(1)} async-done(((bf16[16,144,128]{2,1,0:T(8,128)(2,1)}), bf16[16,144,128]{2,1,0:T(8,128)(2,1)S(1)}, u32[]{:S(2)}, u32[]{:S(2)}) %all-to-all-start) | async-done | bytes 589856 | tf_op jit(solution)/shard_map/all_to_all | solution.py:632
  34.8 5.0 %adapter_terms.1 = (bf16[16,144,128]{2,1,0:T(8,128)(2,1)}, bf16[256,128]{1,0:T(8,128)(2,1)S(1)}) custom-call(bf16[256,8192]{1,0:T(8,128)(2,1)} %x.1, bf16[256,1024]{1,0:T(8,128)(2,1)S(1)} %mask_rows.1.cot.refs_3_, bf16[16,144,128]{2,1,0:T(8,128)(2,1)S(1)} %all-to-all-done.recv), custom_call_target="tpu_custom_call" | custom-call | flops 1 | bytes 1 | tf_op jit(solution)/shard_map/adapter_terms/pallas_call | solution.py:289
  39.8 1.3 %collective-permute-done.6.rest_5_ = bf16[256,512]{1,0:T(8,128)(2,1)S(1)} collective-permute-done((bf16[256,512]{1,0:T(8,128)(2,1)}, bf16[256,512]{1,0:T(8,128)(2,1)S(1)}, u32[]{:S(2)}, u32[]{:S(2)}) %collective-permute-start.6) | collective-permute-done | bytes 262176 | tf_op jit(solution)/shard_map/ppermute | solution.py:620
  41.2 0.0 copy-start
  41.2 3.7 %collective-permute-done.7.rest_6_ = bf16[256,512]{1,0:T(8,128)(2,1)S(1)} collective-permute-done((bf16[256,512]{1,0:T(8,128)(2,1)}, bf16[256,512]{1,0:T(8,128)(2,1)S(1)}, u32[]{:S(2)}, u32[]{:S(2)}) %collective-permute-start.7) | collective-permute-done | bytes 262176 | tf_op jit(solution)/shard_map/ppermute | solution.py:621
  44.9 0.0 copy-start.1
  44.9 0.0 collective-permute-done.5.rest_4_
  44.9 0.0 copy-start.2
  44.9 0.0 collective-permute-done.2.refs_3_.rest_3_
  44.9 1.5 %collective-permute-start.8 = (bf16[512,1024]{1,0:T(8,128)(2,1)}, bf16[512,1024]{1,0:T(8,128)(2,1)S(1)}, u32[]{:S(2)}, u32[]{:S(2)}) collective-permute-start(bf16[512,1024]{1,0:T(8,128)(2,1)} %collective-permute-done.2.refs_3_.rest_3_), channel_id=1, source_target_pairs={{0,4},{1,3},{4,8},{5,1},{8,12},{9,5},{12,14},{13,9},{14,10},{15,13... | collective-permute-start | bytes 3145736 | tf_op jit(solution)/shard_map/ppermute | solution.py:649
  46.4 3.3 %far_products.5 = (bf16[256,512]{1,0:T(8,128)(2,1)}, bf16[256,512]{1,0:T(8,128)(2,1)}, bf16[256,512]{1,0:T(8,128)(2,1)}) custom-call(bf16[256,1024]{1,0:T(8,128)(2,1)S(1)} %collective-permute-done.3.refs_0_, bf16[256,1024]{1,0:T(8,128)(2,1)S(1)} %collective-permute-done.1.refs_1_, bf16[256,1024]{1,0:T(8,128)(2,1)S(1)} %collective-permute-done.4.refs_2_, ...), custom_call_target="tpu_custom_call" | custom-call | flops 1 | bytes 1 | tf_op jit(solution)/shard_map/far_products/pallas_call | solution.py:499
  49.7 0.5 collective-permute-start.11
  50.2 1.3 %collective-permute-start.12 = (bf16[256,512]{1,0:T(8,128)(2,1)}, bf16[256,512]{1,0:T(8,128)(2,1)}, u32[]{:S(2)}, u32[]{:S(2)}) collective-permute-start(bf16[256,512]{1,0:T(8,128)(2,1)} %get-tuple-element.86), channel_id=1, source_target_pairs={{0,17},{1,16},{2,19},{3,18},{4,21},{5,20},{6,23},{7,22},{8,25},{9,... | collective-permute-start | bytes 786440 | tf_op jit(solution)/shard_map/ppermute | solution.py:621
  51.5 0.4 collective-permute-start.10
  51.9 0.0 collective-permute-done.9.rest_1_
  51.9 0.0 copy-done
  51.9 0.0 copy-done.1
  51.9 0.0 copy-done.2
  51.9 4.6 %finish.4.rest_4_ = bf16[256,8192]{1,0:T(8,128)(2,1)} custom-call(bf16[256,1024]{1,0:T(8,128)(2,1)S(1)} %mask_rows.1.cot.refs_3_, bf16[256,128]{1,0:T(8,128)(2,1)S(1)} %get-tuple-element.75.g, bf16[16,144,128]{2,1,0:T(8,128)(2,1)S(1)} %all-to-all-done.recv, bf16[512,1024]{1,0:T(8,128)(2,1)} %rest_0_.1, bf16[512,1024]{1,0:T(8,128)(2,1)} %collective-permute-done.9.rest_1_, ...), custom_call_target="tpu_custom_call" | custom-call | flops 1 | bytes 1 | tf_op jit(solution)/shard_map/finish/pallas_call | solution.py:565
  56.5 3.4 %collective-permute-done.8.refs_4_ = bf16[512,1024]{1,0:T(8,128)(2,1)S(1)} collective-permute-done((bf16[512,1024]{1,0:T(8,128)(2,1)}, bf16[512,1024]{1,0:T(8,128)(2,1)S(1)}, u32[]{:S(2)}, u32[]{:S(2)}) %collective-permute-start.8) | collective-permute-done | bytes 1048608 | tf_op jit(solution)/shard_map/ppermute | solution.py:649
  59.9 2.6 %far_products.6 = (bf16[256,512]{1,0:T(8,128)(2,1)}, bf16[256,512]{1,0:T(8,128)(2,1)}, bf16[256,512]{1,0:T(8,128)(2,1)}, f32[256,512]{1,0:T(8,128)}, bf16[256,1024]{1,0:T(8,128)(2,1)}) custom-call(bf16[256,1024]{1,0:T(8,128)(2,1)S(1)} %collective-permute-done.3.refs_0_, bf16[256,1024]{1,0:T(8,128)(2,1)S(1)} %collective-permute-done.1.refs_1_, ...), custom_call_target="tpu_custom_call" | custom-call | flops 1 | bytes 1 | tf_op jit(solution)/shard_map/far_products/pallas_call | solution.py:499
  62.6 0.0 collective-permute-done.11.rest_2_
  62.6 1.1 %collective-permute-done.12.rest_3_ = bf16[256,512]{1,0:T(8,128)(2,1)} collective-permute-done((bf16[256,512]{1,0:T(8,128)(2,1)}, bf16[256,512]{1,0:T(8,128)(2,1)}, u32[]{:S(2)}, u32[]{:S(2)}) %collective-permute-start.12) | collective-permute-done | bytes 262176 | tf_op jit(solution)/shard_map/ppermute | solution.py:621
  63.7 0.0 collective-permute-done.10.rest_1_
  63.7 0.4 collective-permute-start.13
  64.1 0.6 collective-permute-start.17
  64.7 1.5 %collective-permute-start.18 = (bf16[256,512]{1,0:T(8,128)(2,1)}, bf16[256,512]{1,0:T(8,128)(2,1)}, u32[]{:S(2)}, u32[]{:S(2)}) collective-permute-start(bf16[256,512]{1,0:T(8,128)(2,1)} %get-tuple-element.98), channel_id=1, source_target_pairs={{0,16},{16,0},{1,17},{17,1},{2,18},{18,2},{3,19},{19,3},{4,20},{20... | collective-permute-start | bytes 786440 | tf_op jit(solution)/shard_map/ppermute | solution.py:620
  66.1 0.1 collective-permute-start.19
  66.3 4.9 %all-to-all-start.1 = ((bf16[16,144,128]{2,1,0:T(8,128)(2,1)}), bf16[16,144,128]{2,1,0:T(8,128)(2,1)S(1)}, u32[]{:S(2)}, u32[]{:S(2)}) async-start(bf16[16,144,128]{2,1,0:T(8,128)(2,1)} %get-tuple-element.90), calls=%async_computation.1 | async-start | bytes 1179648 | tf_op jit(solution)/shard_map/all_to_all | solution.py:662
  71.2 2.6 %finish.5.rest_4_ = bf16[256,8192]{1,0:T(8,128)(2,1)} custom-call(bf16[256,1024]{1,0:T(8,128)(2,1)S(1)} %mask_rows.1.cot.refs_3_, bf16[256,128]{1,0:T(8,128)(2,1)S(1)} %get-tuple-element.75.g, bf16[16,144,128]{2,1,0:T(8,128)(2,1)S(1)} %all-to-all-done.recv, f32[256,512]{1,0:T(8,128)} %get-tuple-element.92.rest_0_, ...), custom_call_target="tpu_custom_call", output_to_operand_aliasing={{}: (7, {})} | custom-call | flops 1 | bytes 1 | tf_op jit(solution)/shard_map/finish/pallas_call | solution.py:565
  73.7 0.0 collective-permute-done.13.refs_4_
  73.8 2.6 %far_products.7 = (bf16[256,256]{1,0:T(8,128)(2,1)}, bf16[256,256]{1,0:T(8,128)(2,1)}, bf16[256,256]{1,0:T(8,128)(2,1)}, f32[256,256]{1,0:T(8,128)}) custom-call(bf16[256,1024]{1,0:T(8,128)(2,1)S(1)} %collective-permute-done.3.refs_0_, bf16[256,1024]{1,0:T(8,128)(2,1)S(1)} %collective-permute-done.1.refs_1_, ...), custom_call_target="tpu_custom_call" | custom-call | flops 1 | bytes 1 | tf_op jit(solution)/shard_map/far_products/pallas_call | solution.py:499
  76.3 0.5 collective-permute-start.14
  76.8 0.5 collective-permute-start.15
  77.4 0.0 collective-permute-done.17.rest_1_
  77.4 0.9 %collective-permute-start.16 = (bf16[256,256]{1,0:T(8,128)(2,1)}, bf16[256,256]{1,0:T(8,128)(2,1)S(1)}, u32[]{:S(2)}, u32[]{:S(2)}) collective-permute-start(bf16[256,256]{1,0:T(8,128)(2,1)} %get-tuple-element.104), channel_id=1, source_target_pairs={{0,17},{1,16},{2,19},{3,18},{4,21},{5,20},{6,23},{7,22},{8,25},{9,... | collective-permute-start | bytes 393224 | tf_op jit(solution)/shard_map/ppermute | solution.py:621
  78.3 0.0 collective-permute-done.18.rest_2_
  78.3 0.3 collective-permute-done.19.rest_3_
  78.6 2.4 %finish.6.rest_3_ = bf16[256,8192]{1,0:T(8,128)(2,1)} custom-call(bf16[256,1024]{1,0:T(8,128)(2,1)S(1)} %mask_rows.1.cot.refs_3_, bf16[256,128]{1,0:T(8,128)(2,1)S(1)} %get-tuple-element.75.g, bf16[16,144,128]{2,1,0:T(8,128)(2,1)S(1)} %all-to-all-done.recv, f32[256,256]{1,0:T(8,128)} %get-tuple-element.105.rest_0_, ...), custom_call_target="tpu_custom_call", output_to_operand_aliasing={{}: (7, {})} | custom-call | flops 10000000000 | bytes 1 | tf_op jit(solution)/shard_map/finish/pallas_call | solution.py:565
  81.0 0.0 collective-permute-done.14.rest_0_
  81.0 2.4 %collective-permute-done.15.rest_1_ = bf16[256,256]{1,0:T(8,128)(2,1)S(1)} collective-permute-done((bf16[256,256]{1,0:T(8,128)(2,1)}, bf16[256,256]{1,0:T(8,128)(2,1)S(1)}, u32[]{:S(2)}, u32[]{:S(2)}) %collective-permute-start.15) | collective-permute-done | bytes 131104 | tf_op jit(solution)/shard_map/ppermute | solution.py:620
  83.4 1.1 %collective-permute-done.16.rest_2_ = bf16[256,256]{1,0:T(8,128)(2,1)S(1)} collective-permute-done((bf16[256,256]{1,0:T(8,128)(2,1)}, bf16[256,256]{1,0:T(8,128)(2,1)S(1)}, u32[]{:S(2)}, u32[]{:S(2)}) %collective-permute-start.16) | collective-permute-done | bytes 131104 | tf_op jit(solution)/shard_map/ppermute | solution.py:621
  84.5 1.7 %finish.7 = bf16[256,8192]{1,0:T(8,128)(2,1)} custom-call(bf16[256,1024]{1,0:T(8,128)(2,1)S(1)} %mask_rows.1.cot.refs_3_, bf16[256,128]{1,0:T(8,128)(2,1)S(1)} %get-tuple-element.75.g, bf16[16,144,128]{2,1,0:T(8,128)(2,1)S(1)} %all-to-all-done.recv, bf16[256,256]{1,0:T(8,128)(2,1)S(1)} %collective-permute-done.14.rest_0_, ...), custom_call_target="tpu_custom_call", output_to_operand_aliasing={{}: (6, {})} | custom-call | flops 1 | bytes 1 | tf_op jit(solution)/shard_map/finish/pallas_call | solution.py:565
  86.2 0.5 all-to-all-done.1.recv
  86.7 3.7 %scatter_rows.1 = (f32[512,8192]{1,0:T(8,128)}, f32[512,1024]{1,0:T(8,128)}) custom-call(s32[32]{0:T(128)} %adapter_hbm.1, s32[512]{0:T(512)} %storage_hbm.1, bf16[16,144,128]{2,1,0:T(8,128)(2,1)S(1)} %all-to-all-done.1.recv, f32[512,8192]{1,0:T(8,128)} %get-tuple-element.109._down, ...), custom_call_target="tpu_custom_call", output_to_operand_aliasing={{0}: (3, {}), {1}: (4, {})} | custom-call | flops 1 | bytes 1 | tf_op jit(solution)/shard_map/scatter_rows/pallas_call | solution.py:437
Async XLA Ops:
  0.6 18.5 %collective-permute-start = (bf16[512,1024]{1,0:T(8,128)(2,1)}, bf16[512,1024]{1,0:T(8,128)(2,1)}, u32[]{:S(2)}, u32[]{:S(2)}) collective-permute-start(bf16[512,1024]{1,0:T(8,128)(2,1)} %rest_0_.1), channel_id=1, source_target_pairs={{0,4},{1,3},{4,8},{5,1},{8,12},{9,5},{12,14},{13,9},{14,10},{15,13... | collective-permute-start | bytes 3145736 | tf_op jit(solution)/shard_map/ppermute | solution.py:634
  4.9 14.3 %collective-permute-start.1 = (bf16[256,1024]{1,0:T(8,128)(2,1)S(1)}, bf16[256,1024]{1,0:T(8,128)(2,1)S(1)}, u32[]{:S(2)}, u32[]{:S(2)}) collective-permute-start(bf16[256,1024]{1,0:T(8,128)(2,1)S(1)} %mask_rows.1.cot.refs_3_), channel_id=1, source_target_pairs={{0,16},{16,0},{1,17},{17,1},{2,18},{18,2},{3,19},{19,3},{4,20},{20... | collective-permute-start | bytes 1572872 | tf_op jit(solution)/shard_map/ppermute | solution.py:627
  14.1 20.7 %all-to-all-start = ((bf16[16,144,128]{2,1,0:T(8,128)(2,1)}), bf16[16,144,128]{2,1,0:T(8,128)(2,1)S(1)}, u32[]{:S(2)}, u32[]{:S(2)}) async-start(bf16[16,144,128]{2,1,0:T(8,128)(2,1)} %gather_rows.1._), calls=%async_computation | async-start | bytes 1179648 | tf_op jit(solution)/shard_map/all_to_all | solution.py:632
  19.2 25.7 %collective-permute-start.2 = (bf16[512,1024]{1,0:T(8,128)(2,1)}, bf16[512,1024]{1,0:T(8,128)(2,1)}, u32[]{:S(2)}, u32[]{:S(2)}) collective-permute-start(bf16[512,1024]{1,0:T(8,128)(2,1)} %collective-permute-done.refs_3_.rest_2_), channel_id=1, source_target_pairs={{0,4},{1,3},{4,8},{5,1},{8,12},{9,5},{12,14},{13,9},{14,10},{15,13... | collective-permute-start | bytes 3145736 | tf_op jit(solution)/shard_map/ppermute | solution.py:649
  21.1 7.2 %collective-permute-start.3 = (bf16[256,1024]{1,0:T(8,128)(2,1)S(1)}, bf16[256,1024]{1,0:T(8,128)(2,1)S(1)}, u32[]{:S(2)}, u32[]{:S(2)}) collective-permute-start(bf16[256,1024]{1,0:T(8,128)(2,1)S(1)} %mask_rows.1.cot.refs_3_), channel_id=1, source_target_pairs={{0,1},{1,0},{2,3},{3,2},{4,5},{5,4},{6,7},{7,6},{8,9},{9,8},{10,11... | collective-permute-start | bytes 1572872 | tf_op jit(solution)/shard_map/ppermute | solution.py:626
  21.1 7.2 %collective-permute-start.4 = (bf16[256,1024]{1,0:T(8,128)(2,1)S(1)}, bf16[256,1024]{1,0:T(8,128)(2,1)S(1)}, u32[]{:S(2)}, u32[]{:S(2)}) collective-permute-start(bf16[256,1024]{1,0:T(8,128)(2,1)S(1)} %collective-permute-done.1.refs_1_), channel_id=1, source_target_pairs={{0,1},{1,0},{2,3},{3,2},{4,5},{5,4},{6,7},{7,6},{8,9},{9,8},{10,11... | collective-permute-start | bytes 1572872 | tf_op jit(solution)/shard_map/ppermute | solution.py:641
  31.7 9.5 %collective-permute-start.6 = (bf16[256,512]{1,0:T(8,128)(2,1)}, bf16[256,512]{1,0:T(8,128)(2,1)S(1)}, u32[]{:S(2)}, u32[]{:S(2)}) collective-permute-start(bf16[256,512]{1,0:T(8,128)(2,1)} %get-tuple-element.69), channel_id=1, source_target_pairs={{0,16},{16,0},{1,17},{17,1},{2,18},{18,2},{3,19},{19,3},{4,20},{20... | collective-permute-start | bytes 786440 | tf_op jit(solution)/shard_map/ppermute | solution.py:620
  32.1 12.8 %collective-permute-start.7 = (bf16[256,512]{1,0:T(8,128)(2,1)}, bf16[256,512]{1,0:T(8,128)(2,1)S(1)}, u32[]{:S(2)}, u32[]{:S(2)}) collective-permute-start(bf16[256,512]{1,0:T(8,128)(2,1)} %get-tuple-element.70), channel_id=1, source_target_pairs={{0,17},{1,16},{2,19},{3,18},{4,21},{5,20},{6,23},{7,22},{8,25},{9,... | collective-permute-start | bytes 786440 | tf_op jit(solution)/shard_map/ppermute | solution.py:621
  33.1 11.7 %collective-permute-start.5 = (bf16[256,512]{1,0:T(8,128)(2,1)}, bf16[256,512]{1,0:T(8,128)(2,1)S(1)}, u32[]{:S(2)}, u32[]{:S(2)}) collective-permute-start(bf16[256,512]{1,0:T(8,128)(2,1)} %get-tuple-element.64), channel_id=1, source_target_pairs={{0,1},{1,0},{2,3},{3,2},{4,5},{5,4},{6,7},{7,6},{8,9},{9,8},{10,11... | collective-permute-start | bytes 786440 | tf_op jit(solution)/shard_map/ppermute | solution.py:619
  33.9 18.0 %collective-permute-start.9 = (bf16[512,1024]{1,0:T(8,128)(2,1)}, bf16[512,1024]{1,0:T(8,128)(2,1)}, u32[]{:S(2)}, u32[]{:S(2)}) collective-permute-start(bf16[512,1024]{1,0:T(8,128)(2,1)} %rest_0_.1), channel_id=1, source_target_pairs={{0,1},{1,0},{2,3},{3,2},{4,5},{5,4},{6,7},{7,6},{8,9},{9,8},{10,11... | collective-permute-start | bytes 3145736 | tf_op jit(solution)/shard_map/ppermute | solution.py:624
  41.2 10.8 %copy-start = (bf16[256,512]{1,0:T(8,128)(2,1)}, bf16[256,512]{1,0:T(8,128)(2,1)S(1)}, u32[]{:S(2)}) copy-start(bf16[256,512]{1,0:T(8,128)(2,1)S(1)} %collective-permute-done.6.rest_5_) | copy-start | bytes 786436
  44.9 7.1 %copy-start.1 = (bf16[256,512]{1,0:T(8,128)(2,1)}, bf16[256,512]{1,0:T(8,128)(2,1)S(1)}, u32[]{:S(2)}) copy-start(bf16[256,512]{1,0:T(8,128)(2,1)S(1)} %collective-permute-done.7.rest_6_) | copy-start | bytes 786436
  44.9 7.1 %copy-start.2 = (bf16[256,512]{1,0:T(8,128)(2,1)}, bf16[256,512]{1,0:T(8,128)(2,1)S(1)}, u32[]{:S(2)}) copy-start(bf16[256,512]{1,0:T(8,128)(2,1)S(1)} %collective-permute-done.5.rest_4_) | copy-start | bytes 786436
  44.9 15.1 %collective-permute-start.8 = (bf16[512,1024]{1,0:T(8,128)(2,1)}, bf16[512,1024]{1,0:T(8,128)(2,1)S(1)}, u32[]{:S(2)}, u32[]{:S(2)}) collective-permute-start(bf16[512,1024]{1,0:T(8,128)(2,1)} %collective-permute-done.2.refs_3_.rest_3_), channel_id=1, source_target_pairs={{0,4},{1,3},{4,8},{5,1},{8,12},{9,5},{12,14},{13,9},{14,10},{15,13... | collective-permute-start | bytes 3145736 | tf_op jit(solution)/shard_map/ppermute | solution.py:649
  49.7 12.9 %collective-permute-start.11 = (bf16[256,512]{1,0:T(8,128)(2,1)}, bf16[256,512]{1,0:T(8,128)(2,1)}, u32[]{:S(2)}, u32[]{:S(2)}) collective-permute-start(bf16[256,512]{1,0:T(8,128)(2,1)} %get-tuple-element.85), channel_id=1, source_target_pairs={{0,16},{16,0},{1,17},{17,1},{2,18},{18,2},{3,19},{19,3},{4,20},{20... | collective-permute-start | bytes 786440 | tf_op jit(solution)/shard_map/ppermute | solution.py:620
  50.2 13.5 %collective-permute-start.12 = (bf16[256,512]{1,0:T(8,128)(2,1)}, bf16[256,512]{1,0:T(8,128)(2,1)}, u32[]{:S(2)}, u32[]{:S(2)}) collective-permute-start(bf16[256,512]{1,0:T(8,128)(2,1)} %get-tuple-element.86), channel_id=1, source_target_pairs={{0,17},{1,16},{2,19},{3,18},{4,21},{5,20},{6,23},{7,22},{8,25},{9,... | collective-permute-start | bytes 786440 | tf_op jit(solution)/shard_map/ppermute | solution.py:621
  51.5 12.2 %collective-permute-start.10 = (bf16[256,512]{1,0:T(8,128)(2,1)}, bf16[256,512]{1,0:T(8,128)(2,1)}, u32[]{:S(2)}, u32[]{:S(2)}) collective-permute-start(bf16[256,512]{1,0:T(8,128)(2,1)} %get-tuple-element.73), channel_id=1, source_target_pairs={{0,1},{1,0},{2,3},{3,2},{4,5},{5,4},{6,7},{7,6},{8,9},{9,8},{10,11... | collective-permute-start | bytes 786440 | tf_op jit(solution)/shard_map/ppermute | solution.py:619
  63.7 10.0 %collective-permute-start.13 = (bf16[256,1024]{1,0:T(8,128)(2,1)}, bf16[256,1024]{1,0:T(8,128)(2,1)}, u32[]{:S(2)}, u32[]{:S(2)}) collective-permute-start(bf16[256,1024]{1,0:T(8,128)(2,1)} %get-tuple-element.91), channel_id=1, source_target_pairs={{0,4},{1,3},{4,8},{5,1},{8,12},{9,5},{12,14},{13,9},{14,10},{15,13... | collective-permute-start | bytes 1572872 | tf_op jit(solution)/shard_map/ppermute | solution.py:660
  64.1 13.3 %collective-permute-start.17 = (bf16[256,512]{1,0:T(8,128)(2,1)}, bf16[256,512]{1,0:T(8,128)(2,1)}, u32[]{:S(2)}, u32[]{:S(2)}) collective-permute-start(bf16[256,512]{1,0:T(8,128)(2,1)} %get-tuple-element.97), channel_id=1, source_target_pairs={{0,1},{1,0},{2,3},{3,2},{4,5},{5,4},{6,7},{7,6},{8,9},{9,8},{10,11... | collective-permute-start | bytes 786440 | tf_op jit(solution)/shard_map/ppermute | solution.py:619
  64.7 13.6 %collective-permute-start.18 = (bf16[256,512]{1,0:T(8,128)(2,1)}, bf16[256,512]{1,0:T(8,128)(2,1)}, u32[]{:S(2)}, u32[]{:S(2)}) collective-permute-start(bf16[256,512]{1,0:T(8,128)(2,1)} %get-tuple-element.98), channel_id=1, source_target_pairs={{0,16},{16,0},{1,17},{17,1},{2,18},{18,2},{3,19},{19,3},{4,20},{20... | collective-permute-start | bytes 786440 | tf_op jit(solution)/shard_map/ppermute | solution.py:620
  66.1 12.4 %collective-permute-start.19 = (bf16[256,512]{1,0:T(8,128)(2,1)}, bf16[256,512]{1,0:T(8,128)(2,1)}, u32[]{:S(2)}, u32[]{:S(2)}) collective-permute-start(bf16[256,512]{1,0:T(8,128)(2,1)} %get-tuple-element.99), channel_id=1, source_target_pairs={{0,17},{1,16},{2,19},{3,18},{4,21},{5,20},{6,23},{7,22},{8,25},{9,... | collective-permute-start | bytes 786440 | tf_op jit(solution)/shard_map/ppermute | solution.py:621
  66.3 20.4 %all-to-all-start.1 = ((bf16[16,144,128]{2,1,0:T(8,128)(2,1)}), bf16[16,144,128]{2,1,0:T(8,128)(2,1)S(1)}, u32[]{:S(2)}, u32[]{:S(2)}) async-start(bf16[16,144,128]{2,1,0:T(8,128)(2,1)} %get-tuple-element.90), calls=%async_computation.1 | async-start | bytes 1179648 | tf_op jit(solution)/shard_map/all_to_all | solution.py:662
  76.3 4.7 %collective-permute-start.14 = (bf16[256,256]{1,0:T(8,128)(2,1)}, bf16[256,256]{1,0:T(8,128)(2,1)S(1)}, u32[]{:S(2)}, u32[]{:S(2)}) collective-permute-start(bf16[256,256]{1,0:T(8,128)(2,1)} %get-tuple-element.102), channel_id=1, source_target_pairs={{0,1},{1,0},{2,3},{3,2},{4,5},{5,4},{6,7},{7,6},{8,9},{9,8},{10,11... | collective-permute-start | bytes 393224 | tf_op jit(solution)/shard_map/ppermute | solution.py:619
  76.8 6.6 %collective-permute-start.15 = (bf16[256,256]{1,0:T(8,128)(2,1)}, bf16[256,256]{1,0:T(8,128)(2,1)S(1)}, u32[]{:S(2)}, u32[]{:S(2)}) collective-permute-start(bf16[256,256]{1,0:T(8,128)(2,1)} %get-tuple-element.103), channel_id=1, source_target_pairs={{0,16},{16,0},{1,17},{17,1},{2,18},{18,2},{3,19},{19,3},{4,20},{20... | collective-permute-start | bytes 393224 | tf_op jit(solution)/shard_map/ppermute | solution.py:620
  77.4 7.1 %collective-permute-start.16 = (bf16[256,256]{1,0:T(8,128)(2,1)}, bf16[256,256]{1,0:T(8,128)(2,1)S(1)}, u32[]{:S(2)}, u32[]{:S(2)}) collective-permute-start(bf16[256,256]{1,0:T(8,128)(2,1)} %get-tuple-element.104), channel_id=1, source_target_pairs={{0,17},{1,16},{2,19},{3,18},{4,21},{5,20},{6,23},{7,22},{8,25},{9,... | collective-permute-start | bytes 393224 | tf_op jit(solution)/shard_map/ppermute | solution.py:621
